TPU v7x, 32 devices: a whole 2x2x4 slice. The times are simulated.
32 devices in a mesh: mesh: 16 (over z, y, x), col: 2 (over core).
Axes of the slice: x: 2, y: 2, z: 4, core: 2. Of those that a mesh axis runs over, the one named last changes fastest.
Arguments:
- basis: bfloat16 [49152, 512], P(('mesh', 'col')), may hold values from -6 to 6
- jac_blocks: bfloat16 [768, 8, 64, 64], P(('mesh', 'col')), may hold values from -0.25 to 0.25
- block_cols: int32 [768, 8], P(('mesh', 'col')), may hold values from 0 to 767, as said below
- live_slots: int32 [768], P(('mesh', 'col')), may hold values from 1 to 8
- accumulation: float32 [49152], P(('mesh', 'col')), may hold values from 0.5 to 4
Outputs:
- image: bfloat16 [49152, 512], P(('mesh', 'col'))
- projected: float32 [512, 512], P('mesh', 'col')
Inputs may be any that keep to these rules, and one draw needn't show every extreme that they name: `block_cols`: each block row's column blocks lie within 2 block rows of it, and some lie exactly 2 away on either side.
All inputs are finite; a program needn't handle non-finite values.
Results may differ from a plain program's by a relative error of at most 0.003.
Values may be sent and summed in bfloat16 or wider, within the bound.
No kernel may reach another device: no remote copies, remote signals or barrier semaphores. Data moves between devices by JAX's collectives and lax.ppermute only.
A program may use at most 64 MiB of HBM per device.

v0:
```python
import jax
import jax.numpy as jnp
from jax import lax
from jax.sharding import PartitionSpec as P

REACH = 2


def with_halo(block, sides, width):
    for axis, dim in sides:
        count = lax.axis_size(axis)
        forward = [(i, i + 1) for i in range(count - 1)]
        backward = [(target, source) for source, target in forward]
        low = lax.ppermute(
            lax.slice_in_dim(block, block.shape[dim] - width, None, axis=dim), axis, forward
        )
        high = lax.ppermute(lax.slice_in_dim(block, 0, width, axis=dim), axis, backward)
        block = jnp.concatenate([low, block, high], axis=dim)
    return block


def local(basis, jac_blocks, block_cols, live_slots, accumulation):
    nrows, width = basis.shape
    nblk, slots, bsize, _ = jac_blocks.shape
    padded = with_halo(basis, ((("mesh", "col"), 0),), REACH * bsize)
    first = lax.axis_index(("mesh", "col")) * nblk
    local_cols = block_cols - first + REACH
    pblocks = padded.reshape(nblk + 2 * REACH, bsize, width)
    picked = pblocks[local_cols]
    keep = lax.broadcasted_iota(jnp.int32, (nblk, slots), 1) < live_slots[:, None]
    masked = jnp.where(keep[:, :, None, None], jac_blocks, jnp.zeros_like(jac_blocks))
    coupled = jnp.einsum("rsab,rsbk->rak", masked, picked, preferred_element_type=jnp.float32)
    coupled = coupled.reshape(nrows, width)
    image = (coupled + accumulation[:, None] * basis.astype(jnp.float32)).astype(jnp.bfloat16)
    mesh_count = lax.axis_size("mesh")
    col_count = lax.axis_size("col")
    total_rows = nrows * mesh_count * col_count
    dims = (((0,), (0,)), ((), ()))
    shares = lax.psum_scatter(
        lax.dot_general(basis, image, dims, preferred_element_type=jnp.float32),
        "mesh",
        scatter_dimension=0,
        tiled=True,
    )
    summed = lax.psum_scatter(shares, "col", scatter_dimension=1, tiled=True)
    projected = summed * (1.0 / total_rows)
    return (image, projected)


def solution(mesh):
    return jax.shard_map(
        local,
        mesh=mesh,
        in_specs=(
            P(("mesh", "col"), None),
            P(("mesh", "col"), None, None, None),
            P(("mesh", "col"), None),
            P(("mesh", "col")),
            P(("mesh", "col")),
        ),
        out_specs=(P(("mesh", "col"), None), P("mesh", "col")),
        check_vma=False,
    )
```

profile of v0, /device:TPU:0, one launch (start us, length us, event | category | flops | bytes accessed | tf_op | source)
XLA Modules:
  0.0 134.8 jit_solution(7071872574907153587)
XLA Ops:
  7.2 0.0 reduce-scatter.7.cloned.1.call-start
  7.2 1.0 fusion.6
  8.2 2.4 %collective-permute-start = (bf16[128,512]{1,0:T(8,128)(2,1)S(1)}, bf16[128,512]{1,0:T(8,128)(2,1)S(1)}, u32[]{:S(2)}, u32[]{:S(2)}) collective-permute-start(bf16[128,512]{1,0:T(8,128)(2,1)S(1)} %get-tuple-element.8), channel_id=1, source_target_pairs={{0,1},{1,2},{2,3},{3,4},{4,5},{5,6},{6,7},{7,8},{8,9},{9,10},{10,1... | collective-permute-start | bytes 393224 | tf_op jit(solution)/shard_map/ppermute | solution.py:14
  10.6 1.3 collective-permute-start.1
  11.9 0.7 compare_select_fusion
  12.6 0.7 iota_compare_fusion
  13.3 0.1 copy.10
  13.4 0.1 reshape.34
  13.5 2.4 %collective-permute-done.1 = bf16[128,512]{1,0:T(8,128)(2,1)S(1)} collective-permute-done((bf16[128,512]{1,0:T(8,128)(2,1)S(1)}, bf16[128,512]{1,0:T(8,128)(2,1)S(1)}, u32[]{:S(2)}, u32[]{:S(2)}) %collective-permute-start.1) | collective-permute-done | bytes 131104 | tf_op jit(solution)/shard_map/ppermute | solution.py:17
  15.9 1.5 %pad_maximum_fusion = bf16[1792,512]{1,0:T(8,128)(2,1)S(1)} fusion(bf16[128,512]{1,0:T(8,128)(2,1)S(1)} %collective-permute-done.1, bf16[1536,512]{1,0:T(8,128)(2,1)} %param.5, bf16[128,512]{1,0:T(8,128)(2,1)S(1)} %collective-permute-done), kind=kLoop, calls=%fused_computation.6 | loop fusion | flops 5505024 | bytes 3670016 | tf_op jit(solution)/shard_map/concatenate | solution.py:18
  17.4 8.2 %gather_fusion = bf16[192,64,512]{2,1,0:T(8,128)(2,1)} fusion(bf16[28,64,512]{2,1,0:T(8,128)(2,1)S(1)} %bitcast.15, s32[1024]{0:T(1024)S(1)} %pad_clamp_fusion), kind=kCustom, calls=%fused_computation | custom fusion | bytes 25166592 | tf_op jit(solution)/shard_map/gather | solution.py:29
  25.7 8.3 %fusion.1 = f32[24,64,512,1]{2,1,3,0:T(8,128)S(1)} fusion(bf16[24,8,64,512]{3,2,1,0:T(8,128)(2,1)} %bitcast.16, bf16[24,8,64,64]{3,2,1,0:T(8,128)(2,1)} %param.6, pred[24,8]{1,0:T(8,128)(4,1)S(1)} %iota_compare_fusion), kind=kOutput, calls=%fused_computation.3 | convolution fusion | flops 806092800 | bytes 17301696 | tf_op jit(solution)/shard_map/rsab,rsbk->rak/dot_general | solution.py:32
  34.0 0.4 fusion
  34.4 0.0 copy-start.1
  34.4 1.0 convolution_bitcast_fusion
  35.4 1.3 copy.13
  36.7 0.0 reduce-scatter.7.cloned.1.call-update
  36.8 0.0 reduce-scatter.5.cloned.1.call-start
  36.8 83.2 %reduce-scatter.7.cloned.1.call-done = f32[32,512]{1,0:T(8,128)} async-done(((f32[512,512]{1,0:T(8,128)}), f32[32,512]{1,0:T(8,128)}) %reduce-scatter.7.cloned.1.call-update) | async-done | bytes 65552
  120.0 1.7 %copy.14 = f32[32,512]{0,1:T(8,128)} copy(f32[32,512]{1,0:T(8,128)} %reduce-scatter.7.cloned.1.call-done) | data formatting | bytes 131072
  121.7 0.0 reduce-scatter.5.cloned.1.call-update
  121.7 4.7 %reduce-scatter.5.cloned.1.call-done = f32[32,256]{0,1:T(8,128)} async-done(((f32[32,512]{0,1:T(8,128)}), f32[32,256]{0,1:T(8,128)}) %reduce-scatter.5.cloned.1.call-update) | async-done | bytes 32784 | tf_op jit(solution)/shard_map/reduce_scatter | solution.py:45
  126.4 0.9 broadcast_multiply_fusion
  127.3 0.7 copy.11
  (7 shorter events, 0.0 us)
Async XLA Ops:
  7.2 112.8 %reduce-scatter.7.cloned.1.call-start = ((), (), s32[]{:S(2)}) async-start(), calls=%async_computation.3 | async-start | bytes 1114112
  8.2 5.3 %collective-permute-start = (bf16[128,512]{1,0:T(8,128)(2,1)S(1)}, bf16[128,512]{1,0:T(8,128)(2,1)S(1)}, u32[]{:S(2)}, u32[]{:S(2)}) collective-permute-start(bf16[128,512]{1,0:T(8,128)(2,1)S(1)} %get-tuple-element.8), channel_id=1, source_target_pairs={{0,1},{1,2},{2,3},{3,4},{4,5},{5,6},{6,7},{7,8},{8,9},{9,10},{10,1... | collective-permute-start | bytes 393224 | tf_op jit(solution)/shard_map/ppermute | solution.py:14
  10.6 5.3 %collective-permute-start.1 = (bf16[128,512]{1,0:T(8,128)(2,1)S(1)}, bf16[128,512]{1,0:T(8,128)(2,1)S(1)}, u32[]{:S(2)}, u32[]{:S(2)}) collective-permute-start(bf16[128,512]{1,0:T(8,128)(2,1)S(1)} %get-tuple-element.9), channel_id=1, source_target_pairs={{1,0},{2,1},{3,2},{4,3},{5,4},{6,5},{7,6},{8,7},{9,8},{10,9},{11,1... | collective-permute-start | bytes 393224 | tf_op jit(solution)/shard_map/ppermute | solution.py:17
  25.7 8.3 %copy-start = (bf16[1536,512]{1,0:T(8,128)(2,1)S(1)}, bf16[1536,512]{1,0:T(8,128)(2,1)}, u32[]{:S(2)}) copy-start(bf16[1536,512]{1,0:T(8,128)(2,1)} %param.5) | copy-start | bytes 4718596
  25.7 8.3 %copy-start.2 = (f32[1536]{0:T(1024)S(1)}, f32[1536]{0:T(1024)}, u32[]{:S(2)}) copy-start(f32[1536]{0:T(1024)} %param.9) | copy-start | bytes 18436
  34.4 2.3 %copy-start.1 = (bf16[1536,512]{1,0:T(8,128)(2,1)}, bf16[1536,512]{1,0:T(8,128)(2,1)S(1)}, u32[]{:S(2)}) copy-start(bf16[1536,512]{1,0:T(8,128)(2,1)S(1)} %fusion) | copy-start | bytes 4718596
  36.8 89.6 %reduce-scatter.5.cloned.1.call-start = ((), (), s32[]{:S(2)}) async-start(), calls=%async_computation.2 | async-start | bytes 393216 | tf_op jit(solution)/shard_map/reduce_scatter | solution.py:45
Sparse Core Ops, SparseCore 0:
  36.9 83.0 reduce-scatter.6
  122.3 4.0 reduce-scatter.4
where the time goes:
time: 135 us
  waiting for transfers between devices  90.3 us (67%)
  between operations  14.1 us (10%)
  local copies, waits for them, and re-layouts  13.1 us (10%)
  matrix products  9.26 us (7%)
  other arithmetic  4.29 us (3%)
  starting transfers between devices  3.74 us (3%)
    unnamed x3, waiting for transfers between devices  83.2 us
    dot_general x1, matrix products, local(): jnp.einsum('rsab,rsbk->rak', masked, picked, preferred_element_type=jnp.f...  8.26 us
    gather x1, local copies, waits for them, and re-layouts, local(): picked = pblocks[local_cols]  8.23 us
    reduce_scatter x1, waiting for transfers between devices, local(): summed = lax.psum_scatter(shares, 'col', scatter_dimension=1, tiled=True)  4.67 us
    unnamed x9, local copies, waits for them, and re-layouts  3.69 us
  transfers between devices with their start and end apart: 4, of which 3 were waited for; matrix products, arithmetic and copies ran while one was open for 1% of the time, Pallas kernels for 0%

commit v1 on v0

--- a/solution.py
+++ b/solution.py
@@ -4,6 +4,7 @@
 from jax.sharding import PartitionSpec as P
 
 REACH = 2
+AXES = ("mesh", "col")
 
 
 def with_halo(block, sides, width):
@@ -22,8 +23,8 @@
 def local(basis, jac_blocks, block_cols, live_slots, accumulation):
     nrows, width = basis.shape
     nblk, slots, bsize, _ = jac_blocks.shape
-    padded = with_halo(basis, ((("mesh", "col"), 0),), REACH * bsize)
-    first = lax.axis_index(("mesh", "col")) * nblk
+    padded = with_halo(basis, ((AXES, 0),), REACH * bsize)
+    first = lax.axis_index(AXES) * nblk
     local_cols = block_cols - first + REACH
     pblocks = padded.reshape(nblk + 2 * REACH, bsize, width)
     picked = pblocks[local_cols]
@@ -36,14 +37,14 @@
     col_count = lax.axis_size("col")
     total_rows = nrows * mesh_count * col_count
     dims = (((0,), (0,)), ((), ()))
-    shares = lax.psum_scatter(
-        lax.dot_general(basis, image, dims, preferred_element_type=jnp.float32),
-        "mesh",
-        scatter_dimension=0,
-        tiled=True,
+    part = lax.dot_general(basis, image, dims, preferred_element_type=jnp.float32)
+    part = part.astype(jnp.bfloat16)
+    part = part.reshape(mesh_count, width // mesh_count, col_count, width // col_count)
+    part = part.transpose(0, 2, 1, 3).reshape(
+        mesh_count * col_count, width // mesh_count, width // col_count
     )
-    summed = lax.psum_scatter(shares, "col", scatter_dimension=1, tiled=True)
-    projected = summed * (1.0 / total_rows)
+    got = lax.all_to_all(part, AXES, 0, 0, tiled=True)
+    projected = jnp.sum(got.astype(jnp.float32), axis=0) * (1.0 / total_rows)
     return (image, projected)
 
 
@@ -52,12 +53,12 @@
         local,
         mesh=mesh,
         in_specs=(
-            P(("mesh", "col"), None),
-            P(("mesh", "col"), None, None, None),
-            P(("mesh", "col"), None),
-            P(("mesh", "col")),
-            P(("mesh", "col")),
+            P(AXES, None),
+            P(AXES, None, None, None),
+            P(AXES, None),
+            P(AXES),
+            P(AXES),
         ),
-        out_specs=(P(("mesh", "col"), None), P("mesh", "col")),
+        out_specs=(P(AXES, None), P("mesh", "col")),
         check_vma=False,
     )

time: 135 us -> 55.4 us (0.41)
  waiting for transfers between devices: 90.3 us -> 2.43 us
  blocking collectives: 0 us -> 25.1 us
  between operations: 14.1 us -> 0.75 us
  local copies, waits for them, and re-layouts: 13.1 us -> 9.82 us
    unnamed x3 -> x0, waiting for transfers between devices: 83.2 us -> none
    all_to_all x0 -> x1, blocking collectives: none -> 25.1 us  [local(): got = lax.all_to_all(part, AXES, 0, 0, tiled=True)]
    reduce_scatter x1 -> x0, waiting for transfers between devices: 4.67 us -> none  [local(): summed = lax.psum_scatter(shares, 'col', scatter_dimension=1, tiled=True)]
    unnamed x9 -> x6, local copies, waits for them, and re-layouts: 3.69 us -> 0.01 us
  transfers between devices with their start and end apart: 4 -> 2, of which waited for: 3 -> 1; matrix products, arithmetic and copies ran while one was open for 1% -> 3% of each run, Pallas kernels for 0% -> 0%
where the time goes in v1:
time: 55.4 us; the launch traced here: 55.2 us
  blocking collectives  25.1 us (45%)
  local copies, waits for them, and re-layouts  9.82 us (18%)
  matrix products  9.27 us (17%)
  other arithmetic  4.08 us (7%)
  starting transfers between devices  3.66 us (7%)
  waiting for transfers between devices  2.43 us (4%)
  between operations  0.75 us (1%)
    all_to_all x1, blocking collectives, local(): got = lax.all_to_all(part, AXES, 0, 0, tiled=True)  25.1 us
    dot_general x1, matrix products, local(): jnp.einsum('rsab,rsbk->rak', masked, picked, preferred_element_type=jnp.f...  8.27 us
    gather x1, local copies, waits for them, and re-layouts, local(): picked = pblocks[local_cols]  8.24 us
    ppermute x1, waiting for transfers between devices, with_halo(): lax.ppermute(lax.slice_in_dim(block, 0, width, axis=dim), axis, backward)  2.43 us
    ppermute x1, starting transfers between devices, with_halo(): lax.ppermute(lax.slice_in_dim(block, block.shape[dim] - width, None, axis...  2.36 us
    concatenate x1, other arithmetic, with_halo(): block = jnp.concatenate([low, block, high], axis=dim)  1.53 us
    ppermute x1, starting transfers between devices, with_halo(): lax.ppermute(lax.slice_in_dim(block, 0, width, axis=dim), axis, backward)  1.29 us
  transfers between devices with their start and end apart: 2, of which 1 were waited for; matrix products, arithmetic and copies ran while one was open for 3% of the time, Pallas kernels for 0%

profile of v1, /device:TPU:0, one launch (start us, length us, event | category | flops | bytes accessed | tf_op | source)
XLA Modules:
  0.0 55.2 jit_solution(1209230310840172942)
XLA Ops:
  0.6 1.0 %fusion.7 = (bf16[128,512]{1,0:T(8,128)(2,1)S(1)}, bf16[128,512]{1,0:T(8,128)(2,1)S(1)}) fusion(bf16[1536,512]{1,0:T(8,128)(2,1)} %param.5), kind=kLoop, calls=%fused_computation.16 | loop fusion | bytes 524288 | tf_op jit(solution)/shard_map/slice | solution.py:16
  1.6 2.4 %collective-permute-start = (bf16[128,512]{1,0:T(8,128)(2,1)S(1)}, bf16[128,512]{1,0:T(8,128)(2,1)S(1)}, u32[]{:S(2)}, u32[]{:S(2)}) collective-permute-start(bf16[128,512]{1,0:T(8,128)(2,1)S(1)} %get-tuple-element.2), channel_id=1, source_target_pairs={{0,1},{1,2},{2,3},{3,4},{4,5},{5,6},{6,7},{7,8},{8,9},{9,10},{10,1... | collective-permute-start | bytes 393224 | tf_op jit(solution)/shard_map/ppermute | solution.py:15
  4.0 1.3 %collective-permute-start.1 = (bf16[128,512]{1,0:T(8,128)(2,1)S(1)}, bf16[128,512]{1,0:T(8,128)(2,1)S(1)}, u32[]{:S(2)}, u32[]{:S(2)}) collective-permute-start(bf16[128,512]{1,0:T(8,128)(2,1)S(1)} %get-tuple-element.3), channel_id=1, source_target_pairs={{1,0},{2,1},{3,2},{4,3},{5,4},{6,5},{7,6},{8,7},{9,8},{10,9},{11,1... | collective-permute-start | bytes 393224 | tf_op jit(solution)/shard_map/ppermute | solution.py:18
  5.3 0.7 %compare_select_fusion = s32[24,8]{0,1:T(8,128)S(1)} fusion(s32[24,8]{0,1:T(8,128)} %param.7, s32[]{:T(128)S(6)} %mul.21), kind=kLoop, calls=%fused_computation.13 | loop fusion | flops 960 | bytes 1540 | tf_op jit(solution)/shard_map/select_n | solution.py:30
  6.0 0.7 %iota_compare_fusion = pred[24,8]{1,0:T(8,128)(4,1)S(1)} fusion(s32[24]{0:T(128)} %param.8), kind=kLoop, calls=%fused_computation.12 | loop fusion | flops 192 | bytes 288 | tf_op jit(solution)/shard_map/lt | solution.py:31
  6.7 0.1 copy.7
  6.8 0.1 reshape.42
  6.9 0.0 collective-permute-done
  6.9 2.4 %collective-permute-done.1 = bf16[128,512]{1,0:T(8,128)(2,1)S(1)} collective-permute-done((bf16[128,512]{1,0:T(8,128)(2,1)S(1)}, bf16[128,512]{1,0:T(8,128)(2,1)S(1)}, u32[]{:S(2)}, u32[]{:S(2)}) %collective-permute-start.1) | collective-permute-done | bytes 131104 | tf_op jit(solution)/shard_map/ppermute | solution.py:18
  9.3 1.5 %pad_maximum_fusion = bf16[1792,512]{1,0:T(8,128)(2,1)S(1)} fusion(bf16[128,512]{1,0:T(8,128)(2,1)S(1)} %collective-permute-done.1, bf16[1536,512]{1,0:T(8,128)(2,1)} %param.5, bf16[128,512]{1,0:T(8,128)(2,1)S(1)} %collective-permute-done), kind=kLoop, calls=%fused_computation.6 | loop fusion | flops 5505024 | bytes 3670016 | tf_op jit(solution)/shard_map/concatenate | solution.py:19
  10.9 8.2 %gather_fusion = bf16[192,64,512]{2,1,0:T(8,128)(2,1)} fusion(bf16[28,64,512]{2,1,0:T(8,128)(2,1)S(1)} %bitcast.16, s32[1024]{0:T(1024)S(1)} %pad_clamp_fusion), kind=kCustom, calls=%fused_computation | custom fusion | bytes 25166592 | tf_op jit(solution)/shard_map/gather | solution.py:30
  19.1 8.3 %fusion.1 = f32[24,64,512,1]{2,1,3,0:T(8,128)S(1)} fusion(bf16[24,8,64,512]{3,2,1,0:T(8,128)(2,1)} %bitcast.17, bf16[24,8,64,64]{3,2,1,0:T(8,128)(2,1)} %param.6, pred[24,8]{1,0:T(8,128)(4,1)S(1)} %iota_compare_fusion), kind=kOutput, calls=%fused_computation.3 | convolution fusion | flops 806092800 | bytes 17301696 | tf_op jit(solution)/shard_map/rsab,rsbk->rak/dot_general | solution.py:33
  27.4 0.0 copy-done
  27.4 0.0 copy-done.2
  27.4 0.4 fusion
  27.8 0.0 copy-start.1
  27.8 1.0 %fusion.5 = bf16[512,512]{0,1:T(8,128)(2,1)S(1)} fusion(bf16[1536,512]{1,0:T(8,128)(2,1)S(1)} %fusion, bf16[1536,512]{1,0:T(8,128)(2,1)S(1)} %copy-done), kind=kOutput, calls=%fused_computation.9 | convolution fusion | flops 805568512 | bytes 3670016 | tf_op jit(solution)/shard_map/dot_general | solution.py:40
  28.9 0.2 copy.8
  29.1 0.1 reshape.38
  29.2 0.1 copy.9
  29.3 0.0 copy-done.1
  29.3 25.1 %all_to_all.5 = bf16[32,32,256]{2,1,0:T(8,128)(2,1)S(1)} all-to-all(bf16[32,32,256]{2,1,0:T(8,128)(2,1)S(1)} %bitcast.19), channel_id=1, replica_groups=mesh['mesh'=16,'col'=2] {'mesh','col'}, dimensions={0} | all-to-all | bytes 1048576 | tf_op jit(solution)/shard_map/all_to_all | solution.py:46
  54.4 0.1 convert_reduce_fusion
  54.5 0.6 %broadcast_multiply_fusion = f32[32,256]{1,0:T(8,128)} fusion(f32[32,256]{1,0:T(8,128)S(1)} %convert_reduce_fusion), kind=kLoop, calls=%fused_computation.11 | loop fusion | flops 8192 | bytes 65536 | tf_op jit(solution)/shard_map/mul | solution.py:47
  (3 shorter events, 0.0 us)
Async XLA Ops:
  1.6 5.3 %collective-permute-start = (bf16[128,512]{1,0:T(8,128)(2,1)S(1)}, bf16[128,512]{1,0:T(8,128)(2,1)S(1)}, u32[]{:S(2)}, u32[]{:S(2)}) collective-permute-start(bf16[128,512]{1,0:T(8,128)(2,1)S(1)} %get-tuple-element.2), channel_id=1, source_target_pairs={{0,1},{1,2},{2,3},{3,4},{4,5},{5,6},{6,7},{7,8},{8,9},{9,10},{10,1... | collective-permute-start | bytes 393224 | tf_op jit(solution)/shard_map/ppermute | solution.py:15
  4.0 5.3 %collective-permute-start.1 = (bf16[128,512]{1,0:T(8,128)(2,1)S(1)}, bf16[128,512]{1,0:T(8,128)(2,1)S(1)}, u32[]{:S(2)}, u32[]{:S(2)}) collective-permute-start(bf16[128,512]{1,0:T(8,128)(2,1)S(1)} %get-tuple-element.3), channel_id=1, source_target_pairs={{1,0},{2,1},{3,2},{4,3},{5,4},{6,5},{7,6},{8,7},{9,8},{10,9},{11,1... | collective-permute-start | bytes 393224 | tf_op jit(solution)/shard_map/ppermute | solution.py:18
  19.1 8.3 %copy-start = (bf16[1536,512]{1,0:T(8,128)(2,1)S(1)}, bf16[1536,512]{1,0:T(8,128)(2,1)}, u32[]{:S(2)}) copy-start(bf16[1536,512]{1,0:T(8,128)(2,1)} %param.5) | copy-start | bytes 4718596
  19.1 8.3 %copy-start.2 = (f32[1536]{0:T(1024)S(1)}, f32[1536]{0:T(1024)}, u32[]{:S(2)}) copy-start(f32[1536]{0:T(1024)} %param.9) | copy-start | bytes 18436
  27.8 1.5 %copy-start.1 = (bf16[1536,512]{1,0:T(8,128)(2,1)}, bf16[1536,512]{1,0:T(8,128)(2,1)S(1)}, u32[]{:S(2)}) copy-start(bf16[1536,512]{1,0:T(8,128)(2,1)S(1)} %fusion) | copy-start | bytes 4718596

commit v2 on v1

--- a/solution.py
+++ b/solution.py
@@ -4,7 +4,7 @@
 from jax.sharding import PartitionSpec as P
 
 REACH = 2
-AXES = ("mesh", "col")
+AXES = ("outer", "inner", "col")
 
 
 def with_halo(block, sides, width):
@@ -33,25 +33,30 @@
     coupled = jnp.einsum("rsab,rsbk->rak", masked, picked, preferred_element_type=jnp.float32)
     coupled = coupled.reshape(nrows, width)
     image = (coupled + accumulation[:, None] * basis.astype(jnp.float32)).astype(jnp.bfloat16)
-    mesh_count = lax.axis_size("mesh")
-    col_count = lax.axis_size("col")
-    total_rows = nrows * mesh_count * col_count
+    outer, inner, cols = (lax.axis_size(axis) for axis in AXES)
+    total_rows = nrows * outer * inner * cols
     dims = (((0,), (0,)), ((), ()))
     part = lax.dot_general(basis, image, dims, preferred_element_type=jnp.float32)
     part = part.astype(jnp.bfloat16)
-    part = part.reshape(mesh_count, width // mesh_count, col_count, width // col_count)
-    part = part.transpose(0, 2, 1, 3).reshape(
-        mesh_count * col_count, width // mesh_count, width // col_count
+    part = part.reshape(outer, inner, width // (outer * inner), cols, width // cols)
+    part = part.transpose(1, 3, 0, 2, 4).reshape(
+        inner * cols, width // inner, width // cols
     )
-    got = lax.all_to_all(part, AXES, 0, 0, tiled=True)
+    got = lax.all_to_all(part, AXES[1:], 0, 0, tiled=True)
+    near = jnp.sum(got.astype(jnp.float32), axis=0).astype(jnp.bfloat16)
+    near = near.reshape(outer, width // (outer * inner), width // cols)
+    got = lax.all_to_all(near, AXES[0], 0, 0, tiled=True)
     projected = jnp.sum(got.astype(jnp.float32), axis=0) * (1.0 / total_rows)
     return (image, projected)
 
 
 def solution(mesh):
+    rows, cols = mesh.devices.shape
+    outer = 4 if rows % 4 == 0 else 1
+    split = jax.sharding.Mesh(mesh.devices.reshape(outer, rows // outer, cols), AXES)
     return jax.shard_map(
         local,
-        mesh=mesh,
+        mesh=split,
         in_specs=(
             P(AXES, None),
             P(AXES, None, None, None),
@@ -59,6 +64,6 @@
             P(AXES),
             P(AXES),
         ),
-        out_specs=(P(AXES, None), P("mesh", "col")),
+        out_specs=(P(AXES, None), P(AXES[:2], "col")),
         check_vma=False,
     )

time: 55.4 us -> 58 us (1.047)
  blocking collectives: 25.1 us -> 27.6 us
    all_to_all x1 -> x2, blocking collectives: 25.1 us -> 27.6 us  [the longest x1 18.2 us: local(): got = lax.all_to_all(part, AXES[1:], 0, 0, tiled=True)]
where the time goes in v2:
time: 58 us; the launch traced here: 57.6 us
  blocking collectives  27.6 us (48%)
  local copies, waits for them, and re-layouts  9.84 us (17%)
  matrix products  9.27 us (16%)
  other arithmetic  4.08 us (7%)
  starting transfers between devices  3.66 us (6%)
  waiting for transfers between devices  2.43 us (4%)
  between operations  0.76 us (1%)
    all_to_all x1, blocking collectives, local(): got = lax.all_to_all(part, AXES[1:], 0, 0, tiled=True)  18.2 us
    all_to_all x1, blocking collectives, local(): got = lax.all_to_all(near, AXES[0], 0, 0, tiled=True)  9.4 us
    dot_general x1, matrix products, local(): jnp.einsum('rsab,rsbk->rak', masked, picked, preferred_element_type=jnp.f...  8.27 us
    gather x1, local copies, waits for them, and re-layouts, local(): picked = pblocks[local_cols]  8.26 us
    ppermute x1, waiting for transfers between devices, with_halo(): lax.ppermute(lax.slice_in_dim(block, 0, width, axis=dim), axis, backward)  2.43 us
    ppermute x1, starting transfers between devices, with_halo(): lax.ppermute(lax.slice_in_dim(block, block.shape[dim] - width, None, axis...  2.36 us
    concatenate x1, other arithmetic, with_halo(): block = jnp.concatenate([low, block, high], axis=dim)  1.53 us
    ppermute x1, starting transfers between devices, with_halo(): lax.ppermute(lax.slice_in_dim(block, 0, width, axis=dim), axis, backward)  1.29 us
  transfers between devices with their start and end apart: 2, of which 1 were waited for; matrix products, arithmetic and copies ran while one was open for 3% of the time, Pallas kernels for 0%

profile of v2, /device:TPU:0, one launch (start us, length us, event | category | flops | bytes accessed | tf_op | source)
XLA Modules:
  0.0 57.6 jit_solution(3302254197388419828)
XLA Ops:
  0.6 1.0 %fusion.7 = (bf16[128,512]{1,0:T(8,128)(2,1)S(1)}, bf16[128,512]{1,0:T(8,128)(2,1)S(1)}) fusion(bf16[1536,512]{1,0:T(8,128)(2,1)} %param.5), kind=kLoop, calls=%fused_computation.16 | loop fusion | bytes 524288 | tf_op jit(solution)/shard_map/slice | solution.py:16
  1.6 2.4 %collective-permute-start = (bf16[128,512]{1,0:T(8,128)(2,1)S(1)}, bf16[128,512]{1,0:T(8,128)(2,1)S(1)}, u32[]{:S(2)}, u32[]{:S(2)}) collective-permute-start(bf16[128,512]{1,0:T(8,128)(2,1)S(1)} %get-tuple-element.2), channel_id=1, source_target_pairs={{0,1},{1,2},{2,3},{3,4},{4,5},{5,6},{6,7},{7,8},{8,9},{9,10},{10,1... | collective-permute-start | bytes 393224 | tf_op jit(solution)/shard_map/ppermute | solution.py:15
  4.0 1.3 %collective-permute-start.1 = (bf16[128,512]{1,0:T(8,128)(2,1)S(1)}, bf16[128,512]{1,0:T(8,128)(2,1)S(1)}, u32[]{:S(2)}, u32[]{:S(2)}) collective-permute-start(bf16[128,512]{1,0:T(8,128)(2,1)S(1)} %get-tuple-element.3), channel_id=1, source_target_pairs={{1,0},{2,1},{3,2},{4,3},{5,4},{6,5},{7,6},{8,7},{9,8},{10,9},{11,1... | collective-permute-start | bytes 393224 | tf_op jit(solution)/shard_map/ppermute | solution.py:18
  5.3 0.7 %compare_select_fusion = s32[24,8]{0,1:T(8,128)S(1)} fusion(s32[24,8]{0,1:T(8,128)} %param.7, s32[]{:T(128)S(6)} %mul.25), kind=kLoop, calls=%fused_computation.13 | loop fusion | flops 960 | bytes 1540 | tf_op jit(solution)/shard_map/select_n | solution.py:30
  6.0 0.7 %iota_compare_fusion = pred[24,8]{1,0:T(8,128)(4,1)S(1)} fusion(s32[24]{0:T(128)} %param.8), kind=kLoop, calls=%fused_computation.12 | loop fusion | flops 192 | bytes 288 | tf_op jit(solution)/shard_map/lt | solution.py:31
  6.7 0.1 copy.10
  6.8 0.1 reshape.46
  6.9 0.0 collective-permute-done
  6.9 2.4 %collective-permute-done.1 = bf16[128,512]{1,0:T(8,128)(2,1)S(1)} collective-permute-done((bf16[128,512]{1,0:T(8,128)(2,1)S(1)}, bf16[128,512]{1,0:T(8,128)(2,1)S(1)}, u32[]{:S(2)}, u32[]{:S(2)}) %collective-permute-start.1) | collective-permute-done | bytes 131104 | tf_op jit(solution)/shard_map/ppermute | solution.py:18
  9.3 1.5 %pad_maximum_fusion = bf16[1792,512]{1,0:T(8,128)(2,1)S(1)} fusion(bf16[128,512]{1,0:T(8,128)(2,1)S(1)} %collective-permute-done.1, bf16[1536,512]{1,0:T(8,128)(2,1)} %param.5, bf16[128,512]{1,0:T(8,128)(2,1)S(1)} %collective-permute-done), kind=kLoop, calls=%fused_computation.6 | loop fusion | flops 5505024 | bytes 3670016 | tf_op jit(solution)/shard_map/concatenate | solution.py:19
  10.9 8.3 %gather_fusion = bf16[192,64,512]{2,1,0:T(8,128)(2,1)} fusion(bf16[28,64,512]{2,1,0:T(8,128)(2,1)S(1)} %bitcast.17, s32[1024]{0:T(1024)S(1)} %pad_clamp_fusion), kind=kCustom, calls=%fused_computation | custom fusion | bytes 25166592 | tf_op jit(solution)/shard_map/gather | solution.py:30
  19.1 8.3 %fusion.1 = f32[24,64,512,1]{2,1,3,0:T(8,128)S(1)} fusion(bf16[24,8,64,512]{3,2,1,0:T(8,128)(2,1)} %bitcast.18, bf16[24,8,64,64]{3,2,1,0:T(8,128)(2,1)} %param.6, pred[24,8]{1,0:T(8,128)(4,1)S(1)} %iota_compare_fusion), kind=kOutput, calls=%fused_computation.3 | convolution fusion | flops 806092800 | bytes 17301696 | tf_op jit(solution)/shard_map/rsab,rsbk->rak/dot_general | solution.py:33
  27.4 0.0 copy-done
  27.4 0.0 copy-done.2
  27.4 0.4 fusion
  27.9 0.0 copy-start.1
  27.9 1.0 %fusion.5 = bf16[512,512]{0,1:T(8,128)(2,1)S(1)} fusion(bf16[1536,512]{1,0:T(8,128)(2,1)S(1)} %fusion, bf16[1536,512]{1,0:T(8,128)(2,1)S(1)} %copy-done), kind=kOutput, calls=%fused_computation.9 | convolution fusion | flops 805568512 | bytes 3670016 | tf_op jit(solution)/shard_map/dot_general | solution.py:39
  28.9 0.2 copy.11
  29.1 0.1 reshape.41
  29.2 0.1 copy.12
  29.3 18.2 %all_to_all.10 = bf16[8,128,256]{2,1,0:T(8,128)(2,1)S(1)} all-to-all(bf16[8,128,256]{2,1,0:T(8,128)(2,1)S(1)} %bitcast.20), channel_id=1, replica_groups=mesh['outer'=4,'inner'=4,'col'=2] {'inner','col'}, dimensions={0} | all-to-all | bytes 1048576 | tf_op jit(solution)/shard_map/all_to_all | solution.py:45
  47.5 0.1 reduce_sum.21
  47.6 9.4 %all_to_all.11 = bf16[4,32,256]{2,1,0:T(8,128)(2,1)S(1)} all-to-all(bf16[4,32,256]{2,1,0:T(8,128)(2,1)S(1)} %bitcast.21), channel_id=1, replica_groups=mesh['outer'=4,'inner'=4,'col'=2] {'outer'}, dimensions={0} | all-to-all | bytes 131072 | tf_op jit(solution)/shard_map/all_to_all | solution.py:48
  57.0 0.6 %broadcast_multiply_fusion = f32[32,256]{1,0:T(8,128)} fusion(f32[32,256]{1,0:T(8,128)S(1)} %convert_reduce_fusion), kind=kLoop, calls=%fused_computation.11 | loop fusion | flops 8192 | bytes 65536 | tf_op jit(solution)/shard_map/mul | solution.py:49
  (5 shorter events, 0.0 us)
Async XLA Ops:
  1.6 5.3 %collective-permute-start = (bf16[128,512]{1,0:T(8,128)(2,1)S(1)}, bf16[128,512]{1,0:T(8,128)(2,1)S(1)}, u32[]{:S(2)}, u32[]{:S(2)}) collective-permute-start(bf16[128,512]{1,0:T(8,128)(2,1)S(1)} %get-tuple-element.2), channel_id=1, source_target_pairs={{0,1},{1,2},{2,3},{3,4},{4,5},{5,6},{6,7},{7,8},{8,9},{9,10},{10,1... | collective-permute-start | bytes 393224 | tf_op jit(solution)/shard_map/ppermute | solution.py:15
  4.0 5.3 %collective-permute-start.1 = (bf16[128,512]{1,0:T(8,128)(2,1)S(1)}, bf16[128,512]{1,0:T(8,128)(2,1)S(1)}, u32[]{:S(2)}, u32[]{:S(2)}) collective-permute-start(bf16[128,512]{1,0:T(8,128)(2,1)S(1)} %get-tuple-element.3), channel_id=1, source_target_pairs={{1,0},{2,1},{3,2},{4,3},{5,4},{6,5},{7,6},{8,7},{9,8},{10,9},{11,1... | collective-permute-start | bytes 393224 | tf_op jit(solution)/shard_map/ppermute | solution.py:18
  19.1 8.3 %copy-start = (bf16[1536,512]{1,0:T(8,128)(2,1)S(1)}, bf16[1536,512]{1,0:T(8,128)(2,1)}, u32[]{:S(2)}) copy-start(bf16[1536,512]{1,0:T(8,128)(2,1)} %param.5) | copy-start | bytes 4718596
  19.1 8.3 %copy-start.2 = (f32[1536]{0:T(1024)S(1)}, f32[1536]{0:T(1024)}, u32[]{:S(2)}) copy-start(f32[1536]{0:T(1024)} %param.9) | copy-start | bytes 18436
  27.9 1.5 %copy-start.1 = (bf16[1536,512]{1,0:T(8,128)(2,1)}, bf16[1536,512]{1,0:T(8,128)(2,1)S(1)}, u32[]{:S(2)}) copy-start(bf16[1536,512]{1,0:T(8,128)(2,1)S(1)} %fusion) | copy-start | bytes 4718596

commit v3 on v1

v3 whole, which is shorter than its diff:
```python
import functools

import jax
import jax.numpy as jnp
from jax import lax
from jax.experimental import pallas as pl
from jax.experimental.pallas import tpu as pltpu
from jax.sharding import PartitionSpec as P

REACH = 2
AXES = ("mesh", "col")
ROWS_DOT = (((0,), (0,)), ((), ()))


def strip_of(cols_ref, live_ref, jac_ref, acc_ref, first, pair):
    _, slots, bsize, _ = jac_ref.shape
    tile = 2 * bsize
    half = lax.broadcasted_iota(jnp.int32, (1, tile), 1) // bsize
    halves = []
    for g in (2 * pair, 2 * pair + 1):
        tiles = [None, None, None]
        for s in range(slots):
            place = cols_ref[s, g] - (first + 2 * pair) + REACH
            place = jnp.where(s < live_ref[g], place, -1)
            block = jac_ref[g, s].astype(jnp.float32)
            wide = jnp.concatenate([block, block], axis=1)
            for t in range(3):
                here = jnp.where(half + 2 * t == place, 1.0, 0.0)
                term = wide * here
                tiles[t] = term if tiles[t] is None else tiles[t] + term
        halves.append(jnp.concatenate(tiles, axis=1))
    strip = jnp.concatenate(halves, axis=0)
    row = lax.broadcasted_iota(jnp.int32, strip.shape, 0)
    lane = lax.broadcasted_iota(jnp.int32, strip.shape, 1)
    weight = acc_ref[pl.ds(pair, 1), :]
    weight = jnp.concatenate([weight, weight, weight], axis=1)
    strip = strip + jnp.where(lane == row + tile, weight, 0.0)
    high = strip.astype(jnp.bfloat16)
    low = (strip - high.astype(jnp.float32)).astype(jnp.bfloat16)
    return jnp.concatenate([high, low], axis=0)


def apply_strip(strip, rows):
    both = jnp.dot(strip, rows, preferred_element_type=jnp.float32)
    half = strip.shape[0] // 2
    return both[:half] + both[half:]


def inner_kernel(
    cols_ref, live_ref, jac_ref, basis_ref, acc_ref,
    image_ref, edge_ref, arm_ref, part_ref, staged, sems,
):
    nblk, _, bsize, _ = jac_ref.shape
    nrows = basis_ref.shape[0]
    tile = 2 * bsize
    pairs = nblk // 2
    first = lax.axis_index(AXES) * nblk
    copies = []
    for pair in range(pairs):
        strip = strip_of(cols_ref, live_ref, jac_ref, acc_ref, first, pair)
        start = pair * tile
        if pair == 0:
            edge_ref[0] = apply_strip(strip[:, tile:], basis_ref[: 2 * tile, :])
            arm_ref[0] = strip[:, :tile]
        elif pair == pairs - 1:
            edge_ref[1] = apply_strip(strip[:, : 2 * tile], basis_ref[nrows - 2 * tile :, :])
            arm_ref[1] = strip[:, 2 * tile :]
        else:
            rows = basis_ref[start - tile : start + 2 * tile, :]
            staged[start : start + tile, :] = apply_strip(strip, rows).astype(jnp.bfloat16)
            where = pl.ds(start, tile)
            copy = pltpu.make_async_copy(staged.at[where], image_ref.at[where], sems.at[pair])
            copy.start()
            copies.append(copy)
    part_ref[...] = lax.dot_general(
        basis_ref[tile : nrows - tile, :], staged[tile : nrows - tile, :], ROWS_DOT,
        preferred_element_type=jnp.float32,
    )
    for copy in copies:
        copy.wait()


def edge_kernel(
    chunks, near_ref, far_ref, edge_ref, arm_ref, top_ref, bottom_ref, part_ref, _,
    image_ref, total_ref, staged, sems,
):
    tile, width = top_ref.shape
    nrows = image_ref.shape[0]
    odd = lax.rem(lax.axis_index(AXES), 2) == 1
    near, far = near_ref[...], far_ref[...]
    halos = (jnp.where(odd, near, far), jnp.where(odd, far, near))
    total = part_ref[...]
    copies = []
    for side, own_ref in enumerate((top_ref, bottom_ref)):
        rows = edge_ref[side] + apply_strip(arm_ref[side], halos[side])
        rows = rows.astype(jnp.bfloat16)
        staged[side] = rows
        where = pl.ds(0 if side == 0 else nrows - tile, tile)
        copy = pltpu.make_async_copy(staged.at[side], image_ref.at[where], sems.at[side])
        copy.start()
        copies.append(copy)
        total = total + lax.dot_general(
            own_ref[...], rows, ROWS_DOT, preferred_element_type=jnp.float32
        )
    total = total.astype(jnp.bfloat16)
    if chunks is None:
        total_ref[...] = total
    else:
        down, across = chunks
        high, wide = width // down, width // across
        for i in range(down):
            for j in range(across):
                total_ref[i * across + j] = total[
                    i * high : (i + 1) * high, j * wide : (j + 1) * wide
                ]
    for copy in copies:
        copy.wait()


def whole(memory_space=pltpu.VMEM):
    return pl.BlockSpec(memory_space=memory_space)


def local(basis, jac_blocks, block_cols, live_slots, accumulation):
    nrows, width = basis.shape
    nblk, slots, bsize, _ = jac_blocks.shape
    tile = 2 * bsize
    down, across = (lax.axis_size(axis) for axis in AXES)
    count = down * across
    odd = lax.rem(lax.axis_index(AXES), 2)

    last = nrows - tile
    far_send = lax.dynamic_slice_in_dim(basis, odd * last, tile, axis=0)
    near_send = lax.dynamic_slice_in_dim(basis, (1 - odd) * last, tile, axis=0)
    swaps = [(i, i + 1) for i in range(1, count - 1, 2)]
    far = lax.ppermute(far_send, AXES, swaps + [(j, i) for i, j in swaps])
    swaps = [(i, i + 1) for i in range(0, count, 2)]
    near = lax.ppermute(near_send, AXES, swaps + [(j, i) for i, j in swaps])

    f32, bf16 = jnp.float32, jnp.bfloat16
    image, edge, arm, part = pl.pallas_call(
        inner_kernel,
        out_shape=(
            jax.ShapeDtypeStruct((nrows, width), bf16),
            jax.ShapeDtypeStruct((2, tile, width), f32),
            jax.ShapeDtypeStruct((2, 2 * tile, tile), bf16),
            jax.ShapeDtypeStruct((width, width), f32),
        ),
        in_specs=[whole(pltpu.SMEM), whole(pltpu.SMEM), whole(), whole(), whole()],
        out_specs=(whole(pl.ANY), whole(), whole(), whole()),
        scratch_shapes=[
            pltpu.VMEM((nrows, width), bf16),
            pltpu.SemaphoreType.DMA((nblk // 2,)),
        ],
        compiler_params=pltpu.CompilerParams(vmem_limit_bytes=32 * 2**20),
        cost_estimate=pl.CostEstimate(
            flops=2 * nrows * width * (width + 12 * bsize),
            bytes_accessed=8 * 2**20,
            transcendentals=0,
        ),
        name="inner",
    )(
        block_cols.T,
        live_slots,
        jac_blocks,
        basis,
        accumulation.reshape(nblk // 2, tile),
    )

    in_kernel = (width // down) % 16 == 0 and (width // across) % 128 == 0
    chunk = (count, width // down, width // across)
    image, total = pl.pallas_call(
        functools.partial(edge_kernel, (down, across) if in_kernel else None),
        out_shape=(
            jax.ShapeDtypeStruct((nrows, width), bf16),
            jax.ShapeDtypeStruct(chunk if in_kernel else (width, width), bf16),
        ),
        grid=(1,),
        in_specs=[
            whole(), whole(), whole(), whole(),
            pl.BlockSpec((tile, width), lambda i: (0, 0)),
            pl.BlockSpec((tile, width), lambda i: (nrows // tile - 1, 0)),
            whole(), whole(pl.ANY),
        ],
        out_specs=(whole(pl.ANY), whole()),
        scratch_shapes=[
            pltpu.VMEM((2, tile, width), bf16),
            pltpu.SemaphoreType.DMA((2,)),
        ],
        input_output_aliases={7: 0},
        compiler_params=pltpu.CompilerParams(vmem_limit_bytes=32 * 2**20),
        name="edges",
    )(near, far, edge, arm, basis, basis, part, image)
    if not in_kernel:
        total = total.reshape(down, width // down, across, width // across)
        total = total.transpose(0, 2, 1, 3).reshape(chunk)
    got = lax.all_to_all(total, AXES, 0, 0, tiled=True)
    projected = jnp.sum(got.astype(f32), axis=0) * (1.0 / (nrows * count))
    return (image, projected)


def solution(mesh):
    return jax.shard_map(
        local,
        mesh=mesh,
        in_specs=(
            P(AXES, None),
            P(AXES, None, None, None),
            P(AXES, None),
            P(AXES),
            P(AXES),
        ),
        out_specs=(P(AXES, None), P("mesh", "col")),
        check_vma=False,
    )
```

time: 55.4 us -> 39.2 us (0.71)
  matrix products: 9.27 us -> 0 us
  Pallas kernels: 0 us -> 5.86 us
  blocking collectives: 25.1 us -> 20.3 us
  local copies, waits for them, and re-layouts: 9.82 us -> 6.33 us
  other arithmetic: 4.08 us -> 0.7 us
  waiting for transfers between devices: 2.43 us -> 0.01 us
  starting transfers between devices: 3.66 us -> 5.03 us
    dot_general x2 -> x0, matrix products: 9.27 us -> none  [the longest x1 8.27 us: local(): jnp.einsum('rsab,rsbk->rak', masked, picked, preferred_element_type=jnp.f...]
    gather x1 -> x0, local copies, waits for them, and re-layouts: 8.24 us -> none  [local(): picked = pblocks[local_cols]]
    pallas_call x0 -> x2, Pallas kernels: none -> 5.86 us  [the longest x1 4.61 us: local(): pl.pallas_call(inner_kernel, out_shape=(jax.ShapeDtypeStruct((nrows, widt...]
    unnamed x6 -> x12, local copies, waits for them, and re-layouts: 0.01 us -> 5.34 us
    all_to_all x1, blocking collectives: 25.1 us -> 20.3 us  [local(): got = lax.all_to_all(total, AXES, 0, 0, tiled=True)]
    ppermute x2, waiting for transfers between devices: 2.43 us -> 0.01 us  [the longest x1 0.01 us: local(): far = lax.ppermute(far_send, AXES, swaps + [(j, i) for i, j in swaps])]
    concatenate x1 -> x0, other arithmetic: 1.53 us -> none  [with_halo(): block = jnp.concatenate([low, block, high], axis=dim)]
    ppermute x2, starting transfers between devices: 3.66 us -> 5.03 us  [the longest x1 4.36 us: local(): near = lax.ppermute(near_send, AXES, swaps + [(j, i) for i, j in swaps])]
  transfers between devices with their start and end apart: 2 -> 2, of which waited for: 1 -> 0; matrix products, arithmetic and copies ran while one was open for 3% -> 0% of each run, Pallas kernels for 0% -> 12%
where the time goes in v3:
time: 39.2 us; the launch traced here: 38.9 us
  blocking collectives  20.3 us (52%)
  local copies, waits for them, and re-layouts  6.33 us (16%)
  Pallas kernels  5.86 us (15%)
  starting transfers between devices  5.03 us (13%)
  other arithmetic  0.7 us (2%)
  between operations  0.7 us (2%)
    all_to_all x1, blocking collectives, local(): got = lax.all_to_all(total, AXES, 0, 0, tiled=True)  20.3 us
    unnamed x12, local copies, waits for them, and re-layouts  5.34 us
    pallas_call x1, Pallas kernels, local(): pl.pallas_call(inner_kernel, out_shape=(jax.ShapeDtypeStruct((nrows, widt...  4.61 us
    ppermute x1, starting transfers between devices, local(): near = lax.ppermute(near_send, AXES, swaps + [(j, i) for i, j in swaps])  4.36 us
    pallas_call x1, Pallas kernels, local(): pl.pallas_call(functools.partial(edge_kernel, (down, across) if in_kernel...  1.25 us
    dynamic_slice x1, local copies, waits for them, and re-layouts, local(): far_send = lax.dynamic_slice_in_dim(basis, odd * last, tile, axis=0)  0.99 us
  transfers between devices with their start and end apart: 2, of which 0 were waited for; matrix products, arithmetic and copies ran while one was open for 0% of the time, Pallas kernels for 12%

profile of v3, /device:TPU:0, one launch (start us, length us, event | category | flops | bytes accessed | tf_op | source)
XLA Modules:
  0.0 38.9 jit_solution(9349268731944735854)
XLA Ops:
  0.6 1.0 %constant_dynamic-slice_fusion = (bf16[128,512]{1,0:T(8,128)(2,1)S(1)}, bf16[128,512]{1,0:T(8,128)(2,1)S(1)}) fusion(bf16[1536,512]{1,0:T(8,128)(2,1)} %bottom_ref.1, s32[]{:T(128)S(6)} %select_n.7, s32[]{:T(128)S(6)} %select_n.6), kind=kLoop, calls=%fused_computation.2 | loop fusion | bytes 524296 | tf_op jit(solution)/shard_map/dynamic_slice | solution.py:133
  1.6 0.7 %collective-permute-start.1 = (bf16[128,512]{1,0:T(8,128)(2,1)S(1)}, bf16[128,512]{1,0:T(8,128)(2,1)S(1)}, u32[]{:S(2)}, u32[]{:S(2)}) collective-permute-start(bf16[128,512]{1,0:T(8,128)(2,1)S(1)} %get-tuple-element.14), channel_id=1, source_target_pairs={{1,2},{3,4},{5,6},{7,8},{9,10},{11,12},{13,14},{15,16},{17,18},{19... | collective-permute-start | bytes 393224 | tf_op jit(solution)/shard_map/ppermute | solution.py:136
  2.3 4.4 %collective-permute-start = (bf16[128,512]{1,0:T(8,128)(2,1)S(1)}, bf16[128,512]{1,0:T(8,128)(2,1)S(1)}, u32[]{:S(2)}, u32[]{:S(2)}) collective-permute-start(bf16[128,512]{1,0:T(8,128)(2,1)S(1)} %get-tuple-element.15), channel_id=1, source_target_pairs={{0,1},{2,3},{4,5},{6,7},{8,9},{10,11},{12,13},{14,15},{16,17},{18,... | collective-permute-start | bytes 393224 | tf_op jit(solution)/shard_map/ppermute | solution.py:138
  6.7 0.0 copy-start
  6.7 1.4 %copy-done = bf16[1536,512]{1,0:T(8,128)(2,1)S(1)} copy-done((bf16[1536,512]{1,0:T(8,128)(2,1)S(1)}, bf16[1536,512]{1,0:T(8,128)(2,1)}, u32[]{:S(2)}) %copy-start) | copy-done | bytes 1572888
  8.1 0.0 copy-start.2
  8.1 1.9 %copy-done.2 = bf16[24,8,64,64]{3,2,1,0:T(8,128)(2,1)S(1)} copy-done((bf16[24,8,64,64]{3,2,1,0:T(8,128)(2,1)S(1)}, bf16[24,8,64,64]{3,2,1,0:T(8,128)(2,1)}, u32[]{:S(2)}) %copy-start.2) | copy-done | bytes 1572888
  10.0 0.0 copy-start.3
  10.0 0.7 %copy-done.3 = f32[1536]{0:T(1024)S(1)} copy-done((f32[1536]{0:T(1024)S(1)}, f32[1536]{0:T(1024)}, u32[]{:S(2)}) %copy-start.3) | copy-done | bytes 6168
  10.7 0.0 copy-start.4
  10.7 0.7 %copy-done.4 = s32[24,8]{0,1:T(8,128)S(1)} copy-done((s32[24,8]{0,1:T(8,128)S(1)}, s32[24,8]{0,1:T(8,128)}, u32[]{:S(2)}) %copy-start.4) | copy-done | bytes 792
  11.4 0.0 copy-start.5
  11.4 0.7 %copy-done.5 = s32[24]{0:T(128)S(1)} copy-done((s32[24]{0:T(128)S(1)}, s32[24]{0:T(128)}, u32[]{:S(2)}) %copy-start.5) | copy-done | bytes 120
  12.0 0.0 copy-start.1
  12.0 4.6 %inner.1 = (bf16[1536,512]{1,0:T(8,128)(2,1)}, f32[2,128,512]{2,1,0:T(8,128)S(1)}, bf16[2,256,128]{2,1,0:T(8,128)(2,1)S(1)}, f32[512,512]{1,0:T(8,128)S(1)}) custom-call(s32[8,24]{1,0:T(8,128)S(1)} %bitcast.3, s32[24]{0:T(128)S(1)} %copy-done.5, bf16[24,8,64,64]{3,2,1,0:T(8,128)(2,1)S(1)} %copy-done.2, bf16[1536,512]{1,0:T(8,128)(2,1)S(1)} %copy-done, ...), custom_call_target="tpu_custom_call" | custom-call | flops 2013265920 | bytes 8388608 | tf_op jit(solution)/shard_map/inner/pallas_call | solution.py:141
  16.6 0.0 collective-permute-done.1.far_ref
  16.6 0.0 collective-permute-done.near_ref
  16.7 0.0 copy-done.1
  16.7 1.2 %edges.1 = (bf16[1536,512]{1,0:T(8,128)(2,1)}, bf16[32,32,256]{2,1,0:T(8,128)(2,1)S(1)}) custom-call(bf16[128,512]{1,0:T(8,128)(2,1)S(1)} %collective-permute-done.near_ref, bf16[128,512]{1,0:T(8,128)(2,1)S(1)} %collective-permute-done.1.far_ref, f32[2,128,512]{2,1,0:T(8,128)S(1)} %get-tuple-element.8.edge_ref, ...), custom_call_target="tpu_custom_call", output_to_operand_aliasing={{0}: (7, {})} | custom-call | tf_op jit(solution)/shard_map/edges/pallas_call | solution.py:172
  17.9 20.3 %all_to_all.5 = bf16[32,32,256]{2,1,0:T(8,128)(2,1)S(1)} all-to-all(bf16[32,32,256]{2,1,0:T(8,128)(2,1)S(1)} %get-tuple-element.13), channel_id=1, replica_groups=mesh['mesh'=16,'col'=2] {'mesh','col'}, dimensions={0} | all-to-all | bytes 1048576 | tf_op jit(solution)/shard_map/all_to_all | solution.py:197
  38.2 0.1 convert_reduce_fusion
  38.3 0.6 %broadcast_multiply_fusion = f32[32,256]{1,0:T(8,128)} fusion(f32[32,256]{1,0:T(8,128)S(1)} %convert_reduce_fusion), kind=kLoop, calls=%fused_computation.1 | loop fusion | flops 8192 | bytes 65536 | tf_op jit(solution)/shard_map/mul | solution.py:198
Async XLA Ops:
  1.6 15.0 %collective-permute-start.1 = (bf16[128,512]{1,0:T(8,128)(2,1)S(1)}, bf16[128,512]{1,0:T(8,128)(2,1)S(1)}, u32[]{:S(2)}, u32[]{:S(2)}) collective-permute-start(bf16[128,512]{1,0:T(8,128)(2,1)S(1)} %get-tuple-element.14), channel_id=1, source_target_pairs={{1,2},{3,4},{5,6},{7,8},{9,10},{11,12},{13,14},{15,16},{17,18},{19... | collective-permute-start | bytes 393224 | tf_op jit(solution)/shard_map/ppermute | solution.py:136
  2.3 14.3 %collective-permute-start = (bf16[128,512]{1,0:T(8,128)(2,1)S(1)}, bf16[128,512]{1,0:T(8,128)(2,1)S(1)}, u32[]{:S(2)}, u32[]{:S(2)}) collective-permute-start(bf16[128,512]{1,0:T(8,128)(2,1)S(1)} %get-tuple-element.15), channel_id=1, source_target_pairs={{0,1},{2,3},{4,5},{6,7},{8,9},{10,11},{12,13},{14,15},{16,17},{18,... | collective-permute-start | bytes 393224 | tf_op jit(solution)/shard_map/ppermute | solution.py:138
  6.7 1.4 %copy-start = (bf16[1536,512]{1,0:T(8,128)(2,1)S(1)}, bf16[1536,512]{1,0:T(8,128)(2,1)}, u32[]{:S(2)}) copy-start(bf16[1536,512]{1,0:T(8,128)(2,1)} %bottom_ref.1) | copy-start | bytes 4718596
  8.1 1.9 %copy-start.2 = (bf16[24,8,64,64]{3,2,1,0:T(8,128)(2,1)S(1)}, bf16[24,8,64,64]{3,2,1,0:T(8,128)(2,1)}, u32[]{:S(2)}) copy-start(bf16[24,8,64,64]{3,2,1,0:T(8,128)(2,1)} %jac_ref.1) | copy-start | bytes 4718596
  10.0 0.7 %copy-start.3 = (f32[1536]{0:T(1024)S(1)}, f32[1536]{0:T(1024)}, u32[]{:S(2)}) copy-start(f32[1536]{0:T(1024)} %param.9) | copy-start | bytes 18436
  10.7 0.7 %copy-start.4 = (s32[24,8]{0,1:T(8,128)S(1)}, s32[24,8]{0,1:T(8,128)}, u32[]{:S(2)}) copy-start(s32[24,8]{0,1:T(8,128)} %param.7) | copy-start | bytes 2308
  11.4 0.7 %copy-start.5 = (s32[24]{0:T(128)S(1)}, s32[24]{0:T(128)}, u32[]{:S(2)}) copy-start(s32[24]{0:T(128)} %live_ref.1) | copy-start | bytes 292
  12.0 4.6 %copy-start.1 = (bf16[1536,512]{1,0:T(8,128)(2,1)S(1)}, bf16[1536,512]{1,0:T(8,128)(2,1)}, u32[]{:S(2)}) copy-start(bf16[1536,512]{1,0:T(8,128)(2,1)} %bottom_ref.1) | copy-start | bytes 4718596

commit v4 on v3

--- a/solution.py
+++ b/solution.py
@@ -16,25 +16,24 @@
     _, slots, bsize, _ = jac_ref.shape
     tile = 2 * bsize
     half = lax.broadcasted_iota(jnp.int32, (1, tile), 1) // bsize
+    row = lax.broadcasted_iota(jnp.int32, (bsize, tile), 0)
+    lane = lax.broadcasted_iota(jnp.int32, (bsize, tile), 1)
+    weight = acc_ref[pair : pair + 1, :]
     halves = []
-    for g in (2 * pair, 2 * pair + 1):
-        tiles = [None, None, None]
+    for side in range(2):
+        g = 2 * pair + side
+        tiles = [None, jnp.where(lane == row + side * bsize, weight, 0.0), None]
         for s in range(slots):
             place = cols_ref[s, g] - (first + 2 * pair) + REACH
             place = jnp.where(s < live_ref[g], place, -1)
-            block = jac_ref[g, s].astype(jnp.float32)
-            wide = jnp.concatenate([block, block], axis=1)
+            block = jac_ref[g, s]
+            wide = jnp.concatenate([block, block], axis=1).astype(jnp.float32)
             for t in range(3):
                 here = jnp.where(half + 2 * t == place, 1.0, 0.0)
                 term = wide * here
                 tiles[t] = term if tiles[t] is None else tiles[t] + term
         halves.append(jnp.concatenate(tiles, axis=1))
     strip = jnp.concatenate(halves, axis=0)
-    row = lax.broadcasted_iota(jnp.int32, strip.shape, 0)
-    lane = lax.broadcasted_iota(jnp.int32, strip.shape, 1)
-    weight = acc_ref[pl.ds(pair, 1), :]
-    weight = jnp.concatenate([weight, weight, weight], axis=1)
-    strip = strip + jnp.where(lane == row + tile, weight, 0.0)
     high = strip.astype(jnp.bfloat16)
     low = (strip - high.astype(jnp.float32)).astype(jnp.bfloat16)
     return jnp.concatenate([high, low], axis=0)
@@ -47,17 +46,61 @@
 
 
 def inner_kernel(
-    cols_ref, live_ref, jac_ref, basis_ref, acc_ref,
-    image_ref, edge_ref, arm_ref, part_ref, staged, sems,
+    cols_hbm, live_hbm, jac_hbm, basis_hbm, acc_hbm,
+    image_ref, edge_ref, arm_ref, part_ref,
+    cols_ref, live_ref, jac_ref, basis_ref, acc_ref, strips, staged, load_sems, store_sems,
 ):
     nblk, _, bsize, _ = jac_ref.shape
     nrows = basis_ref.shape[0]
     tile = 2 * bsize
     pairs = nblk // 2
+    groups = 3 if pairs % 3 == 0 else 1
+    size = pairs // groups
     first = lax.axis_index(AXES) * nblk
-    copies = []
+
+    def load(source, target, at):
+        copy = pltpu.make_async_copy(source, target, load_sems.at[at])
+        copy.start()
+        return copy
+
+    small = [
+        load(cols_hbm, cols_ref, 0),
+        load(live_hbm, live_ref, 1),
+        load(acc_hbm, acc_ref, 2),
+    ]
+    blocks = []
+    for i in range(groups):
+        where = pl.ds(2 * size * i, 2 * size)
+        blocks.append(load(jac_hbm.at[where], jac_ref.at[where], 4 + i))
+        if i == 0:
+            rows = load(basis_hbm, basis_ref, 3)
+
+    def build(pair):
+        if pair % size == 0:
+            blocks[pair // size].wait()
+        strips[pair % 2] = strip_of(cols_ref, live_ref, jac_ref, acc_ref, first, pair)
+
+    def project(start, stop):
+        return lax.dot_general(
+            basis_ref[start:stop, :], staged[start:stop, :], ROWS_DOT,
+            preferred_element_type=jnp.float32,
+        )
+
+    def store(start, stop, at):
+        where = pl.ds(start, stop - start)
+        copy = pltpu.make_async_copy(staged.at[where], image_ref.at[where], store_sems.at[at])
+        copy.start()
+        return copy
+
+    for copy in small:
+        copy.wait()
+    build(0)
+    rows.wait()
+    middle = (pairs // 2) * tile
     for pair in range(pairs):
-        strip = strip_of(cols_ref, live_ref, jac_ref, acc_ref, first, pair)
+        if pair + 1 < pairs:
+            build(pair + 1)
+        strip = strips[pair % 2]
         start = pair * tile
         if pair == 0:
             edge_ref[0] = apply_strip(strip[:, tile:], basis_ref[: 2 * tile, :])
@@ -66,18 +109,15 @@
             edge_ref[1] = apply_strip(strip[:, : 2 * tile], basis_ref[nrows - 2 * tile :, :])
             arm_ref[1] = strip[:, 2 * tile :]
         else:
-            rows = basis_ref[start - tile : start + 2 * tile, :]
-            staged[start : start + tile, :] = apply_strip(strip, rows).astype(jnp.bfloat16)
-            where = pl.ds(start, tile)
-            copy = pltpu.make_async_copy(staged.at[where], image_ref.at[where], sems.at[pair])
-            copy.start()
-            copies.append(copy)
-    part_ref[...] = lax.dot_general(
-        basis_ref[tile : nrows - tile, :], staged[tile : nrows - tile, :], ROWS_DOT,
-        preferred_element_type=jnp.float32,
-    )
-    for copy in copies:
-        copy.wait()
+            block = basis_ref[start - tile : start + 2 * tile, :]
+            staged[start : start + tile, :] = apply_strip(strip, block).astype(jnp.bfloat16)
+        if start + tile == middle:
+            early = store(tile, middle, 0)
+            part_ref[...] = project(tile, middle)
+    late = store(middle, nrows - tile, 1)
+    part_ref[...] += project(middle, nrows - tile)
+    early.wait()
+    late.wait()
 
 
 def edge_kernel(
@@ -146,11 +186,18 @@
             jax.ShapeDtypeStruct((2, 2 * tile, tile), bf16),
             jax.ShapeDtypeStruct((width, width), f32),
         ),
-        in_specs=[whole(pltpu.SMEM), whole(pltpu.SMEM), whole(), whole(), whole()],
-        out_specs=(whole(pl.ANY), whole(), whole(), whole()),
+        in_specs=[whole(pltpu.HBM)] * 5,
+        out_specs=(whole(pltpu.HBM), whole(), whole(), whole()),
         scratch_shapes=[
+            pltpu.SMEM((slots, nblk), jnp.int32),
+            pltpu.SMEM((nblk,), jnp.int32),
+            pltpu.VMEM(jac_blocks.shape, bf16),
             pltpu.VMEM((nrows, width), bf16),
-            pltpu.SemaphoreType.DMA((nblk // 2,)),
+            pltpu.VMEM((nblk // 2, tile), f32),
+            pltpu.VMEM((2, 2 * tile, 3 * tile), bf16),
+            pltpu.VMEM((nrows, width), bf16),
+            pltpu.SemaphoreType.DMA((7,)),
+            pltpu.SemaphoreType.DMA((2,)),
         ],
         compiler_params=pltpu.CompilerParams(vmem_limit_bytes=32 * 2**20),
         cost_estimate=pl.CostEstimate(
@@ -160,11 +207,16 @@
         ),
         name="inner",
     )(
-        block_cols.T,
-        live_slots,
-        jac_blocks,
-        basis,
-        accumulation.reshape(nblk // 2, tile),
+        *(
+            pltpu.with_memory_space_constraint(array, pltpu.HBM)
+            for array in (
+                block_cols.T,
+                live_slots,
+                jac_blocks,
+                basis,
+                accumulation.reshape(nblk // 2, tile),
+            )
+        )
     )
 
     in_kernel = (width // down) % 16 == 0 and (width // across) % 128 == 0

time: 39.2 us -> 35.2 us (0.90)
  local copies, waits for them, and re-layouts: 6.33 us -> 1 us
  Pallas kernels: 5.86 us -> 7.37 us
    unnamed x12 -> x2, local copies, waits for them, and re-layouts: 5.34 us -> 0.01 us
    pallas_call x1, Pallas kernels: 4.61 us -> 6.12 us  [local(): pl.pallas_call(inner_kernel, out_shape=(jax.ShapeDtypeStruct((nrows, widt...]
  transfers between devices with their start and end apart: 2 -> 2, of which waited for: 0 -> 0; matrix products, arithmetic and copies ran while one was open for 0% -> 0% of each run, Pallas kernels for 12% -> 17%
where the time goes in v4:
time: 35.2 us; the launch traced here: 35.1 us
  blocking collectives  20.3 us (58%)
  Pallas kernels  7.37 us (21%)
  starting transfers between devices  5.03 us (14%)
  local copies, waits for them, and re-layouts  1 us (3%)
  other arithmetic  0.7 us (2%)
  between operations  0.69 us (2%)
    all_to_all x1, blocking collectives, local(): got = lax.all_to_all(total, AXES, 0, 0, tiled=True)  20.3 us
    pallas_call x1, Pallas kernels, local(): pl.pallas_call(inner_kernel, out_shape=(jax.ShapeDtypeStruct((nrows, widt...  6.12 us
    ppermute x1, starting transfers between devices, local(): near = lax.ppermute(near_send, AXES, swaps + [(j, i) for i, j in swaps])  4.36 us
    pallas_call x1, Pallas kernels, local(): pl.pallas_call(functools.partial(edge_kernel, (down, across) if in_kernel...  1.25 us
    dynamic_slice x1, local copies, waits for them, and re-layouts, local(): far_send = lax.dynamic_slice_in_dim(basis, odd * last, tile, axis=0)  0.99 us
  transfers between devices with their start and end apart: 2, of which 0 were waited for; matrix products, arithmetic and copies ran while one was open for 0% of the time, Pallas kernels for 17%

profile of v4, /device:TPU:0, one launch (start us, length us, event | category | flops | bytes accessed | tf_op | source)
XLA Modules:
  0.0 35.1 jit_solution(17194537259113631467)
XLA Ops:
  0.6 1.0 %constant_dynamic-slice_fusion = (bf16[128,512]{1,0:T(8,128)(2,1)S(1)}, bf16[128,512]{1,0:T(8,128)(2,1)S(1)}) fusion(bf16[1536,512]{1,0:T(8,128)(2,1)} %bottom_ref.1, s32[]{:T(128)S(6)} %select_n.7, s32[]{:T(128)S(6)} %select_n.6), kind=kLoop, calls=%fused_computation.2 | loop fusion | bytes 524296 | tf_op jit(solution)/shard_map/dynamic_slice | solution.py:173
  1.6 0.7 %collective-permute-start.1 = (bf16[128,512]{1,0:T(8,128)(2,1)S(1)}, bf16[128,512]{1,0:T(8,128)(2,1)S(1)}, u32[]{:S(2)}, u32[]{:S(2)}) collective-permute-start(bf16[128,512]{1,0:T(8,128)(2,1)S(1)} %get-tuple-element.14), channel_id=1, source_target_pairs={{1,2},{3,4},{5,6},{7,8},{9,10},{11,12},{13,14},{15,16},{17,18},{19... | collective-permute-start | bytes 393224 | tf_op jit(solution)/shard_map/ppermute | solution.py:176
  2.3 4.4 %collective-permute-start = (bf16[128,512]{1,0:T(8,128)(2,1)S(1)}, bf16[128,512]{1,0:T(8,128)(2,1)S(1)}, u32[]{:S(2)}, u32[]{:S(2)}) collective-permute-start(bf16[128,512]{1,0:T(8,128)(2,1)S(1)} %get-tuple-element.15), channel_id=1, source_target_pairs={{0,1},{2,3},{4,5},{6,7},{8,9},{10,11},{12,13},{14,15},{16,17},{18,... | collective-permute-start | bytes 393224 | tf_op jit(solution)/shard_map/ppermute | solution.py:178
  6.7 0.0 copy-start
  6.7 6.1 %inner.1 = (bf16[1536,512]{1,0:T(8,128)(2,1)}, f32[2,128,512]{2,1,0:T(8,128)S(1)}, bf16[2,256,128]{2,1,0:T(8,128)(2,1)S(1)}, f32[512,512]{1,0:T(8,128)S(1)}) custom-call(s32[8,24]{1,0:T(8,128)} %bitcast.3, s32[24]{0:T(128)} %live_hbm.1, bf16[24,8,64,64]{3,2,1,0:T(8,128)(2,1)} %jac_hbm.1, bf16[1536,512]{1,0:T(8,128)(2,1)} %bottom_ref.1, f32[12,128]{1,0:T(8,128)} %bitcast.2), custom_call_target="tpu_custom_call" | custom-call | flops 2013265920 | bytes 8388608 | tf_op jit(solution)/shard_map/inner/pallas_call | solution.py:181
  12.8 0.0 collective-permute-done.1.far_ref
  12.8 0.0 collective-permute-done.near_ref
  12.8 0.0 copy-done
  12.8 1.3 %edges.1 = (bf16[1536,512]{1,0:T(8,128)(2,1)}, bf16[32,32,256]{2,1,0:T(8,128)(2,1)S(1)}) custom-call(bf16[128,512]{1,0:T(8,128)(2,1)S(1)} %collective-permute-done.near_ref, bf16[128,512]{1,0:T(8,128)(2,1)S(1)} %collective-permute-done.1.far_ref, f32[2,128,512]{2,1,0:T(8,128)S(1)} %get-tuple-element.8.edge_ref, ...), custom_call_target="tpu_custom_call", output_to_operand_aliasing={{0}: (7, {})} | custom-call | tf_op jit(solution)/shard_map/edges/pallas_call | solution.py:224
  14.1 20.3 %all_to_all.5 = bf16[32,32,256]{2,1,0:T(8,128)(2,1)S(1)} all-to-all(bf16[32,32,256]{2,1,0:T(8,128)(2,1)S(1)} %get-tuple-element.13), channel_id=1, replica_groups=mesh['mesh'=16,'col'=2] {'mesh','col'}, dimensions={0} | all-to-all | bytes 1048576 | tf_op jit(solution)/shard_map/all_to_all | solution.py:249
  34.4 0.1 convert_reduce_fusion
  34.4 0.6 %broadcast_multiply_fusion = f32[32,256]{1,0:T(8,128)} fusion(f32[32,256]{1,0:T(8,128)S(1)} %convert_reduce_fusion), kind=kLoop, calls=%fused_computation.1 | loop fusion | flops 8192 | bytes 65536 | tf_op jit(solution)/shard_map/mul | solution.py:250
Async XLA Ops:
  1.6 11.2 %collective-permute-start.1 = (bf16[128,512]{1,0:T(8,128)(2,1)S(1)}, bf16[128,512]{1,0:T(8,128)(2,1)S(1)}, u32[]{:S(2)}, u32[]{:S(2)}) collective-permute-start(bf16[128,512]{1,0:T(8,128)(2,1)S(1)} %get-tuple-element.14), channel_id=1, source_target_pairs={{1,2},{3,4},{5,6},{7,8},{9,10},{11,12},{13,14},{15,16},{17,18},{19... | collective-permute-start | bytes 393224 | tf_op jit(solution)/shard_map/ppermute | solution.py:176
  2.3 10.5 %collective-permute-start = (bf16[128,512]{1,0:T(8,128)(2,1)S(1)}, bf16[128,512]{1,0:T(8,128)(2,1)S(1)}, u32[]{:S(2)}, u32[]{:S(2)}) collective-permute-start(bf16[128,512]{1,0:T(8,128)(2,1)S(1)} %get-tuple-element.15), channel_id=1, source_target_pairs={{0,1},{2,3},{4,5},{6,7},{8,9},{10,11},{12,13},{14,15},{16,17},{18,... | collective-permute-start | bytes 393224 | tf_op jit(solution)/shard_map/ppermute | solution.py:178
  6.7 6.2 %copy-start = (bf16[1536,512]{1,0:T(8,128)(2,1)S(1)}, bf16[1536,512]{1,0:T(8,128)(2,1)}, u32[]{:S(2)}) copy-start(bf16[1536,512]{1,0:T(8,128)(2,1)} %bottom_ref.1) | copy-start | bytes 4718596

commit v5 on v4

--- a/solution.py
+++ b/solution.py
@@ -1,5 +1,3 @@
-import functools
-
 import jax
 import jax.numpy as jnp
 from jax import lax
@@ -121,9 +119,9 @@
 
 
 def edge_kernel(
-    chunks, near_ref, far_ref, edge_ref, arm_ref, top_ref, bottom_ref, part_ref, _,
-    image_ref, total_ref, staged, sems,
+    near_ref, far_ref, edge_ref, arm_ref, top_ref, bottom_ref, part_ref, _, image_ref, *rest,
 ):
+    *total_refs, staged, sems = rest
     tile, width = top_ref.shape
     nrows = image_ref.shape[0]
     odd = lax.rem(lax.axis_index(AXES), 2) == 1
@@ -142,17 +140,14 @@
         total = total + lax.dot_general(
             own_ref[...], rows, ROWS_DOT, preferred_element_type=jnp.float32
         )
-    total = total.astype(jnp.bfloat16)
-    if chunks is None:
-        total_ref[...] = total
+    if len(total_refs) == 1:
+        total_refs[0][...] = total.astype(jnp.bfloat16)
     else:
-        down, across = chunks
-        high, wide = width // down, width // across
-        for i in range(down):
-            for j in range(across):
-                total_ref[i * across + j] = total[
-                    i * high : (i + 1) * high, j * wide : (j + 1) * wide
-                ]
+        keep_ref, send_ref = total_refs
+        left, right = total[:, : width // 2], total[:, width // 2 :]
+        second = lax.axis_index("col") == 1
+        keep_ref[...] = jnp.where(second, right, left)
+        send_ref[...] = jnp.where(second, left, right).astype(jnp.bfloat16)
     for copy in copies:
         copy.wait()
 
@@ -219,13 +214,15 @@
         )
     )
 
-    in_kernel = (width // down) % 16 == 0 and (width // across) % 128 == 0
-    chunk = (count, width // down, width // across)
-    image, total = pl.pallas_call(
-        functools.partial(edge_kernel, (down, across) if in_kernel else None),
+    halved = across == 2
+    image, *totals = pl.pallas_call(
+        edge_kernel,
         out_shape=(
             jax.ShapeDtypeStruct((nrows, width), bf16),
-            jax.ShapeDtypeStruct(chunk if in_kernel else (width, width), bf16),
+            *(
+                jax.ShapeDtypeStruct((width, width // 2 if halved else width), kind)
+                for kind in ((f32, bf16) if halved else (bf16,))
+            ),
         ),
         grid=(1,),
         in_specs=[
@@ -234,7 +231,7 @@
             pl.BlockSpec((tile, width), lambda i: (nrows // tile - 1, 0)),
             whole(), whole(pl.ANY),
         ],
-        out_specs=(whole(pl.ANY), whole()),
+        out_specs=(whole(pl.ANY), *([whole()] * (1 + halved))),
         scratch_shapes=[
             pltpu.VMEM((2, tile, width), bf16),
             pltpu.SemaphoreType.DMA((2,)),
@@ -243,10 +240,17 @@
         compiler_params=pltpu.CompilerParams(vmem_limit_bytes=32 * 2**20),
         name="edges",
     )(near, far, edge, arm, basis, basis, part, image)
-    if not in_kernel:
-        total = total.reshape(down, width // down, across, width // across)
-        total = total.transpose(0, 2, 1, 3).reshape(chunk)
-    got = lax.all_to_all(total, AXES, 0, 0, tiled=True)
+    if halved:
+        keep, send = totals
+        got = lax.ppermute(send, "col", [(0, 1), (1, 0)])
+        total = (keep + got.astype(f32)).astype(bf16)
+        total = total.reshape(down, width // down, width // across)
+        got = lax.all_to_all(total, "mesh", 0, 0, tiled=True)
+    else:
+        total = totals[0].reshape(down, width // down, across, width // across)
+        total = total.transpose(0, 2, 1, 3)
+        total = total.reshape(count, width // down, width // across)
+        got = lax.all_to_all(total, AXES, 0, 0, tiled=True)
     projected = jnp.sum(got.astype(f32), axis=0) * (1.0 / (nrows * count))
     return (image, projected)
 

time: 35.2 us -> 32.5 us (0.923)
  blocking collectives: 20.3 us -> 15.9 us
  waiting for transfers between devices: 0.01 us -> 1.51 us
    all_to_all x1, blocking collectives: 20.3 us -> 15.9 us  [local(): got = lax.all_to_all(total, 'mesh', 0, 0, tiled=True)]
    ppermute x0 -> x1, waiting for transfers between devices: none -> 1.5 us  [local(): got = lax.ppermute(send, 'col', [(0, 1), (1, 0)])]
  transfers between devices with their start and end apart: 2 -> 3, of which waited for: 0 -> 1; matrix products, arithmetic and copies ran while one was open for 0% -> 0% of each run, Pallas kernels for 17% -> 19%
where the time goes in v5:
time: 32.5 us; the launch traced here: 32.3 us
  blocking collectives  15.9 us (49%)
  Pallas kernels  7.37 us (23%)
  starting transfers between devices  5.12 us (16%)
  waiting for transfers between devices  1.51 us (5%)
  local copies, waits for them, and re-layouts  1 us (3%)
  other arithmetic  0.72 us (2%)
  between operations  0.7 us (2%)
    all_to_all x1, blocking collectives, local(): got = lax.all_to_all(total, 'mesh', 0, 0, tiled=True)  15.9 us
    pallas_call x1, Pallas kernels, local(): pl.pallas_call(inner_kernel, out_shape=(jax.ShapeDtypeStruct((nrows, widt...  6.12 us
    ppermute x1, starting transfers between devices, local(): near = lax.ppermute(near_send, AXES, swaps + [(j, i) for i, j in swaps])  4.36 us
    ppermute x1, waiting for transfers between devices, local(): got = lax.ppermute(send, 'col', [(0, 1), (1, 0)])  1.5 us
    pallas_call x1, Pallas kernels, local(): pl.pallas_call(edge_kernel, out_shape=(jax.ShapeDtypeStruct((nrows, width...  1.25 us
    dynamic_slice x1, local copies, waits for them, and re-layouts, local(): far_send = lax.dynamic_slice_in_dim(basis, odd * last, tile, axis=0)  0.99 us
    ppermute x1, starting transfers between devices, local(): far = lax.ppermute(far_send, AXES, swaps + [(j, i) for i, j in swaps])  0.67 us
  transfers between devices with their start and end apart: 3, of which 1 were waited for; matrix products, arithmetic and copies ran while one was open for 0% of the time, Pallas kernels for 19%

profile of v5, /device:TPU:0, one launch (start us, length us, event | category | flops | bytes accessed | tf_op | source)
XLA Modules:
  0.0 32.3 jit_solution(8522704058989563916)
XLA Ops:
  0.6 1.0 %constant_dynamic-slice_fusion = (bf16[128,512]{1,0:T(8,128)(2,1)S(1)}, bf16[128,512]{1,0:T(8,128)(2,1)S(1)}) fusion(bf16[1536,512]{1,0:T(8,128)(2,1)} %bottom_ref.1, s32[]{:T(128)S(6)} %select_n.7, s32[]{:T(128)S(6)} %select_n.6), kind=kLoop, calls=%fused_computation.3 | loop fusion | bytes 524296 | tf_op jit(solution)/shard_map/dynamic_slice | solution.py:168
  1.6 0.7 %collective-permute-start.1 = (bf16[128,512]{1,0:T(8,128)(2,1)S(1)}, bf16[128,512]{1,0:T(8,128)(2,1)S(1)}, u32[]{:S(2)}, u32[]{:S(2)}) collective-permute-start(bf16[128,512]{1,0:T(8,128)(2,1)S(1)} %get-tuple-element.16), channel_id=1, source_target_pairs={{1,2},{3,4},{5,6},{7,8},{9,10},{11,12},{13,14},{15,16},{17,18},{19... | collective-permute-start | bytes 393224 | tf_op jit(solution)/shard_map/ppermute | solution.py:171
  2.3 4.4 %collective-permute-start = (bf16[128,512]{1,0:T(8,128)(2,1)S(1)}, bf16[128,512]{1,0:T(8,128)(2,1)S(1)}, u32[]{:S(2)}, u32[]{:S(2)}) collective-permute-start(bf16[128,512]{1,0:T(8,128)(2,1)S(1)} %get-tuple-element.17), channel_id=1, source_target_pairs={{0,1},{2,3},{4,5},{6,7},{8,9},{10,11},{12,13},{14,15},{16,17},{18,... | collective-permute-start | bytes 393224 | tf_op jit(solution)/shard_map/ppermute | solution.py:173
  6.7 0.0 copy-start
  6.7 6.1 %inner.1 = (bf16[1536,512]{1,0:T(8,128)(2,1)}, f32[2,128,512]{2,1,0:T(8,128)S(1)}, bf16[2,256,128]{2,1,0:T(8,128)(2,1)S(1)}, f32[512,512]{1,0:T(8,128)S(1)}) custom-call(s32[8,24]{1,0:T(8,128)} %bitcast.5, s32[24]{0:T(128)} %live_hbm.1, bf16[24,8,64,64]{3,2,1,0:T(8,128)(2,1)} %jac_hbm.1, bf16[1536,512]{1,0:T(8,128)(2,1)} %bottom_ref.1, f32[12,128]{1,0:T(8,128)} %bitcast.4), custom_call_target="tpu_custom_call" | custom-call | flops 2013265920 | bytes 8388608 | tf_op jit(solution)/shard_map/inner/pallas_call | solution.py:176
  12.8 0.0 collective-permute-done.1.far_ref
  12.8 0.0 collective-permute-done.near_ref
  12.8 0.0 copy-done
  12.8 1.3 %edges.1 = (bf16[1536,512]{1,0:T(8,128)(2,1)}, f32[512,256]{1,0:T(8,128)S(1)}, bf16[512,256]{1,0:T(8,128)(2,1)S(1)}) custom-call(bf16[128,512]{1,0:T(8,128)(2,1)S(1)} %collective-permute-done.near_ref, bf16[128,512]{1,0:T(8,128)(2,1)S(1)} %collective-permute-done.1.far_ref, ...), custom_call_target="tpu_custom_call", output_to_operand_aliasing={{0}: (7, {})} | custom-call | tf_op jit(solution)/shard_map/edges/pallas_call | solution.py:218
  14.1 0.1 collective-permute-start.2
  14.2 1.5 %collective-permute-done.2 = bf16[512,256]{1,0:T(8,128)(2,1)S(1)} collective-permute-done((bf16[512,256]{1,0:T(8,128)(2,1)S(1)}, bf16[512,256]{1,0:T(8,128)(2,1)S(1)}, u32[]{:S(2)}, u32[]{:S(2)}) %collective-permute-start.2) | collective-permute-done | bytes 262176 | tf_op jit(solution)/shard_map/ppermute | solution.py:245
  15.7 0.1 add_convert_fusion
  15.8 15.9 %all_to_all.5 = bf16[16,32,256]{2,1,0:T(8,128)(2,1)S(1)} all-to-all(bf16[16,32,256]{2,1,0:T(8,128)(2,1)S(1)} %bitcast.3), channel_id=1, replica_groups=mesh['mesh'=16,'col'=2] {'mesh'}, dimensions={0} | all-to-all | bytes 524288 | tf_op jit(solution)/shard_map/all_to_all | solution.py:248
  31.7 0.6 %broadcast_multiply_fusion = f32[32,256]{1,0:T(8,128)} fusion(f32[32,256]{1,0:T(8,128)S(1)} %convert_reduce_fusion), kind=kLoop, calls=%fused_computation.2 | loop fusion | flops 8192 | bytes 65536 | tf_op jit(solution)/shard_map/mul | solution.py:254
  (1 shorter events, 0.0 us)
Async XLA Ops:
  1.6 11.2 %collective-permute-start.1 = (bf16[128,512]{1,0:T(8,128)(2,1)S(1)}, bf16[128,512]{1,0:T(8,128)(2,1)S(1)}, u32[]{:S(2)}, u32[]{:S(2)}) collective-permute-start(bf16[128,512]{1,0:T(8,128)(2,1)S(1)} %get-tuple-element.16), channel_id=1, source_target_pairs={{1,2},{3,4},{5,6},{7,8},{9,10},{11,12},{13,14},{15,16},{17,18},{19... | collective-permute-start | bytes 393224 | tf_op jit(solution)/shard_map/ppermute | solution.py:171
  2.3 10.5 %collective-permute-start = (bf16[128,512]{1,0:T(8,128)(2,1)S(1)}, bf16[128,512]{1,0:T(8,128)(2,1)S(1)}, u32[]{:S(2)}, u32[]{:S(2)}) collective-permute-start(bf16[128,512]{1,0:T(8,128)(2,1)S(1)} %get-tuple-element.17), channel_id=1, source_target_pairs={{0,1},{2,3},{4,5},{6,7},{8,9},{10,11},{12,13},{14,15},{16,17},{18,... | collective-permute-start | bytes 393224 | tf_op jit(solution)/shard_map/ppermute | solution.py:173
  6.7 6.2 %copy-start = (bf16[1536,512]{1,0:T(8,128)(2,1)S(1)}, bf16[1536,512]{1,0:T(8,128)(2,1)}, u32[]{:S(2)}) copy-start(bf16[1536,512]{1,0:T(8,128)(2,1)} %bottom_ref.1) | copy-start | bytes 4718596
  14.1 1.6 %collective-permute-start.2 = (bf16[512,256]{1,0:T(8,128)(2,1)S(1)}, bf16[512,256]{1,0:T(8,128)(2,1)S(1)}, u32[]{:S(2)}, u32[]{:S(2)}) collective-permute-start(bf16[512,256]{1,0:T(8,128)(2,1)S(1)} %get-tuple-element.15), channel_id=1, source_target_pairs={{0,1},{1,0},{2,3},{3,2},{4,5},{5,4},{6,7},{7,6},{8,9},{9,8},{10,11... | collective-permute-start | bytes 786440 | tf_op jit(solution)/shard_map/ppermute | solution.py:245

commit v6 on v5

--- a/solution.py
+++ b/solution.py
@@ -37,6 +37,19 @@
     return jnp.concatenate([high, low], axis=0)
 
 
+def gathered_rows(cols_ref, live_ref, jac_ref, basis_ref, first, g):
+    nblk, slots, bsize, _ = jac_ref.shape
+    lane = lax.broadcasted_iota(jnp.int32, (1, slots * bsize), 1)
+    keep = jnp.where(lane < live_ref[g] * bsize, 1.0, 0.0).astype(jnp.bfloat16)
+    blocks = jnp.concatenate([jac_ref[g, s] for s in range(slots)], axis=1) * keep
+    rows = []
+    for s in range(slots):
+        at = jnp.clip(cols_ref[s, g] - first, 0, nblk - 1) * bsize
+        rows.append(basis_ref[pl.ds(pl.multiple_of(at, bsize), bsize), :])
+    rows = jnp.concatenate(rows, axis=0)
+    return jnp.dot(blocks, rows, preferred_element_type=jnp.float32)
+
+
 def apply_strip(strip, rows):
     both = jnp.dot(strip, rows, preferred_element_type=jnp.float32)
     half = strip.shape[0] // 2
@@ -46,7 +59,7 @@
 def inner_kernel(
     cols_hbm, live_hbm, jac_hbm, basis_hbm, acc_hbm,
     image_ref, edge_ref, arm_ref, part_ref,
-    cols_ref, live_ref, jac_ref, basis_ref, acc_ref, strips, staged, load_sems, store_sems,
+    cols_ref, live_ref, jac_ref, basis_ref, acc_ref, staged, load_sems, store_sems,
 ):
     nblk, _, bsize, _ = jac_ref.shape
     nrows = basis_ref.shape[0]
@@ -73,10 +86,11 @@
         if i == 0:
             rows = load(basis_hbm, basis_ref, 3)
 
-    def build(pair):
-        if pair % size == 0:
-            blocks[pair // size].wait()
-        strips[pair % 2] = strip_of(cols_ref, live_ref, jac_ref, acc_ref, first, pair)
+    def edge_strip(pair):
+        return strip_of(cols_ref, live_ref, jac_ref, acc_ref, first, pair)
+
+    row = lax.broadcasted_iota(jnp.int32, (tile, tile), 0)
+    lane = lax.broadcasted_iota(jnp.int32, (tile, tile), 1)
 
     def project(start, stop):
         return lax.dot_general(
@@ -92,23 +106,30 @@
 
     for copy in small:
         copy.wait()
-    build(0)
     rows.wait()
     middle = (pairs // 2) * tile
     for pair in range(pairs):
-        if pair + 1 < pairs:
-            build(pair + 1)
-        strip = strips[pair % 2]
+        if pair % size == 0:
+            blocks[pair // size].wait()
         start = pair * tile
         if pair == 0:
+            strip = edge_strip(pair)
             edge_ref[0] = apply_strip(strip[:, tile:], basis_ref[: 2 * tile, :])
             arm_ref[0] = strip[:, :tile]
         elif pair == pairs - 1:
+            strip = edge_strip(pair)
             edge_ref[1] = apply_strip(strip[:, : 2 * tile], basis_ref[nrows - 2 * tile :, :])
             arm_ref[1] = strip[:, 2 * tile :]
         else:
-            block = basis_ref[start - tile : start + 2 * tile, :]
-            staged[start : start + tile, :] = apply_strip(strip, block).astype(jnp.bfloat16)
+            weight = jnp.where(lane == row, acc_ref[pair : pair + 1, :], 0.0)
+            weight = jnp.sum(weight, axis=1, keepdims=True)
+            coupled = [
+                gathered_rows(cols_ref, live_ref, jac_ref, basis_ref, first, 2 * pair + side)
+                for side in range(2)
+            ]
+            own = basis_ref[start : start + tile, :].astype(jnp.float32)
+            total = jnp.concatenate(coupled, axis=0) + weight * own
+            staged[start : start + tile, :] = total.astype(jnp.bfloat16)
         if start + tile == middle:
             early = store(tile, middle, 0)
             part_ref[...] = project(tile, middle)
@@ -189,7 +210,6 @@
             pltpu.VMEM(jac_blocks.shape, bf16),
             pltpu.VMEM((nrows, width), bf16),
             pltpu.VMEM((nblk // 2, tile), f32),
-            pltpu.VMEM((2, 2 * tile, 3 * tile), bf16),
             pltpu.VMEM((nrows, width), bf16),
             pltpu.SemaphoreType.DMA((7,)),
             pltpu.SemaphoreType.DMA((2,)),

time: 32.5 us -> 32.5 us (level)
  no operation moved by 1% of the time
where the time goes in v6:
time: 32.5 us; the launch traced here: 32.3 us
  blocking collectives  15.9 us (49%)
  Pallas kernels  7.32 us (23%)
  starting transfers between devices  5.13 us (16%)
  waiting for transfers between devices  1.5 us (5%)
  local copies, waits for them, and re-layouts  1 us (3%)
  other arithmetic  0.72 us (2%)
  between operations  0.7 us (2%)
    all_to_all x1, blocking collectives, local(): got = lax.all_to_all(total, 'mesh', 0, 0, tiled=True)  15.9 us
    pallas_call x1, Pallas kernels, local(): pl.pallas_call(inner_kernel, out_shape=(jax.ShapeDtypeStruct((nrows, widt...  6.07 us
    ppermute x1, starting transfers between devices, local(): near = lax.ppermute(near_send, AXES, swaps + [(j, i) for i, j in swaps])  4.36 us
    ppermute x1, waiting for transfers between devices, local(): got = lax.ppermute(send, 'col', [(0, 1), (1, 0)])  1.5 us
    pallas_call x1, Pallas kernels, local(): pl.pallas_call(edge_kernel, out_shape=(jax.ShapeDtypeStruct((nrows, width...  1.25 us
    dynamic_slice x1, local copies, waits for them, and re-layouts, local(): far_send = lax.dynamic_slice_in_dim(basis, odd * last, tile, axis=0)  0.99 us
    ppermute x1, starting transfers between devices, local(): far = lax.ppermute(far_send, AXES, swaps + [(j, i) for i, j in swaps])  0.67 us
  transfers between devices with their start and end apart: 3, of which 1 were waited for; matrix products, arithmetic and copies ran while one was open for 0% of the time, Pallas kernels for 19%

profile of v6, /device:TPU:0, one launch (start us, length us, event | category | flops | bytes accessed | tf_op | source)
XLA Modules:
  0.0 32.3 jit_solution(7996765050518249937)
XLA Ops:
  0.6 1.0 %constant_dynamic-slice_fusion = (bf16[128,512]{1,0:T(8,128)(2,1)S(1)}, bf16[128,512]{1,0:T(8,128)(2,1)S(1)}) fusion(bf16[1536,512]{1,0:T(8,128)(2,1)} %bottom_ref.1, s32[]{:T(128)S(6)} %select_n.7, s32[]{:T(128)S(6)} %select_n.6), kind=kLoop, calls=%fused_computation.3 | loop fusion | bytes 524296 | tf_op jit(solution)/shard_map/dynamic_slice | solution.py:189
  1.6 0.7 %collective-permute-start.1 = (bf16[128,512]{1,0:T(8,128)(2,1)S(1)}, bf16[128,512]{1,0:T(8,128)(2,1)S(1)}, u32[]{:S(2)}, u32[]{:S(2)}) collective-permute-start(bf16[128,512]{1,0:T(8,128)(2,1)S(1)} %get-tuple-element.16), channel_id=1, source_target_pairs={{1,2},{3,4},{5,6},{7,8},{9,10},{11,12},{13,14},{15,16},{17,18},{19... | collective-permute-start | bytes 393224 | tf_op jit(solution)/shard_map/ppermute | solution.py:192
  2.3 4.4 %collective-permute-start = (bf16[128,512]{1,0:T(8,128)(2,1)S(1)}, bf16[128,512]{1,0:T(8,128)(2,1)S(1)}, u32[]{:S(2)}, u32[]{:S(2)}) collective-permute-start(bf16[128,512]{1,0:T(8,128)(2,1)S(1)} %get-tuple-element.17), channel_id=1, source_target_pairs={{0,1},{2,3},{4,5},{6,7},{8,9},{10,11},{12,13},{14,15},{16,17},{18,... | collective-permute-start | bytes 393224 | tf_op jit(solution)/shard_map/ppermute | solution.py:194
  6.7 0.0 copy-start
  6.7 6.1 %inner.1 = (bf16[1536,512]{1,0:T(8,128)(2,1)}, f32[2,128,512]{2,1,0:T(8,128)S(1)}, bf16[2,256,128]{2,1,0:T(8,128)(2,1)S(1)}, f32[512,512]{1,0:T(8,128)S(1)}) custom-call(s32[8,24]{1,0:T(8,128)} %bitcast.5, s32[24]{0:T(128)} %live_hbm.1, bf16[24,8,64,64]{3,2,1,0:T(8,128)(2,1)} %jac_hbm.1, bf16[1536,512]{1,0:T(8,128)(2,1)} %bottom_ref.1, f32[12,128]{1,0:T(8,128)} %bitcast.4), custom_call_target="tpu_custom_call" | custom-call | flops 2013265920 | bytes 8388608 | tf_op jit(solution)/shard_map/inner/pallas_call | solution.py:197
  12.7 0.0 collective-permute-done.1.far_ref
  12.8 0.0 collective-permute-done.near_ref
  12.8 0.0 copy-done
  12.8 1.2 %edges.1 = (bf16[1536,512]{1,0:T(8,128)(2,1)}, f32[512,256]{1,0:T(8,128)S(1)}, bf16[512,256]{1,0:T(8,128)(2,1)S(1)}) custom-call(bf16[128,512]{1,0:T(8,128)(2,1)S(1)} %collective-permute-done.near_ref, bf16[128,512]{1,0:T(8,128)(2,1)S(1)} %collective-permute-done.1.far_ref, ...), custom_call_target="tpu_custom_call", output_to_operand_aliasing={{0}: (7, {})} | custom-call | tf_op jit(solution)/shard_map/edges/pallas_call | solution.py:238
  14.0 0.1 collective-permute-start.2
  14.1 1.5 %collective-permute-done.2 = bf16[512,256]{1,0:T(8,128)(2,1)S(1)} collective-permute-done((bf16[512,256]{1,0:T(8,128)(2,1)S(1)}, bf16[512,256]{1,0:T(8,128)(2,1)S(1)}, u32[]{:S(2)}, u32[]{:S(2)}) %collective-permute-start.2) | collective-permute-done | bytes 262176 | tf_op jit(solution)/shard_map/ppermute | solution.py:265
  15.6 0.1 add_convert_fusion
  15.7 15.9 %all_to_all.5 = bf16[16,32,256]{2,1,0:T(8,128)(2,1)S(1)} all-to-all(bf16[16,32,256]{2,1,0:T(8,128)(2,1)S(1)} %bitcast.3), channel_id=1, replica_groups=mesh['mesh'=16,'col'=2] {'mesh'}, dimensions={0} | all-to-all | bytes 524288 | tf_op jit(solution)/shard_map/all_to_all | solution.py:268
  31.7 0.6 %broadcast_multiply_fusion = f32[32,256]{1,0:T(8,128)} fusion(f32[32,256]{1,0:T(8,128)S(1)} %convert_reduce_fusion), kind=kLoop, calls=%fused_computation.2 | loop fusion | flops 8192 | bytes 65536 | tf_op jit(solution)/shard_map/mul | solution.py:274
  (1 shorter events, 0.0 us)
Async XLA Ops:
  1.6 11.1 %collective-permute-start.1 = (bf16[128,512]{1,0:T(8,128)(2,1)S(1)}, bf16[128,512]{1,0:T(8,128)(2,1)S(1)}, u32[]{:S(2)}, u32[]{:S(2)}) collective-permute-start(bf16[128,512]{1,0:T(8,128)(2,1)S(1)} %get-tuple-element.16), channel_id=1, source_target_pairs={{1,2},{3,4},{5,6},{7,8},{9,10},{11,12},{13,14},{15,16},{17,18},{19... | collective-permute-start | bytes 393224 | tf_op jit(solution)/shard_map/ppermute | solution.py:192
  2.3 10.4 %collective-permute-start = (bf16[128,512]{1,0:T(8,128)(2,1)S(1)}, bf16[128,512]{1,0:T(8,128)(2,1)S(1)}, u32[]{:S(2)}, u32[]{:S(2)}) collective-permute-start(bf16[128,512]{1,0:T(8,128)(2,1)S(1)} %get-tuple-element.17), channel_id=1, source_target_pairs={{0,1},{2,3},{4,5},{6,7},{8,9},{10,11},{12,13},{14,15},{16,17},{18,... | collective-permute-start | bytes 393224 | tf_op jit(solution)/shard_map/ppermute | solution.py:194
  6.7 6.1 %copy-start = (bf16[1536,512]{1,0:T(8,128)(2,1)S(1)}, bf16[1536,512]{1,0:T(8,128)(2,1)}, u32[]{:S(2)}) copy-start(bf16[1536,512]{1,0:T(8,128)(2,1)} %bottom_ref.1) | copy-start | bytes 4718596
  14.0 1.6 %collective-permute-start.2 = (bf16[512,256]{1,0:T(8,128)(2,1)S(1)}, bf16[512,256]{1,0:T(8,128)(2,1)S(1)}, u32[]{:S(2)}, u32[]{:S(2)}) collective-permute-start(bf16[512,256]{1,0:T(8,128)(2,1)S(1)} %get-tuple-element.15), channel_id=1, source_target_pairs={{0,1},{1,0},{2,3},{3,2},{4,5},{5,4},{6,7},{7,6},{8,9},{9,8},{10,11... | collective-permute-start | bytes 786440 | tf_op jit(solution)/shard_map/ppermute | solution.py:265

commit v7 on v6

--- a/solution.py
+++ b/solution.py
@@ -56,35 +56,28 @@
     return both[:half] + both[half:]
 
 
+def slice_kernel(basis_hbm, far_ref, near_ref, sems):
+    tile = far_ref.shape[0]
+    last = basis_hbm.shape[0] - tile
+    odd = lax.rem(lax.axis_index(AXES), 2)
+    copies = []
+    for i, (at, target) in enumerate(((odd, far_ref), (1 - odd, near_ref))):
+        where = pl.ds(pl.multiple_of(at * last, tile), tile)
+        copies.append(pltpu.make_async_copy(basis_hbm.at[where], target, sems.at[i]))
+        copies[i].start()
+    for copy in copies:
+        copy.wait()
+
+
 def inner_kernel(
-    cols_hbm, live_hbm, jac_hbm, basis_hbm, acc_hbm,
-    image_ref, edge_ref, arm_ref, part_ref,
-    cols_ref, live_ref, jac_ref, basis_ref, acc_ref, staged, load_sems, store_sems,
+    cols_ref, live_ref, jac_ref, basis_ref, acc_ref,
+    image_ref, edge_ref, arm_ref, part_ref, staged, sems,
 ):
     nblk, _, bsize, _ = jac_ref.shape
     nrows = basis_ref.shape[0]
     tile = 2 * bsize
     pairs = nblk // 2
-    groups = 3 if pairs % 3 == 0 else 1
-    size = pairs // groups
     first = lax.axis_index(AXES) * nblk
-
-    def load(source, target, at):
-        copy = pltpu.make_async_copy(source, target, load_sems.at[at])
-        copy.start()
-        return copy
-
-    small = [
-        load(cols_hbm, cols_ref, 0),
-        load(live_hbm, live_ref, 1),
-        load(acc_hbm, acc_ref, 2),
-    ]
-    blocks = []
-    for i in range(groups):
-        where = pl.ds(2 * size * i, 2 * size)
-        blocks.append(load(jac_hbm.at[where], jac_ref.at[where], 4 + i))
-        if i == 0:
-            rows = load(basis_hbm, basis_ref, 3)
 
     def edge_strip(pair):
         return strip_of(cols_ref, live_ref, jac_ref, acc_ref, first, pair)
@@ -100,17 +93,12 @@
 
     def store(start, stop, at):
         where = pl.ds(start, stop - start)
-        copy = pltpu.make_async_copy(staged.at[where], image_ref.at[where], store_sems.at[at])
+        copy = pltpu.make_async_copy(staged.at[where], image_ref.at[where], sems.at[at])
         copy.start()
         return copy
 
-    for copy in small:
-        copy.wait()
-    rows.wait()
     middle = (pairs // 2) * tile
     for pair in range(pairs):
-        if pair % size == 0:
-            blocks[pair // size].wait()
         start = pair * tile
         if pair == 0:
             strip = edge_strip(pair)
@@ -140,7 +128,7 @@
 
 
 def edge_kernel(
-    near_ref, far_ref, edge_ref, arm_ref, top_ref, bottom_ref, part_ref, _, image_ref, *rest,
+    far_ref, near_ref, edge_ref, arm_ref, top_ref, bottom_ref, part_ref, _, image_ref, *rest,
 ):
     *total_refs, staged, sems = rest
     tile, width = top_ref.shape
@@ -183,17 +171,25 @@
     tile = 2 * bsize
     down, across = (lax.axis_size(axis) for axis in AXES)
     count = down * across
-    odd = lax.rem(lax.axis_index(AXES), 2)
-
-    last = nrows - tile
-    far_send = lax.dynamic_slice_in_dim(basis, odd * last, tile, axis=0)
-    near_send = lax.dynamic_slice_in_dim(basis, (1 - odd) * last, tile, axis=0)
+    f32, bf16 = jnp.float32, jnp.bfloat16
+    edge_shape = jax.ShapeDtypeStruct((tile, width), bf16)
+    far_send, near_send = pl.pallas_call(
+        slice_kernel,
+        out_shape=(edge_shape, edge_shape),
+        in_specs=[whole(pltpu.HBM)],
+        out_specs=(whole(), whole()),
+        scratch_shapes=[pltpu.SemaphoreType.DMA((2,))],
+        compiler_params=pltpu.CompilerParams(vmem_limit_bytes=4 * 2**20),
+        cost_estimate=pl.CostEstimate(
+            flops=2 * nrows * width * width * slots, bytes_accessed=0, transcendentals=0
+        ),
+        name="halo_rows",
+    )(pltpu.with_memory_space_constraint(basis, pltpu.HBM))
     swaps = [(i, i + 1) for i in range(1, count - 1, 2)]
     far = lax.ppermute(far_send, AXES, swaps + [(j, i) for i, j in swaps])
     swaps = [(i, i + 1) for i in range(0, count, 2)]
     near = lax.ppermute(near_send, AXES, swaps + [(j, i) for i, j in swaps])
 
-    f32, bf16 = jnp.float32, jnp.bfloat16
     image, edge, arm, part = pl.pallas_call(
         inner_kernel,
         out_shape=(
@@ -202,16 +198,10 @@
             jax.ShapeDtypeStruct((2, 2 * tile, tile), bf16),
             jax.ShapeDtypeStruct((width, width), f32),
         ),
-        in_specs=[whole(pltpu.HBM)] * 5,
+        in_specs=[whole(pltpu.SMEM), whole(pltpu.SMEM), whole(), whole(), whole()],
         out_specs=(whole(pltpu.HBM), whole(), whole(), whole()),
         scratch_shapes=[
-            pltpu.SMEM((slots, nblk), jnp.int32),
-            pltpu.SMEM((nblk,), jnp.int32),
-            pltpu.VMEM(jac_blocks.shape, bf16),
             pltpu.VMEM((nrows, width), bf16),
-            pltpu.VMEM((nblk // 2, tile), f32),
-            pltpu.VMEM((nrows, width), bf16),
-            pltpu.SemaphoreType.DMA((7,)),
             pltpu.SemaphoreType.DMA((2,)),
         ],
         compiler_params=pltpu.CompilerParams(vmem_limit_bytes=32 * 2**20),
@@ -222,16 +212,11 @@
         ),
         name="inner",
     )(
-        *(
-            pltpu.with_memory_space_constraint(array, pltpu.HBM)
-            for array in (
-                block_cols.T,
-                live_slots,
-                jac_blocks,
-                basis,
-                accumulation.reshape(nblk // 2, tile),
-            )
-        )
+        block_cols.T,
+        live_slots,
+        jac_blocks,
+        basis,
+        accumulation.reshape(nblk // 2, tile),
     )
 
     halved = across == 2
@@ -259,7 +244,7 @@
         input_output_aliases={7: 0},
         compiler_params=pltpu.CompilerParams(vmem_limit_bytes=32 * 2**20),
         name="edges",
-    )(near, far, edge, arm, basis, basis, part, image)
+    )(far, near, edge, arm, basis, basis, part, image)
     if halved:
         keep, send = totals
         got = lax.ppermute(send, "col", [(0, 1), (1, 0)])

time: 32.5 us -> 31.7 us (0.975)
  local copies, waits for them, and re-layouts: 1 us -> 0.02 us
  Pallas kernels: 7.32 us -> 6.52 us
  blocking collectives: 15.9 us -> 16.7 us
    pallas_call x1, Pallas kernels: 6.07 us -> 4.12 us  [local(): pl.pallas_call(inner_kernel, out_shape=(jax.ShapeDtypeStruct((nrows, widt...]
    pallas_call x0 -> x1, Pallas kernels: none -> 1.15 us  [local(): pl.pallas_call(slice_kernel, out_shape=(edge_shape, edge_shape), in_specs...]
    dynamic_slice x1 -> x0, local copies, waits for them, and re-layouts: 0.99 us -> none  [local(): far_send = lax.dynamic_slice_in_dim(basis, odd * last, tile, axis=0)]
    all_to_all x1, blocking collectives: 15.9 us -> 16.7 us  [local(): got = lax.all_to_all(total, 'mesh', 0, 0, tiled=True)]
  transfers between devices with their start and end apart: 3 -> 3, of which waited for: 1 -> 1; matrix products, arithmetic and copies ran while one was open for 0% -> 0% of each run, Pallas kernels for 19% -> 13%
where the time goes in v7:
time: 31.7 us; the launch traced here: 31.5 us
  blocking collectives  16.7 us (53%)
  Pallas kernels  6.52 us (21%)
  starting transfers between devices  5.26 us (17%)
  waiting for transfers between devices  1.5 us (5%)
  between operations  0.74 us (2%)
  other arithmetic  0.72 us (2%)
    all_to_all x1, blocking collectives, local(): got = lax.all_to_all(total, 'mesh', 0, 0, tiled=True)  16.7 us
    ppermute x1, starting transfers between devices, local(): near = lax.ppermute(near_send, AXES, swaps + [(j, i) for i, j in swaps])  4.36 us
    pallas_call x1, Pallas kernels, local(): pl.pallas_call(inner_kernel, out_shape=(jax.ShapeDtypeStruct((nrows, widt...  4.12 us
    ppermute x1, waiting for transfers between devices, local(): got = lax.ppermute(send, 'col', [(0, 1), (1, 0)])  1.5 us
    pallas_call x1, Pallas kernels, local(): pl.pallas_call(edge_kernel, out_shape=(jax.ShapeDtypeStruct((nrows, width...  1.25 us
    pallas_call x1, Pallas kernels, local(): pl.pallas_call(slice_kernel, out_shape=(edge_shape, edge_shape), in_specs...  1.15 us
    ppermute x1, starting transfers between devices, local(): far = lax.ppermute(far_send, AXES, swaps + [(j, i) for i, j in swaps])  0.8 us
  transfers between devices with their start and end apart: 3, of which 1 were waited for; matrix products, arithmetic and copies ran while one was open for 0% of the time, Pallas kernels for 13%

profile of v7, /device:TPU:0, one launch (start us, length us, event | category | flops | bytes accessed | tf_op | source)
XLA Modules:
  0.0 31.5 jit_solution(15320707220409069353)
XLA Ops:
  0.6 0.0 copy-start
  0.6 0.0 copy-start.2
  0.7 0.0 copy-start.4
  0.7 0.0 copy-start.3
  0.7 0.0 copy-start.1
  0.7 1.1 %halo_rows.1 = (bf16[128,512]{1,0:T(8,128)(2,1)S(1)}, bf16[128,512]{1,0:T(8,128)(2,1)S(1)}) custom-call(bf16[1536,512]{1,0:T(8,128)(2,1)} %bottom_ref.1), custom_call_target="tpu_custom_call" | custom-call | flops 6442450944 | tf_op jit(solution)/shard_map/halo_rows/pallas_call | solution.py:176
  1.8 0.8 %collective-permute-start = (bf16[128,512]{1,0:T(8,128)(2,1)S(1)}, bf16[128,512]{1,0:T(8,128)(2,1)S(1)}, u32[]{:S(2)}, u32[]{:S(2)}) collective-permute-start(bf16[128,512]{1,0:T(8,128)(2,1)S(1)} %get-tuple-element.11), channel_id=1, source_target_pairs={{1,2},{3,4},{5,6},{7,8},{9,10},{11,12},{13,14},{15,16},{17,18},{19... | collective-permute-start | bytes 393224 | tf_op jit(solution)/shard_map/ppermute | solution.py:189
  2.6 4.4 %collective-permute-start.1 = (bf16[128,512]{1,0:T(8,128)(2,1)S(1)}, bf16[128,512]{1,0:T(8,128)(2,1)S(1)}, u32[]{:S(2)}, u32[]{:S(2)}) collective-permute-start(bf16[128,512]{1,0:T(8,128)(2,1)S(1)} %get-tuple-element.12), channel_id=1, source_target_pairs={{0,1},{2,3},{4,5},{6,7},{8,9},{10,11},{12,13},{14,15},{16,17},{18,... | collective-permute-start | bytes 393224 | tf_op jit(solution)/shard_map/ppermute | solution.py:191
  7.0 0.0 copy-done
  7.0 0.0 copy-done.2
  7.0 0.0 copy-done.4
  7.0 0.0 copy-done.3
  7.0 0.0 copy-done.1
  7.0 4.1 %inner.1 = (bf16[1536,512]{1,0:T(8,128)(2,1)}, f32[2,128,512]{2,1,0:T(8,128)S(1)}, bf16[2,256,128]{2,1,0:T(8,128)(2,1)S(1)}, f32[512,512]{1,0:T(8,128)S(1)}) custom-call(s32[8,24]{1,0:T(8,128)S(1)} %bitcast.4, s32[24]{0:T(128)S(1)} %copy-done.4, bf16[24,8,64,64]{3,2,1,0:T(8,128)(2,1)S(1)} %copy-done.1, bf16[1536,512]{1,0:T(8,128)(2,1)S(1)} %copy-done, ...), custom_call_target="tpu_custom_call" | custom-call | flops 2013265920 | bytes 8388608 | tf_op jit(solution)/shard_map/inner/pallas_call | solution.py:193
  11.2 0.0 collective-permute-done.far_ref
  11.2 0.0 collective-permute-done.1.near_ref
  11.2 1.2 %edges.1 = (bf16[1536,512]{1,0:T(8,128)(2,1)}, f32[512,256]{1,0:T(8,128)S(1)}, bf16[512,256]{1,0:T(8,128)(2,1)S(1)}) custom-call(bf16[128,512]{1,0:T(8,128)(2,1)S(1)} %collective-permute-done.far_ref, bf16[128,512]{1,0:T(8,128)(2,1)S(1)} %collective-permute-done.1.near_ref, ...), custom_call_target="tpu_custom_call", output_to_operand_aliasing={{0}: (7, {})} | custom-call | tf_op jit(solution)/shard_map/edges/pallas_call | solution.py:223
  12.4 0.1 collective-permute-start.2
  12.5 1.5 %collective-permute-done.2 = bf16[512,256]{1,0:T(8,128)(2,1)S(1)} collective-permute-done((bf16[512,256]{1,0:T(8,128)(2,1)S(1)}, bf16[512,256]{1,0:T(8,128)(2,1)S(1)}, u32[]{:S(2)}, u32[]{:S(2)}) %collective-permute-start.2) | collective-permute-done | bytes 262176 | tf_op jit(solution)/shard_map/ppermute | solution.py:250
  14.0 0.1 add_convert_fusion
  14.1 16.7 %all_to_all.5 = bf16[16,32,256]{2,1,0:T(8,128)(2,1)S(1)} all-to-all(bf16[16,32,256]{2,1,0:T(8,128)(2,1)S(1)} %bitcast.5), channel_id=1, replica_groups=mesh['mesh'=16,'col'=2] {'mesh'}, dimensions={0} | all-to-all | bytes 524288 | tf_op jit(solution)/shard_map/all_to_all | solution.py:253
  30.9 0.6 %broadcast_multiply_fusion = f32[32,256]{1,0:T(8,128)} fusion(f32[32,256]{1,0:T(8,128)S(1)} %convert_reduce_fusion), kind=kLoop, calls=%fused_computation.2 | loop fusion | flops 8192 | bytes 65536 | tf_op jit(solution)/shard_map/mul | solution.py:259
  (1 shorter events, 0.0 us)
Async XLA Ops:
  0.6 6.4 %copy-start = (bf16[1536,512]{1,0:T(8,128)(2,1)S(1)}, bf16[1536,512]{1,0:T(8,128)(2,1)}, u32[]{:S(2)}) copy-start(bf16[1536,512]{1,0:T(8,128)(2,1)} %bottom_ref.1) | copy-start | bytes 4718596
  0.6 6.4 %copy-start.2 = (f32[1536]{0:T(1024)S(1)}, f32[1536]{0:T(1024)}, u32[]{:S(2)}) copy-start(f32[1536]{0:T(1024)} %param.9) | copy-start | bytes 18436
  0.7 6.4 %copy-start.4 = (s32[24]{0:T(128)S(1)}, s32[24]{0:T(128)}, u32[]{:S(2)}) copy-start(s32[24]{0:T(128)} %live_ref.1) | copy-start | bytes 292
  0.7 6.4 %copy-start.3 = (s32[24,8]{0,1:T(8,128)S(1)}, s32[24,8]{0,1:T(8,128)}, u32[]{:S(2)}) copy-start(s32[24,8]{0,1:T(8,128)} %param.7) | copy-start | bytes 2308
  0.7 6.4 %copy-start.1 = (bf16[24,8,64,64]{3,2,1,0:T(8,128)(2,1)S(1)}, bf16[24,8,64,64]{3,2,1,0:T(8,128)(2,1)}, u32[]{:S(2)}) copy-start(bf16[24,8,64,64]{3,2,1,0:T(8,128)(2,1)} %jac_ref.1) | copy-start | bytes 4718596
  1.8 9.3 %collective-permute-start = (bf16[128,512]{1,0:T(8,128)(2,1)S(1)}, bf16[128,512]{1,0:T(8,128)(2,1)S(1)}, u32[]{:S(2)}, u32[]{:S(2)}) collective-permute-start(bf16[128,512]{1,0:T(8,128)(2,1)S(1)} %get-tuple-element.11), channel_id=1, source_target_pairs={{1,2},{3,4},{5,6},{7,8},{9,10},{11,12},{13,14},{15,16},{17,18},{19... | collective-permute-start | bytes 393224 | tf_op jit(solution)/shard_map/ppermute | solution.py:189
  2.6 8.5 %collective-permute-start.1 = (bf16[128,512]{1,0:T(8,128)(2,1)S(1)}, bf16[128,512]{1,0:T(8,128)(2,1)S(1)}, u32[]{:S(2)}, u32[]{:S(2)}) collective-permute-start(bf16[128,512]{1,0:T(8,128)(2,1)S(1)} %get-tuple-element.12), channel_id=1, source_target_pairs={{0,1},{2,3},{4,5},{6,7},{8,9},{10,11},{12,13},{14,15},{16,17},{18,... | collective-permute-start | bytes 393224 | tf_op jit(solution)/shard_map/ppermute | solution.py:191
  12.4 1.6 %collective-permute-start.2 = (bf16[512,256]{1,0:T(8,128)(2,1)S(1)}, bf16[512,256]{1,0:T(8,128)(2,1)S(1)}, u32[]{:S(2)}, u32[]{:S(2)}) collective-permute-start(bf16[512,256]{1,0:T(8,128)(2,1)S(1)} %get-tuple-element.19), channel_id=1, source_target_pairs={{0,1},{1,0},{2,3},{3,2},{4,5},{5,4},{6,7},{7,6},{8,9},{9,8},{10,11... | collective-permute-start | bytes 786440 | tf_op jit(solution)/shard_map/ppermute | solution.py:250

commit v8 on v7

--- a/solution.py
+++ b/solution.py
@@ -37,19 +37,6 @@
     return jnp.concatenate([high, low], axis=0)
 
 
-def gathered_rows(cols_ref, live_ref, jac_ref, basis_ref, first, g):
-    nblk, slots, bsize, _ = jac_ref.shape
-    lane = lax.broadcasted_iota(jnp.int32, (1, slots * bsize), 1)
-    keep = jnp.where(lane < live_ref[g] * bsize, 1.0, 0.0).astype(jnp.bfloat16)
-    blocks = jnp.concatenate([jac_ref[g, s] for s in range(slots)], axis=1) * keep
-    rows = []
-    for s in range(slots):
-        at = jnp.clip(cols_ref[s, g] - first, 0, nblk - 1) * bsize
-        rows.append(basis_ref[pl.ds(pl.multiple_of(at, bsize), bsize), :])
-    rows = jnp.concatenate(rows, axis=0)
-    return jnp.dot(blocks, rows, preferred_element_type=jnp.float32)
-
-
 def apply_strip(strip, rows):
     both = jnp.dot(strip, rows, preferred_element_type=jnp.float32)
     half = strip.shape[0] // 2
@@ -71,7 +58,7 @@
 
 def inner_kernel(
     cols_ref, live_ref, jac_ref, basis_ref, acc_ref,
-    image_ref, edge_ref, arm_ref, part_ref, staged, sems,
+    image_ref, edge_ref, arm_ref, part_ref, strips, staged, sems,
 ):
     nblk, _, bsize, _ = jac_ref.shape
     nrows = basis_ref.shape[0]
@@ -79,12 +66,6 @@
     pairs = nblk // 2
     first = lax.axis_index(AXES) * nblk
 
-    def edge_strip(pair):
-        return strip_of(cols_ref, live_ref, jac_ref, acc_ref, first, pair)
-
-    row = lax.broadcasted_iota(jnp.int32, (tile, tile), 0)
-    lane = lax.broadcasted_iota(jnp.int32, (tile, tile), 1)
-
     def project(start, stop):
         return lax.dot_general(
             basis_ref[start:stop, :], staged[start:stop, :], ROWS_DOT,
@@ -97,34 +78,38 @@
         copy.start()
         return copy
 
+    def build(at):
+        strips[at % 2] = strip_of(cols_ref, live_ref, jac_ref, acc_ref, first, order[at])
+
+    order = [*range(1, pairs - 1), 0, pairs - 1]
     middle = (pairs // 2) * tile
-    for pair in range(pairs):
+    stored = tile
+    copies = []
+    build(0)
+    for at, pair in enumerate(order):
+        if at + 1 < pairs:
+            build(at + 1)
+        strip = strips[at % 2]
         start = pair * tile
+        stop = start + tile
         if pair == 0:
-            strip = edge_strip(pair)
             edge_ref[0] = apply_strip(strip[:, tile:], basis_ref[: 2 * tile, :])
             arm_ref[0] = strip[:, :tile]
         elif pair == pairs - 1:
-            strip = edge_strip(pair)
             edge_ref[1] = apply_strip(strip[:, : 2 * tile], basis_ref[nrows - 2 * tile :, :])
             arm_ref[1] = strip[:, 2 * tile :]
         else:
-            weight = jnp.where(lane == row, acc_ref[pair : pair + 1, :], 0.0)
-            weight = jnp.sum(weight, axis=1, keepdims=True)
-            coupled = [
-                gathered_rows(cols_ref, live_ref, jac_ref, basis_ref, first, 2 * pair + side)
-                for side in range(2)
-            ]
-            own = basis_ref[start : start + tile, :].astype(jnp.float32)
-            total = jnp.concatenate(coupled, axis=0) + weight * own
-            staged[start : start + tile, :] = total.astype(jnp.bfloat16)
-        if start + tile == middle:
-            early = store(tile, middle, 0)
+            block = basis_ref[start - tile : start + 2 * tile, :]
+            staged[start:stop, :] = apply_strip(strip, block).astype(jnp.bfloat16)
+            if pair % 3 == 0 or pair == pairs - 2:
+                copies.append(store(stored, stop, len(copies)))
+                stored = stop
+        if stop == middle:
             part_ref[...] = project(tile, middle)
-    late = store(middle, nrows - tile, 1)
-    part_ref[...] += project(middle, nrows - tile)
-    early.wait()
-    late.wait()
+        if pair == pairs - 2:
+            part_ref[...] += project(middle, nrows - tile)
+    for copy in copies:
+        copy.wait()
 
 
 def edge_kernel(
@@ -201,8 +186,9 @@
         in_specs=[whole(pltpu.SMEM), whole(pltpu.SMEM), whole(), whole(), whole()],
         out_specs=(whole(pltpu.HBM), whole(), whole(), whole()),
         scratch_shapes=[
+            pltpu.VMEM((2, 2 * tile, 3 * tile), bf16),
             pltpu.VMEM((nrows, width), bf16),
-            pltpu.SemaphoreType.DMA((2,)),
+            pltpu.SemaphoreType.DMA((nblk // 6 + 1,)),
         ],
         compiler_params=pltpu.CompilerParams(vmem_limit_bytes=32 * 2**20),
         cost_estimate=pl.CostEstimate(

time: 31.7 us -> 31.7 us (level)
  Pallas kernels: 6.52 us -> 6.88 us
    pallas_call x1, Pallas kernels: 4.12 us -> 4.49 us  [local(): pl.pallas_call(inner_kernel, out_shape=(jax.ShapeDtypeStruct((nrows, widt...]
    all_to_all x1, blocking collectives: 16.7 us -> 16.4 us  [local(): got = lax.all_to_all(total, 'mesh', 0, 0, tiled=True)]
  transfers between devices with their start and end apart: 3 -> 3, of which waited for: 1 -> 1; matrix products, arithmetic and copies ran while one was open for 0% -> 0% of each run, Pallas kernels for 13% -> 14%
where the time goes in v8:
time: 31.7 us; the launch traced here: 31.5 us
  blocking collectives  16.4 us (52%)
  Pallas kernels  6.88 us (22%)
  starting transfers between devices  5.27 us (17%)
  waiting for transfers between devices  1.49 us (5%)
  between operations  0.74 us (2%)
  other arithmetic  0.72 us (2%)
    all_to_all x1, blocking collectives, local(): got = lax.all_to_all(total, 'mesh', 0, 0, tiled=True)  16.4 us
    pallas_call x1, Pallas kernels, local(): pl.pallas_call(inner_kernel, out_shape=(jax.ShapeDtypeStruct((nrows, widt...  4.49 us
    ppermute x1, starting transfers between devices, local(): near = lax.ppermute(near_send, AXES, swaps + [(j, i) for i, j in swaps])  4.36 us
    ppermute x1, waiting for transfers between devices, local(): got = lax.ppermute(send, 'col', [(0, 1), (1, 0)])  1.49 us
    pallas_call x1, Pallas kernels, local(): pl.pallas_call(edge_kernel, out_shape=(jax.ShapeDtypeStruct((nrows, width...  1.24 us
    pallas_call x1, Pallas kernels, local(): pl.pallas_call(slice_kernel, out_shape=(edge_shape, edge_shape), in_specs...  1.15 us
    ppermute x1, starting transfers between devices, local(): far = lax.ppermute(far_send, AXES, swaps + [(j, i) for i, j in swaps])  0.8 us
  transfers between devices with their start and end apart: 3, of which 1 were waited for; matrix products, arithmetic and copies ran while one was open for 0% of the time, Pallas kernels for 14%

profile of v8, /device:TPU:0, one launch (start us, length us, event | category | flops | bytes accessed | tf_op | source)
XLA Modules:
  0.0 31.5 jit_solution(1581128217419955708)
XLA Ops:
  0.6 0.0 copy-start
  0.6 0.0 copy-start.2
  0.7 0.0 copy-start.4
  0.7 0.0 copy-start.3
  0.7 0.0 copy-start.1
  0.7 1.1 %halo_rows.1 = (bf16[128,512]{1,0:T(8,128)(2,1)S(1)}, bf16[128,512]{1,0:T(8,128)(2,1)S(1)}) custom-call(bf16[1536,512]{1,0:T(8,128)(2,1)} %bottom_ref.1), custom_call_target="tpu_custom_call" | custom-call | flops 6442450944 | tf_op jit(solution)/shard_map/halo_rows/pallas_call | solution.py:161
  1.8 0.8 %collective-permute-start = (bf16[128,512]{1,0:T(8,128)(2,1)S(1)}, bf16[128,512]{1,0:T(8,128)(2,1)S(1)}, u32[]{:S(2)}, u32[]{:S(2)}) collective-permute-start(bf16[128,512]{1,0:T(8,128)(2,1)S(1)} %get-tuple-element.11), channel_id=1, source_target_pairs={{1,2},{3,4},{5,6},{7,8},{9,10},{11,12},{13,14},{15,16},{17,18},{19... | collective-permute-start | bytes 393224 | tf_op jit(solution)/shard_map/ppermute | solution.py:174
  2.6 4.4 %collective-permute-start.1 = (bf16[128,512]{1,0:T(8,128)(2,1)S(1)}, bf16[128,512]{1,0:T(8,128)(2,1)S(1)}, u32[]{:S(2)}, u32[]{:S(2)}) collective-permute-start(bf16[128,512]{1,0:T(8,128)(2,1)S(1)} %get-tuple-element.12), channel_id=1, source_target_pairs={{0,1},{2,3},{4,5},{6,7},{8,9},{10,11},{12,13},{14,15},{16,17},{18,... | collective-permute-start | bytes 393224 | tf_op jit(solution)/shard_map/ppermute | solution.py:176
  7.0 0.0 copy-done
  7.0 0.0 copy-done.2
  7.0 0.0 copy-done.4
  7.0 0.0 copy-done.3
  7.0 0.0 copy-done.1
  7.0 4.5 %inner.1 = (bf16[1536,512]{1,0:T(8,128)(2,1)}, f32[2,128,512]{2,1,0:T(8,128)S(1)}, bf16[2,256,128]{2,1,0:T(8,128)(2,1)S(1)}, f32[512,512]{1,0:T(8,128)S(1)}) custom-call(s32[8,24]{1,0:T(8,128)S(1)} %bitcast.4, s32[24]{0:T(128)S(1)} %copy-done.4, bf16[24,8,64,64]{3,2,1,0:T(8,128)(2,1)S(1)} %copy-done.1, bf16[1536,512]{1,0:T(8,128)(2,1)S(1)} %copy-done, ...), custom_call_target="tpu_custom_call" | custom-call | flops 2013265920 | bytes 8388608 | tf_op jit(solution)/shard_map/inner/pallas_call | solution.py:178
  11.5 0.0 collective-permute-done.far_ref
  11.5 0.0 collective-permute-done.1.near_ref
  11.5 1.2 %edges.1 = (bf16[1536,512]{1,0:T(8,128)(2,1)}, f32[512,256]{1,0:T(8,128)S(1)}, bf16[512,256]{1,0:T(8,128)(2,1)S(1)}) custom-call(bf16[128,512]{1,0:T(8,128)(2,1)S(1)} %collective-permute-done.far_ref, bf16[128,512]{1,0:T(8,128)(2,1)S(1)} %collective-permute-done.1.near_ref, ...), custom_call_target="tpu_custom_call", output_to_operand_aliasing={{0}: (7, {})} | custom-call | tf_op jit(solution)/shard_map/edges/pallas_call | solution.py:209
  12.8 0.1 collective-permute-start.2
  12.9 1.5 %collective-permute-done.2 = bf16[512,256]{1,0:T(8,128)(2,1)S(1)} collective-permute-done((bf16[512,256]{1,0:T(8,128)(2,1)S(1)}, bf16[512,256]{1,0:T(8,128)(2,1)S(1)}, u32[]{:S(2)}, u32[]{:S(2)}) %collective-permute-start.2) | collective-permute-done | bytes 262176 | tf_op jit(solution)/shard_map/ppermute | solution.py:236
  14.4 0.1 add_convert_fusion
  14.5 16.4 %all_to_all.5 = bf16[16,32,256]{2,1,0:T(8,128)(2,1)S(1)} all-to-all(bf16[16,32,256]{2,1,0:T(8,128)(2,1)S(1)} %bitcast.5), channel_id=1, replica_groups=mesh['mesh'=16,'col'=2] {'mesh'}, dimensions={0} | all-to-all | bytes 524288 | tf_op jit(solution)/shard_map/all_to_all | solution.py:239
  30.9 0.6 %broadcast_multiply_fusion = f32[32,256]{1,0:T(8,128)} fusion(f32[32,256]{1,0:T(8,128)S(1)} %convert_reduce_fusion), kind=kLoop, calls=%fused_computation.2 | loop fusion | flops 8192 | bytes 65536 | tf_op jit(solution)/shard_map/mul | solution.py:245
  (1 shorter events, 0.0 us)
Async XLA Ops:
  0.6 6.4 %copy-start = (bf16[1536,512]{1,0:T(8,128)(2,1)S(1)}, bf16[1536,512]{1,0:T(8,128)(2,1)}, u32[]{:S(2)}) copy-start(bf16[1536,512]{1,0:T(8,128)(2,1)} %bottom_ref.1) | copy-start | bytes 4718596
  0.6 6.4 %copy-start.2 = (f32[1536]{0:T(1024)S(1)}, f32[1536]{0:T(1024)}, u32[]{:S(2)}) copy-start(f32[1536]{0:T(1024)} %param.9) | copy-start | bytes 18436
  0.7 6.4 %copy-start.4 = (s32[24]{0:T(128)S(1)}, s32[24]{0:T(128)}, u32[]{:S(2)}) copy-start(s32[24]{0:T(128)} %live_ref.1) | copy-start | bytes 292
  0.7 6.4 %copy-start.3 = (s32[24,8]{0,1:T(8,128)S(1)}, s32[24,8]{0,1:T(8,128)}, u32[]{:S(2)}) copy-start(s32[24,8]{0,1:T(8,128)} %param.7) | copy-start | bytes 2308
  0.7 6.4 %copy-start.1 = (bf16[24,8,64,64]{3,2,1,0:T(8,128)(2,1)S(1)}, bf16[24,8,64,64]{3,2,1,0:T(8,128)(2,1)}, u32[]{:S(2)}) copy-start(bf16[24,8,64,64]{3,2,1,0:T(8,128)(2,1)} %jac_ref.1) | copy-start | bytes 4718596
  1.8 9.7 %collective-permute-start = (bf16[128,512]{1,0:T(8,128)(2,1)S(1)}, bf16[128,512]{1,0:T(8,128)(2,1)S(1)}, u32[]{:S(2)}, u32[]{:S(2)}) collective-permute-start(bf16[128,512]{1,0:T(8,128)(2,1)S(1)} %get-tuple-element.11), channel_id=1, source_target_pairs={{1,2},{3,4},{5,6},{7,8},{9,10},{11,12},{13,14},{15,16},{17,18},{19... | collective-permute-start | bytes 393224 | tf_op jit(solution)/shard_map/ppermute | solution.py:174
  2.6 8.9 %collective-permute-start.1 = (bf16[128,512]{1,0:T(8,128)(2,1)S(1)}, bf16[128,512]{1,0:T(8,128)(2,1)S(1)}, u32[]{:S(2)}, u32[]{:S(2)}) collective-permute-start(bf16[128,512]{1,0:T(8,128)(2,1)S(1)} %get-tuple-element.12), channel_id=1, source_target_pairs={{0,1},{2,3},{4,5},{6,7},{8,9},{10,11},{12,13},{14,15},{16,17},{18,... | collective-permute-start | bytes 393224 | tf_op jit(solution)/shard_map/ppermute | solution.py:176
  12.8 1.6 %collective-permute-start.2 = (bf16[512,256]{1,0:T(8,128)(2,1)S(1)}, bf16[512,256]{1,0:T(8,128)(2,1)S(1)}, u32[]{:S(2)}, u32[]{:S(2)}) collective-permute-start(bf16[512,256]{1,0:T(8,128)(2,1)S(1)} %get-tuple-element.19), channel_id=1, source_target_pairs={{0,1},{1,0},{2,3},{3,2},{4,5},{5,4},{6,7},{7,6},{8,9},{9,8},{10,11... | collective-permute-start | bytes 786440 | tf_op jit(solution)/shard_map/ppermute | solution.py:236

commit v9 on v7

--- a/solution.py
+++ b/solution.py
@@ -79,17 +79,13 @@
     pairs = nblk // 2
     first = lax.axis_index(AXES) * nblk
 
-    def edge_strip(pair):
-        return strip_of(cols_ref, live_ref, jac_ref, acc_ref, first, pair)
-
-    row = lax.broadcasted_iota(jnp.int32, (tile, tile), 0)
-    lane = lax.broadcasted_iota(jnp.int32, (tile, tile), 1)
-
     def project(start, stop):
-        return lax.dot_general(
+        total = lax.dot_general(
             basis_ref[start:stop, :], staged[start:stop, :], ROWS_DOT,
             preferred_element_type=jnp.float32,
         )
+        parts, _, wide = part_ref.shape
+        return [total[:, i * wide : (i + 1) * wide] for i in range(parts)]
 
     def store(start, stop, at):
         where = pl.ds(start, stop - start)
@@ -97,68 +93,85 @@
         copy.start()
         return copy
 
+    row = lax.broadcasted_iota(jnp.int32, (tile, tile), 0)
+    lane = lax.broadcasted_iota(jnp.int32, (tile, tile), 1)
     middle = (pairs // 2) * tile
-    for pair in range(pairs):
+    stored = tile
+    copies = []
+    for pair in range(1, pairs - 1):
         start = pair * tile
-        if pair == 0:
-            strip = edge_strip(pair)
+        stop = start + tile
+        weight = jnp.where(lane == row, acc_ref[pair : pair + 1, :], 0.0)
+        weight = jnp.sum(weight, axis=1, keepdims=True)
+        coupled = [
+            gathered_rows(cols_ref, live_ref, jac_ref, basis_ref, first, 2 * pair + side)
+            for side in range(2)
+        ]
+        own = basis_ref[start:stop, :].astype(jnp.float32)
+        total = jnp.concatenate(coupled, axis=0) + weight * own
+        staged[start:stop, :] = total.astype(jnp.bfloat16)
+        if pair % 3 == 0 or pair == pairs - 2:
+            copies.append(store(stored, stop, len(copies)))
+            stored = stop
+        if stop == middle:
+            for i, half in enumerate(project(tile, middle)):
+                part_ref[i] = half
+    for side, pair in enumerate((0, pairs - 1)):
+        strip = strip_of(cols_ref, live_ref, jac_ref, acc_ref, first, pair)
+        if side == 0:
             edge_ref[0] = apply_strip(strip[:, tile:], basis_ref[: 2 * tile, :])
             arm_ref[0] = strip[:, :tile]
-        elif pair == pairs - 1:
-            strip = edge_strip(pair)
+        else:
             edge_ref[1] = apply_strip(strip[:, : 2 * tile], basis_ref[nrows - 2 * tile :, :])
             arm_ref[1] = strip[:, 2 * tile :]
-        else:
-            weight = jnp.where(lane == row, acc_ref[pair : pair + 1, :], 0.0)
-            weight = jnp.sum(weight, axis=1, keepdims=True)
-            coupled = [
-                gathered_rows(cols_ref, live_ref, jac_ref, basis_ref, first, 2 * pair + side)
-                for side in range(2)
-            ]
-            own = basis_ref[start : start + tile, :].astype(jnp.float32)
-            total = jnp.concatenate(coupled, axis=0) + weight * own
-            staged[start : start + tile, :] = total.astype(jnp.bfloat16)
-        if start + tile == middle:
-            early = store(tile, middle, 0)
-            part_ref[...] = project(tile, middle)
-    late = store(middle, nrows - tile, 1)
-    part_ref[...] += project(middle, nrows - tile)
-    early.wait()
-    late.wait()
+    for i, half in enumerate(project(middle, nrows - tile)):
+        part_ref[i] += half
+    for copy in copies:
+        copy.wait()
+
+
+def add_edges(part_ref, tiles, rows_ref, half):
+    update = lax.dot_general(
+        tiles, rows_ref[half], ROWS_DOT, preferred_element_type=jnp.float32
+    )
+    return part_ref[half] + update
+
+
+def leaving_half(parts):
+    return 1 - lax.axis_index("col") if parts == 2 else 0
 
 
 def edge_kernel(
-    far_ref, near_ref, edge_ref, arm_ref, top_ref, bottom_ref, part_ref, _, image_ref, *rest,
+    far_ref, near_ref, edge_ref, arm_ref, top_ref, bottom_ref, part_ref, _,
+    image_ref, rows_ref, send_ref, staged, sems,
 ):
-    *total_refs, staged, sems = rest
-    tile, width = top_ref.shape
+    tile = top_ref.shape[0]
     nrows = image_ref.shape[0]
+    parts, _, wide = rows_ref.shape
     odd = lax.rem(lax.axis_index(AXES), 2) == 1
     near, far = near_ref[...], far_ref[...]
     halos = (jnp.where(odd, near, far), jnp.where(odd, far, near))
-    total = part_ref[...]
     copies = []
-    for side, own_ref in enumerate((top_ref, bottom_ref)):
+    for side in range(2):
         rows = edge_ref[side] + apply_strip(arm_ref[side], halos[side])
         rows = rows.astype(jnp.bfloat16)
         staged[side] = rows
+        for i in range(parts):
+            rows_ref[i, side * tile : (side + 1) * tile, :] = rows[:, i * wide : (i + 1) * wide]
         where = pl.ds(0 if side == 0 else nrows - tile, tile)
         copy = pltpu.make_async_copy(staged.at[side], image_ref.at[where], sems.at[side])
         copy.start()
         copies.append(copy)
-        total = total + lax.dot_general(
-            own_ref[...], rows, ROWS_DOT, preferred_element_type=jnp.float32
-        )
-    if len(total_refs) == 1:
-        total_refs[0][...] = total.astype(jnp.bfloat16)
-    else:
-        keep_ref, send_ref = total_refs
-        left, right = total[:, : width // 2], total[:, width // 2 :]
-        second = lax.axis_index("col") == 1
-        keep_ref[...] = jnp.where(second, right, left)
-        send_ref[...] = jnp.where(second, left, right).astype(jnp.bfloat16)
+    tiles = jnp.concatenate([top_ref[...], bottom_ref[...]], axis=0)
+    send = add_edges(part_ref, tiles, rows_ref, leaving_half(parts))
+    send_ref[...] = send.astype(jnp.bfloat16)
     for copy in copies:
         copy.wait()
+
+
+def keep_kernel(top_ref, bottom_ref, rows_ref, part_ref, keep_ref):
+    tiles = jnp.concatenate([top_ref[...], bottom_ref[...]], axis=0)
+    keep_ref[...] = add_edges(part_ref, tiles, rows_ref, 1 - leaving_half(2))
 
 
 def whole(memory_space=pltpu.VMEM):
@@ -190,19 +203,22 @@
     swaps = [(i, i + 1) for i in range(0, count, 2)]
     near = lax.ppermute(near_send, AXES, swaps + [(j, i) for i, j in swaps])
 
+    halved = across == 2
+    parts = 2 if halved else 1
+    wide = width // parts
     image, edge, arm, part = pl.pallas_call(
         inner_kernel,
         out_shape=(
             jax.ShapeDtypeStruct((nrows, width), bf16),
             jax.ShapeDtypeStruct((2, tile, width), f32),
             jax.ShapeDtypeStruct((2, 2 * tile, tile), bf16),
-            jax.ShapeDtypeStruct((width, width), f32),
+            jax.ShapeDtypeStruct((parts, width, wide), f32),
         ),
         in_specs=[whole(pltpu.SMEM), whole(pltpu.SMEM), whole(), whole(), whole()],
         out_specs=(whole(pltpu.HBM), whole(), whole(), whole()),
         scratch_shapes=[
             pltpu.VMEM((nrows, width), bf16),
-            pltpu.SemaphoreType.DMA((2,)),
+            pltpu.SemaphoreType.DMA((nblk // 6 + 1,)),
         ],
         compiler_params=pltpu.CompilerParams(vmem_limit_bytes=32 * 2**20),
         cost_estimate=pl.CostEstimate(
@@ -219,24 +235,20 @@
         accumulation.reshape(nblk // 2, tile),
     )
 
-    halved = across == 2
-    image, *totals = pl.pallas_call(
+    ends = [
+        pl.BlockSpec((tile, width), lambda i: (0, 0)),
+        pl.BlockSpec((tile, width), lambda i: (nrows // tile - 1, 0)),
+    ]
+    image, rows, send = pl.pallas_call(
         edge_kernel,
         out_shape=(
             jax.ShapeDtypeStruct((nrows, width), bf16),
-            *(
-                jax.ShapeDtypeStruct((width, width // 2 if halved else width), kind)
-                for kind in ((f32, bf16) if halved else (bf16,))
-            ),
+            jax.ShapeDtypeStruct((parts, 2 * tile, wide), bf16),
+            jax.ShapeDtypeStruct((width, wide), bf16),
         ),
         grid=(1,),
-        in_specs=[
-            whole(), whole(), whole(), whole(),
-            pl.BlockSpec((tile, width), lambda i: (0, 0)),
-            pl.BlockSpec((tile, width), lambda i: (nrows // tile - 1, 0)),
-            whole(), whole(pl.ANY),
-        ],
-        out_specs=(whole(pl.ANY), *([whole()] * (1 + halved))),
+        in_specs=[whole(), whole(), whole(), whole(), *ends, whole(), whole(pl.ANY)],
+        out_specs=(whole(pl.ANY), whole(), whole()),
         scratch_shapes=[
             pltpu.VMEM((2, tile, width), bf16),
             pltpu.SemaphoreType.DMA((2,)),
@@ -246,13 +258,24 @@
         name="edges",
     )(far, near, edge, arm, basis, basis, part, image)
     if halved:
-        keep, send = totals
         got = lax.ppermute(send, "col", [(0, 1), (1, 0)])
+        keep = pl.pallas_call(
+            keep_kernel,
+            out_shape=jax.ShapeDtypeStruct((width, wide), f32),
+            grid=(1,),
+            in_specs=[*ends, whole(), whole()],
+            out_specs=whole(),
+            compiler_params=pltpu.CompilerParams(vmem_limit_bytes=32 * 2**20),
+            cost_estimate=pl.CostEstimate(
+                flops=4 * tile * width * width, bytes_accessed=2**21, transcendentals=0
+            ),
+            name="kept_half",
+        )(basis, basis, rows, part)
         total = (keep + got.astype(f32)).astype(bf16)
         total = total.reshape(down, width // down, width // across)
         got = lax.all_to_all(total, "mesh", 0, 0, tiled=True)
     else:
-        total = totals[0].reshape(down, width // down, across, width // across)
+        total = send.reshape(down, width // down, across, width // across)
         total = total.transpose(0, 2, 1, 3)
         total = total.reshape(count, width // down, width // across)
         got = lax.all_to_all(total, AXES, 0, 0, tiled=True)

time: 31.7 us -> 31.5 us (level)
  no operation moved by 1% of the time
where the time goes in v9:
time: 31.5 us; the launch traced here: 31.3 us
  blocking collectives  17 us (54%)
  Pallas kernels  6.27 us (20%)
  starting transfers between devices  5.25 us (17%)
  waiting for transfers between devices  1.24 us (4%)
  between operations  0.74 us (2%)
  other arithmetic  0.72 us (2%)
    all_to_all x1, blocking collectives, local(): got = lax.all_to_all(total, 'mesh', 0, 0, tiled=True)  17 us
    ppermute x1, starting transfers between devices, local(): near = lax.ppermute(near_send, AXES, swaps + [(j, i) for i, j in swaps])  4.36 us
    pallas_call x1, Pallas kernels, local(): pl.pallas_call(inner_kernel, out_shape=(jax.ShapeDtypeStruct((nrows, widt...  3.81 us
    ppermute x1, waiting for transfers between devices, local(): got = lax.ppermute(send, 'col', [(0, 1), (1, 0)])  1.24 us
    pallas_call x1, Pallas kernels, local(): pl.pallas_call(slice_kernel, out_shape=(edge_shape, edge_shape), in_specs...  1.15 us
    pallas_call x1, Pallas kernels, local(): pl.pallas_call(edge_kernel, out_shape=(jax.ShapeDtypeStruct((nrows, width...  1.04 us
    ppermute x1, starting transfers between devices, local(): far = lax.ppermute(far_send, AXES, swaps + [(j, i) for i, j in swaps])  0.8 us
  transfers between devices with their start and end apart: 3, of which 1 were waited for; matrix products, arithmetic and copies ran while one was open for 0% of the time, Pallas kernels for 13%

profile of v9, /device:TPU:0, one launch (start us, length us, event | category | flops | bytes accessed | tf_op | source)
XLA Modules:
  0.0 31.3 jit_solution(15532905004688114805)
XLA Ops:
  0.6 0.0 copy-start
  0.6 0.0 copy-start.2
  0.7 0.0 copy-start.4
  0.7 0.0 copy-start.3
  0.7 0.0 copy-start.1
  0.7 1.1 %halo_rows.1 = (bf16[128,512]{1,0:T(8,128)(2,1)S(1)}, bf16[128,512]{1,0:T(8,128)(2,1)S(1)}) custom-call(bf16[1536,512]{1,0:T(8,128)(2,1)} %bottom_ref.3), custom_call_target="tpu_custom_call" | custom-call | flops 6442450944 | tf_op jit(solution)/shard_map/halo_rows/pallas_call | solution.py:189
  1.8 0.8 %collective-permute-start = (bf16[128,512]{1,0:T(8,128)(2,1)S(1)}, bf16[128,512]{1,0:T(8,128)(2,1)S(1)}, u32[]{:S(2)}, u32[]{:S(2)}) collective-permute-start(bf16[128,512]{1,0:T(8,128)(2,1)S(1)} %get-tuple-element.11), channel_id=1, source_target_pairs={{1,2},{3,4},{5,6},{7,8},{9,10},{11,12},{13,14},{15,16},{17,18},{19... | collective-permute-start | bytes 393224 | tf_op jit(solution)/shard_map/ppermute | solution.py:202
  2.6 4.4 %collective-permute-start.1 = (bf16[128,512]{1,0:T(8,128)(2,1)S(1)}, bf16[128,512]{1,0:T(8,128)(2,1)S(1)}, u32[]{:S(2)}, u32[]{:S(2)}) collective-permute-start(bf16[128,512]{1,0:T(8,128)(2,1)S(1)} %get-tuple-element.12), channel_id=1, source_target_pairs={{0,1},{2,3},{4,5},{6,7},{8,9},{10,11},{12,13},{14,15},{16,17},{18,... | collective-permute-start | bytes 393224 | tf_op jit(solution)/shard_map/ppermute | solution.py:204
  7.0 0.0 copy-done
  7.0 0.0 copy-done.2
  7.0 0.0 copy-done.4
  7.0 0.0 copy-done.3
  7.0 0.0 copy-done.1
  7.0 3.8 %inner.1 = (bf16[1536,512]{1,0:T(8,128)(2,1)}, f32[2,128,512]{2,1,0:T(8,128)S(1)}, bf16[2,256,128]{2,1,0:T(8,128)(2,1)S(1)}, f32[2,512,256]{2,1,0:T(8,128)S(1)}) custom-call(s32[8,24]{1,0:T(8,128)S(1)} %bitcast.4, s32[24]{0:T(128)S(1)} %copy-done.4, bf16[24,8,64,64]{3,2,1,0:T(8,128)(2,1)S(1)} %copy-done.1, bf16[1536,512]{1,0:T(8,128)(2,1)S(1)} %copy-done, ...), custom_call_target="tpu_custom_call" | custom-call | flops 2013265920 | bytes 8388608 | tf_op jit(solution)/shard_map/inner/pallas_call | solution.py:209
  10.8 0.0 collective-permute-done.far_ref
  10.9 0.0 collective-permute-done.1.near_ref
  10.9 1.0 %edges.1 = (bf16[1536,512]{1,0:T(8,128)(2,1)}, bf16[2,256,256]{2,1,0:T(8,128)(2,1)S(1)}, bf16[512,256]{1,0:T(8,128)(2,1)S(1)}) custom-call(bf16[128,512]{1,0:T(8,128)(2,1)S(1)} %collective-permute-done.far_ref, bf16[128,512]{1,0:T(8,128)(2,1)S(1)} %collective-permute-done.1.near_ref, ...), custom_call_target="tpu_custom_call", output_to_operand_aliasing={{0}: (7, {})} | custom-call | tf_op jit(solution)/shard_map/edges/pallas_call | solution.py:242
  11.9 0.1 collective-permute-start.2
  12.0 0.3 kept_half.1
  12.3 1.2 %collective-permute-done.2 = bf16[512,256]{1,0:T(8,128)(2,1)S(1)} collective-permute-done((bf16[512,256]{1,0:T(8,128)(2,1)S(1)}, bf16[512,256]{1,0:T(8,128)(2,1)S(1)}, u32[]{:S(2)}, u32[]{:S(2)}) %collective-permute-start.2) | collective-permute-done | bytes 262176 | tf_op jit(solution)/shard_map/ppermute | solution.py:261
  13.5 0.1 add_convert_fusion
  13.6 17.0 %all_to_all.5 = bf16[16,32,256]{2,1,0:T(8,128)(2,1)S(1)} all-to-all(bf16[16,32,256]{2,1,0:T(8,128)(2,1)S(1)} %bitcast.5), channel_id=1, replica_groups=mesh['mesh'=16,'col'=2] {'mesh'}, dimensions={0} | all-to-all | bytes 524288 | tf_op jit(solution)/shard_map/all_to_all | solution.py:276
  30.7 0.6 %broadcast_multiply_fusion = f32[32,256]{1,0:T(8,128)} fusion(f32[32,256]{1,0:T(8,128)S(1)} %convert_reduce_fusion), kind=kLoop, calls=%fused_computation.2 | loop fusion | flops 8192 | bytes 65536 | tf_op jit(solution)/shard_map/mul | solution.py:282
  (1 shorter events, 0.0 us)
Async XLA Ops:
  0.6 6.4 %copy-start = (bf16[1536,512]{1,0:T(8,128)(2,1)S(1)}, bf16[1536,512]{1,0:T(8,128)(2,1)}, u32[]{:S(2)}) copy-start(bf16[1536,512]{1,0:T(8,128)(2,1)} %bottom_ref.3) | copy-start | bytes 4718596
  0.6 6.4 %copy-start.2 = (f32[1536]{0:T(1024)S(1)}, f32[1536]{0:T(1024)}, u32[]{:S(2)}) copy-start(f32[1536]{0:T(1024)} %param.9) | copy-start | bytes 18436
  0.7 6.4 %copy-start.4 = (s32[24]{0:T(128)S(1)}, s32[24]{0:T(128)}, u32[]{:S(2)}) copy-start(s32[24]{0:T(128)} %live_ref.1) | copy-start | bytes 292
  0.7 6.4 %copy-start.3 = (s32[24,8]{0,1:T(8,128)S(1)}, s32[24,8]{0,1:T(8,128)}, u32[]{:S(2)}) copy-start(s32[24,8]{0,1:T(8,128)} %param.7) | copy-start | bytes 2308
  0.7 6.4 %copy-start.1 = (bf16[24,8,64,64]{3,2,1,0:T(8,128)(2,1)S(1)}, bf16[24,8,64,64]{3,2,1,0:T(8,128)(2,1)}, u32[]{:S(2)}) copy-start(bf16[24,8,64,64]{3,2,1,0:T(8,128)(2,1)} %jac_ref.1) | copy-start | bytes 4718596
  1.8 9.0 %collective-permute-start = (bf16[128,512]{1,0:T(8,128)(2,1)S(1)}, bf16[128,512]{1,0:T(8,128)(2,1)S(1)}, u32[]{:S(2)}, u32[]{:S(2)}) collective-permute-start(bf16[128,512]{1,0:T(8,128)(2,1)S(1)} %get-tuple-element.11), channel_id=1, source_target_pairs={{1,2},{3,4},{5,6},{7,8},{9,10},{11,12},{13,14},{15,16},{17,18},{19... | collective-permute-start | bytes 393224 | tf_op jit(solution)/shard_map/ppermute | solution.py:202
  2.6 8.2 %collective-permute-start.1 = (bf16[128,512]{1,0:T(8,128)(2,1)S(1)}, bf16[128,512]{1,0:T(8,128)(2,1)S(1)}, u32[]{:S(2)}, u32[]{:S(2)}) collective-permute-start(bf16[128,512]{1,0:T(8,128)(2,1)S(1)} %get-tuple-element.12), channel_id=1, source_target_pairs={{0,1},{2,3},{4,5},{6,7},{8,9},{10,11},{12,13},{14,15},{16,17},{18,... | collective-permute-start | bytes 393224 | tf_op jit(solution)/shard_map/ppermute | solution.py:204
  11.9 1.6 %collective-permute-start.2 = (bf16[512,256]{1,0:T(8,128)(2,1)S(1)}, bf16[512,256]{1,0:T(8,128)(2,1)S(1)}, u32[]{:S(2)}, u32[]{:S(2)}) collective-permute-start(bf16[512,256]{1,0:T(8,128)(2,1)S(1)} %get-tuple-element.19), channel_id=1, source_target_pairs={{0,1},{1,0},{2,3},{3,2},{4,5},{5,4},{6,7},{7,6},{8,9},{9,8},{10,11... | collective-permute-start | bytes 786440 | tf_op jit(solution)/shard_map/ppermute | solution.py:261

commit v10 on v9

--- a/solution.py
+++ b/solution.py
@@ -1,3 +1,5 @@
+import functools
+
 import jax
 import jax.numpy as jnp
 from jax import lax
@@ -6,7 +8,7 @@
 from jax.sharding import PartitionSpec as P
 
 REACH = 2
-AXES = ("mesh", "col")
+AXES = ("outer", "inner", "col")
 ROWS_DOT = (((0,), (0,)), ((), ()))
 
 
@@ -137,12 +139,22 @@
     return part_ref[half] + update
 
 
+def put_blocks(ref, value, order):
+    if order is None:
+        ref[...] = value.astype(ref.dtype)
+        return
+    high = value.shape[0] // len(order)
+    for to, source in enumerate(order):
+        block = value[source * high : (source + 1) * high, :]
+        ref[to * high : (to + 1) * high, :] = block.astype(ref.dtype)
+
+
 def leaving_half(parts):
     return 1 - lax.axis_index("col") if parts == 2 else 0
 
 
 def edge_kernel(
-    far_ref, near_ref, edge_ref, arm_ref, top_ref, bottom_ref, part_ref, _,
+    order, far_ref, near_ref, edge_ref, arm_ref, top_ref, bottom_ref, part_ref, _,
     image_ref, rows_ref, send_ref, staged, sems,
 ):
     tile = top_ref.shape[0]
@@ -164,14 +176,15 @@
         copies.append(copy)
     tiles = jnp.concatenate([top_ref[...], bottom_ref[...]], axis=0)
     send = add_edges(part_ref, tiles, rows_ref, leaving_half(parts))
-    send_ref[...] = send.astype(jnp.bfloat16)
+    put_blocks(send_ref, send, order)
     for copy in copies:
         copy.wait()
 
 
-def keep_kernel(top_ref, bottom_ref, rows_ref, part_ref, keep_ref):
+def keep_kernel(order, top_ref, bottom_ref, rows_ref, part_ref, keep_ref):
     tiles = jnp.concatenate([top_ref[...], bottom_ref[...]], axis=0)
-    keep_ref[...] = add_edges(part_ref, tiles, rows_ref, 1 - leaving_half(2))
+    keep = add_edges(part_ref, tiles, rows_ref, 1 - leaving_half(2))
+    put_blocks(keep_ref, keep, order)
 
 
 def whole(memory_space=pltpu.VMEM):
@@ -182,7 +195,8 @@
     nrows, width = basis.shape
     nblk, slots, bsize, _ = jac_blocks.shape
     tile = 2 * bsize
-    down, across = (lax.axis_size(axis) for axis in AXES)
+    outer, inner, across = (lax.axis_size(axis) for axis in AXES)
+    down = outer * inner
     count = down * across
     f32, bf16 = jnp.float32, jnp.bfloat16
     edge_shape = jax.ShapeDtypeStruct((tile, width), bf16)
@@ -206,6 +220,9 @@
     halved = across == 2
     parts = 2 if halved else 1
     wide = width // parts
+    order = None
+    if halved and (width // down) % 16 == 0:
+        order = [o * inner + i for i in range(inner) for o in range(outer)]
     image, edge, arm, part = pl.pallas_call(
         inner_kernel,
         out_shape=(
@@ -240,7 +257,7 @@
         pl.BlockSpec((tile, width), lambda i: (nrows // tile - 1, 0)),
     ]
     image, rows, send = pl.pallas_call(
-        edge_kernel,
+        functools.partial(edge_kernel, order),
         out_shape=(
             jax.ShapeDtypeStruct((nrows, width), bf16),
             jax.ShapeDtypeStruct((parts, 2 * tile, wide), bf16),
@@ -260,7 +277,7 @@
     if halved:
         got = lax.ppermute(send, "col", [(0, 1), (1, 0)])
         keep = pl.pallas_call(
-            keep_kernel,
+            functools.partial(keep_kernel, order),
             out_shape=jax.ShapeDtypeStruct((width, wide), f32),
             grid=(1,),
             in_specs=[*ends, whole(), whole()],
@@ -272,8 +289,9 @@
             name="kept_half",
         )(basis, basis, rows, part)
         total = (keep + got.astype(f32)).astype(bf16)
-        total = total.reshape(down, width // down, width // across)
-        got = lax.all_to_all(total, "mesh", 0, 0, tiled=True)
+        total = total.reshape(down, width // down, wide)
+        group = AXES[:2] if order is None else (AXES[1], AXES[0])
+        got = lax.all_to_all(total, group, 0, 0, tiled=True)
     else:
         total = send.reshape(down, width // down, across, width // across)
         total = total.transpose(0, 2, 1, 3)
@@ -284,9 +302,12 @@
 
 
 def solution(mesh):
+    rows, cols = mesh.devices.shape
+    outer = 4 if rows % 4 == 0 else 1
+    split = jax.sharding.Mesh(mesh.devices.reshape(outer, rows // outer, cols), AXES)
     return jax.shard_map(
         local,
-        mesh=mesh,
+        mesh=split,
         in_specs=(
             P(AXES, None),
             P(AXES, None, None, None),
@@ -294,6 +315,6 @@
             P(AXES),
             P(AXES),
         ),
-        out_specs=(P(AXES, None), P("mesh", "col")),
+        out_specs=(P(AXES, None), P(AXES[:2], "col")),
         check_vma=False,
     )

time: 31.5 us -> 32.2 us (1.022)
  blocking collectives: 17 us -> 17.7 us
    all_to_all x1, blocking collectives: 17 us -> 17.7 us  [local(): got = lax.all_to_all(total, group, 0, 0, tiled=True)]
where the time goes in v10:
time: 32.2 us; the launch traced here: 32 us
  blocking collectives  17.7 us (55%)
  Pallas kernels  6.28 us (20%)
  starting transfers between devices  5.25 us (16%)
  waiting for transfers between devices  1.24 us (4%)
  between operations  0.75 us (2%)
  other arithmetic  0.72 us (2%)
    all_to_all x1, blocking collectives, local(): got = lax.all_to_all(total, group, 0, 0, tiled=True)  17.7 us
    ppermute x1, starting transfers between devices, local(): near = lax.ppermute(near_send, AXES, swaps + [(j, i) for i, j in swaps])  4.36 us
    pallas_call x1, Pallas kernels, local(): pl.pallas_call(inner_kernel, out_shape=(jax.ShapeDtypeStruct((nrows, widt...  3.81 us
    ppermute x1, waiting for transfers between devices, local(): got = lax.ppermute(send, 'col', [(0, 1), (1, 0)])  1.23 us
    pallas_call x1, Pallas kernels, local(): pl.pallas_call(slice_kernel, out_shape=(edge_shape, edge_shape), in_specs...  1.15 us
    pallas_call x1, Pallas kernels, local(): pl.pallas_call(functools.partial(edge_kernel, order), out_shape=(jax.Shap...  1.05 us
    ppermute x1, starting transfers between devices, local(): far = lax.ppermute(far_send, AXES, swaps + [(j, i) for i, j in swaps])  0.8 us
  transfers between devices with their start and end apart: 3, of which 1 were waited for; matrix products, arithmetic and copies ran while one was open for 0% of the time, Pallas kernels for 13%

profile of v10, /device:TPU:0, one launch (start us, length us, event | category | flops | bytes accessed | tf_op | source)
XLA Modules:
  0.0 32.0 jit_solution(14596511065781126789)
XLA Ops:
  0.6 0.0 copy-start
  0.6 0.0 copy-start.2
  0.7 0.0 copy-start.4
  0.7 0.0 copy-start.3
  0.7 0.0 copy-start.1
  0.7 1.2 %halo_rows.1 = (bf16[128,512]{1,0:T(8,128)(2,1)S(1)}, bf16[128,512]{1,0:T(8,128)(2,1)S(1)}) custom-call(bf16[1536,512]{1,0:T(8,128)(2,1)} %bottom_ref.3), custom_call_target="tpu_custom_call" | custom-call | flops 6442450944 | tf_op jit(solution)/shard_map/halo_rows/pallas_call | solution.py:203
  1.8 0.8 %collective-permute-start = (bf16[128,512]{1,0:T(8,128)(2,1)S(1)}, bf16[128,512]{1,0:T(8,128)(2,1)S(1)}, u32[]{:S(2)}, u32[]{:S(2)}) collective-permute-start(bf16[128,512]{1,0:T(8,128)(2,1)S(1)} %get-tuple-element.11), channel_id=1, source_target_pairs={{1,2},{3,4},{5,6},{7,8},{9,10},{11,12},{13,14},{15,16},{17,18},{19... | collective-permute-start | bytes 393224 | tf_op jit(solution)/shard_map/ppermute | solution.py:216
  2.6 4.4 %collective-permute-start.1 = (bf16[128,512]{1,0:T(8,128)(2,1)S(1)}, bf16[128,512]{1,0:T(8,128)(2,1)S(1)}, u32[]{:S(2)}, u32[]{:S(2)}) collective-permute-start(bf16[128,512]{1,0:T(8,128)(2,1)S(1)} %get-tuple-element.12), channel_id=1, source_target_pairs={{0,1},{2,3},{4,5},{6,7},{8,9},{10,11},{12,13},{14,15},{16,17},{18,... | collective-permute-start | bytes 393224 | tf_op jit(solution)/shard_map/ppermute | solution.py:218
  7.0 0.0 copy-done
  7.0 0.0 copy-done.2
  7.0 0.0 copy-done.4
  7.0 0.0 copy-done.3
  7.0 0.0 copy-done.1
  7.0 3.8 %inner.1 = (bf16[1536,512]{1,0:T(8,128)(2,1)}, f32[2,128,512]{2,1,0:T(8,128)S(1)}, bf16[2,256,128]{2,1,0:T(8,128)(2,1)S(1)}, f32[2,512,256]{2,1,0:T(8,128)S(1)}) custom-call(s32[8,24]{1,0:T(8,128)S(1)} %bitcast.4, s32[24]{0:T(128)S(1)} %copy-done.4, bf16[24,8,64,64]{3,2,1,0:T(8,128)(2,1)S(1)} %copy-done.1, bf16[1536,512]{1,0:T(8,128)(2,1)S(1)} %copy-done, ...), custom_call_target="tpu_custom_call" | custom-call | flops 2013265920 | bytes 8388608 | tf_op jit(solution)/shard_map/inner/pallas_call | solution.py:226
  10.9 0.0 collective-permute-done.far_ref
  10.9 0.0 collective-permute-done.1.near_ref
  10.9 1.0 %edges.1 = (bf16[1536,512]{1,0:T(8,128)(2,1)}, bf16[2,256,256]{2,1,0:T(8,128)(2,1)S(1)}, bf16[512,256]{1,0:T(8,128)(2,1)S(1)}) custom-call(bf16[128,512]{1,0:T(8,128)(2,1)S(1)} %collective-permute-done.far_ref, bf16[128,512]{1,0:T(8,128)(2,1)S(1)} %collective-permute-done.1.near_ref, ...), custom_call_target="tpu_custom_call", output_to_operand_aliasing={{0}: (7, {})} | custom-call | tf_op jit(solution)/shard_map/edges/pallas_call | solution.py:259
  11.9 0.1 collective-permute-start.2
  12.0 0.3 kept_half.1
  12.3 1.2 %collective-permute-done.2 = bf16[512,256]{1,0:T(8,128)(2,1)S(1)} collective-permute-done((bf16[512,256]{1,0:T(8,128)(2,1)S(1)}, bf16[512,256]{1,0:T(8,128)(2,1)S(1)}, u32[]{:S(2)}, u32[]{:S(2)}) %collective-permute-start.2) | collective-permute-done | bytes 262176 | tf_op jit(solution)/shard_map/ppermute | solution.py:278
  13.5 0.1 add_convert_fusion
  13.6 17.7 %all_to_all.5 = bf16[16,32,256]{2,1,0:T(8,128)(2,1)S(1)} all-to-all(bf16[16,32,256]{2,1,0:T(8,128)(2,1)S(1)} %bitcast.5), channel_id=1, replica_groups=mesh['outer'=4,'inner'=4,'col'=2] {'inner','outer'}, dimensions={0} | all-to-all | bytes 524288 | tf_op jit(solution)/shard_map/all_to_all | solution.py:294
  31.4 0.6 %broadcast_multiply_fusion = f32[32,256]{1,0:T(8,128)} fusion(f32[32,256]{1,0:T(8,128)S(1)} %convert_reduce_fusion), kind=kLoop, calls=%fused_computation.2 | loop fusion | flops 8192 | bytes 65536 | tf_op jit(solution)/shard_map/mul | solution.py:300
  (1 shorter events, 0.0 us)
Async XLA Ops:
  0.6 6.4 %copy-start = (bf16[1536,512]{1,0:T(8,128)(2,1)S(1)}, bf16[1536,512]{1,0:T(8,128)(2,1)}, u32[]{:S(2)}) copy-start(bf16[1536,512]{1,0:T(8,128)(2,1)} %bottom_ref.3) | copy-start | bytes 4718596
  0.6 6.4 %copy-start.2 = (f32[1536]{0:T(1024)S(1)}, f32[1536]{0:T(1024)}, u32[]{:S(2)}) copy-start(f32[1536]{0:T(1024)} %param.9) | copy-start | bytes 18436
  0.7 6.4 %copy-start.4 = (s32[24]{0:T(128)S(1)}, s32[24]{0:T(128)}, u32[]{:S(2)}) copy-start(s32[24]{0:T(128)} %live_ref.1) | copy-start | bytes 292
  0.7 6.4 %copy-start.3 = (s32[24,8]{0,1:T(8,128)S(1)}, s32[24,8]{0,1:T(8,128)}, u32[]{:S(2)}) copy-start(s32[24,8]{0,1:T(8,128)} %param.7) | copy-start | bytes 2308
  0.7 6.4 %copy-start.1 = (bf16[24,8,64,64]{3,2,1,0:T(8,128)(2,1)S(1)}, bf16[24,8,64,64]{3,2,1,0:T(8,128)(2,1)}, u32[]{:S(2)}) copy-start(bf16[24,8,64,64]{3,2,1,0:T(8,128)(2,1)} %jac_ref.1) | copy-start | bytes 4718596
  1.8 9.0 %collective-permute-start = (bf16[128,512]{1,0:T(8,128)(2,1)S(1)}, bf16[128,512]{1,0:T(8,128)(2,1)S(1)}, u32[]{:S(2)}, u32[]{:S(2)}) collective-permute-start(bf16[128,512]{1,0:T(8,128)(2,1)S(1)} %get-tuple-element.11), channel_id=1, source_target_pairs={{1,2},{3,4},{5,6},{7,8},{9,10},{11,12},{13,14},{15,16},{17,18},{19... | collective-permute-start | bytes 393224 | tf_op jit(solution)/shard_map/ppermute | solution.py:216
  2.6 8.2 %collective-permute-start.1 = (bf16[128,512]{1,0:T(8,128)(2,1)S(1)}, bf16[128,512]{1,0:T(8,128)(2,1)S(1)}, u32[]{:S(2)}, u32[]{:S(2)}) collective-permute-start(bf16[128,512]{1,0:T(8,128)(2,1)S(1)} %get-tuple-element.12), channel_id=1, source_target_pairs={{0,1},{2,3},{4,5},{6,7},{8,9},{10,11},{12,13},{14,15},{16,17},{18,... | collective-permute-start | bytes 393224 | tf_op jit(solution)/shard_map/ppermute | solution.py:218
  11.9 1.6 %collective-permute-start.2 = (bf16[512,256]{1,0:T(8,128)(2,1)S(1)}, bf16[512,256]{1,0:T(8,128)(2,1)S(1)}, u32[]{:S(2)}, u32[]{:S(2)}) collective-permute-start(bf16[512,256]{1,0:T(8,128)(2,1)S(1)} %get-tuple-element.19), channel_id=1, source_target_pairs={{0,1},{1,0},{2,3},{3,2},{4,5},{5,4},{6,7},{7,6},{8,9},{9,8},{10,11... | collective-permute-start | bytes 786440 | tf_op jit(solution)/shard_map/ppermute | solution.py:278

commit v11 on v10

--- a/solution.py
+++ b/solution.py
@@ -140,7 +140,7 @@
 
 
 def put_blocks(ref, value, order):
-    if order is None:
+    if order == sorted(order):
         ref[...] = value.astype(ref.dtype)
         return
     high = value.shape[0] // len(order)
@@ -220,9 +220,9 @@
     halved = across == 2
     parts = 2 if halved else 1
     wide = width // parts
-    order = None
+    order = list(range(down))
     if halved and (width // down) % 16 == 0:
-        order = [o * inner + i for i in range(inner) for o in range(outer)]
+        order = [o * inner + i for i in range(inner) for o in reversed(range(outer))]
     image, edge, arm, part = pl.pallas_call(
         inner_kernel,
         out_shape=(
@@ -290,8 +290,8 @@
         )(basis, basis, rows, part)
         total = (keep + got.astype(f32)).astype(bf16)
         total = total.reshape(down, width // down, wide)
-        group = AXES[:2] if order is None else (AXES[1], AXES[0])
-        got = lax.all_to_all(total, group, 0, 0, tiled=True)
+        groups = [[m * across + c for m in order] for c in range(across)]
+        got = lax.all_to_all(total, AXES, 0, 0, axis_index_groups=groups, tiled=True)
     else:
         total = send.reshape(down, width // down, across, width // across)
         total = total.transpose(0, 2, 1, 3)

time: 32.2 us -> 28.3 us (0.88)
  blocking collectives: 17.7 us -> 13.9 us
    all_to_all x1, blocking collectives: 17.7 us -> 13.9 us  [local(): lax.all_to_all(total, AXES, 0, 0, axis_index_groups=groups, tiled=True)]
  transfers between devices with their start and end apart: 3 -> 3, of which waited for: 1 -> 1; matrix products, arithmetic and copies ran while one was open for 0% -> 0% of each run, Pallas kernels for 13% -> 15%
where the time goes in v11:
time: 28.3 us; the launch traced here: 28.1 us
  blocking collectives  13.9 us (49%)
  Pallas kernels  6.28 us (22%)
  starting transfers between devices  5.25 us (19%)
  waiting for transfers between devices  1.24 us (4%)
  between operations  0.75 us (3%)
  other arithmetic  0.72 us (3%)
    all_to_all x1, blocking collectives, local(): lax.all_to_all(total, AXES, 0, 0, axis_index_groups=groups, tiled=True)  13.9 us
    ppermute x1, starting transfers between devices, local(): near = lax.ppermute(near_send, AXES, swaps + [(j, i) for i, j in swaps])  4.36 us
    pallas_call x1, Pallas kernels, local(): pl.pallas_call(inner_kernel, out_shape=(jax.ShapeDtypeStruct((nrows, widt...  3.81 us
    ppermute x1, waiting for transfers between devices, local(): got = lax.ppermute(send, 'col', [(0, 1), (1, 0)])  1.23 us
    pallas_call x1, Pallas kernels, local(): pl.pallas_call(slice_kernel, out_shape=(edge_shape, edge_shape), in_specs...  1.15 us
    pallas_call x1, Pallas kernels, local(): pl.pallas_call(functools.partial(edge_kernel, order), out_shape=(jax.Shap...  1.05 us
    ppermute x1, starting transfers between devices, local(): far = lax.ppermute(far_send, AXES, swaps + [(j, i) for i, j in swaps])  0.8 us
    mul x1, other arithmetic, local(): projected = jnp.sum(got.astype(f32), axis=0) * (1.0 / (nrows * count))  0.62 us
  transfers between devices with their start and end apart: 3, of which 1 were waited for; matrix products, arithmetic and copies ran while one was open for 0% of the time, Pallas kernels for 15%

profile of v11, /device:TPU:0, one launch (start us, length us, event | category | flops | bytes accessed | tf_op | source)
XLA Modules:
  0.0 28.1 jit_solution(6422862881948402110)
XLA Ops:
  0.6 0.0 copy-start
  0.6 0.0 copy-start.2
  0.7 0.0 copy-start.4
  0.7 0.0 copy-start.3
  0.7 0.0 copy-start.1
  0.7 1.2 %halo_rows.1 = (bf16[128,512]{1,0:T(8,128)(2,1)S(1)}, bf16[128,512]{1,0:T(8,128)(2,1)S(1)}) custom-call(bf16[1536,512]{1,0:T(8,128)(2,1)} %bottom_ref.3), custom_call_target="tpu_custom_call" | custom-call | flops 6442450944 | tf_op jit(solution)/shard_map/halo_rows/pallas_call | solution.py:203
  1.8 0.8 %collective-permute-start = (bf16[128,512]{1,0:T(8,128)(2,1)S(1)}, bf16[128,512]{1,0:T(8,128)(2,1)S(1)}, u32[]{:S(2)}, u32[]{:S(2)}) collective-permute-start(bf16[128,512]{1,0:T(8,128)(2,1)S(1)} %get-tuple-element.11), channel_id=1, source_target_pairs={{1,2},{3,4},{5,6},{7,8},{9,10},{11,12},{13,14},{15,16},{17,18},{19... | collective-permute-start | bytes 393224 | tf_op jit(solution)/shard_map/ppermute | solution.py:216
  2.6 4.4 %collective-permute-start.1 = (bf16[128,512]{1,0:T(8,128)(2,1)S(1)}, bf16[128,512]{1,0:T(8,128)(2,1)S(1)}, u32[]{:S(2)}, u32[]{:S(2)}) collective-permute-start(bf16[128,512]{1,0:T(8,128)(2,1)S(1)} %get-tuple-element.12), channel_id=1, source_target_pairs={{0,1},{2,3},{4,5},{6,7},{8,9},{10,11},{12,13},{14,15},{16,17},{18,... | collective-permute-start | bytes 393224 | tf_op jit(solution)/shard_map/ppermute | solution.py:218
  7.0 0.0 copy-done
  7.0 0.0 copy-done.2
  7.0 0.0 copy-done.4
  7.0 0.0 copy-done.3
  7.0 0.0 copy-done.1
  7.0 3.8 %inner.1 = (bf16[1536,512]{1,0:T(8,128)(2,1)}, f32[2,128,512]{2,1,0:T(8,128)S(1)}, bf16[2,256,128]{2,1,0:T(8,128)(2,1)S(1)}, f32[2,512,256]{2,1,0:T(8,128)S(1)}) custom-call(s32[8,24]{1,0:T(8,128)S(1)} %bitcast.4, s32[24]{0:T(128)S(1)} %copy-done.4, bf16[24,8,64,64]{3,2,1,0:T(8,128)(2,1)S(1)} %copy-done.1, bf16[1536,512]{1,0:T(8,128)(2,1)S(1)} %copy-done, ...), custom_call_target="tpu_custom_call" | custom-call | flops 2013265920 | bytes 8388608 | tf_op jit(solution)/shard_map/inner/pallas_call | solution.py:226
  10.9 0.0 collective-permute-done.far_ref
  10.9 0.0 collective-permute-done.1.near_ref
  10.9 1.0 %edges.1 = (bf16[1536,512]{1,0:T(8,128)(2,1)}, bf16[2,256,256]{2,1,0:T(8,128)(2,1)S(1)}, bf16[512,256]{1,0:T(8,128)(2,1)S(1)}) custom-call(bf16[128,512]{1,0:T(8,128)(2,1)S(1)} %collective-permute-done.far_ref, bf16[128,512]{1,0:T(8,128)(2,1)S(1)} %collective-permute-done.1.near_ref, ...), custom_call_target="tpu_custom_call", output_to_operand_aliasing={{0}: (7, {})} | custom-call | tf_op jit(solution)/shard_map/edges/pallas_call | solution.py:259
  11.9 0.1 collective-permute-start.2
  12.0 0.3 kept_half.1
  12.3 1.2 %collective-permute-done.2 = bf16[512,256]{1,0:T(8,128)(2,1)S(1)} collective-permute-done((bf16[512,256]{1,0:T(8,128)(2,1)S(1)}, bf16[512,256]{1,0:T(8,128)(2,1)S(1)}, u32[]{:S(2)}, u32[]{:S(2)}) %collective-permute-start.2) | collective-permute-done | bytes 262176 | tf_op jit(solution)/shard_map/ppermute | solution.py:278
  13.5 0.1 add_convert_fusion
  13.6 13.9 %all_to_all.5 = bf16[16,32,256]{2,1,0:T(8,128)(2,1)S(1)} all-to-all(bf16[16,32,256]{2,1,0:T(8,128)(2,1)S(1)} %bitcast.5), channel_id=1, replica_groups={{24,16,8,0,26,18,10,2,28,20,12,4,30,22,14,6},{25,17,9,1,27,19,11,3,29,2..., dimensions={0} | all-to-all | bytes 524288 | tf_op jit(solution)/shard_map/all_to_all | solution.py:294
  27.5 0.6 %broadcast_multiply_fusion = f32[32,256]{1,0:T(8,128)} fusion(f32[32,256]{1,0:T(8,128)S(1)} %convert_reduce_fusion), kind=kLoop, calls=%fused_computation.2 | loop fusion | flops 8192 | bytes 65536 | tf_op jit(solution)/shard_map/mul | solution.py:300
  (1 shorter events, 0.0 us)
Async XLA Ops:
  0.6 6.4 %copy-start = (bf16[1536,512]{1,0:T(8,128)(2,1)S(1)}, bf16[1536,512]{1,0:T(8,128)(2,1)}, u32[]{:S(2)}) copy-start(bf16[1536,512]{1,0:T(8,128)(2,1)} %bottom_ref.3) | copy-start | bytes 4718596
  0.6 6.4 %copy-start.2 = (f32[1536]{0:T(1024)S(1)}, f32[1536]{0:T(1024)}, u32[]{:S(2)}) copy-start(f32[1536]{0:T(1024)} %param.9) | copy-start | bytes 18436
  0.7 6.4 %copy-start.4 = (s32[24]{0:T(128)S(1)}, s32[24]{0:T(128)}, u32[]{:S(2)}) copy-start(s32[24]{0:T(128)} %live_ref.1) | copy-start | bytes 292
  0.7 6.4 %copy-start.3 = (s32[24,8]{0,1:T(8,128)S(1)}, s32[24,8]{0,1:T(8,128)}, u32[]{:S(2)}) copy-start(s32[24,8]{0,1:T(8,128)} %param.7) | copy-start | bytes 2308
  0.7 6.4 %copy-start.1 = (bf16[24,8,64,64]{3,2,1,0:T(8,128)(2,1)S(1)}, bf16[24,8,64,64]{3,2,1,0:T(8,128)(2,1)}, u32[]{:S(2)}) copy-start(bf16[24,8,64,64]{3,2,1,0:T(8,128)(2,1)} %jac_ref.1) | copy-start | bytes 4718596
  1.8 9.0 %collective-permute-start = (bf16[128,512]{1,0:T(8,128)(2,1)S(1)}, bf16[128,512]{1,0:T(8,128)(2,1)S(1)}, u32[]{:S(2)}, u32[]{:S(2)}) collective-permute-start(bf16[128,512]{1,0:T(8,128)(2,1)S(1)} %get-tuple-element.11), channel_id=1, source_target_pairs={{1,2},{3,4},{5,6},{7,8},{9,10},{11,12},{13,14},{15,16},{17,18},{19... | collective-permute-start | bytes 393224 | tf_op jit(solution)/shard_map/ppermute | solution.py:216
  2.6 8.2 %collective-permute-start.1 = (bf16[128,512]{1,0:T(8,128)(2,1)S(1)}, bf16[128,512]{1,0:T(8,128)(2,1)S(1)}, u32[]{:S(2)}, u32[]{:S(2)}) collective-permute-start(bf16[128,512]{1,0:T(8,128)(2,1)S(1)} %get-tuple-element.12), channel_id=1, source_target_pairs={{0,1},{2,3},{4,5},{6,7},{8,9},{10,11},{12,13},{14,15},{16,17},{18,... | collective-permute-start | bytes 393224 | tf_op jit(solution)/shard_map/ppermute | solution.py:218
  11.9 1.6 %collective-permute-start.2 = (bf16[512,256]{1,0:T(8,128)(2,1)S(1)}, bf16[512,256]{1,0:T(8,128)(2,1)S(1)}, u32[]{:S(2)}, u32[]{:S(2)}) collective-permute-start(bf16[512,256]{1,0:T(8,128)(2,1)S(1)} %get-tuple-element.19), channel_id=1, source_target_pairs={{0,1},{1,0},{2,3},{3,2},{4,5},{5,4},{6,7},{7,6},{8,9},{9,8},{10,11... | collective-permute-start | bytes 786440 | tf_op jit(solution)/shard_map/ppermute | solution.py:278

commit v12 on v11

--- a/solution.py
+++ b/solution.py
@@ -222,7 +222,7 @@
     wide = width // parts
     order = list(range(down))
     if halved and (width // down) % 16 == 0:
-        order = [o * inner + i for i in range(inner) for o in reversed(range(outer))]
+        order = [o * inner + i for i in reversed(range(inner)) for o in reversed(range(outer))]
     image, edge, arm, part = pl.pallas_call(
         inner_kernel,
         out_shape=(

time: 28.3 us -> 29.7 us (1.049)
  blocking collectives: 13.9 us -> 15.3 us
    all_to_all x1, blocking collectives: 13.9 us -> 15.3 us  [local(): lax.all_to_all(total, AXES, 0, 0, axis_index_groups=groups, tiled=True)]
  transfers between devices with their start and end apart: 3 -> 3, of which waited for: 1 -> 1; matrix products, arithmetic and copies ran while one was open for 0% -> 0% of each run, Pallas kernels for 15% -> 14%
where the time goes in v12:
time: 29.7 us; the launch traced here: 29.5 us
  blocking collectives  15.3 us (52%)
  Pallas kernels  6.28 us (21%)
  starting transfers between devices  5.25 us (18%)
  waiting for transfers between devices  1.24 us (4%)
  between operations  0.75 us (3%)
  other arithmetic  0.72 us (2%)
    all_to_all x1, blocking collectives, local(): lax.all_to_all(total, AXES, 0, 0, axis_index_groups=groups, tiled=True)  15.3 us
    ppermute x1, starting transfers between devices, local(): near = lax.ppermute(near_send, AXES, swaps + [(j, i) for i, j in swaps])  4.36 us
    pallas_call x1, Pallas kernels, local(): pl.pallas_call(inner_kernel, out_shape=(jax.ShapeDtypeStruct((nrows, widt...  3.81 us
    ppermute x1, waiting for transfers between devices, local(): got = lax.ppermute(send, 'col', [(0, 1), (1, 0)])  1.23 us
    pallas_call x1, Pallas kernels, local(): pl.pallas_call(slice_kernel, out_shape=(edge_shape, edge_shape), in_specs...  1.15 us
    pallas_call x1, Pallas kernels, local(): pl.pallas_call(functools.partial(edge_kernel, order), out_shape=(jax.Shap...  1.05 us
    ppermute x1, starting transfers between devices, local(): far = lax.ppermute(far_send, AXES, swaps + [(j, i) for i, j in swaps])  0.8 us
    mul x1, other arithmetic, local(): projected = jnp.sum(got.astype(f32), axis=0) * (1.0 / (nrows * count))  0.62 us
  transfers between devices with their start and end apart: 3, of which 1 were waited for; matrix products, arithmetic and copies ran while one was open for 0% of the time, Pallas kernels for 14%

profile of v12, /device:TPU:0, one launch (start us, length us, event | category | flops | bytes accessed | tf_op | source)
XLA Modules:
  0.0 29.5 jit_solution(13746637969934923069)
XLA Ops:
  0.6 0.0 copy-start
  0.6 0.0 copy-start.2
  0.7 0.0 copy-start.4
  0.7 0.0 copy-start.3
  0.7 0.0 copy-start.1
  0.7 1.2 %halo_rows.1 = (bf16[128,512]{1,0:T(8,128)(2,1)S(1)}, bf16[128,512]{1,0:T(8,128)(2,1)S(1)}) custom-call(bf16[1536,512]{1,0:T(8,128)(2,1)} %bottom_ref.3), custom_call_target="tpu_custom_call" | custom-call | flops 6442450944 | tf_op jit(solution)/shard_map/halo_rows/pallas_call | solution.py:203
  1.8 0.8 %collective-permute-start = (bf16[128,512]{1,0:T(8,128)(2,1)S(1)}, bf16[128,512]{1,0:T(8,128)(2,1)S(1)}, u32[]{:S(2)}, u32[]{:S(2)}) collective-permute-start(bf16[128,512]{1,0:T(8,128)(2,1)S(1)} %get-tuple-element.11), channel_id=1, source_target_pairs={{1,2},{3,4},{5,6},{7,8},{9,10},{11,12},{13,14},{15,16},{17,18},{19... | collective-permute-start | bytes 393224 | tf_op jit(solution)/shard_map/ppermute | solution.py:216
  2.6 4.4 %collective-permute-start.1 = (bf16[128,512]{1,0:T(8,128)(2,1)S(1)}, bf16[128,512]{1,0:T(8,128)(2,1)S(1)}, u32[]{:S(2)}, u32[]{:S(2)}) collective-permute-start(bf16[128,512]{1,0:T(8,128)(2,1)S(1)} %get-tuple-element.12), channel_id=1, source_target_pairs={{0,1},{2,3},{4,5},{6,7},{8,9},{10,11},{12,13},{14,15},{16,17},{18,... | collective-permute-start | bytes 393224 | tf_op jit(solution)/shard_map/ppermute | solution.py:218
  7.0 0.0 copy-done
  7.0 0.0 copy-done.2
  7.0 0.0 copy-done.4
  7.0 0.0 copy-done.3
  7.0 0.0 copy-done.1
  7.0 3.8 %inner.1 = (bf16[1536,512]{1,0:T(8,128)(2,1)}, f32[2,128,512]{2,1,0:T(8,128)S(1)}, bf16[2,256,128]{2,1,0:T(8,128)(2,1)S(1)}, f32[2,512,256]{2,1,0:T(8,128)S(1)}) custom-call(s32[8,24]{1,0:T(8,128)S(1)} %bitcast.4, s32[24]{0:T(128)S(1)} %copy-done.4, bf16[24,8,64,64]{3,2,1,0:T(8,128)(2,1)S(1)} %copy-done.1, bf16[1536,512]{1,0:T(8,128)(2,1)S(1)} %copy-done, ...), custom_call_target="tpu_custom_call" | custom-call | flops 2013265920 | bytes 8388608 | tf_op jit(solution)/shard_map/inner/pallas_call | solution.py:226
  10.9 0.0 collective-permute-done.far_ref
  10.9 0.0 collective-permute-done.1.near_ref
  10.9 1.0 %edges.1 = (bf16[1536,512]{1,0:T(8,128)(2,1)}, bf16[2,256,256]{2,1,0:T(8,128)(2,1)S(1)}, bf16[512,256]{1,0:T(8,128)(2,1)S(1)}) custom-call(bf16[128,512]{1,0:T(8,128)(2,1)S(1)} %collective-permute-done.far_ref, bf16[128,512]{1,0:T(8,128)(2,1)S(1)} %collective-permute-done.1.near_ref, ...), custom_call_target="tpu_custom_call", output_to_operand_aliasing={{0}: (7, {})} | custom-call | tf_op jit(solution)/shard_map/edges/pallas_call | solution.py:259
  11.9 0.1 collective-permute-start.2
  12.0 0.3 kept_half.1
  12.3 1.2 %collective-permute-done.2 = bf16[512,256]{1,0:T(8,128)(2,1)S(1)} collective-permute-done((bf16[512,256]{1,0:T(8,128)(2,1)S(1)}, bf16[512,256]{1,0:T(8,128)(2,1)S(1)}, u32[]{:S(2)}, u32[]{:S(2)}) %collective-permute-start.2) | collective-permute-done | bytes 262176 | tf_op jit(solution)/shard_map/ppermute | solution.py:278
  13.5 0.1 add_convert_fusion
  13.6 15.3 %all_to_all.5 = bf16[16,32,256]{2,1,0:T(8,128)(2,1)S(1)} all-to-all(bf16[16,32,256]{2,1,0:T(8,128)(2,1)S(1)} %bitcast.5), channel_id=1, replica_groups={{30,22,14,6,28,20,12,4,26,18,10,2,24,16,8,0},{31,23,15,7,29,21,13,5,27,..., dimensions={0} | all-to-all | bytes 524288 | tf_op jit(solution)/shard_map/all_to_all | solution.py:294
  28.9 0.6 %broadcast_multiply_fusion = f32[32,256]{1,0:T(8,128)} fusion(f32[32,256]{1,0:T(8,128)S(1)} %convert_reduce_fusion), kind=kLoop, calls=%fused_computation.2 | loop fusion | flops 8192 | bytes 65536 | tf_op jit(solution)/shard_map/mul | solution.py:300
  (1 shorter events, 0.0 us)
Async XLA Ops:
  0.6 6.4 %copy-start = (bf16[1536,512]{1,0:T(8,128)(2,1)S(1)}, bf16[1536,512]{1,0:T(8,128)(2,1)}, u32[]{:S(2)}) copy-start(bf16[1536,512]{1,0:T(8,128)(2,1)} %bottom_ref.3) | copy-start | bytes 4718596
  0.6 6.4 %copy-start.2 = (f32[1536]{0:T(1024)S(1)}, f32[1536]{0:T(1024)}, u32[]{:S(2)}) copy-start(f32[1536]{0:T(1024)} %param.9) | copy-start | bytes 18436
  0.7 6.4 %copy-start.4 = (s32[24]{0:T(128)S(1)}, s32[24]{0:T(128)}, u32[]{:S(2)}) copy-start(s32[24]{0:T(128)} %live_ref.1) | copy-start | bytes 292
  0.7 6.4 %copy-start.3 = (s32[24,8]{0,1:T(8,128)S(1)}, s32[24,8]{0,1:T(8,128)}, u32[]{:S(2)}) copy-start(s32[24,8]{0,1:T(8,128)} %param.7) | copy-start | bytes 2308
  0.7 6.4 %copy-start.1 = (bf16[24,8,64,64]{3,2,1,0:T(8,128)(2,1)S(1)}, bf16[24,8,64,64]{3,2,1,0:T(8,128)(2,1)}, u32[]{:S(2)}) copy-start(bf16[24,8,64,64]{3,2,1,0:T(8,128)(2,1)} %jac_ref.1) | copy-start | bytes 4718596
  1.8 9.0 %collective-permute-start = (bf16[128,512]{1,0:T(8,128)(2,1)S(1)}, bf16[128,512]{1,0:T(8,128)(2,1)S(1)}, u32[]{:S(2)}, u32[]{:S(2)}) collective-permute-start(bf16[128,512]{1,0:T(8,128)(2,1)S(1)} %get-tuple-element.11), channel_id=1, source_target_pairs={{1,2},{3,4},{5,6},{7,8},{9,10},{11,12},{13,14},{15,16},{17,18},{19... | collective-permute-start | bytes 393224 | tf_op jit(solution)/shard_map/ppermute | solution.py:216
  2.6 8.2 %collective-permute-start.1 = (bf16[128,512]{1,0:T(8,128)(2,1)S(1)}, bf16[128,512]{1,0:T(8,128)(2,1)S(1)}, u32[]{:S(2)}, u32[]{:S(2)}) collective-permute-start(bf16[128,512]{1,0:T(8,128)(2,1)S(1)} %get-tuple-element.12), channel_id=1, source_target_pairs={{0,1},{2,3},{4,5},{6,7},{8,9},{10,11},{12,13},{14,15},{16,17},{18,... | collective-permute-start | bytes 393224 | tf_op jit(solution)/shard_map/ppermute | solution.py:218
  11.9 1.6 %collective-permute-start.2 = (bf16[512,256]{1,0:T(8,128)(2,1)S(1)}, bf16[512,256]{1,0:T(8,128)(2,1)S(1)}, u32[]{:S(2)}, u32[]{:S(2)}) collective-permute-start(bf16[512,256]{1,0:T(8,128)(2,1)S(1)} %get-tuple-element.19), channel_id=1, source_target_pairs={{0,1},{1,0},{2,3},{3,2},{4,5},{5,4},{6,7},{7,6},{8,9},{9,8},{10,11... | collective-permute-start | bytes 786440 | tf_op jit(solution)/shard_map/ppermute | solution.py:278

commit v13 on v12

--- a/solution.py
+++ b/solution.py
@@ -222,7 +222,7 @@
     wide = width // parts
     order = list(range(down))
     if halved and (width // down) % 16 == 0:
-        order = [o * inner + i for i in reversed(range(inner)) for o in reversed(range(outer))]
+        order = [o * inner + i for o in reversed(range(outer)) for i in range(inner)]
     image, edge, arm, part = pl.pallas_call(
         inner_kernel,
         out_shape=(

time: 29.7 us -> 30 us (1.010)
    all_to_all x1, blocking collectives: 15.3 us -> 15.6 us  [local(): lax.all_to_all(total, AXES, 0, 0, axis_index_groups=groups, tiled=True)]
where the time goes in v13:
time: 30 us; the launch traced here: 29.8 us
  blocking collectives  15.6 us (52%)
  Pallas kernels  6.28 us (21%)
  starting transfers between devices  5.25 us (18%)
  waiting for transfers between devices  1.24 us (4%)
  between operations  0.75 us (2%)
  other arithmetic  0.72 us (2%)
    all_to_all x1, blocking collectives, local(): lax.all_to_all(total, AXES, 0, 0, axis_index_groups=groups, tiled=True)  15.6 us
    ppermute x1, starting transfers between devices, local(): near = lax.ppermute(near_send, AXES, swaps + [(j, i) for i, j in swaps])  4.36 us
    pallas_call x1, Pallas kernels, local(): pl.pallas_call(inner_kernel, out_shape=(jax.ShapeDtypeStruct((nrows, widt...  3.81 us
    ppermute x1, waiting for transfers between devices, local(): got = lax.ppermute(send, 'col', [(0, 1), (1, 0)])  1.23 us
    pallas_call x1, Pallas kernels, local(): pl.pallas_call(slice_kernel, out_shape=(edge_shape, edge_shape), in_specs...  1.15 us
    pallas_call x1, Pallas kernels, local(): pl.pallas_call(functools.partial(edge_kernel, order), out_shape=(jax.Shap...  1.05 us
    ppermute x1, starting transfers between devices, local(): far = lax.ppermute(far_send, AXES, swaps + [(j, i) for i, j in swaps])  0.8 us
    mul x1, other arithmetic, local(): projected = jnp.sum(got.astype(f32), axis=0) * (1.0 / (nrows * count))  0.62 us
  transfers between devices with their start and end apart: 3, of which 1 were waited for; matrix products, arithmetic and copies ran while one was open for 0% of the time, Pallas kernels for 14%

profile of v13, /device:TPU:0, one launch (start us, length us, event | category | flops | bytes accessed | tf_op | source)
XLA Modules:
  0.0 29.8 jit_solution(14849840699166328921)
XLA Ops:
  0.6 0.0 copy-start
  0.6 0.0 copy-start.2
  0.7 0.0 copy-start.4
  0.7 0.0 copy-start.3
  0.7 0.0 copy-start.1
  0.7 1.2 %halo_rows.1 = (bf16[128,512]{1,0:T(8,128)(2,1)S(1)}, bf16[128,512]{1,0:T(8,128)(2,1)S(1)}) custom-call(bf16[1536,512]{1,0:T(8,128)(2,1)} %bottom_ref.3), custom_call_target="tpu_custom_call" | custom-call | flops 6442450944 | tf_op jit(solution)/shard_map/halo_rows/pallas_call | solution.py:203
  1.8 0.8 %collective-permute-start = (bf16[128,512]{1,0:T(8,128)(2,1)S(1)}, bf16[128,512]{1,0:T(8,128)(2,1)S(1)}, u32[]{:S(2)}, u32[]{:S(2)}) collective-permute-start(bf16[128,512]{1,0:T(8,128)(2,1)S(1)} %get-tuple-element.11), channel_id=1, source_target_pairs={{1,2},{3,4},{5,6},{7,8},{9,10},{11,12},{13,14},{15,16},{17,18},{19... | collective-permute-start | bytes 393224 | tf_op jit(solution)/shard_map/ppermute | solution.py:216
  2.6 4.4 %collective-permute-start.1 = (bf16[128,512]{1,0:T(8,128)(2,1)S(1)}, bf16[128,512]{1,0:T(8,128)(2,1)S(1)}, u32[]{:S(2)}, u32[]{:S(2)}) collective-permute-start(bf16[128,512]{1,0:T(8,128)(2,1)S(1)} %get-tuple-element.12), channel_id=1, source_target_pairs={{0,1},{2,3},{4,5},{6,7},{8,9},{10,11},{12,13},{14,15},{16,17},{18,... | collective-permute-start | bytes 393224 | tf_op jit(solution)/shard_map/ppermute | solution.py:218
  7.0 0.0 copy-done
  7.0 0.0 copy-done.2
  7.0 0.0 copy-done.4
  7.0 0.0 copy-done.3
  7.0 0.0 copy-done.1
  7.0 3.8 %inner.1 = (bf16[1536,512]{1,0:T(8,128)(2,1)}, f32[2,128,512]{2,1,0:T(8,128)S(1)}, bf16[2,256,128]{2,1,0:T(8,128)(2,1)S(1)}, f32[2,512,256]{2,1,0:T(8,128)S(1)}) custom-call(s32[8,24]{1,0:T(8,128)S(1)} %bitcast.4, s32[24]{0:T(128)S(1)} %copy-done.4, bf16[24,8,64,64]{3,2,1,0:T(8,128)(2,1)S(1)} %copy-done.1, bf16[1536,512]{1,0:T(8,128)(2,1)S(1)} %copy-done, ...), custom_call_target="tpu_custom_call" | custom-call | flops 2013265920 | bytes 8388608 | tf_op jit(solution)/shard_map/inner/pallas_call | solution.py:226
  10.9 0.0 collective-permute-done.far_ref
  10.9 0.0 collective-permute-done.1.near_ref
  10.9 1.0 %edges.1 = (bf16[1536,512]{1,0:T(8,128)(2,1)}, bf16[2,256,256]{2,1,0:T(8,128)(2,1)S(1)}, bf16[512,256]{1,0:T(8,128)(2,1)S(1)}) custom-call(bf16[128,512]{1,0:T(8,128)(2,1)S(1)} %collective-permute-done.far_ref, bf16[128,512]{1,0:T(8,128)(2,1)S(1)} %collective-permute-done.1.near_ref, ...), custom_call_target="tpu_custom_call", output_to_operand_aliasing={{0}: (7, {})} | custom-call | tf_op jit(solution)/shard_map/edges/pallas_call | solution.py:259
  11.9 0.1 collective-permute-start.2
  12.0 0.3 kept_half.1
  12.3 1.2 %collective-permute-done.2 = bf16[512,256]{1,0:T(8,128)(2,1)S(1)} collective-permute-done((bf16[512,256]{1,0:T(8,128)(2,1)S(1)}, bf16[512,256]{1,0:T(8,128)(2,1)S(1)}, u32[]{:S(2)}, u32[]{:S(2)}) %collective-permute-start.2) | collective-permute-done | bytes 262176 | tf_op jit(solution)/shard_map/ppermute | solution.py:278
  13.5 0.1 add_convert_fusion
  13.6 15.6 %all_to_all.5 = bf16[16,32,256]{2,1,0:T(8,128)(2,1)S(1)} all-to-all(bf16[16,32,256]{2,1,0:T(8,128)(2,1)S(1)} %bitcast.5), channel_id=1, replica_groups={{24,26,28,30,16,18,20,22,8,10,12,14,0,2,4,6},{25,27,29,31,17,19,21,23,9..., dimensions={0} | all-to-all | bytes 524288 | tf_op jit(solution)/shard_map/all_to_all | solution.py:294
  29.2 0.6 %broadcast_multiply_fusion = f32[32,256]{1,0:T(8,128)} fusion(f32[32,256]{1,0:T(8,128)S(1)} %convert_reduce_fusion), kind=kLoop, calls=%fused_computation.2 | loop fusion | flops 8192 | bytes 65536 | tf_op jit(solution)/shard_map/mul | solution.py:300
  (1 shorter events, 0.0 us)
Async XLA Ops:
  0.6 6.4 %copy-start = (bf16[1536,512]{1,0:T(8,128)(2,1)S(1)}, bf16[1536,512]{1,0:T(8,128)(2,1)}, u32[]{:S(2)}) copy-start(bf16[1536,512]{1,0:T(8,128)(2,1)} %bottom_ref.3) | copy-start | bytes 4718596
  0.6 6.4 %copy-start.2 = (f32[1536]{0:T(1024)S(1)}, f32[1536]{0:T(1024)}, u32[]{:S(2)}) copy-start(f32[1536]{0:T(1024)} %param.9) | copy-start | bytes 18436
  0.7 6.4 %copy-start.4 = (s32[24]{0:T(128)S(1)}, s32[24]{0:T(128)}, u32[]{:S(2)}) copy-start(s32[24]{0:T(128)} %live_ref.1) | copy-start | bytes 292
  0.7 6.4 %copy-start.3 = (s32[24,8]{0,1:T(8,128)S(1)}, s32[24,8]{0,1:T(8,128)}, u32[]{:S(2)}) copy-start(s32[24,8]{0,1:T(8,128)} %param.7) | copy-start | bytes 2308
  0.7 6.4 %copy-start.1 = (bf16[24,8,64,64]{3,2,1,0:T(8,128)(2,1)S(1)}, bf16[24,8,64,64]{3,2,1,0:T(8,128)(2,1)}, u32[]{:S(2)}) copy-start(bf16[24,8,64,64]{3,2,1,0:T(8,128)(2,1)} %jac_ref.1) | copy-start | bytes 4718596
  1.8 9.0 %collective-permute-start = (bf16[128,512]{1,0:T(8,128)(2,1)S(1)}, bf16[128,512]{1,0:T(8,128)(2,1)S(1)}, u32[]{:S(2)}, u32[]{:S(2)}) collective-permute-start(bf16[128,512]{1,0:T(8,128)(2,1)S(1)} %get-tuple-element.11), channel_id=1, source_target_pairs={{1,2},{3,4},{5,6},{7,8},{9,10},{11,12},{13,14},{15,16},{17,18},{19... | collective-permute-start | bytes 393224 | tf_op jit(solution)/shard_map/ppermute | solution.py:216
  2.6 8.2 %collective-permute-start.1 = (bf16[128,512]{1,0:T(8,128)(2,1)S(1)}, bf16[128,512]{1,0:T(8,128)(2,1)S(1)}, u32[]{:S(2)}, u32[]{:S(2)}) collective-permute-start(bf16[128,512]{1,0:T(8,128)(2,1)S(1)} %get-tuple-element.12), channel_id=1, source_target_pairs={{0,1},{2,3},{4,5},{6,7},{8,9},{10,11},{12,13},{14,15},{16,17},{18,... | collective-permute-start | bytes 393224 | tf_op jit(solution)/shard_map/ppermute | solution.py:218
  11.9 1.6 %collective-permute-start.2 = (bf16[512,256]{1,0:T(8,128)(2,1)S(1)}, bf16[512,256]{1,0:T(8,128)(2,1)S(1)}, u32[]{:S(2)}, u32[]{:S(2)}) collective-permute-start(bf16[512,256]{1,0:T(8,128)(2,1)S(1)} %get-tuple-element.19), channel_id=1, source_target_pairs={{0,1},{1,0},{2,3},{3,2},{4,5},{5,4},{6,7},{7,6},{8,9},{9,8},{10,11... | collective-permute-start | bytes 786440 | tf_op jit(solution)/shard_map/ppermute | solution.py:278

commit v14 on v13

--- a/solution.py
+++ b/solution.py
@@ -222,7 +222,7 @@
     wide = width // parts
     order = list(range(down))
     if halved and (width // down) % 16 == 0:
-        order = [o * inner + i for o in reversed(range(outer)) for i in range(inner)]
+        order = [down - 1, 0, *range(down - 2, 0, -1)]
     image, edge, arm, part = pl.pallas_call(
         inner_kernel,
         out_shape=(

time: 30 us -> 29.6 us (0.987)
  blocking collectives: 15.6 us -> 15.2 us
    all_to_all x1, blocking collectives: 15.6 us -> 15.2 us  [local(): lax.all_to_all(total, AXES, 0, 0, axis_index_groups=groups, tiled=True)]
where the time goes in v14:
time: 29.6 us; the launch traced here: 29.5 us
  blocking collectives  15.2 us (51%)
  Pallas kernels  6.28 us (21%)
  starting transfers between devices  5.25 us (18%)
  waiting for transfers between devices  1.24 us (4%)
  between operations  0.75 us (3%)
  other arithmetic  0.72 us (2%)
    all_to_all x1, blocking collectives, local(): lax.all_to_all(total, AXES, 0, 0, axis_index_groups=groups, tiled=True)  15.2 us
    ppermute x1, starting transfers between devices, local(): near = lax.ppermute(near_send, AXES, swaps + [(j, i) for i, j in swaps])  4.36 us
    pallas_call x1, Pallas kernels, local(): pl.pallas_call(inner_kernel, out_shape=(jax.ShapeDtypeStruct((nrows, widt...  3.81 us
    ppermute x1, waiting for transfers between devices, local(): got = lax.ppermute(send, 'col', [(0, 1), (1, 0)])  1.23 us
    pallas_call x1, Pallas kernels, local(): pl.pallas_call(slice_kernel, out_shape=(edge_shape, edge_shape), in_specs...  1.15 us
    pallas_call x1, Pallas kernels, local(): pl.pallas_call(functools.partial(edge_kernel, order), out_shape=(jax.Shap...  1.05 us
    ppermute x1, starting transfers between devices, local(): far = lax.ppermute(far_send, AXES, swaps + [(j, i) for i, j in swaps])  0.8 us
    mul x1, other arithmetic, local(): projected = jnp.sum(got.astype(f32), axis=0) * (1.0 / (nrows * count))  0.62 us
  transfers between devices with their start and end apart: 3, of which 1 were waited for; matrix products, arithmetic and copies ran while one was open for 0% of the time, Pallas kernels for 14%

profile of v14, /device:TPU:0, one launch (start us, length us, event | category | flops | bytes accessed | tf_op | source)
XLA Modules:
  0.0 29.5 jit_solution(1720773784097418422)
XLA Ops:
  0.6 0.0 copy-start
  0.6 0.0 copy-start.2
  0.7 0.0 copy-start.4
  0.7 0.0 copy-start.3
  0.7 0.0 copy-start.1
  0.7 1.2 %halo_rows.1 = (bf16[128,512]{1,0:T(8,128)(2,1)S(1)}, bf16[128,512]{1,0:T(8,128)(2,1)S(1)}) custom-call(bf16[1536,512]{1,0:T(8,128)(2,1)} %bottom_ref.3), custom_call_target="tpu_custom_call" | custom-call | flops 6442450944 | tf_op jit(solution)/shard_map/halo_rows/pallas_call | solution.py:203
  1.8 0.8 %collective-permute-start = (bf16[128,512]{1,0:T(8,128)(2,1)S(1)}, bf16[128,512]{1,0:T(8,128)(2,1)S(1)}, u32[]{:S(2)}, u32[]{:S(2)}) collective-permute-start(bf16[128,512]{1,0:T(8,128)(2,1)S(1)} %get-tuple-element.11), channel_id=1, source_target_pairs={{1,2},{3,4},{5,6},{7,8},{9,10},{11,12},{13,14},{15,16},{17,18},{19... | collective-permute-start | bytes 393224 | tf_op jit(solution)/shard_map/ppermute | solution.py:216
  2.6 4.4 %collective-permute-start.1 = (bf16[128,512]{1,0:T(8,128)(2,1)S(1)}, bf16[128,512]{1,0:T(8,128)(2,1)S(1)}, u32[]{:S(2)}, u32[]{:S(2)}) collective-permute-start(bf16[128,512]{1,0:T(8,128)(2,1)S(1)} %get-tuple-element.12), channel_id=1, source_target_pairs={{0,1},{2,3},{4,5},{6,7},{8,9},{10,11},{12,13},{14,15},{16,17},{18,... | collective-permute-start | bytes 393224 | tf_op jit(solution)/shard_map/ppermute | solution.py:218
  7.0 0.0 copy-done
  7.0 0.0 copy-done.2
  7.0 0.0 copy-done.4
  7.0 0.0 copy-done.3
  7.0 0.0 copy-done.1
  7.0 3.8 %inner.1 = (bf16[1536,512]{1,0:T(8,128)(2,1)}, f32[2,128,512]{2,1,0:T(8,128)S(1)}, bf16[2,256,128]{2,1,0:T(8,128)(2,1)S(1)}, f32[2,512,256]{2,1,0:T(8,128)S(1)}) custom-call(s32[8,24]{1,0:T(8,128)S(1)} %bitcast.4, s32[24]{0:T(128)S(1)} %copy-done.4, bf16[24,8,64,64]{3,2,1,0:T(8,128)(2,1)S(1)} %copy-done.1, bf16[1536,512]{1,0:T(8,128)(2,1)S(1)} %copy-done, ...), custom_call_target="tpu_custom_call" | custom-call | flops 2013265920 | bytes 8388608 | tf_op jit(solution)/shard_map/inner/pallas_call | solution.py:226
  10.9 0.0 collective-permute-done.far_ref
  10.9 0.0 collective-permute-done.1.near_ref
  10.9 1.0 %edges.1 = (bf16[1536,512]{1,0:T(8,128)(2,1)}, bf16[2,256,256]{2,1,0:T(8,128)(2,1)S(1)}, bf16[512,256]{1,0:T(8,128)(2,1)S(1)}) custom-call(bf16[128,512]{1,0:T(8,128)(2,1)S(1)} %collective-permute-done.far_ref, bf16[128,512]{1,0:T(8,128)(2,1)S(1)} %collective-permute-done.1.near_ref, ...), custom_call_target="tpu_custom_call", output_to_operand_aliasing={{0}: (7, {})} | custom-call | tf_op jit(solution)/shard_map/edges/pallas_call | solution.py:259
  11.9 0.1 collective-permute-start.2
  12.0 0.3 kept_half.1
  12.3 1.2 %collective-permute-done.2 = bf16[512,256]{1,0:T(8,128)(2,1)S(1)} collective-permute-done((bf16[512,256]{1,0:T(8,128)(2,1)S(1)}, bf16[512,256]{1,0:T(8,128)(2,1)S(1)}, u32[]{:S(2)}, u32[]{:S(2)}) %collective-permute-start.2) | collective-permute-done | bytes 262176 | tf_op jit(solution)/shard_map/ppermute | solution.py:278
  13.5 0.1 add_convert_fusion
  13.6 15.2 %all_to_all.5 = bf16[16,32,256]{2,1,0:T(8,128)(2,1)S(1)} all-to-all(bf16[16,32,256]{2,1,0:T(8,128)(2,1)S(1)} %bitcast.5), channel_id=1, replica_groups={{30,0,28,26,24,22,20,18,16,14,12,10,8,6,4,2},{31,1,29,27,25,23,21,19,17..., dimensions={0} | all-to-all | bytes 524288 | tf_op jit(solution)/shard_map/all_to_all | solution.py:294
  28.8 0.6 %broadcast_multiply_fusion = f32[32,256]{1,0:T(8,128)} fusion(f32[32,256]{1,0:T(8,128)S(1)} %convert_reduce_fusion), kind=kLoop, calls=%fused_computation.2 | loop fusion | flops 8192 | bytes 65536 | tf_op jit(solution)/shard_map/mul | solution.py:300
  (1 shorter events, 0.0 us)
Async XLA Ops:
  0.6 6.4 %copy-start = (bf16[1536,512]{1,0:T(8,128)(2,1)S(1)}, bf16[1536,512]{1,0:T(8,128)(2,1)}, u32[]{:S(2)}) copy-start(bf16[1536,512]{1,0:T(8,128)(2,1)} %bottom_ref.3) | copy-start | bytes 4718596
  0.6 6.4 %copy-start.2 = (f32[1536]{0:T(1024)S(1)}, f32[1536]{0:T(1024)}, u32[]{:S(2)}) copy-start(f32[1536]{0:T(1024)} %param.9) | copy-start | bytes 18436
  0.7 6.4 %copy-start.4 = (s32[24]{0:T(128)S(1)}, s32[24]{0:T(128)}, u32[]{:S(2)}) copy-start(s32[24]{0:T(128)} %live_ref.1) | copy-start | bytes 292
  0.7 6.4 %copy-start.3 = (s32[24,8]{0,1:T(8,128)S(1)}, s32[24,8]{0,1:T(8,128)}, u32[]{:S(2)}) copy-start(s32[24,8]{0,1:T(8,128)} %param.7) | copy-start | bytes 2308
  0.7 6.4 %copy-start.1 = (bf16[24,8,64,64]{3,2,1,0:T(8,128)(2,1)S(1)}, bf16[24,8,64,64]{3,2,1,0:T(8,128)(2,1)}, u32[]{:S(2)}) copy-start(bf16[24,8,64,64]{3,2,1,0:T(8,128)(2,1)} %jac_ref.1) | copy-start | bytes 4718596
  1.8 9.0 %collective-permute-start = (bf16[128,512]{1,0:T(8,128)(2,1)S(1)}, bf16[128,512]{1,0:T(8,128)(2,1)S(1)}, u32[]{:S(2)}, u32[]{:S(2)}) collective-permute-start(bf16[128,512]{1,0:T(8,128)(2,1)S(1)} %get-tuple-element.11), channel_id=1, source_target_pairs={{1,2},{3,4},{5,6},{7,8},{9,10},{11,12},{13,14},{15,16},{17,18},{19... | collective-permute-start | bytes 393224 | tf_op jit(solution)/shard_map/ppermute | solution.py:216
  2.6 8.2 %collective-permute-start.1 = (bf16[128,512]{1,0:T(8,128)(2,1)S(1)}, bf16[128,512]{1,0:T(8,128)(2,1)S(1)}, u32[]{:S(2)}, u32[]{:S(2)}) collective-permute-start(bf16[128,512]{1,0:T(8,128)(2,1)S(1)} %get-tuple-element.12), channel_id=1, source_target_pairs={{0,1},{2,3},{4,5},{6,7},{8,9},{10,11},{12,13},{14,15},{16,17},{18,... | collective-permute-start | bytes 393224 | tf_op jit(solution)/shard_map/ppermute | solution.py:218
  11.9 1.6 %collective-permute-start.2 = (bf16[512,256]{1,0:T(8,128)(2,1)S(1)}, bf16[512,256]{1,0:T(8,128)(2,1)S(1)}, u32[]{:S(2)}, u32[]{:S(2)}) collective-permute-start(bf16[512,256]{1,0:T(8,128)(2,1)S(1)} %get-tuple-element.19), channel_id=1, source_target_pairs={{0,1},{1,0},{2,3},{3,2},{4,5},{5,4},{6,7},{7,6},{8,9},{9,8},{10,11... | collective-permute-start | bytes 786440 | tf_op jit(solution)/shard_map/ppermute | solution.py:278

commit v15 on v11

--- a/solution.py
+++ b/solution.py
@@ -58,23 +58,28 @@
     return both[:half] + both[half:]
 
 
-def slice_kernel(basis_hbm, far_ref, near_ref, sems):
+def slice_kernel(basis_hbm, far_ref, tiles_ref, sems):
     tile = far_ref.shape[0]
     last = basis_hbm.shape[0] - tile
     odd = lax.rem(lax.axis_index(AXES), 2)
+    far = pl.ds(pl.multiple_of(odd * last, tile), tile)
     copies = []
-    for i, (at, target) in enumerate(((odd, far_ref), (1 - odd, near_ref))):
-        where = pl.ds(pl.multiple_of(at * last, tile), tile)
-        copies.append(pltpu.make_async_copy(basis_hbm.at[where], target, sems.at[i]))
-        copies[i].start()
+    for i, (source, target) in enumerate((
+        (far, far_ref),
+        (pl.ds(0, tile), tiles_ref.at[pl.ds(0, tile)]),
+        (pl.ds(last, tile), tiles_ref.at[pl.ds(tile, tile)]),
+    )):
+        copies.append(pltpu.make_async_copy(basis_hbm.at[source], target, sems.at[i]))
+        copies[i].start(priority=1)
     for copy in copies:
         copy.wait()
 
 
 def inner_kernel(
     cols_ref, live_ref, jac_ref, basis_ref, acc_ref,
-    image_ref, edge_ref, arm_ref, part_ref, staged, sems,
+    image_ref, edge_ref, arm_ref, *rest,
 ):
+    *sum_refs, part_ref, staged, sems = rest
     nblk, _, bsize, _ = jac_ref.shape
     nrows = basis_ref.shape[0]
     tile = 2 * bsize
@@ -126,17 +131,15 @@
         else:
             edge_ref[1] = apply_strip(strip[:, : 2 * tile], basis_ref[nrows - 2 * tile :, :])
             arm_ref[1] = strip[:, 2 * tile :]
-    for i, half in enumerate(project(middle, nrows - tile)):
-        part_ref[i] += half
+    sums = [part_ref[i] + half for i, half in enumerate(project(middle, nrows - tile))]
+    if len(sums) == 1:
+        sum_refs[0][...] = sums[0]
+    else:
+        second = lax.axis_index("col") == 1
+        sum_refs[0][...] = jnp.where(second, sums[1], sums[0])
+        sum_refs[1][...] = jnp.where(second, sums[0], sums[1]).astype(jnp.bfloat16)
     for copy in copies:
         copy.wait()
-
-
-def add_edges(part_ref, tiles, rows_ref, half):
-    update = lax.dot_general(
-        tiles, rows_ref[half], ROWS_DOT, preferred_element_type=jnp.float32
-    )
-    return part_ref[half] + update
 
 
 def put_blocks(ref, value, order):
@@ -149,42 +152,63 @@
         ref[to * high : (to + 1) * high, :] = block.astype(ref.dtype)
 
 
-def leaving_half(parts):
-    return 1 - lax.axis_index("col") if parts == 2 else 0
-
-
 def edge_kernel(
-    order, far_ref, near_ref, edge_ref, arm_ref, top_ref, bottom_ref, part_ref, _,
-    image_ref, rows_ref, send_ref, staged, sems,
+    far_ref, near_ref, edge_ref, arm_ref, _, image_ref, *rest,
 ):
-    tile = top_ref.shape[0]
+    *rows_refs, staged, sems = rest
+    tile, width = far_ref.shape
     nrows = image_ref.shape[0]
-    parts, _, wide = rows_ref.shape
     odd = lax.rem(lax.axis_index(AXES), 2) == 1
-    near, far = near_ref[...], far_ref[...]
-    halos = (jnp.where(odd, near, far), jnp.where(odd, far, near))
+    far = far_ref[...]
+    halos = (
+        jnp.where(odd, near_ref[tile:, :], far),
+        jnp.where(odd, far, near_ref[:tile, :]),
+    )
     copies = []
     for side in range(2):
         rows = edge_ref[side] + apply_strip(arm_ref[side], halos[side])
         rows = rows.astype(jnp.bfloat16)
         staged[side] = rows
-        for i in range(parts):
-            rows_ref[i, side * tile : (side + 1) * tile, :] = rows[:, i * wide : (i + 1) * wide]
+        at = slice(side * tile, (side + 1) * tile)
+        if len(rows_refs) == 1:
+            rows_refs[0][at, :] = rows
+        else:
+            second = lax.axis_index("col") == 1
+            left, right = rows[:, : width // 2], rows[:, width // 2 :]
+            rows_refs[0][at, :] = jnp.where(second, right, left)
+            rows_refs[1][at, :] = jnp.where(second, left, right)
         where = pl.ds(0 if side == 0 else nrows - tile, tile)
         copy = pltpu.make_async_copy(staged.at[side], image_ref.at[where], sems.at[side])
         copy.start()
         copies.append(copy)
-    tiles = jnp.concatenate([top_ref[...], bottom_ref[...]], axis=0)
-    send = add_edges(part_ref, tiles, rows_ref, leaving_half(parts))
-    put_blocks(send_ref, send, order)
     for copy in copies:
         copy.wait()
 
 
-def keep_kernel(order, top_ref, bottom_ref, rows_ref, part_ref, keep_ref):
-    tiles = jnp.concatenate([top_ref[...], bottom_ref[...]], axis=0)
-    keep = add_edges(part_ref, tiles, rows_ref, 1 - leaving_half(2))
-    put_blocks(keep_ref, keep, order)
+def update_kernel(order, tiles_ref, rows_ref, *refs):
+    *terms, out_ref = refs
+    total = lax.dot_general(
+        tiles_ref[...], rows_ref[...], ROWS_DOT, preferred_element_type=jnp.float32
+    )
+    for term in terms:
+        total = total + term[...].astype(jnp.float32)
+    put_blocks(out_ref, total, order)
+
+
+def update(name, order, kind, *arrays):
+    tiles, rows = arrays[:2]
+    shape = (tiles.shape[1], rows.shape[1])
+    return pl.pallas_call(
+        functools.partial(update_kernel, order),
+        out_shape=jax.ShapeDtypeStruct(shape, kind),
+        in_specs=[whole()] * len(arrays),
+        out_specs=whole(),
+        compiler_params=pltpu.CompilerParams(vmem_limit_bytes=32 * 2**20),
+        cost_estimate=pl.CostEstimate(
+            flops=2 * rows.size * shape[0], bytes_accessed=2**21, transcendentals=0
+        ),
+        name=name,
+    )(*arrays)
 
 
 def whole(memory_space=pltpu.VMEM):
@@ -200,12 +224,12 @@
     count = down * across
     f32, bf16 = jnp.float32, jnp.bfloat16
     edge_shape = jax.ShapeDtypeStruct((tile, width), bf16)
-    far_send, near_send = pl.pallas_call(
+    far_send, tiles = pl.pallas_call(
         slice_kernel,
-        out_shape=(edge_shape, edge_shape),
+        out_shape=(edge_shape, jax.ShapeDtypeStruct((2 * tile, width), bf16)),
         in_specs=[whole(pltpu.HBM)],
         out_specs=(whole(), whole()),
-        scratch_shapes=[pltpu.SemaphoreType.DMA((2,))],
+        scratch_shapes=[pltpu.SemaphoreType.DMA((3,))],
         compiler_params=pltpu.CompilerParams(vmem_limit_bytes=4 * 2**20),
         cost_estimate=pl.CostEstimate(
             flops=2 * nrows * width * width * slots, bytes_accessed=0, transcendentals=0
@@ -215,7 +239,7 @@
     swaps = [(i, i + 1) for i in range(1, count - 1, 2)]
     far = lax.ppermute(far_send, AXES, swaps + [(j, i) for i, j in swaps])
     swaps = [(i, i + 1) for i in range(0, count, 2)]
-    near = lax.ppermute(near_send, AXES, swaps + [(j, i) for i, j in swaps])
+    near = lax.ppermute(tiles, AXES, swaps + [(j, i) for i, j in swaps])
 
     halved = across == 2
     parts = 2 if halved else 1
@@ -223,17 +247,18 @@
     order = list(range(down))
     if halved and (width // down) % 16 == 0:
         order = [o * inner + i for i in range(inner) for o in reversed(range(outer))]
-    image, edge, arm, part = pl.pallas_call(
+    image, edge, arm, *sums = pl.pallas_call(
         inner_kernel,
         out_shape=(
             jax.ShapeDtypeStruct((nrows, width), bf16),
             jax.ShapeDtypeStruct((2, tile, width), f32),
             jax.ShapeDtypeStruct((2, 2 * tile, tile), bf16),
-            jax.ShapeDtypeStruct((parts, width, wide), f32),
+            *(jax.ShapeDtypeStruct((width, wide), kind) for kind in (f32, bf16)[:parts]),
         ),
         in_specs=[whole(pltpu.SMEM), whole(pltpu.SMEM), whole(), whole(), whole()],
-        out_specs=(whole(pltpu.HBM), whole(), whole(), whole()),
+        out_specs=(whole(pltpu.HBM), *([whole()] * (2 + parts))),
         scratch_shapes=[
+            pltpu.VMEM((parts, width, wide), f32),
             pltpu.VMEM((nrows, width), bf16),
             pltpu.SemaphoreType.DMA((nblk // 6 + 1,)),
         ],
@@ -252,48 +277,36 @@
         accumulation.reshape(nblk // 2, tile),
     )
 
-    ends = [
-        pl.BlockSpec((tile, width), lambda i: (0, 0)),
-        pl.BlockSpec((tile, width), lambda i: (nrows // tile - 1, 0)),
-    ]
-    image, rows, send = pl.pallas_call(
-        functools.partial(edge_kernel, order),
+    if halved:
+        swap = [(0, 1), (1, 0)]
+        leaving, far = lax.optimization_barrier((sums[1], far))
+        early = lax.ppermute(leaving, "col", swap)
+    image, *rows = pl.pallas_call(
+        edge_kernel,
         out_shape=(
             jax.ShapeDtypeStruct((nrows, width), bf16),
-            jax.ShapeDtypeStruct((parts, 2 * tile, wide), bf16),
-            jax.ShapeDtypeStruct((width, wide), bf16),
-        ),
-        grid=(1,),
-        in_specs=[whole(), whole(), whole(), whole(), *ends, whole(), whole(pl.ANY)],
-        out_specs=(whole(pl.ANY), whole(), whole()),
+            *([jax.ShapeDtypeStruct((2 * tile, wide), bf16)] * parts),
+        ),
+        in_specs=[whole(), whole(), whole(), whole(), whole(pl.ANY)],
+        out_specs=(whole(pl.ANY), *([whole()] * parts)),
         scratch_shapes=[
             pltpu.VMEM((2, tile, width), bf16),
             pltpu.SemaphoreType.DMA((2,)),
         ],
-        input_output_aliases={7: 0},
+        input_output_aliases={4: 0},
         compiler_params=pltpu.CompilerParams(vmem_limit_bytes=32 * 2**20),
         name="edges",
-    )(far, near, edge, arm, basis, basis, part, image)
+    )(far, near, edge, arm, image)
     if halved:
-        got = lax.ppermute(send, "col", [(0, 1), (1, 0)])
-        keep = pl.pallas_call(
-            functools.partial(keep_kernel, order),
-            out_shape=jax.ShapeDtypeStruct((width, wide), f32),
-            grid=(1,),
-            in_specs=[*ends, whole(), whole()],
-            out_specs=whole(),
-            compiler_params=pltpu.CompilerParams(vmem_limit_bytes=32 * 2**20),
-            cost_estimate=pl.CostEstimate(
-                flops=4 * tile * width * width, bytes_accessed=2**21, transcendentals=0
-            ),
-            name="kept_half",
-        )(basis, basis, rows, part)
-        total = (keep + got.astype(f32)).astype(bf16)
+        late = lax.ppermute(rows[1], "col", swap)
+        kept = update("own_rows", [0], f32, tiles, rows[0], sums[0])
+        total = update("sibling_rows", order, bf16, near, late, kept, early)
         total = total.reshape(down, width // down, wide)
         groups = [[m * across + c for m in order] for c in range(across)]
         got = lax.all_to_all(total, AXES, 0, 0, axis_index_groups=groups, tiled=True)
     else:
-        total = send.reshape(down, width // down, across, width // across)
+        total = update("own_rows", [0], bf16, tiles, rows[0], sums[0])
+        total = total.reshape(down, width // down, across, width // across)
         total = total.transpose(0, 2, 1, 3)
         total = total.reshape(count, width // down, width // across)
         got = lax.all_to_all(total, AXES, 0, 0, tiled=True)

time: 28.3 us -> 28.7 us (1.014)
  starting transfers between devices: 5.25 us -> 5.8 us
  waiting for transfers between devices: 1.24 us -> 0.72 us
  Pallas kernels: 6.28 us -> 6.8 us
    ppermute x2 -> x3, starting transfers between devices: 4.45 us -> 5 us  [the longest x1 4.36 us: local(): near = lax.ppermute(tiles, AXES, swaps + [(j, i) for i, j in swaps])]
    ppermute x2 -> x3, waiting for transfers between devices: 1.23 us -> 0.72 us  [the longest x1 0.71 us: local(): late = lax.ppermute(rows[1], 'col', swap)]
    pallas_call x3 -> x4, Pallas kernels: 2.47 us -> 2.73 us  [the longest x1 1.22 us: local(): pl.pallas_call(slice_kernel, out_shape=(edge_shape, jax.ShapeDtypeStruct(...]
  transfers between devices with their start and end apart: 3 -> 4, of which waited for: 1 -> 1; matrix products, arithmetic and copies ran while one was open for 0% -> 0% of each run, Pallas kernels for 15% -> 19%
where the time goes in v15:
time: 28.7 us; the launch traced here: 28.5 us
  blocking collectives  13.8 us (48%)
  Pallas kernels  6.8 us (24%)
  starting transfers between devices  5.8 us (20%)
  between operations  0.74 us (3%)
  waiting for transfers between devices  0.72 us (3%)
  other arithmetic  0.66 us (2%)
    all_to_all x1, blocking collectives, local(): lax.all_to_all(total, AXES, 0, 0, axis_index_groups=groups, tiled=True)  13.8 us
    ppermute x1, starting transfers between devices, local(): near = lax.ppermute(tiles, AXES, swaps + [(j, i) for i, j in swaps])  4.36 us
    pallas_call x1, Pallas kernels, local(): pl.pallas_call(inner_kernel, out_shape=(jax.ShapeDtypeStruct((nrows, widt...  4.07 us
    pallas_call x1, Pallas kernels, local(): pl.pallas_call(slice_kernel, out_shape=(edge_shape, jax.ShapeDtypeStruct(...  1.22 us
    pallas_call x1, Pallas kernels, local(): pl.pallas_call(edge_kernel, out_shape=(jax.ShapeDtypeStruct((nrows, width...  0.97 us
    ppermute x1, starting transfers between devices, local(): far = lax.ppermute(far_send, AXES, swaps + [(j, i) for i, j in swaps])  0.8 us
    ppermute x1, waiting for transfers between devices, local(): late = lax.ppermute(rows[1], 'col', swap)  0.71 us
    mul x1, other arithmetic, local(): projected = jnp.sum(got.astype(f32), axis=0) * (1.0 / (nrows * count))  0.62 us
  transfers between devices with their start and end apart: 4, of which 1 were waited for; matrix products, arithmetic and copies ran while one was open for 0% of the time, Pallas kernels for 19%

profile of v15, /device:TPU:0, one launch (start us, length us, event | category | flops | bytes accessed | tf_op | source)
XLA Modules:
  0.0 28.5 jit_solution(18436541442000949367)
XLA Ops:
  0.6 0.0 copy-start.1
  0.6 0.0 copy-start.2
  0.7 0.0 copy-start.4
  0.7 0.0 copy-start.3
  0.7 0.0 copy-start
  0.7 1.2 %halo_rows.1 = (bf16[128,512]{1,0:T(8,128)(2,1)S(1)}, bf16[256,512]{1,0:T(8,128)(2,1)S(1)}) custom-call(bf16[1536,512]{1,0:T(8,128)(2,1)} %basis_hbm.1), custom_call_target="tpu_custom_call" | custom-call | flops 6442450944 | tf_op jit(solution)/shard_map/halo_rows/pallas_call | solution.py:227
  1.9 0.8 %collective-permute-start = (bf16[128,512]{1,0:T(8,128)(2,1)S(1)}, bf16[128,512]{1,0:T(8,128)(2,1)S(1)}, u32[]{:S(2)}, u32[]{:S(2)}) collective-permute-start(bf16[128,512]{1,0:T(8,128)(2,1)S(1)} %get-tuple-element.15), channel_id=1, source_target_pairs={{1,2},{3,4},{5,6},{7,8},{9,10},{11,12},{13,14},{15,16},{17,18},{19... | collective-permute-start | bytes 393224 | tf_op jit(solution)/shard_map/ppermute | solution.py:240
  2.7 4.4 %collective-permute-start.1 = (bf16[256,512]{1,0:T(8,128)(2,1)S(1)}, bf16[256,512]{1,0:T(8,128)(2,1)S(1)}, u32[]{:S(2)}, u32[]{:S(2)}) collective-permute-start(bf16[256,512]{1,0:T(8,128)(2,1)S(1)} %get-tuple-element.17.tiles_ref), channel_id=1, source_target_pairs={{0,1},{2,3},{4,5},{6,7},{8,9},{10,11},{12,13},{14,15},{16,17},{18,... | collective-permute-start | bytes 786440 | tf_op jit(solution)/shard_map/ppermute | solution.py:242
  7.1 0.0 copy-done.1
  7.1 0.0 copy-done.2
  7.1 0.0 copy-done.4
  7.1 0.0 copy-done.3
  7.1 4.1 %inner.1 = (bf16[1536,512]{1,0:T(8,128)(2,1)}, f32[2,128,512]{2,1,0:T(8,128)S(1)}, bf16[2,256,128]{2,1,0:T(8,128)(2,1)S(1)}, f32[512,256]{1,0:T(8,128)S(1)}, bf16[512,256]{1,0:T(8,128)(2,1)S(1)}) custom-call(s32[8,24]{1,0:T(8,128)S(1)} %bitcast.5, s32[24]{0:T(128)S(1)} %copy-done.4, bf16[24,8,64,64]{3,2,1,0:T(8,128)(2,1)S(1)} %copy-done, ...), custom_call_target="tpu_custom_call" | custom-call | flops 2013265920 | bytes 8388608 | tf_op jit(solution)/shard_map/inner/pallas_call | solution.py:250
  11.2 0.0 collective-permute-done.far_ref
  11.2 0.1 collective-permute-start.3
  11.3 0.0 collective-permute-done.1.near_ref.tiles_ref
  11.3 1.0 %edges.1 = (bf16[1536,512]{1,0:T(8,128)(2,1)}, bf16[256,256]{1,0:T(8,128)(2,1)S(1)}, bf16[256,256]{1,0:T(8,128)(2,1)S(1)}) custom-call(bf16[128,512]{1,0:T(8,128)(2,1)S(1)} %collective-permute-done.far_ref, bf16[256,512]{1,0:T(8,128)(2,1)S(1)} %collective-permute-done.1.near_ref.tiles_ref, ...), custom_call_target="tpu_custom_call", output_to_operand_aliasing={{0}: (4, {})} | custom-call | tf_op jit(solution)/shard_map/edges/pallas_call | solution.py:284
  12.3 0.5 %collective-permute-start.2 = (bf16[256,256]{1,0:T(8,128)(2,1)S(1)}, bf16[256,256]{1,0:T(8,128)(2,1)S(1)}, u32[]{:S(2)}, u32[]{:S(2)}) collective-permute-start(bf16[256,256]{1,0:T(8,128)(2,1)S(1)} %get-tuple-element.22), channel_id=1, source_target_pairs={{0,1},{1,0},{2,3},{3,2},{4,5},{5,4},{6,7},{7,6},{8,9},{9,8},{10,11... | collective-permute-start | bytes 393224 | tf_op jit(solution)/shard_map/ppermute | solution.py:301
  12.8 0.3 own_rows.1.refs_0_
  13.1 0.7 %collective-permute-done.2.rows_ref = bf16[256,256]{1,0:T(8,128)(2,1)S(1)} collective-permute-done((bf16[256,256]{1,0:T(8,128)(2,1)S(1)}, bf16[256,256]{1,0:T(8,128)(2,1)S(1)}, u32[]{:S(2)}, u32[]{:S(2)}) %collective-permute-start.2) | collective-permute-done | bytes 131104 | tf_op jit(solution)/shard_map/ppermute | solution.py:301
  13.8 0.0 collective-permute-done.3.refs_1_
  13.8 0.3 sibling_rows.1
  14.1 13.8 %all_to_all.5 = bf16[16,32,256]{2,1,0:T(8,128)(2,1)S(1)} all-to-all(bf16[16,32,256]{2,1,0:T(8,128)(2,1)S(1)} %bitcast.3), channel_id=1, replica_groups={{24,16,8,0,26,18,10,2,28,20,12,4,30,22,14,6},{25,17,9,1,27,19,11,3,29,2..., dimensions={0} | all-to-all | bytes 524288 | tf_op jit(solution)/shard_map/all_to_all | solution.py:306
  27.9 0.6 %broadcast_multiply_fusion = f32[32,256]{1,0:T(8,128)} fusion(f32[32,256]{1,0:T(8,128)S(1)} %convert_reduce_fusion), kind=kLoop, calls=%fused_computation.1 | loop fusion | flops 8192 | bytes 65536 | tf_op jit(solution)/shard_map/mul | solution.py:313
  (2 shorter events, 0.0 us)
Async XLA Ops:
  0.6 6.5 %copy-start.1 = (bf16[1536,512]{1,0:T(8,128)(2,1)S(1)}, bf16[1536,512]{1,0:T(8,128)(2,1)}, u32[]{:S(2)}) copy-start(bf16[1536,512]{1,0:T(8,128)(2,1)} %basis_hbm.1) | copy-start | bytes 4718596
  0.6 6.4 %copy-start.2 = (f32[1536]{0:T(1024)S(1)}, f32[1536]{0:T(1024)}, u32[]{:S(2)}) copy-start(f32[1536]{0:T(1024)} %param.9) | copy-start | bytes 18436
  0.7 6.4 %copy-start.4 = (s32[24]{0:T(128)S(1)}, s32[24]{0:T(128)}, u32[]{:S(2)}) copy-start(s32[24]{0:T(128)} %live_ref.1) | copy-start | bytes 292
  0.7 6.4 %copy-start.3 = (s32[24,8]{0,1:T(8,128)S(1)}, s32[24,8]{0,1:T(8,128)}, u32[]{:S(2)}) copy-start(s32[24,8]{0,1:T(8,128)} %param.7) | copy-start | bytes 2308
  0.7 6.4 %copy-start = (bf16[24,8,64,64]{3,2,1,0:T(8,128)(2,1)S(1)}, bf16[24,8,64,64]{3,2,1,0:T(8,128)(2,1)}, u32[]{:S(2)}) copy-start(bf16[24,8,64,64]{3,2,1,0:T(8,128)(2,1)} %jac_ref.1) | copy-start | bytes 4718596
  1.9 9.3 %collective-permute-start = (bf16[128,512]{1,0:T(8,128)(2,1)S(1)}, bf16[128,512]{1,0:T(8,128)(2,1)S(1)}, u32[]{:S(2)}, u32[]{:S(2)}) collective-permute-start(bf16[128,512]{1,0:T(8,128)(2,1)S(1)} %get-tuple-element.15), channel_id=1, source_target_pairs={{1,2},{3,4},{5,6},{7,8},{9,10},{11,12},{13,14},{15,16},{17,18},{19... | collective-permute-start | bytes 393224 | tf_op jit(solution)/shard_map/ppermute | solution.py:240
  2.7 8.6 %collective-permute-start.1 = (bf16[256,512]{1,0:T(8,128)(2,1)S(1)}, bf16[256,512]{1,0:T(8,128)(2,1)S(1)}, u32[]{:S(2)}, u32[]{:S(2)}) collective-permute-start(bf16[256,512]{1,0:T(8,128)(2,1)S(1)} %get-tuple-element.17.tiles_ref), channel_id=1, source_target_pairs={{0,1},{2,3},{4,5},{6,7},{8,9},{10,11},{12,13},{14,15},{16,17},{18,... | collective-permute-start | bytes 786440 | tf_op jit(solution)/shard_map/ppermute | solution.py:242
  11.2 2.6 %collective-permute-start.3 = (bf16[512,256]{1,0:T(8,128)(2,1)S(1)}, bf16[512,256]{1,0:T(8,128)(2,1)S(1)}, u32[]{:S(2)}, u32[]{:S(2)}) collective-permute-start(bf16[512,256]{1,0:T(8,128)(2,1)S(1)} %get-tuple-element.25), channel_id=1, source_target_pairs={{0,1},{1,0},{2,3},{3,2},{4,5},{5,4},{6,7},{7,6},{8,9},{9,8},{10,11... | collective-permute-start | bytes 786440 | tf_op jit(solution)/shard_map/ppermute | solution.py:283
  12.3 1.5 %collective-permute-start.2 = (bf16[256,256]{1,0:T(8,128)(2,1)S(1)}, bf16[256,256]{1,0:T(8,128)(2,1)S(1)}, u32[]{:S(2)}, u32[]{:S(2)}) collective-permute-start(bf16[256,256]{1,0:T(8,128)(2,1)S(1)} %get-tuple-element.22), channel_id=1, source_target_pairs={{0,1},{1,0},{2,3},{3,2},{4,5},{5,4},{6,7},{7,6},{8,9},{9,8},{10,11... | collective-permute-start | bytes 393224 | tf_op jit(solution)/shard_map/ppermute | solution.py:301

commit v16 on v11

--- a/solution.py
+++ b/solution.py
@@ -132,6 +132,11 @@
         copy.wait()
 
 
+def end_tiles(basis_ref, tile):
+    nrows = basis_ref.shape[0]
+    return jnp.concatenate([basis_ref[:tile, :], basis_ref[nrows - tile :, :]], axis=0)
+
+
 def add_edges(part_ref, tiles, rows_ref, half):
     update = lax.dot_general(
         tiles, rows_ref[half], ROWS_DOT, preferred_element_type=jnp.float32
@@ -154,37 +159,40 @@
 
 
 def edge_kernel(
-    order, far_ref, near_ref, edge_ref, arm_ref, top_ref, bottom_ref, part_ref, _,
-    image_ref, rows_ref, send_ref, staged, sems,
+    order, far_ref, near_ref, edge_ref, arm_ref, basis_ref, part_ref, rows_ref, send_ref,
 ):
-    tile = top_ref.shape[0]
-    nrows = image_ref.shape[0]
+    tile = far_ref.shape[0]
     parts, _, wide = rows_ref.shape
     odd = lax.rem(lax.axis_index(AXES), 2) == 1
     near, far = near_ref[...], far_ref[...]
     halos = (jnp.where(odd, near, far), jnp.where(odd, far, near))
-    copies = []
     for side in range(2):
         rows = edge_ref[side] + apply_strip(arm_ref[side], halos[side])
         rows = rows.astype(jnp.bfloat16)
-        staged[side] = rows
         for i in range(parts):
             rows_ref[i, side * tile : (side + 1) * tile, :] = rows[:, i * wide : (i + 1) * wide]
-        where = pl.ds(0 if side == 0 else nrows - tile, tile)
-        copy = pltpu.make_async_copy(staged.at[side], image_ref.at[where], sems.at[side])
-        copy.start()
-        copies.append(copy)
-    tiles = jnp.concatenate([top_ref[...], bottom_ref[...]], axis=0)
-    send = add_edges(part_ref, tiles, rows_ref, leaving_half(parts))
+    send = add_edges(part_ref, end_tiles(basis_ref, tile), rows_ref, leaving_half(parts))
     put_blocks(send_ref, send, order)
+
+
+def keep_kernel(order, basis_ref, rows_ref, part_ref, _, image_ref, *rest):
+    *keep_refs, sems = rest
+    nrows = image_ref.shape[0]
+    parts, rows, wide = rows_ref.shape
+    tile = rows // 2
+    copies = []
+    for side, start in enumerate((0, nrows - tile)):
+        for i in range(parts):
+            source = rows_ref.at[i, pl.ds(side * tile, tile)]
+            target = image_ref.at[pl.ds(start, tile), pl.ds(i * wide, wide)]
+            copy = pltpu.make_async_copy(source, target, sems.at[side * parts + i])
+            copy.start()
+            copies.append(copy)
+    for keep_ref in keep_refs:
+        keep = add_edges(part_ref, end_tiles(basis_ref, tile), rows_ref, 1 - leaving_half(parts))
+        put_blocks(keep_ref, keep, order)
     for copy in copies:
         copy.wait()
-
-
-def keep_kernel(order, top_ref, bottom_ref, rows_ref, part_ref, keep_ref):
-    tiles = jnp.concatenate([top_ref[...], bottom_ref[...]], axis=0)
-    keep = add_edges(part_ref, tiles, rows_ref, 1 - leaving_half(2))
-    put_blocks(keep_ref, keep, order)
 
 
 def whole(memory_space=pltpu.VMEM):
@@ -252,43 +260,36 @@
         accumulation.reshape(nblk // 2, tile),
     )
 
-    ends = [
-        pl.BlockSpec((tile, width), lambda i: (0, 0)),
-        pl.BlockSpec((tile, width), lambda i: (nrows // tile - 1, 0)),
-    ]
-    image, rows, send = pl.pallas_call(
+    rows, send = pl.pallas_call(
         functools.partial(edge_kernel, order),
         out_shape=(
-            jax.ShapeDtypeStruct((nrows, width), bf16),
             jax.ShapeDtypeStruct((parts, 2 * tile, wide), bf16),
             jax.ShapeDtypeStruct((width, wide), bf16),
         ),
-        grid=(1,),
-        in_specs=[whole(), whole(), whole(), whole(), *ends, whole(), whole(pl.ANY)],
-        out_specs=(whole(pl.ANY), whole(), whole()),
-        scratch_shapes=[
-            pltpu.VMEM((2, tile, width), bf16),
-            pltpu.SemaphoreType.DMA((2,)),
-        ],
-        input_output_aliases={7: 0},
+        in_specs=[whole()] * 6,
+        out_specs=(whole(), whole()),
         compiler_params=pltpu.CompilerParams(vmem_limit_bytes=32 * 2**20),
         name="edges",
-    )(far, near, edge, arm, basis, basis, part, image)
+    )(far, near, edge, arm, basis, part)
+    image, *keep = pl.pallas_call(
+        functools.partial(keep_kernel, order),
+        out_shape=(
+            jax.ShapeDtypeStruct((nrows, width), bf16),
+            *([jax.ShapeDtypeStruct((width, wide), f32)] if halved else []),
+        ),
+        in_specs=[whole(), whole(), whole(), whole(pl.ANY)],
+        out_specs=(whole(pl.ANY), *([whole()] if halved else [])),
+        scratch_shapes=[pltpu.SemaphoreType.DMA((2 * parts,))],
+        input_output_aliases={3: 0},
+        compiler_params=pltpu.CompilerParams(vmem_limit_bytes=32 * 2**20),
+        cost_estimate=pl.CostEstimate(
+            flops=4 * tile * width * width, bytes_accessed=2**21, transcendentals=0
+        ),
+        name="kept_half",
+    )(basis, rows, part, image)
     if halved:
         got = lax.ppermute(send, "col", [(0, 1), (1, 0)])
-        keep = pl.pallas_call(
-            functools.partial(keep_kernel, order),
-            out_shape=jax.ShapeDtypeStruct((width, wide), f32),
-            grid=(1,),
-            in_specs=[*ends, whole(), whole()],
-            out_specs=whole(),
-            compiler_params=pltpu.CompilerParams(vmem_limit_bytes=32 * 2**20),
-            cost_estimate=pl.CostEstimate(
-                flops=4 * tile * width * width, bytes_accessed=2**21, transcendentals=0
-            ),
-            name="kept_half",
-        )(basis, basis, rows, part)
-        total = (keep + got.astype(f32)).astype(bf16)
+        total = (keep[0] + got.astype(f32)).astype(bf16)
         total = total.reshape(down, width // down, wide)
         groups = [[m * across + c for m in order] for c in range(across)]
         got = lax.all_to_all(total, AXES, 0, 0, axis_index_groups=groups, tiled=True)

time: 28.3 us -> 27.9 us (0.986)
  waiting for transfers between devices: 1.24 us -> 0.75 us
    pallas_call x1, Pallas kernels: 0.27 us -> 0.76 us  [local(): pl.pallas_call(functools.partial(keep_kernel, order), out_shape=(jax.Shap...]
    ppermute x1, waiting for transfers between devices: 1.23 us -> 0.74 us  [local(): got = lax.ppermute(send, 'col', [(0, 1), (1, 0)])]
    pallas_call x1, Pallas kernels: 1.05 us -> 0.63 us  [local(): pl.pallas_call(functools.partial(edge_kernel, order), out_shape=(jax.Shap...]
  transfers between devices with their start and end apart: 3 -> 3, of which waited for: 1 -> 1; matrix products, arithmetic and copies ran while one was open for 0% -> 0% of each run, Pallas kernels for 15% -> 17%
where the time goes in v16:
time: 27.9 us; the launch traced here: 27.7 us
  blocking collectives  13.9 us (50%)
  Pallas kernels  6.35 us (23%)
  starting transfers between devices  5.25 us (19%)
  waiting for transfers between devices  0.75 us (3%)
  between operations  0.74 us (3%)
  other arithmetic  0.72 us (3%)
    all_to_all x1, blocking collectives, local(): lax.all_to_all(total, AXES, 0, 0, axis_index_groups=groups, tiled=True)  13.9 us
    ppermute x1, starting transfers between devices, local(): near = lax.ppermute(near_send, AXES, swaps + [(j, i) for i, j in swaps])  4.36 us
    pallas_call x1, Pallas kernels, local(): pl.pallas_call(inner_kernel, out_shape=(jax.ShapeDtypeStruct((nrows, widt...  3.81 us
    pallas_call x1, Pallas kernels, local(): pl.pallas_call(slice_kernel, out_shape=(edge_shape, edge_shape), in_specs...  1.15 us
    ppermute x1, starting transfers between devices, local(): far = lax.ppermute(far_send, AXES, swaps + [(j, i) for i, j in swaps])  0.8 us
    pallas_call x1, Pallas kernels, local(): pl.pallas_call(functools.partial(keep_kernel, order), out_shape=(jax.Shap...  0.76 us
    ppermute x1, waiting for transfers between devices, local(): got = lax.ppermute(send, 'col', [(0, 1), (1, 0)])  0.74 us
    pallas_call x1, Pallas kernels, local(): pl.pallas_call(functools.partial(edge_kernel, order), out_shape=(jax.Shap...  0.63 us
  transfers between devices with their start and end apart: 3, of which 1 were waited for; matrix products, arithmetic and copies ran while one was open for 0% of the time, Pallas kernels for 17%

profile of v16, /device:TPU:0, one launch (start us, length us, event | category | flops | bytes accessed | tf_op | source)
XLA Modules:
  0.0 27.7 jit_solution(11745521228669051361)
XLA Ops:
  0.6 0.0 copy-start
  0.6 0.0 copy-start.2
  0.7 0.0 copy-start.4
  0.7 0.0 copy-start.3
  0.7 0.0 copy-start.1
  0.7 1.2 %halo_rows.1 = (bf16[128,512]{1,0:T(8,128)(2,1)S(1)}, bf16[128,512]{1,0:T(8,128)(2,1)S(1)}) custom-call(bf16[1536,512]{1,0:T(8,128)(2,1)} %basis_ref.5), custom_call_target="tpu_custom_call" | custom-call | flops 6442450944 | tf_op jit(solution)/shard_map/halo_rows/pallas_call | solution.py:211
  1.8 0.8 %collective-permute-start = (bf16[128,512]{1,0:T(8,128)(2,1)S(1)}, bf16[128,512]{1,0:T(8,128)(2,1)S(1)}, u32[]{:S(2)}, u32[]{:S(2)}) collective-permute-start(bf16[128,512]{1,0:T(8,128)(2,1)S(1)} %get-tuple-element.12), channel_id=1, source_target_pairs={{1,2},{3,4},{5,6},{7,8},{9,10},{11,12},{13,14},{15,16},{17,18},{19... | collective-permute-start | bytes 393224 | tf_op jit(solution)/shard_map/ppermute | solution.py:224
  2.6 4.4 %collective-permute-start.1 = (bf16[128,512]{1,0:T(8,128)(2,1)S(1)}, bf16[128,512]{1,0:T(8,128)(2,1)S(1)}, u32[]{:S(2)}, u32[]{:S(2)}) collective-permute-start(bf16[128,512]{1,0:T(8,128)(2,1)S(1)} %get-tuple-element.13), channel_id=1, source_target_pairs={{0,1},{2,3},{4,5},{6,7},{8,9},{10,11},{12,13},{14,15},{16,17},{18,... | collective-permute-start | bytes 393224 | tf_op jit(solution)/shard_map/ppermute | solution.py:226
  7.0 0.0 copy-done
  7.0 0.0 copy-done.2
  7.0 0.0 copy-done.4
  7.0 0.0 copy-done.3
  7.0 0.0 copy-done.1
  7.0 3.8 %inner.1 = (bf16[1536,512]{1,0:T(8,128)(2,1)}, f32[2,128,512]{2,1,0:T(8,128)S(1)}, bf16[2,256,128]{2,1,0:T(8,128)(2,1)S(1)}, f32[2,512,256]{2,1,0:T(8,128)S(1)}) custom-call(s32[8,24]{1,0:T(8,128)S(1)} %bitcast.4, s32[24]{0:T(128)S(1)} %copy-done.4, bf16[24,8,64,64]{3,2,1,0:T(8,128)(2,1)S(1)} %copy-done.1, bf16[1536,512]{1,0:T(8,128)(2,1)S(1)} %copy-done, ...), custom_call_target="tpu_custom_call" | custom-call | flops 2013265920 | bytes 8388608 | tf_op jit(solution)/shard_map/inner/pallas_call | solution.py:234
  10.9 0.0 collective-permute-done.far_ref
  10.9 0.0 collective-permute-done.1.near_ref
  10.9 0.6 %edges.1 = (bf16[2,256,256]{2,1,0:T(8,128)(2,1)S(1)}, bf16[512,256]{1,0:T(8,128)(2,1)S(1)}) custom-call(bf16[128,512]{1,0:T(8,128)(2,1)S(1)} %collective-permute-done.far_ref, bf16[128,512]{1,0:T(8,128)(2,1)S(1)} %collective-permute-done.1.near_ref, f32[2,128,512]{2,1,0:T(8,128)S(1)} %get-tuple-element.14.edge_ref, ...), custom_call_target="tpu_custom_call" | custom-call | tf_op jit(solution)/shard_map/edges/pallas_call | solution.py:263
  11.5 0.1 collective-permute-start.2
  11.6 0.8 %kept_half.1 = (bf16[1536,512]{1,0:T(8,128)(2,1)}, f32[512,256]{1,0:T(8,128)S(1)}) custom-call(bf16[1536,512]{1,0:T(8,128)(2,1)S(1)} %copy-done, bf16[2,256,256]{2,1,0:T(8,128)(2,1)S(1)} %get-tuple-element.17.rows_ref, f32[2,512,256]{2,1,0:T(8,128)S(1)} %get-tuple-element.16.part_ref, ...), custom_call_target="tpu_custom_call", output_to_operand_aliasing={{0}: (3, {})} | custom-call | flops 134217728 | bytes 2097152 | tf_op jit(solution)/shard_map/kept_half/pallas_call | solution.py:274
  12.4 0.7 %collective-permute-done.2 = bf16[512,256]{1,0:T(8,128)(2,1)S(1)} collective-permute-done((bf16[512,256]{1,0:T(8,128)(2,1)S(1)}, bf16[512,256]{1,0:T(8,128)(2,1)S(1)}, u32[]{:S(2)}, u32[]{:S(2)}) %collective-permute-start.2) | collective-permute-done | bytes 262176 | tf_op jit(solution)/shard_map/ppermute | solution.py:291
  13.1 0.1 add_convert_fusion
  13.2 13.9 %all_to_all.5 = bf16[16,32,256]{2,1,0:T(8,128)(2,1)S(1)} all-to-all(bf16[16,32,256]{2,1,0:T(8,128)(2,1)S(1)} %bitcast.5), channel_id=1, replica_groups={{24,16,8,0,26,18,10,2,28,20,12,4,30,22,14,6},{25,17,9,1,27,19,11,3,29,2..., dimensions={0} | all-to-all | bytes 524288 | tf_op jit(solution)/shard_map/all_to_all | solution.py:295
  27.1 0.6 %broadcast_multiply_fusion = f32[32,256]{1,0:T(8,128)} fusion(f32[32,256]{1,0:T(8,128)S(1)} %convert_reduce_fusion), kind=kLoop, calls=%fused_computation.2 | loop fusion | flops 8192 | bytes 65536 | tf_op jit(solution)/shard_map/mul | solution.py:301
  (1 shorter events, 0.0 us)
Async XLA Ops:
  0.6 6.4 %copy-start = (bf16[1536,512]{1,0:T(8,128)(2,1)S(1)}, bf16[1536,512]{1,0:T(8,128)(2,1)}, u32[]{:S(2)}) copy-start(bf16[1536,512]{1,0:T(8,128)(2,1)} %basis_ref.5) | copy-start | bytes 4718596
  0.6 6.4 %copy-start.2 = (f32[1536]{0:T(1024)S(1)}, f32[1536]{0:T(1024)}, u32[]{:S(2)}) copy-start(f32[1536]{0:T(1024)} %param.9) | copy-start | bytes 18436
  0.7 6.4 %copy-start.4 = (s32[24]{0:T(128)S(1)}, s32[24]{0:T(128)}, u32[]{:S(2)}) copy-start(s32[24]{0:T(128)} %live_ref.1) | copy-start | bytes 292
  0.7 6.4 %copy-start.3 = (s32[24,8]{0,1:T(8,128)S(1)}, s32[24,8]{0,1:T(8,128)}, u32[]{:S(2)}) copy-start(s32[24,8]{0,1:T(8,128)} %param.7) | copy-start | bytes 2308
  0.7 6.4 %copy-start.1 = (bf16[24,8,64,64]{3,2,1,0:T(8,128)(2,1)S(1)}, bf16[24,8,64,64]{3,2,1,0:T(8,128)(2,1)}, u32[]{:S(2)}) copy-start(bf16[24,8,64,64]{3,2,1,0:T(8,128)(2,1)} %jac_ref.1) | copy-start | bytes 4718596
  1.8 9.0 %collective-permute-start = (bf16[128,512]{1,0:T(8,128)(2,1)S(1)}, bf16[128,512]{1,0:T(8,128)(2,1)S(1)}, u32[]{:S(2)}, u32[]{:S(2)}) collective-permute-start(bf16[128,512]{1,0:T(8,128)(2,1)S(1)} %get-tuple-element.12), channel_id=1, source_target_pairs={{1,2},{3,4},{5,6},{7,8},{9,10},{11,12},{13,14},{15,16},{17,18},{19... | collective-permute-start | bytes 393224 | tf_op jit(solution)/shard_map/ppermute | solution.py:224
  2.6 8.2 %collective-permute-start.1 = (bf16[128,512]{1,0:T(8,128)(2,1)S(1)}, bf16[128,512]{1,0:T(8,128)(2,1)S(1)}, u32[]{:S(2)}, u32[]{:S(2)}) collective-permute-start(bf16[128,512]{1,0:T(8,128)(2,1)S(1)} %get-tuple-element.13), channel_id=1, source_target_pairs={{0,1},{2,3},{4,5},{6,7},{8,9},{10,11},{12,13},{14,15},{16,17},{18,... | collective-permute-start | bytes 393224 | tf_op jit(solution)/shard_map/ppermute | solution.py:226
  11.5 1.6 %collective-permute-start.2 = (bf16[512,256]{1,0:T(8,128)(2,1)S(1)}, bf16[512,256]{1,0:T(8,128)(2,1)S(1)}, u32[]{:S(2)}, u32[]{:S(2)}) collective-permute-start(bf16[512,256]{1,0:T(8,128)(2,1)S(1)} %get-tuple-element.21), channel_id=1, source_target_pairs={{0,1},{1,0},{2,3},{3,2},{4,5},{5,4},{6,7},{7,6},{8,9},{9,8},{10,11... | collective-permute-start | bytes 786440 | tf_op jit(solution)/shard_map/ppermute | solution.py:291

commit v17 on v16

--- a/solution.py
+++ b/solution.py
@@ -144,13 +144,13 @@
     return part_ref[half] + update
 
 
-def put_blocks(ref, value, order):
-    if order == sorted(order):
-        ref[...] = value.astype(ref.dtype)
-        return
-    high = value.shape[0] // len(order)
-    for to, source in enumerate(order):
-        block = value[source * high : (source + 1) * high, :]
+def put_blocks(ref, value, orders, core):
+    high = value.shape[0] // len(orders[0])
+    blocks = [value[i * high : (i + 1) * high, :] for i in range(len(orders[0]))]
+    for to, (first, second) in enumerate(zip(orders[0], orders[-1])):
+        block = blocks[first]
+        if first != second:
+            block = jnp.where(core == 1, blocks[second], block)
         ref[to * high : (to + 1) * high, :] = block.astype(ref.dtype)
 
 
@@ -159,7 +159,7 @@
 
 
 def edge_kernel(
-    order, far_ref, near_ref, edge_ref, arm_ref, basis_ref, part_ref, rows_ref, send_ref,
+    orders, far_ref, near_ref, edge_ref, arm_ref, basis_ref, part_ref, rows_ref, send_ref,
 ):
     tile = far_ref.shape[0]
     parts, _, wide = rows_ref.shape
@@ -171,11 +171,12 @@
         rows = rows.astype(jnp.bfloat16)
         for i in range(parts):
             rows_ref[i, side * tile : (side + 1) * tile, :] = rows[:, i * wide : (i + 1) * wide]
-    send = add_edges(part_ref, end_tiles(basis_ref, tile), rows_ref, leaving_half(parts))
-    put_blocks(send_ref, send, order)
-
-
-def keep_kernel(order, basis_ref, rows_ref, part_ref, _, image_ref, *rest):
+    leaving = leaving_half(parts)
+    send = add_edges(part_ref, end_tiles(basis_ref, tile), rows_ref, leaving)
+    put_blocks(send_ref, send, orders, leaving)
+
+
+def keep_kernel(orders, basis_ref, rows_ref, part_ref, _, image_ref, *rest):
     *keep_refs, sems = rest
     nrows = image_ref.shape[0]
     parts, rows, wide = rows_ref.shape
@@ -189,8 +190,9 @@
             copy.start()
             copies.append(copy)
     for keep_ref in keep_refs:
-        keep = add_edges(part_ref, end_tiles(basis_ref, tile), rows_ref, 1 - leaving_half(parts))
-        put_blocks(keep_ref, keep, order)
+        own = 1 - leaving_half(parts)
+        keep = add_edges(part_ref, end_tiles(basis_ref, tile), rows_ref, own)
+        put_blocks(keep_ref, keep, orders, own)
     for copy in copies:
         copy.wait()
 
@@ -228,9 +230,12 @@
     halved = across == 2
     parts = 2 if halved else 1
     wide = width // parts
-    order = list(range(down))
-    if halved and (width // down) % 16 == 0:
-        order = [o * inner + i for i in range(inner) for o in reversed(range(outer))]
+    orders = [[0]]
+    if halved:
+        orders = [list(range(down))] * 2
+        if (width // down) % 16 == 0:
+            lines = [[o * inner + i for o in reversed(range(outer))] for i in range(inner)]
+            orders = [sum(lines, []), sum(lines[:1] + lines[:0:-1], [])]
     image, edge, arm, part = pl.pallas_call(
         inner_kernel,
         out_shape=(
@@ -261,7 +266,7 @@
     )
 
     rows, send = pl.pallas_call(
-        functools.partial(edge_kernel, order),
+        functools.partial(edge_kernel, orders),
         out_shape=(
             jax.ShapeDtypeStruct((parts, 2 * tile, wide), bf16),
             jax.ShapeDtypeStruct((width, wide), bf16),
@@ -272,7 +277,7 @@
         name="edges",
     )(far, near, edge, arm, basis, part)
     image, *keep = pl.pallas_call(
-        functools.partial(keep_kernel, order),
+        functools.partial(keep_kernel, orders),
         out_shape=(
             jax.ShapeDtypeStruct((nrows, width), bf16),
             *([jax.ShapeDtypeStruct((width, wide), f32)] if halved else []),
@@ -291,7 +296,7 @@
         got = lax.ppermute(send, "col", [(0, 1), (1, 0)])
         total = (keep[0] + got.astype(f32)).astype(bf16)
         total = total.reshape(down, width // down, wide)
-        groups = [[m * across + c for m in order] for c in range(across)]
+        groups = [[m * across + c for m in orders[c]] for c in range(across)]
         got = lax.all_to_all(total, AXES, 0, 0, axis_index_groups=groups, tiled=True)
     else:
         total = send.reshape(down, width // down, across, width // across)

time: 27.9 us -> 27.9 us (level)
  no operation moved by 1% of the time
where the time goes in v17:
time: 27.9 us; the launch traced here: 27.7 us
  blocking collectives  13.9 us (50%)
  Pallas kernels  6.35 us (23%)
  starting transfers between devices  5.25 us (19%)
  waiting for transfers between devices  0.75 us (3%)
  between operations  0.75 us (3%)
  other arithmetic  0.72 us (3%)
    all_to_all x1, blocking collectives, local(): lax.all_to_all(total, AXES, 0, 0, axis_index_groups=groups, tiled=True)  13.9 us
    ppermute x1, starting transfers between devices, local(): near = lax.ppermute(near_send, AXES, swaps + [(j, i) for i, j in swaps])  4.36 us
    pallas_call x1, Pallas kernels, local(): pl.pallas_call(inner_kernel, out_shape=(jax.ShapeDtypeStruct((nrows, widt...  3.81 us
    pallas_call x1, Pallas kernels, local(): pl.pallas_call(slice_kernel, out_shape=(edge_shape, edge_shape), in_specs...  1.15 us
    ppermute x1, starting transfers between devices, local(): far = lax.ppermute(far_send, AXES, swaps + [(j, i) for i, j in swaps])  0.8 us
    pallas_call x1, Pallas kernels, local(): pl.pallas_call(functools.partial(keep_kernel, orders), out_shape=(jax.Sha...  0.76 us
    ppermute x1, waiting for transfers between devices, local(): got = lax.ppermute(send, 'col', [(0, 1), (1, 0)])  0.74 us
    pallas_call x1, Pallas kernels, local(): pl.pallas_call(functools.partial(edge_kernel, orders), out_shape=(jax.Sha...  0.63 us
  transfers between devices with their start and end apart: 3, of which 1 were waited for; matrix products, arithmetic and copies ran while one was open for 0% of the time, Pallas kernels for 17%

profile of v17, /device:TPU:0, one launch (start us, length us, event | category | flops | bytes accessed | tf_op | source)
XLA Modules:
  0.0 27.7 jit_solution(10489763300140964105)
XLA Ops:
  0.6 0.0 copy-start
  0.6 0.0 copy-start.2
  0.7 0.0 copy-start.4
  0.7 0.0 copy-start.3
  0.7 0.0 copy-start.1
  0.7 1.2 %halo_rows.1 = (bf16[128,512]{1,0:T(8,128)(2,1)S(1)}, bf16[128,512]{1,0:T(8,128)(2,1)S(1)}) custom-call(bf16[1536,512]{1,0:T(8,128)(2,1)} %basis_ref.5), custom_call_target="tpu_custom_call" | custom-call | flops 6442450944 | tf_op jit(solution)/shard_map/halo_rows/pallas_call | solution.py:213
  1.8 0.8 %collective-permute-start = (bf16[128,512]{1,0:T(8,128)(2,1)S(1)}, bf16[128,512]{1,0:T(8,128)(2,1)S(1)}, u32[]{:S(2)}, u32[]{:S(2)}) collective-permute-start(bf16[128,512]{1,0:T(8,128)(2,1)S(1)} %get-tuple-element.12), channel_id=1, source_target_pairs={{1,2},{3,4},{5,6},{7,8},{9,10},{11,12},{13,14},{15,16},{17,18},{19... | collective-permute-start | bytes 393224 | tf_op jit(solution)/shard_map/ppermute | solution.py:226
  2.6 4.4 %collective-permute-start.1 = (bf16[128,512]{1,0:T(8,128)(2,1)S(1)}, bf16[128,512]{1,0:T(8,128)(2,1)S(1)}, u32[]{:S(2)}, u32[]{:S(2)}) collective-permute-start(bf16[128,512]{1,0:T(8,128)(2,1)S(1)} %get-tuple-element.13), channel_id=1, source_target_pairs={{0,1},{2,3},{4,5},{6,7},{8,9},{10,11},{12,13},{14,15},{16,17},{18,... | collective-permute-start | bytes 393224 | tf_op jit(solution)/shard_map/ppermute | solution.py:228
  7.0 0.0 copy-done
  7.0 0.0 copy-done.2
  7.0 0.0 copy-done.4
  7.0 0.0 copy-done.3
  7.0 0.0 copy-done.1
  7.0 3.8 %inner.1 = (bf16[1536,512]{1,0:T(8,128)(2,1)}, f32[2,128,512]{2,1,0:T(8,128)S(1)}, bf16[2,256,128]{2,1,0:T(8,128)(2,1)S(1)}, f32[2,512,256]{2,1,0:T(8,128)S(1)}) custom-call(s32[8,24]{1,0:T(8,128)S(1)} %bitcast.4, s32[24]{0:T(128)S(1)} %copy-done.4, bf16[24,8,64,64]{3,2,1,0:T(8,128)(2,1)S(1)} %copy-done.1, bf16[1536,512]{1,0:T(8,128)(2,1)S(1)} %copy-done, ...), custom_call_target="tpu_custom_call" | custom-call | flops 2013265920 | bytes 8388608 | tf_op jit(solution)/shard_map/inner/pallas_call | solution.py:239
  10.9 0.0 collective-permute-done.far_ref
  10.9 0.0 collective-permute-done.1.near_ref
  10.9 0.6 %edges.1 = (bf16[2,256,256]{2,1,0:T(8,128)(2,1)S(1)}, bf16[512,256]{1,0:T(8,128)(2,1)S(1)}) custom-call(bf16[128,512]{1,0:T(8,128)(2,1)S(1)} %collective-permute-done.far_ref, bf16[128,512]{1,0:T(8,128)(2,1)S(1)} %collective-permute-done.1.near_ref, f32[2,128,512]{2,1,0:T(8,128)S(1)} %get-tuple-element.14.edge_ref, ...), custom_call_target="tpu_custom_call" | custom-call | tf_op jit(solution)/shard_map/edges/pallas_call | solution.py:268
  11.5 0.1 collective-permute-start.2
  11.6 0.8 %kept_half.1 = (bf16[1536,512]{1,0:T(8,128)(2,1)}, f32[512,256]{1,0:T(8,128)S(1)}) custom-call(bf16[1536,512]{1,0:T(8,128)(2,1)S(1)} %copy-done, bf16[2,256,256]{2,1,0:T(8,128)(2,1)S(1)} %get-tuple-element.17.rows_ref, f32[2,512,256]{2,1,0:T(8,128)S(1)} %get-tuple-element.16.part_ref, ...), custom_call_target="tpu_custom_call", output_to_operand_aliasing={{0}: (3, {})} | custom-call | flops 134217728 | bytes 2097152 | tf_op jit(solution)/shard_map/kept_half/pallas_call | solution.py:279
  12.4 0.7 %collective-permute-done.2 = bf16[512,256]{1,0:T(8,128)(2,1)S(1)} collective-permute-done((bf16[512,256]{1,0:T(8,128)(2,1)S(1)}, bf16[512,256]{1,0:T(8,128)(2,1)S(1)}, u32[]{:S(2)}, u32[]{:S(2)}) %collective-permute-start.2) | collective-permute-done | bytes 262176 | tf_op jit(solution)/shard_map/ppermute | solution.py:296
  13.1 0.1 add_convert_fusion
  13.2 13.9 %all_to_all.5 = bf16[16,32,256]{2,1,0:T(8,128)(2,1)S(1)} all-to-all(bf16[16,32,256]{2,1,0:T(8,128)(2,1)S(1)} %bitcast.5), channel_id=1, replica_groups={{24,16,8,0,26,18,10,2,28,20,12,4,30,22,14,6},{25,17,9,1,31,23,15,7,29,2..., dimensions={0} | all-to-all | bytes 524288 | tf_op jit(solution)/shard_map/all_to_all | solution.py:300
  27.1 0.6 %broadcast_multiply_fusion = f32[32,256]{1,0:T(8,128)} fusion(f32[32,256]{1,0:T(8,128)S(1)} %convert_reduce_fusion), kind=kLoop, calls=%fused_computation.2 | loop fusion | flops 8192 | bytes 65536 | tf_op jit(solution)/shard_map/mul | solution.py:306
  (1 shorter events, 0.0 us)
Async XLA Ops:
  0.6 6.4 %copy-start = (bf16[1536,512]{1,0:T(8,128)(2,1)S(1)}, bf16[1536,512]{1,0:T(8,128)(2,1)}, u32[]{:S(2)}) copy-start(bf16[1536,512]{1,0:T(8,128)(2,1)} %basis_ref.5) | copy-start | bytes 4718596
  0.6 6.4 %copy-start.2 = (f32[1536]{0:T(1024)S(1)}, f32[1536]{0:T(1024)}, u32[]{:S(2)}) copy-start(f32[1536]{0:T(1024)} %param.9) | copy-start | bytes 18436
  0.7 6.4 %copy-start.4 = (s32[24]{0:T(128)S(1)}, s32[24]{0:T(128)}, u32[]{:S(2)}) copy-start(s32[24]{0:T(128)} %live_ref.1) | copy-start | bytes 292
  0.7 6.4 %copy-start.3 = (s32[24,8]{0,1:T(8,128)S(1)}, s32[24,8]{0,1:T(8,128)}, u32[]{:S(2)}) copy-start(s32[24,8]{0,1:T(8,128)} %param.7) | copy-start | bytes 2308
  0.7 6.4 %copy-start.1 = (bf16[24,8,64,64]{3,2,1,0:T(8,128)(2,1)S(1)}, bf16[24,8,64,64]{3,2,1,0:T(8,128)(2,1)}, u32[]{:S(2)}) copy-start(bf16[24,8,64,64]{3,2,1,0:T(8,128)(2,1)} %jac_ref.1) | copy-start | bytes 4718596
  1.8 9.0 %collective-permute-start = (bf16[128,512]{1,0:T(8,128)(2,1)S(1)}, bf16[128,512]{1,0:T(8,128)(2,1)S(1)}, u32[]{:S(2)}, u32[]{:S(2)}) collective-permute-start(bf16[128,512]{1,0:T(8,128)(2,1)S(1)} %get-tuple-element.12), channel_id=1, source_target_pairs={{1,2},{3,4},{5,6},{7,8},{9,10},{11,12},{13,14},{15,16},{17,18},{19... | collective-permute-start | bytes 393224 | tf_op jit(solution)/shard_map/ppermute | solution.py:226
  2.6 8.2 %collective-permute-start.1 = (bf16[128,512]{1,0:T(8,128)(2,1)S(1)}, bf16[128,512]{1,0:T(8,128)(2,1)S(1)}, u32[]{:S(2)}, u32[]{:S(2)}) collective-permute-start(bf16[128,512]{1,0:T(8,128)(2,1)S(1)} %get-tuple-element.13), channel_id=1, source_target_pairs={{0,1},{2,3},{4,5},{6,7},{8,9},{10,11},{12,13},{14,15},{16,17},{18,... | collective-permute-start | bytes 393224 | tf_op jit(solution)/shard_map/ppermute | solution.py:228
  11.5 1.6 %collective-permute-start.2 = (bf16[512,256]{1,0:T(8,128)(2,1)S(1)}, bf16[512,256]{1,0:T(8,128)(2,1)S(1)}, u32[]{:S(2)}, u32[]{:S(2)}) collective-permute-start(bf16[512,256]{1,0:T(8,128)(2,1)S(1)} %get-tuple-element.21), channel_id=1, source_target_pairs={{0,1},{1,0},{2,3},{3,2},{4,5},{5,4},{6,7},{7,6},{8,9},{9,8},{10,11... | collective-permute-start | bytes 786440 | tf_op jit(solution)/shard_map/ppermute | solution.py:296

commit v18 on v17

--- a/solution.py
+++ b/solution.py
@@ -58,17 +58,22 @@
     return both[:half] + both[half:]
 
 
-def slice_kernel(basis_hbm, far_ref, near_ref, sems):
+def far_kernel(basis_hbm, far_ref, sem):
     tile = far_ref.shape[0]
     last = basis_hbm.shape[0] - tile
     odd = lax.rem(lax.axis_index(AXES), 2)
-    copies = []
-    for i, (at, target) in enumerate(((odd, far_ref), (1 - odd, near_ref))):
-        where = pl.ds(pl.multiple_of(at * last, tile), tile)
-        copies.append(pltpu.make_async_copy(basis_hbm.at[where], target, sems.at[i]))
-        copies[i].start()
-    for copy in copies:
-        copy.wait()
+    where = pl.ds(pl.multiple_of(odd * last, tile), tile)
+    copy = pltpu.make_async_copy(basis_hbm.at[where], far_ref, sem)
+    copy.start()
+    copy.wait()
+
+
+def near_kernel(basis_ref, near_ref):
+    tile = near_ref.shape[0]
+    last = basis_ref.shape[0] - tile
+    odd = lax.rem(lax.axis_index(AXES), 2)
+    where = pl.ds(pl.multiple_of((1 - odd) * last, tile), tile)
+    near_ref[...] = basis_ref[where, :]
 
 
 def inner_kernel(
@@ -210,18 +215,26 @@
     count = down * across
     f32, bf16 = jnp.float32, jnp.bfloat16
     edge_shape = jax.ShapeDtypeStruct((tile, width), bf16)
-    far_send, near_send = pl.pallas_call(
-        slice_kernel,
-        out_shape=(edge_shape, edge_shape),
+    far_send = pl.pallas_call(
+        far_kernel,
+        out_shape=edge_shape,
         in_specs=[whole(pltpu.HBM)],
-        out_specs=(whole(), whole()),
-        scratch_shapes=[pltpu.SemaphoreType.DMA((2,))],
+        out_specs=whole(),
+        scratch_shapes=[pltpu.SemaphoreType.DMA],
         compiler_params=pltpu.CompilerParams(vmem_limit_bytes=4 * 2**20),
         cost_estimate=pl.CostEstimate(
             flops=2 * nrows * width * width * slots, bytes_accessed=0, transcendentals=0
         ),
-        name="halo_rows",
+        name="far_rows",
     )(pltpu.with_memory_space_constraint(basis, pltpu.HBM))
+    near_send = pl.pallas_call(
+        near_kernel,
+        out_shape=edge_shape,
+        in_specs=[whole()],
+        out_specs=whole(),
+        compiler_params=pltpu.CompilerParams(vmem_limit_bytes=4 * 2**20),
+        name="near_rows",
+    )(basis)
     swaps = [(i, i + 1) for i in range(1, count - 1, 2)]
     far = lax.ppermute(far_send, AXES, swaps + [(j, i) for i, j in swaps])
     swaps = [(i, i + 1) for i in range(0, count, 2)]

time: 27.9 us -> 27.8 us (level)
    pallas_call x1 -> x2, Pallas kernels: 1.15 us -> 1.11 us  [the longest x1 1.08 us: local(): pl.pallas_call(far_kernel, out_shape=edge_shape, in_specs=[whole(pltpu.HB...]
where the time goes in v18:
time: 27.8 us; the launch traced here: 27.6 us
  blocking collectives  13.8 us (50%)
  Pallas kernels  6.31 us (23%)
  starting transfers between devices  5.25 us (19%)
  waiting for transfers between devices  0.75 us (3%)
  between operations  0.75 us (3%)
  other arithmetic  0.72 us (3%)
    all_to_all x1, blocking collectives, local(): lax.all_to_all(total, AXES, 0, 0, axis_index_groups=groups, tiled=True)  13.8 us
    ppermute x1, starting transfers between devices, local(): near = lax.ppermute(near_send, AXES, swaps + [(j, i) for i, j in swaps])  4.36 us
    pallas_call x1, Pallas kernels, local(): pl.pallas_call(inner_kernel, out_shape=(jax.ShapeDtypeStruct((nrows, widt...  3.81 us
    pallas_call x1, Pallas kernels, local(): pl.pallas_call(far_kernel, out_shape=edge_shape, in_specs=[whole(pltpu.HB...  1.08 us
    ppermute x1, starting transfers between devices, local(): far = lax.ppermute(far_send, AXES, swaps + [(j, i) for i, j in swaps])  0.8 us
    pallas_call x1, Pallas kernels, local(): pl.pallas_call(functools.partial(keep_kernel, orders), out_shape=(jax.Sha...  0.76 us
    ppermute x1, waiting for transfers between devices, local(): got = lax.ppermute(send, 'col', [(0, 1), (1, 0)])  0.74 us
    pallas_call x1, Pallas kernels, local(): pl.pallas_call(functools.partial(edge_kernel, orders), out_shape=(jax.Sha...  0.63 us
  transfers between devices with their start and end apart: 3, of which 1 were waited for; matrix products, arithmetic and copies ran while one was open for 0% of the time, Pallas kernels for 17%

profile of v18, /device:TPU:0, one launch (start us, length us, event | category | flops | bytes accessed | tf_op | source)
XLA Modules:
  0.0 27.6 jit_solution(11014380002147922043)
XLA Ops:
  0.6 0.0 copy-start
  0.6 0.0 copy-start.1
  0.6 1.1 %far_rows.1 = bf16[128,512]{1,0:T(8,128)(2,1)S(1)} custom-call(bf16[1536,512]{1,0:T(8,128)(2,1)} %basis_ref.7), custom_call_target="tpu_custom_call" | custom-call | flops 6442450944 | tf_op jit(solution)/shard_map/far_rows/pallas_call | solution.py:218
  1.7 0.0 copy-start.2
  1.8 0.0 copy-start.3
  1.8 0.0 copy-start.4
  1.8 0.8 %collective-permute-start = (bf16[128,512]{1,0:T(8,128)(2,1)S(1)}, bf16[128,512]{1,0:T(8,128)(2,1)S(1)}, u32[]{:S(2)}, u32[]{:S(2)}) collective-permute-start(bf16[128,512]{1,0:T(8,128)(2,1)S(1)} %far_rows.1), channel_id=1, source_target_pairs={{1,2},{3,4},{5,6},{7,8},{9,10},{11,12},{13,14},{15,16},{17,18},{19... | collective-permute-start | bytes 393224 | tf_op jit(solution)/shard_map/ppermute | solution.py:239
  2.6 0.0 copy-done
  2.6 4.4 %collective-permute-start.1 = (bf16[128,512]{1,0:T(8,128)(2,1)S(1)}, bf16[128,512]{1,0:T(8,128)(2,1)S(1)}, u32[]{:S(2)}, u32[]{:S(2)}) collective-permute-start(bf16[128,512]{1,0:T(8,128)(2,1)S(1)} %near_rows.1), channel_id=1, source_target_pairs={{0,1},{2,3},{4,5},{6,7},{8,9},{10,11},{12,13},{14,15},{16,17},{18,... | collective-permute-start | bytes 393224 | tf_op jit(solution)/shard_map/ppermute | solution.py:241
  7.0 0.0 copy-done.1
  7.0 0.0 copy-done.2
  7.0 0.0 copy-done.3
  7.0 0.0 copy-done.4
  7.0 3.8 %inner.1 = (bf16[1536,512]{1,0:T(8,128)(2,1)}, f32[2,128,512]{2,1,0:T(8,128)S(1)}, bf16[2,256,128]{2,1,0:T(8,128)(2,1)S(1)}, f32[2,512,256]{2,1,0:T(8,128)S(1)}) custom-call(s32[8,24]{1,0:T(8,128)S(1)} %bitcast.4, s32[24]{0:T(128)S(1)} %copy-done.4, bf16[24,8,64,64]{3,2,1,0:T(8,128)(2,1)S(1)} %copy-done.1, bf16[1536,512]{1,0:T(8,128)(2,1)S(1)} %copy-done, ...), custom_call_target="tpu_custom_call" | custom-call | flops 2013265920 | bytes 8388608 | tf_op jit(solution)/shard_map/inner/pallas_call | solution.py:252
  10.8 0.0 collective-permute-done.far_ref
  10.8 0.0 collective-permute-done.1.near_ref
  10.8 0.6 %edges.1 = (bf16[2,256,256]{2,1,0:T(8,128)(2,1)S(1)}, bf16[512,256]{1,0:T(8,128)(2,1)S(1)}) custom-call(bf16[128,512]{1,0:T(8,128)(2,1)S(1)} %collective-permute-done.far_ref, bf16[128,512]{1,0:T(8,128)(2,1)S(1)} %collective-permute-done.1.near_ref, f32[2,128,512]{2,1,0:T(8,128)S(1)} %get-tuple-element.10.edge_ref, ...), custom_call_target="tpu_custom_call" | custom-call | tf_op jit(solution)/shard_map/edges/pallas_call | solution.py:281
  11.5 0.1 collective-permute-start.2
  11.6 0.8 %kept_half.1 = (bf16[1536,512]{1,0:T(8,128)(2,1)}, f32[512,256]{1,0:T(8,128)S(1)}) custom-call(bf16[1536,512]{1,0:T(8,128)(2,1)S(1)} %copy-done, bf16[2,256,256]{2,1,0:T(8,128)(2,1)S(1)} %get-tuple-element.13.rows_ref, f32[2,512,256]{2,1,0:T(8,128)S(1)} %get-tuple-element.12.part_ref, ...), custom_call_target="tpu_custom_call", output_to_operand_aliasing={{0}: (3, {})} | custom-call | flops 134217728 | bytes 2097152 | tf_op jit(solution)/shard_map/kept_half/pallas_call | solution.py:292
  12.3 0.7 %collective-permute-done.2 = bf16[512,256]{1,0:T(8,128)(2,1)S(1)} collective-permute-done((bf16[512,256]{1,0:T(8,128)(2,1)S(1)}, bf16[512,256]{1,0:T(8,128)(2,1)S(1)}, u32[]{:S(2)}, u32[]{:S(2)}) %collective-permute-start.2) | collective-permute-done | bytes 262176 | tf_op jit(solution)/shard_map/ppermute | solution.py:309
  13.1 0.1 add_convert_fusion
  13.1 13.8 %all_to_all.5 = bf16[16,32,256]{2,1,0:T(8,128)(2,1)S(1)} all-to-all(bf16[16,32,256]{2,1,0:T(8,128)(2,1)S(1)} %bitcast.5), channel_id=1, replica_groups={{24,16,8,0,26,18,10,2,28,20,12,4,30,22,14,6},{25,17,9,1,31,23,15,7,29,2..., dimensions={0} | all-to-all | bytes 524288 | tf_op jit(solution)/shard_map/all_to_all | solution.py:313
  27.0 0.6 %broadcast_multiply_fusion = f32[32,256]{1,0:T(8,128)} fusion(f32[32,256]{1,0:T(8,128)S(1)} %convert_reduce_fusion), kind=kLoop, calls=%fused_computation.2 | loop fusion | flops 8192 | bytes 65536 | tf_op jit(solution)/shard_map/mul | solution.py:319
  (2 shorter events, 0.1 us)
Async XLA Ops:
  0.6 2.0 %copy-start = (bf16[1536,512]{1,0:T(8,128)(2,1)S(1)}, bf16[1536,512]{1,0:T(8,128)(2,1)}, u32[]{:S(2)}) copy-start(bf16[1536,512]{1,0:T(8,128)(2,1)} %basis_ref.7) | copy-start | bytes 4718596
  0.6 6.4 %copy-start.1 = (bf16[24,8,64,64]{3,2,1,0:T(8,128)(2,1)S(1)}, bf16[24,8,64,64]{3,2,1,0:T(8,128)(2,1)}, u32[]{:S(2)}) copy-start(bf16[24,8,64,64]{3,2,1,0:T(8,128)(2,1)} %jac_ref.1) | copy-start | bytes 4718596
  1.7 5.3 %copy-start.2 = (f32[1536]{0:T(1024)S(1)}, f32[1536]{0:T(1024)}, u32[]{:S(2)}) copy-start(f32[1536]{0:T(1024)} %param.9) | copy-start | bytes 18436
  1.8 5.2 %copy-start.3 = (s32[24,8]{0,1:T(8,128)S(1)}, s32[24,8]{0,1:T(8,128)}, u32[]{:S(2)}) copy-start(s32[24,8]{0,1:T(8,128)} %param.7) | copy-start | bytes 2308
  1.8 5.2 %copy-start.4 = (s32[24]{0:T(128)S(1)}, s32[24]{0:T(128)}, u32[]{:S(2)}) copy-start(s32[24]{0:T(128)} %live_ref.1) | copy-start | bytes 292
  1.8 9.0 %collective-permute-start = (bf16[128,512]{1,0:T(8,128)(2,1)S(1)}, bf16[128,512]{1,0:T(8,128)(2,1)S(1)}, u32[]{:S(2)}, u32[]{:S(2)}) collective-permute-start(bf16[128,512]{1,0:T(8,128)(2,1)S(1)} %far_rows.1), channel_id=1, source_target_pairs={{1,2},{3,4},{5,6},{7,8},{9,10},{11,12},{13,14},{15,16},{17,18},{19... | collective-permute-start | bytes 393224 | tf_op jit(solution)/shard_map/ppermute | solution.py:239
  2.6 8.2 %collective-permute-start.1 = (bf16[128,512]{1,0:T(8,128)(2,1)S(1)}, bf16[128,512]{1,0:T(8,128)(2,1)S(1)}, u32[]{:S(2)}, u32[]{:S(2)}) collective-permute-start(bf16[128,512]{1,0:T(8,128)(2,1)S(1)} %near_rows.1), channel_id=1, source_target_pairs={{0,1},{2,3},{4,5},{6,7},{8,9},{10,11},{12,13},{14,15},{16,17},{18,... | collective-permute-start | bytes 393224 | tf_op jit(solution)/shard_map/ppermute | solution.py:241
  11.5 1.6 %collective-permute-start.2 = (bf16[512,256]{1,0:T(8,128)(2,1)S(1)}, bf16[512,256]{1,0:T(8,128)(2,1)S(1)}, u32[]{:S(2)}, u32[]{:S(2)}) collective-permute-start(bf16[512,256]{1,0:T(8,128)(2,1)S(1)} %get-tuple-element.17), channel_id=1, source_target_pairs={{0,1},{1,0},{2,3},{3,2},{4,5},{5,4},{6,7},{7,6},{8,9},{9,8},{10,11... | collective-permute-start | bytes 786440 | tf_op jit(solution)/shard_map/ppermute | solution.py:309

commit v19 on v18

--- a/solution.py
+++ b/solution.py
@@ -66,6 +66,10 @@
     copy = pltpu.make_async_copy(basis_hbm.at[where], far_ref, sem)
     copy.start()
     copy.wait()
+
+
+def hand_on_kernel(rows_ref, out_ref):
+    out_ref[...] = rows_ref[...]
 
 
 def near_kernel(basis_ref, near_ref):
@@ -215,18 +219,27 @@
     count = down * across
     f32, bf16 = jnp.float32, jnp.bfloat16
     edge_shape = jax.ShapeDtypeStruct((tile, width), bf16)
-    far_send = pl.pallas_call(
+    far_rows = pl.pallas_call(
         far_kernel,
         out_shape=edge_shape,
         in_specs=[whole(pltpu.HBM)],
         out_specs=whole(),
         scratch_shapes=[pltpu.SemaphoreType.DMA],
         compiler_params=pltpu.CompilerParams(vmem_limit_bytes=4 * 2**20),
+        cost_estimate=pl.CostEstimate(flops=0, bytes_accessed=0, transcendentals=0),
+        name="far_rows",
+    )(pltpu.with_memory_space_constraint(basis, pltpu.HBM))
+    far_send = pl.pallas_call(
+        hand_on_kernel,
+        out_shape=edge_shape,
+        in_specs=[whole()],
+        out_specs=whole(),
+        compiler_params=pltpu.CompilerParams(vmem_limit_bytes=4 * 2**20),
         cost_estimate=pl.CostEstimate(
             flops=2 * nrows * width * width * slots, bytes_accessed=0, transcendentals=0
         ),
-        name="far_rows",
-    )(pltpu.with_memory_space_constraint(basis, pltpu.HBM))
+        name="hand_on",
+    )(far_rows)
     near_send = pl.pallas_call(
         near_kernel,
         out_shape=edge_shape,

time: 27.8 us -> 27.8 us (level)
  local copies, waits for them, and re-layouts: 0.03 us -> 0.55 us
  starting transfers between devices: 5.25 us -> 4.89 us
    unnamed x10, local copies, waits for them, and re-layouts: 0.03 us -> 0.55 us
    ppermute x1, starting transfers between devices: 4.36 us -> 4 us  [local(): near = lax.ppermute(near_send, AXES, swaps + [(j, i) for i, j in swaps])]
where the time goes in v19:
time: 27.8 us; the launch traced here: 27.6 us
  blocking collectives  13.8 us (50%)
  Pallas kernels  6.15 us (22%)
  starting transfers between devices  4.89 us (18%)
  waiting for transfers between devices  0.75 us (3%)
  between operations  0.75 us (3%)
  other arithmetic  0.72 us (3%)
  local copies, waits for them, and re-layouts  0.55 us (2%)
    all_to_all x1, blocking collectives, local(): lax.all_to_all(total, AXES, 0, 0, axis_index_groups=groups, tiled=True)  13.8 us
    ppermute x1, starting transfers between devices, local(): near = lax.ppermute(near_send, AXES, swaps + [(j, i) for i, j in swaps])  4 us
    pallas_call x1, Pallas kernels, local(): pl.pallas_call(inner_kernel, out_shape=(jax.ShapeDtypeStruct((nrows, widt...  3.81 us
    pallas_call x1, Pallas kernels, local(): pl.pallas_call(far_kernel, out_shape=edge_shape, in_specs=[whole(pltpu.HB...  0.93 us
    ppermute x1, starting transfers between devices, local(): far = lax.ppermute(far_send, AXES, swaps + [(j, i) for i, j in swaps])  0.8 us
    pallas_call x1, Pallas kernels, local(): pl.pallas_call(functools.partial(keep_kernel, orders), out_shape=(jax.Sha...  0.76 us
    ppermute x1, waiting for transfers between devices, local(): got = lax.ppermute(send, 'col', [(0, 1), (1, 0)])  0.74 us
    pallas_call x1, Pallas kernels, local(): pl.pallas_call(functools.partial(edge_kernel, orders), out_shape=(jax.Sha...  0.63 us
  transfers between devices with their start and end apart: 3, of which 1 were waited for; matrix products, arithmetic and copies ran while one was open for 0% of the time, Pallas kernels for 17%

profile of v19, /device:TPU:0, one launch (start us, length us, event | category | flops | bytes accessed | tf_op | source)
XLA Modules:
  0.0 27.6 jit_solution(1313877319194914697)
XLA Ops:
  0.6 0.9 %far_rows.1.rows_ref = bf16[128,512]{1,0:T(8,128)(2,1)S(1)} custom-call(bf16[1536,512]{1,0:T(8,128)(2,1)} %basis_ref.7), custom_call_target="tpu_custom_call" | custom-call | tf_op jit(solution)/shard_map/far_rows/pallas_call | solution.py:222
  1.6 0.0 copy-start
  1.6 0.0 copy-start.1
  1.6 0.0 copy-start.2
  1.6 0.0 copy-start.3
  1.6 0.0 copy-start.4
  1.6 0.8 %collective-permute-start = (bf16[128,512]{1,0:T(8,128)(2,1)S(1)}, bf16[128,512]{1,0:T(8,128)(2,1)S(1)}, u32[]{:S(2)}, u32[]{:S(2)}) collective-permute-start(bf16[128,512]{1,0:T(8,128)(2,1)S(1)} %hand_on.1), channel_id=1, source_target_pairs={{1,2},{3,4},{5,6},{7,8},{9,10},{11,12},{13,14},{15,16},{17,18},{19... | collective-permute-start | bytes 393224 | tf_op jit(solution)/shard_map/ppermute | solution.py:252
  2.5 0.5 %copy-done = bf16[1536,512]{1,0:T(8,128)(2,1)S(1)} copy-done((bf16[1536,512]{1,0:T(8,128)(2,1)S(1)}, bf16[1536,512]{1,0:T(8,128)(2,1)}, u32[]{:S(2)}) %copy-start) | copy-done | bytes 1572888
  3.0 4.0 %collective-permute-start.1 = (bf16[128,512]{1,0:T(8,128)(2,1)S(1)}, bf16[128,512]{1,0:T(8,128)(2,1)S(1)}, u32[]{:S(2)}, u32[]{:S(2)}) collective-permute-start(bf16[128,512]{1,0:T(8,128)(2,1)S(1)} %near_rows.1), channel_id=1, source_target_pairs={{0,1},{2,3},{4,5},{6,7},{8,9},{10,11},{12,13},{14,15},{16,17},{18,... | collective-permute-start | bytes 393224 | tf_op jit(solution)/shard_map/ppermute | solution.py:254
  7.0 0.0 copy-done.1
  7.0 0.0 copy-done.2
  7.0 0.0 copy-done.3
  7.0 0.0 copy-done.4
  7.0 3.8 %inner.1 = (bf16[1536,512]{1,0:T(8,128)(2,1)}, f32[2,128,512]{2,1,0:T(8,128)S(1)}, bf16[2,256,128]{2,1,0:T(8,128)(2,1)S(1)}, f32[2,512,256]{2,1,0:T(8,128)S(1)}) custom-call(s32[8,24]{1,0:T(8,128)S(1)} %bitcast.4, s32[24]{0:T(128)S(1)} %copy-done.4, bf16[24,8,64,64]{3,2,1,0:T(8,128)(2,1)S(1)} %copy-done.1, bf16[1536,512]{1,0:T(8,128)(2,1)S(1)} %copy-done, ...), custom_call_target="tpu_custom_call" | custom-call | flops 2013265920 | bytes 8388608 | tf_op jit(solution)/shard_map/inner/pallas_call | solution.py:265
  10.8 0.0 collective-permute-done.far_ref
  10.8 0.0 collective-permute-done.1.near_ref
  10.8 0.6 %edges.1 = (bf16[2,256,256]{2,1,0:T(8,128)(2,1)S(1)}, bf16[512,256]{1,0:T(8,128)(2,1)S(1)}) custom-call(bf16[128,512]{1,0:T(8,128)(2,1)S(1)} %collective-permute-done.far_ref, bf16[128,512]{1,0:T(8,128)(2,1)S(1)} %collective-permute-done.1.near_ref, f32[2,128,512]{2,1,0:T(8,128)S(1)} %get-tuple-element.10.edge_ref, ...), custom_call_target="tpu_custom_call" | custom-call | tf_op jit(solution)/shard_map/edges/pallas_call | solution.py:294
  11.5 0.1 collective-permute-start.2
  11.6 0.8 %kept_half.1 = (bf16[1536,512]{1,0:T(8,128)(2,1)}, f32[512,256]{1,0:T(8,128)S(1)}) custom-call(bf16[1536,512]{1,0:T(8,128)(2,1)S(1)} %copy-done, bf16[2,256,256]{2,1,0:T(8,128)(2,1)S(1)} %get-tuple-element.13.rows_ref, f32[2,512,256]{2,1,0:T(8,128)S(1)} %get-tuple-element.12.part_ref, ...), custom_call_target="tpu_custom_call", output_to_operand_aliasing={{0}: (3, {})} | custom-call | flops 134217728 | bytes 2097152 | tf_op jit(solution)/shard_map/kept_half/pallas_call | solution.py:305
  12.3 0.7 %collective-permute-done.2 = bf16[512,256]{1,0:T(8,128)(2,1)S(1)} collective-permute-done((bf16[512,256]{1,0:T(8,128)(2,1)S(1)}, bf16[512,256]{1,0:T(8,128)(2,1)S(1)}, u32[]{:S(2)}, u32[]{:S(2)}) %collective-permute-start.2) | collective-permute-done | bytes 262176 | tf_op jit(solution)/shard_map/ppermute | solution.py:322
  13.1 0.1 add_convert_fusion
  13.1 13.8 %all_to_all.5 = bf16[16,32,256]{2,1,0:T(8,128)(2,1)S(1)} all-to-all(bf16[16,32,256]{2,1,0:T(8,128)(2,1)S(1)} %bitcast.5), channel_id=1, replica_groups={{24,16,8,0,26,18,10,2,28,20,12,4,30,22,14,6},{25,17,9,1,31,23,15,7,29,2..., dimensions={0} | all-to-all | bytes 524288 | tf_op jit(solution)/shard_map/all_to_all | solution.py:326
  27.0 0.6 %broadcast_multiply_fusion = f32[32,256]{1,0:T(8,128)} fusion(f32[32,256]{1,0:T(8,128)S(1)} %convert_reduce_fusion), kind=kLoop, calls=%fused_computation.2 | loop fusion | flops 8192 | bytes 65536 | tf_op jit(solution)/shard_map/mul | solution.py:332
  (3 shorter events, 0.1 us)
Async XLA Ops:
  1.6 1.4 %copy-start = (bf16[1536,512]{1,0:T(8,128)(2,1)S(1)}, bf16[1536,512]{1,0:T(8,128)(2,1)}, u32[]{:S(2)}) copy-start(bf16[1536,512]{1,0:T(8,128)(2,1)} %basis_ref.7) | copy-start | bytes 4718596
  1.6 5.4 %copy-start.1 = (bf16[24,8,64,64]{3,2,1,0:T(8,128)(2,1)S(1)}, bf16[24,8,64,64]{3,2,1,0:T(8,128)(2,1)}, u32[]{:S(2)}) copy-start(bf16[24,8,64,64]{3,2,1,0:T(8,128)(2,1)} %jac_ref.1) | copy-start | bytes 4718596
  1.6 5.4 %copy-start.2 = (f32[1536]{0:T(1024)S(1)}, f32[1536]{0:T(1024)}, u32[]{:S(2)}) copy-start(f32[1536]{0:T(1024)} %param.9) | copy-start | bytes 18436
  1.6 5.4 %copy-start.3 = (s32[24,8]{0,1:T(8,128)S(1)}, s32[24,8]{0,1:T(8,128)}, u32[]{:S(2)}) copy-start(s32[24,8]{0,1:T(8,128)} %param.7) | copy-start | bytes 2308
  1.6 5.4 %copy-start.4 = (s32[24]{0:T(128)S(1)}, s32[24]{0:T(128)}, u32[]{:S(2)}) copy-start(s32[24]{0:T(128)} %live_ref.1) | copy-start | bytes 292
  1.6 9.2 %collective-permute-start = (bf16[128,512]{1,0:T(8,128)(2,1)S(1)}, bf16[128,512]{1,0:T(8,128)(2,1)S(1)}, u32[]{:S(2)}, u32[]{:S(2)}) collective-permute-start(bf16[128,512]{1,0:T(8,128)(2,1)S(1)} %hand_on.1), channel_id=1, source_target_pairs={{1,2},{3,4},{5,6},{7,8},{9,10},{11,12},{13,14},{15,16},{17,18},{19... | collective-permute-start | bytes 393224 | tf_op jit(solution)/shard_map/ppermute | solution.py:252
  3.0 7.8 %collective-permute-start.1 = (bf16[128,512]{1,0:T(8,128)(2,1)S(1)}, bf16[128,512]{1,0:T(8,128)(2,1)S(1)}, u32[]{:S(2)}, u32[]{:S(2)}) collective-permute-start(bf16[128,512]{1,0:T(8,128)(2,1)S(1)} %near_rows.1), channel_id=1, source_target_pairs={{0,1},{2,3},{4,5},{6,7},{8,9},{10,11},{12,13},{14,15},{16,17},{18,... | collective-permute-start | bytes 393224 | tf_op jit(solution)/shard_map/ppermute | solution.py:254
  11.5 1.6 %collective-permute-start.2 = (bf16[512,256]{1,0:T(8,128)(2,1)S(1)}, bf16[512,256]{1,0:T(8,128)(2,1)S(1)}, u32[]{:S(2)}, u32[]{:S(2)}) collective-permute-start(bf16[512,256]{1,0:T(8,128)(2,1)S(1)} %get-tuple-element.17), channel_id=1, source_target_pairs={{0,1},{1,0},{2,3},{3,2},{4,5},{5,4},{6,7},{7,6},{8,9},{9,8},{10,11... | collective-permute-start | bytes 786440 | tf_op jit(solution)/shard_map/ppermute | solution.py:322

commit v20 on v19

--- a/solution.py
+++ b/solution.py
@@ -260,7 +260,8 @@
     if halved:
         orders = [list(range(down))] * 2
         if (width // down) % 16 == 0:
-            lines = [[o * inner + i for o in reversed(range(outer))] for i in range(inner)]
+            around = [*range(0, inner, 2), *range(1, inner, 2)[::-1]]
+            lines = [[o * inner + i for o in reversed(range(outer))] for i in around]
             orders = [sum(lines, []), sum(lines[:1] + lines[:0:-1], [])]
     image, edge, arm, part = pl.pallas_call(
         inner_kernel,

time: 27.8 us -> 28 us (level)
  transfers between devices with their start and end apart: 3 -> 3, of which waited for: 1 -> 1; matrix products, arithmetic and copies ran while one was open for 0% -> 0% of each run, Pallas kernels for 17% -> 16%
where the time goes in v20:
time: 28 us; the launch traced here: 27.8 us
  blocking collectives  14 us (50%)
  Pallas kernels  6.15 us (22%)
  starting transfers between devices  4.89 us (17%)
  waiting for transfers between devices  0.75 us (3%)
  between operations  0.75 us (3%)
  other arithmetic  0.72 us (3%)
  local copies, waits for them, and re-layouts  0.55 us (2%)
    all_to_all x1, blocking collectives, local(): lax.all_to_all(total, AXES, 0, 0, axis_index_groups=groups, tiled=True)  14 us
    ppermute x1, starting transfers between devices, local(): near = lax.ppermute(near_send, AXES, swaps + [(j, i) for i, j in swaps])  4 us
    pallas_call x1, Pallas kernels, local(): pl.pallas_call(inner_kernel, out_shape=(jax.ShapeDtypeStruct((nrows, widt...  3.81 us
    pallas_call x1, Pallas kernels, local(): pl.pallas_call(far_kernel, out_shape=edge_shape, in_specs=[whole(pltpu.HB...  0.93 us
    ppermute x1, starting transfers between devices, local(): far = lax.ppermute(far_send, AXES, swaps + [(j, i) for i, j in swaps])  0.8 us
    pallas_call x1, Pallas kernels, local(): pl.pallas_call(functools.partial(keep_kernel, orders), out_shape=(jax.Sha...  0.76 us
    ppermute x1, waiting for transfers between devices, local(): got = lax.ppermute(send, 'col', [(0, 1), (1, 0)])  0.74 us
    pallas_call x1, Pallas kernels, local(): pl.pallas_call(functools.partial(edge_kernel, orders), out_shape=(jax.Sha...  0.63 us
  transfers between devices with their start and end apart: 3, of which 1 were waited for; matrix products, arithmetic and copies ran while one was open for 0% of the time, Pallas kernels for 16%

profile of v20, /device:TPU:0, one launch (start us, length us, event | category | flops | bytes accessed | tf_op | source)
XLA Modules:
  0.0 27.8 jit_solution(5135568422187555139)
XLA Ops:
  0.6 0.9 %far_rows.1.rows_ref = bf16[128,512]{1,0:T(8,128)(2,1)S(1)} custom-call(bf16[1536,512]{1,0:T(8,128)(2,1)} %basis_ref.7), custom_call_target="tpu_custom_call" | custom-call | tf_op jit(solution)/shard_map/far_rows/pallas_call | solution.py:222
  1.6 0.0 copy-start
  1.6 0.0 copy-start.1
  1.6 0.0 copy-start.2
  1.6 0.0 copy-start.3
  1.6 0.0 copy-start.4
  1.6 0.8 %collective-permute-start = (bf16[128,512]{1,0:T(8,128)(2,1)S(1)}, bf16[128,512]{1,0:T(8,128)(2,1)S(1)}, u32[]{:S(2)}, u32[]{:S(2)}) collective-permute-start(bf16[128,512]{1,0:T(8,128)(2,1)S(1)} %hand_on.1), channel_id=1, source_target_pairs={{1,2},{3,4},{5,6},{7,8},{9,10},{11,12},{13,14},{15,16},{17,18},{19... | collective-permute-start | bytes 393224 | tf_op jit(solution)/shard_map/ppermute | solution.py:252
  2.5 0.5 %copy-done = bf16[1536,512]{1,0:T(8,128)(2,1)S(1)} copy-done((bf16[1536,512]{1,0:T(8,128)(2,1)S(1)}, bf16[1536,512]{1,0:T(8,128)(2,1)}, u32[]{:S(2)}) %copy-start) | copy-done | bytes 1572888
  3.0 4.0 %collective-permute-start.1 = (bf16[128,512]{1,0:T(8,128)(2,1)S(1)}, bf16[128,512]{1,0:T(8,128)(2,1)S(1)}, u32[]{:S(2)}, u32[]{:S(2)}) collective-permute-start(bf16[128,512]{1,0:T(8,128)(2,1)S(1)} %near_rows.1), channel_id=1, source_target_pairs={{0,1},{2,3},{4,5},{6,7},{8,9},{10,11},{12,13},{14,15},{16,17},{18,... | collective-permute-start | bytes 393224 | tf_op jit(solution)/shard_map/ppermute | solution.py:254
  7.0 0.0 copy-done.1
  7.0 0.0 copy-done.2
  7.0 0.0 copy-done.3
  7.0 0.0 copy-done.4
  7.0 3.8 %inner.1 = (bf16[1536,512]{1,0:T(8,128)(2,1)}, f32[2,128,512]{2,1,0:T(8,128)S(1)}, bf16[2,256,128]{2,1,0:T(8,128)(2,1)S(1)}, f32[2,512,256]{2,1,0:T(8,128)S(1)}) custom-call(s32[8,24]{1,0:T(8,128)S(1)} %bitcast.4, s32[24]{0:T(128)S(1)} %copy-done.4, bf16[24,8,64,64]{3,2,1,0:T(8,128)(2,1)S(1)} %copy-done.1, bf16[1536,512]{1,0:T(8,128)(2,1)S(1)} %copy-done, ...), custom_call_target="tpu_custom_call" | custom-call | flops 2013265920 | bytes 8388608 | tf_op jit(solution)/shard_map/inner/pallas_call | solution.py:266
  10.8 0.0 collective-permute-done.far_ref
  10.8 0.0 collective-permute-done.1.near_ref
  10.8 0.6 %edges.1 = (bf16[2,256,256]{2,1,0:T(8,128)(2,1)S(1)}, bf16[512,256]{1,0:T(8,128)(2,1)S(1)}) custom-call(bf16[128,512]{1,0:T(8,128)(2,1)S(1)} %collective-permute-done.far_ref, bf16[128,512]{1,0:T(8,128)(2,1)S(1)} %collective-permute-done.1.near_ref, f32[2,128,512]{2,1,0:T(8,128)S(1)} %get-tuple-element.10.edge_ref, ...), custom_call_target="tpu_custom_call" | custom-call | tf_op jit(solution)/shard_map/edges/pallas_call | solution.py:295
  11.5 0.1 collective-permute-start.2
  11.6 0.8 %kept_half.1 = (bf16[1536,512]{1,0:T(8,128)(2,1)}, f32[512,256]{1,0:T(8,128)S(1)}) custom-call(bf16[1536,512]{1,0:T(8,128)(2,1)S(1)} %copy-done, bf16[2,256,256]{2,1,0:T(8,128)(2,1)S(1)} %get-tuple-element.13.rows_ref, f32[2,512,256]{2,1,0:T(8,128)S(1)} %get-tuple-element.12.part_ref, ...), custom_call_target="tpu_custom_call", output_to_operand_aliasing={{0}: (3, {})} | custom-call | flops 134217728 | bytes 2097152 | tf_op jit(solution)/shard_map/kept_half/pallas_call | solution.py:306
  12.3 0.7 %collective-permute-done.2 = bf16[512,256]{1,0:T(8,128)(2,1)S(1)} collective-permute-done((bf16[512,256]{1,0:T(8,128)(2,1)S(1)}, bf16[512,256]{1,0:T(8,128)(2,1)S(1)}, u32[]{:S(2)}, u32[]{:S(2)}) %collective-permute-start.2) | collective-permute-done | bytes 262176 | tf_op jit(solution)/shard_map/ppermute | solution.py:323
  13.1 0.1 add_convert_fusion
  13.1 14.0 %all_to_all.5 = bf16[16,32,256]{2,1,0:T(8,128)(2,1)S(1)} all-to-all(bf16[16,32,256]{2,1,0:T(8,128)(2,1)S(1)} %bitcast.5), channel_id=1, replica_groups={{24,16,8,0,28,20,12,4,30,22,14,6,26,18,10,2},{25,17,9,1,27,19,11,3,31,2..., dimensions={0} | all-to-all | bytes 524288 | tf_op jit(solution)/shard_map/all_to_all | solution.py:327
  27.2 0.6 %broadcast_multiply_fusion = f32[32,256]{1,0:T(8,128)} fusion(f32[32,256]{1,0:T(8,128)S(1)} %convert_reduce_fusion), kind=kLoop, calls=%fused_computation.2 | loop fusion | flops 8192 | bytes 65536 | tf_op jit(solution)/shard_map/mul | solution.py:333
  (3 shorter events, 0.1 us)
Async XLA Ops:
  1.6 1.4 %copy-start = (bf16[1536,512]{1,0:T(8,128)(2,1)S(1)}, bf16[1536,512]{1,0:T(8,128)(2,1)}, u32[]{:S(2)}) copy-start(bf16[1536,512]{1,0:T(8,128)(2,1)} %basis_ref.7) | copy-start | bytes 4718596
  1.6 5.4 %copy-start.1 = (bf16[24,8,64,64]{3,2,1,0:T(8,128)(2,1)S(1)}, bf16[24,8,64,64]{3,2,1,0:T(8,128)(2,1)}, u32[]{:S(2)}) copy-start(bf16[24,8,64,64]{3,2,1,0:T(8,128)(2,1)} %jac_ref.1) | copy-start | bytes 4718596
  1.6 5.4 %copy-start.2 = (f32[1536]{0:T(1024)S(1)}, f32[1536]{0:T(1024)}, u32[]{:S(2)}) copy-start(f32[1536]{0:T(1024)} %param.9) | copy-start | bytes 18436
  1.6 5.4 %copy-start.3 = (s32[24,8]{0,1:T(8,128)S(1)}, s32[24,8]{0,1:T(8,128)}, u32[]{:S(2)}) copy-start(s32[24,8]{0,1:T(8,128)} %param.7) | copy-start | bytes 2308
  1.6 5.4 %copy-start.4 = (s32[24]{0:T(128)S(1)}, s32[24]{0:T(128)}, u32[]{:S(2)}) copy-start(s32[24]{0:T(128)} %live_ref.1) | copy-start | bytes 292
  1.6 9.2 %collective-permute-start = (bf16[128,512]{1,0:T(8,128)(2,1)S(1)}, bf16[128,512]{1,0:T(8,128)(2,1)S(1)}, u32[]{:S(2)}, u32[]{:S(2)}) collective-permute-start(bf16[128,512]{1,0:T(8,128)(2,1)S(1)} %hand_on.1), channel_id=1, source_target_pairs={{1,2},{3,4},{5,6},{7,8},{9,10},{11,12},{13,14},{15,16},{17,18},{19... | collective-permute-start | bytes 393224 | tf_op jit(solution)/shard_map/ppermute | solution.py:252
  3.0 7.8 %collective-permute-start.1 = (bf16[128,512]{1,0:T(8,128)(2,1)S(1)}, bf16[128,512]{1,0:T(8,128)(2,1)S(1)}, u32[]{:S(2)}, u32[]{:S(2)}) collective-permute-start(bf16[128,512]{1,0:T(8,128)(2,1)S(1)} %near_rows.1), channel_id=1, source_target_pairs={{0,1},{2,3},{4,5},{6,7},{8,9},{10,11},{12,13},{14,15},{16,17},{18,... | collective-permute-start | bytes 393224 | tf_op jit(solution)/shard_map/ppermute | solution.py:254
  11.5 1.6 %collective-permute-start.2 = (bf16[512,256]{1,0:T(8,128)(2,1)S(1)}, bf16[512,256]{1,0:T(8,128)(2,1)S(1)}, u32[]{:S(2)}, u32[]{:S(2)}) collective-permute-start(bf16[512,256]{1,0:T(8,128)(2,1)S(1)} %get-tuple-element.17), channel_id=1, source_target_pairs={{0,1},{1,0},{2,3},{3,2},{4,5},{5,4},{6,7},{7,6},{8,9},{9,8},{10,11... | collective-permute-start | bytes 786440 | tf_op jit(solution)/shard_map/ppermute | solution.py:323

commit v21 on v19

--- a/solution.py
+++ b/solution.py
@@ -58,14 +58,20 @@
     return both[:half] + both[half:]
 
 
-def far_kernel(basis_hbm, far_ref, sem):
+def far_kernel(basis_hbm, far_ref, sems):
     tile = far_ref.shape[0]
     last = basis_hbm.shape[0] - tile
     odd = lax.rem(lax.axis_index(AXES), 2)
-    where = pl.ds(pl.multiple_of(odd * last, tile), tile)
-    copy = pltpu.make_async_copy(basis_hbm.at[where], far_ref, sem)
-    copy.start()
-    copy.wait()
+    count = sems.shape[0]
+    size = tile // count
+    copies = []
+    for i in range(count):
+        source = pl.ds(pl.multiple_of(odd * last + i * size, size), size)
+        target = far_ref.at[pl.ds(i * size, size)]
+        copies.append(pltpu.make_async_copy(basis_hbm.at[source], target, sems.at[i]))
+        copies[i].start()
+    for copy in copies:
+        copy.wait()
 
 
 def hand_on_kernel(rows_ref, out_ref):
@@ -224,7 +230,7 @@
         out_shape=edge_shape,
         in_specs=[whole(pltpu.HBM)],
         out_specs=whole(),
-        scratch_shapes=[pltpu.SemaphoreType.DMA],
+        scratch_shapes=[pltpu.SemaphoreType.DMA((4,))],
         compiler_params=pltpu.CompilerParams(vmem_limit_bytes=4 * 2**20),
         cost_estimate=pl.CostEstimate(flops=0, bytes_accessed=0, transcendentals=0),
         name="far_rows",

time: 27.8 us -> 27.8 us (level)
  no operation moved by 1% of the time
where the time goes in v21:
time: 27.8 us; the launch traced here: 27.6 us
  blocking collectives  13.8 us (50%)
  Pallas kernels  6.07 us (22%)
  starting transfers between devices  4.9 us (18%)
  between operations  0.75 us (3%)
  waiting for transfers between devices  0.74 us (3%)
  other arithmetic  0.72 us (3%)
  local copies, waits for them, and re-layouts  0.55 us (2%)
    all_to_all x1, blocking collectives, local(): lax.all_to_all(total, AXES, 0, 0, axis_index_groups=groups, tiled=True)  13.8 us
    ppermute x1, starting transfers between devices, local(): near = lax.ppermute(near_send, AXES, swaps + [(j, i) for i, j in swaps])  4 us
    pallas_call x1, Pallas kernels, local(): pl.pallas_call(inner_kernel, out_shape=(jax.ShapeDtypeStruct((nrows, widt...  3.8 us
    pallas_call x1, Pallas kernels, local(): pl.pallas_call(far_kernel, out_shape=edge_shape, in_specs=[whole(pltpu.HB...  0.86 us
    ppermute x1, starting transfers between devices, local(): far = lax.ppermute(far_send, AXES, swaps + [(j, i) for i, j in swaps])  0.8 us
    pallas_call x1, Pallas kernels, local(): pl.pallas_call(functools.partial(keep_kernel, orders), out_shape=(jax.Sha...  0.76 us
    ppermute x1, waiting for transfers between devices, local(): got = lax.ppermute(send, 'col', [(0, 1), (1, 0)])  0.73 us
    pallas_call x1, Pallas kernels, local(): pl.pallas_call(functools.partial(edge_kernel, orders), out_shape=(jax.Sha...  0.63 us
  transfers between devices with their start and end apart: 3, of which 1 were waited for; matrix products, arithmetic and copies ran while one was open for 0% of the time, Pallas kernels for 17%

profile of v21, /device:TPU:0, one launch (start us, length us, event | category | flops | bytes accessed | tf_op | source)
XLA Modules:
  0.0 27.6 jit_solution(7340637376546551218)
XLA Ops:
  0.6 0.9 %far_rows.1.rows_ref = bf16[128,512]{1,0:T(8,128)(2,1)S(1)} custom-call(bf16[1536,512]{1,0:T(8,128)(2,1)} %basis_ref.7), custom_call_target="tpu_custom_call" | custom-call | tf_op jit(solution)/shard_map/far_rows/pallas_call | solution.py:228
  1.5 0.0 copy-start
  1.5 0.0 copy-start.1
  1.5 0.0 copy-start.2
  1.6 0.0 copy-start.3
  1.6 0.0 copy-start.4
  1.6 0.8 %collective-permute-start = (bf16[128,512]{1,0:T(8,128)(2,1)S(1)}, bf16[128,512]{1,0:T(8,128)(2,1)S(1)}, u32[]{:S(2)}, u32[]{:S(2)}) collective-permute-start(bf16[128,512]{1,0:T(8,128)(2,1)S(1)} %hand_on.1), channel_id=1, source_target_pairs={{1,2},{3,4},{5,6},{7,8},{9,10},{11,12},{13,14},{15,16},{17,18},{19... | collective-permute-start | bytes 393224 | tf_op jit(solution)/shard_map/ppermute | solution.py:258
  2.4 0.5 %copy-done = bf16[1536,512]{1,0:T(8,128)(2,1)S(1)} copy-done((bf16[1536,512]{1,0:T(8,128)(2,1)S(1)}, bf16[1536,512]{1,0:T(8,128)(2,1)}, u32[]{:S(2)}) %copy-start) | copy-done | bytes 1572888
  2.9 4.0 %collective-permute-start.1 = (bf16[128,512]{1,0:T(8,128)(2,1)S(1)}, bf16[128,512]{1,0:T(8,128)(2,1)S(1)}, u32[]{:S(2)}, u32[]{:S(2)}) collective-permute-start(bf16[128,512]{1,0:T(8,128)(2,1)S(1)} %near_rows.1), channel_id=1, source_target_pairs={{0,1},{2,3},{4,5},{6,7},{8,9},{10,11},{12,13},{14,15},{16,17},{18,... | collective-permute-start | bytes 393224 | tf_op jit(solution)/shard_map/ppermute | solution.py:260
  6.9 0.0 copy-done.1
  6.9 0.0 copy-done.2
  6.9 0.0 copy-done.3
  6.9 0.0 copy-done.4
  6.9 3.8 %inner.1 = (bf16[1536,512]{1,0:T(8,128)(2,1)}, f32[2,128,512]{2,1,0:T(8,128)S(1)}, bf16[2,256,128]{2,1,0:T(8,128)(2,1)S(1)}, f32[2,512,256]{2,1,0:T(8,128)S(1)}) custom-call(s32[8,24]{1,0:T(8,128)S(1)} %bitcast.4, s32[24]{0:T(128)S(1)} %copy-done.4, bf16[24,8,64,64]{3,2,1,0:T(8,128)(2,1)S(1)} %copy-done.1, bf16[1536,512]{1,0:T(8,128)(2,1)S(1)} %copy-done, ...), custom_call_target="tpu_custom_call" | custom-call | flops 2013265920 | bytes 8388608 | tf_op jit(solution)/shard_map/inner/pallas_call | solution.py:271
  10.7 0.0 collective-permute-done.far_ref
  10.8 0.0 collective-permute-done.1.near_ref
  10.8 0.6 %edges.1 = (bf16[2,256,256]{2,1,0:T(8,128)(2,1)S(1)}, bf16[512,256]{1,0:T(8,128)(2,1)S(1)}) custom-call(bf16[128,512]{1,0:T(8,128)(2,1)S(1)} %collective-permute-done.far_ref, bf16[128,512]{1,0:T(8,128)(2,1)S(1)} %collective-permute-done.1.near_ref, f32[2,128,512]{2,1,0:T(8,128)S(1)} %get-tuple-element.10.edge_ref, ...), custom_call_target="tpu_custom_call" | custom-call | tf_op jit(solution)/shard_map/edges/pallas_call | solution.py:300
  11.4 0.1 collective-permute-start.2
  11.5 0.8 %kept_half.1 = (bf16[1536,512]{1,0:T(8,128)(2,1)}, f32[512,256]{1,0:T(8,128)S(1)}) custom-call(bf16[1536,512]{1,0:T(8,128)(2,1)S(1)} %copy-done, bf16[2,256,256]{2,1,0:T(8,128)(2,1)S(1)} %get-tuple-element.13.rows_ref, f32[2,512,256]{2,1,0:T(8,128)S(1)} %get-tuple-element.12.part_ref, ...), custom_call_target="tpu_custom_call", output_to_operand_aliasing={{0}: (3, {})} | custom-call | flops 134217728 | bytes 2097152 | tf_op jit(solution)/shard_map/kept_half/pallas_call | solution.py:311
  12.3 0.7 %collective-permute-done.2 = bf16[512,256]{1,0:T(8,128)(2,1)S(1)} collective-permute-done((bf16[512,256]{1,0:T(8,128)(2,1)S(1)}, bf16[512,256]{1,0:T(8,128)(2,1)S(1)}, u32[]{:S(2)}, u32[]{:S(2)}) %collective-permute-start.2) | collective-permute-done | bytes 262176 | tf_op jit(solution)/shard_map/ppermute | solution.py:328
  13.0 0.1 add_convert_fusion
  13.1 13.8 %all_to_all.5 = bf16[16,32,256]{2,1,0:T(8,128)(2,1)S(1)} all-to-all(bf16[16,32,256]{2,1,0:T(8,128)(2,1)S(1)} %bitcast.5), channel_id=1, replica_groups={{24,16,8,0,26,18,10,2,28,20,12,4,30,22,14,6},{25,17,9,1,31,23,15,7,29,2..., dimensions={0} | all-to-all | bytes 524288 | tf_op jit(solution)/shard_map/all_to_all | solution.py:332
  26.9 0.6 %broadcast_multiply_fusion = f32[32,256]{1,0:T(8,128)} fusion(f32[32,256]{1,0:T(8,128)S(1)} %convert_reduce_fusion), kind=kLoop, calls=%fused_computation.2 | loop fusion | flops 8192 | bytes 65536 | tf_op jit(solution)/shard_map/mul | solution.py:338
  (3 shorter events, 0.1 us)
Async XLA Ops:
  1.5 1.4 %copy-start = (bf16[1536,512]{1,0:T(8,128)(2,1)S(1)}, bf16[1536,512]{1,0:T(8,128)(2,1)}, u32[]{:S(2)}) copy-start(bf16[1536,512]{1,0:T(8,128)(2,1)} %basis_ref.7) | copy-start | bytes 4718596
  1.5 5.4 %copy-start.1 = (bf16[24,8,64,64]{3,2,1,0:T(8,128)(2,1)S(1)}, bf16[24,8,64,64]{3,2,1,0:T(8,128)(2,1)}, u32[]{:S(2)}) copy-start(bf16[24,8,64,64]{3,2,1,0:T(8,128)(2,1)} %jac_ref.1) | copy-start | bytes 4718596
  1.5 5.4 %copy-start.2 = (f32[1536]{0:T(1024)S(1)}, f32[1536]{0:T(1024)}, u32[]{:S(2)}) copy-start(f32[1536]{0:T(1024)} %param.9) | copy-start | bytes 18436
  1.6 5.4 %copy-start.3 = (s32[24,8]{0,1:T(8,128)S(1)}, s32[24,8]{0,1:T(8,128)}, u32[]{:S(2)}) copy-start(s32[24,8]{0,1:T(8,128)} %param.7) | copy-start | bytes 2308
  1.6 5.4 %copy-start.4 = (s32[24]{0:T(128)S(1)}, s32[24]{0:T(128)}, u32[]{:S(2)}) copy-start(s32[24]{0:T(128)} %live_ref.1) | copy-start | bytes 292
  1.6 9.2 %collective-permute-start = (bf16[128,512]{1,0:T(8,128)(2,1)S(1)}, bf16[128,512]{1,0:T(8,128)(2,1)S(1)}, u32[]{:S(2)}, u32[]{:S(2)}) collective-permute-start(bf16[128,512]{1,0:T(8,128)(2,1)S(1)} %hand_on.1), channel_id=1, source_target_pairs={{1,2},{3,4},{5,6},{7,8},{9,10},{11,12},{13,14},{15,16},{17,18},{19... | collective-permute-start | bytes 393224 | tf_op jit(solution)/shard_map/ppermute | solution.py:258
  2.9 7.8 %collective-permute-start.1 = (bf16[128,512]{1,0:T(8,128)(2,1)S(1)}, bf16[128,512]{1,0:T(8,128)(2,1)S(1)}, u32[]{:S(2)}, u32[]{:S(2)}) collective-permute-start(bf16[128,512]{1,0:T(8,128)(2,1)S(1)} %near_rows.1), channel_id=1, source_target_pairs={{0,1},{2,3},{4,5},{6,7},{8,9},{10,11},{12,13},{14,15},{16,17},{18,... | collective-permute-start | bytes 393224 | tf_op jit(solution)/shard_map/ppermute | solution.py:260
  11.4 1.6 %collective-permute-start.2 = (bf16[512,256]{1,0:T(8,128)(2,1)S(1)}, bf16[512,256]{1,0:T(8,128)(2,1)S(1)}, u32[]{:S(2)}, u32[]{:S(2)}) collective-permute-start(bf16[512,256]{1,0:T(8,128)(2,1)S(1)} %get-tuple-element.17), channel_id=1, source_target_pairs={{0,1},{1,0},{2,3},{3,2},{4,5},{5,4},{6,7},{7,6},{8,9},{9,8},{10,11... | collective-permute-start | bytes 786440 | tf_op jit(solution)/shard_map/ppermute | solution.py:328

commit v22 on v21

--- a/solution.py
+++ b/solution.py
@@ -147,14 +147,26 @@
         copy.wait()
 
 
-def end_tiles(basis_ref, tile):
-    nrows = basis_ref.shape[0]
-    return jnp.concatenate([basis_ref[:tile, :], basis_ref[nrows - tile :, :]], axis=0)
-
-
-def add_edges(part_ref, tiles, rows_ref, half):
+def side_of(odd, near):
+    return 1 - odd if near else odd
+
+
+def edge_tile(basis_ref, side, tile):
+    last = basis_ref.shape[0] - tile
+    return basis_ref[pl.ds(pl.multiple_of(side * last, tile), tile), :]
+
+
+def edge_image(halo_ref, edge_ref, arm_ref, side, rows_ref):
+    rows = edge_ref[side] + apply_strip(arm_ref[side], halo_ref[...])
+    rows = rows.astype(jnp.bfloat16)
+    parts, _, wide = rows_ref.shape
+    for i in range(parts):
+        rows_ref[i] = rows[:, i * wide : (i + 1) * wide]
+
+
+def add_edge(part_ref, tile_rows, rows_ref, half):
     update = lax.dot_general(
-        tiles, rows_ref[half], ROWS_DOT, preferred_element_type=jnp.float32
+        tile_rows, rows_ref[half], ROWS_DOT, preferred_element_type=jnp.float32
     )
     return part_ref[half] + update
 
@@ -173,41 +185,43 @@
     return 1 - lax.axis_index("col") if parts == 2 else 0
 
 
-def edge_kernel(
-    orders, far_ref, near_ref, edge_ref, arm_ref, basis_ref, part_ref, rows_ref, send_ref,
+def near_edge_kernel(near_ref, edge_ref, arm_ref, basis_ref, part_ref, rows_ref, sum_ref):
+    tile = near_ref.shape[0]
+    side = side_of(lax.rem(lax.axis_index(AXES), 2), True)
+    edge_image(near_ref, edge_ref, arm_ref, side, rows_ref)
+    tile_rows = edge_tile(basis_ref, side, tile)
+    for half in range(rows_ref.shape[0]):
+        sum_ref[half] = add_edge(part_ref, tile_rows, rows_ref, half)
+
+
+def far_edge_kernel(
+    orders, far_ref, edge_ref, arm_ref, basis_ref, part_ref, rows_ref, send_ref,
 ):
     tile = far_ref.shape[0]
-    parts, _, wide = rows_ref.shape
-    odd = lax.rem(lax.axis_index(AXES), 2) == 1
-    near, far = near_ref[...], far_ref[...]
-    halos = (jnp.where(odd, near, far), jnp.where(odd, far, near))
-    for side in range(2):
-        rows = edge_ref[side] + apply_strip(arm_ref[side], halos[side])
-        rows = rows.astype(jnp.bfloat16)
-        for i in range(parts):
-            rows_ref[i, side * tile : (side + 1) * tile, :] = rows[:, i * wide : (i + 1) * wide]
-    leaving = leaving_half(parts)
-    send = add_edges(part_ref, end_tiles(basis_ref, tile), rows_ref, leaving)
+    side = side_of(lax.rem(lax.axis_index(AXES), 2), False)
+    edge_image(far_ref, edge_ref, arm_ref, side, rows_ref)
+    leaving = leaving_half(rows_ref.shape[0])
+    send = add_edge(part_ref, edge_tile(basis_ref, side, tile), rows_ref, leaving)
     put_blocks(send_ref, send, orders, leaving)
 
 
-def keep_kernel(orders, basis_ref, rows_ref, part_ref, _, image_ref, *rest):
+def keep_kernel(orders, basis_ref, near_ref, far_ref, part_ref, _, image_ref, *rest):
     *keep_refs, sems = rest
     nrows = image_ref.shape[0]
-    parts, rows, wide = rows_ref.shape
-    tile = rows // 2
+    parts, tile, wide = far_ref.shape
+    odd = lax.rem(lax.axis_index(AXES), 2)
     copies = []
-    for side, start in enumerate((0, nrows - tile)):
+    for at, rows_ref in enumerate((far_ref, near_ref)):
+        start = pl.multiple_of(side_of(odd, at == 1) * (nrows - tile), tile)
         for i in range(parts):
-            source = rows_ref.at[i, pl.ds(side * tile, tile)]
             target = image_ref.at[pl.ds(start, tile), pl.ds(i * wide, wide)]
-            copy = pltpu.make_async_copy(source, target, sems.at[side * parts + i])
+            copy = pltpu.make_async_copy(rows_ref.at[i], target, sems.at[at * parts + i])
             copy.start()
             copies.append(copy)
     for keep_ref in keep_refs:
         own = 1 - leaving_half(parts)
-        keep = add_edges(part_ref, end_tiles(basis_ref, tile), rows_ref, own)
-        put_blocks(keep_ref, keep, orders, own)
+        tile_rows = edge_tile(basis_ref, side_of(odd, False), tile)
+        put_blocks(keep_ref, add_edge(part_ref, tile_rows, far_ref, own), orders, own)
     for copy in copies:
         copy.wait()
 
@@ -297,33 +311,43 @@
         accumulation.reshape(nblk // 2, tile),
     )
 
-    rows, send = pl.pallas_call(
-        functools.partial(edge_kernel, orders),
-        out_shape=(
-            jax.ShapeDtypeStruct((parts, 2 * tile, wide), bf16),
-            jax.ShapeDtypeStruct((width, wide), bf16),
-        ),
-        in_specs=[whole()] * 6,
+    limit = pltpu.CompilerParams(vmem_limit_bytes=32 * 2**20)
+    rows_shape = jax.ShapeDtypeStruct((parts, tile, wide), bf16)
+    near_rows, part = pl.pallas_call(
+        near_edge_kernel,
+        out_shape=(rows_shape, jax.ShapeDtypeStruct((parts, width, wide), f32)),
+        in_specs=[whole()] * 5,
         out_specs=(whole(), whole()),
-        compiler_params=pltpu.CompilerParams(vmem_limit_bytes=32 * 2**20),
-        name="edges",
-    )(far, near, edge, arm, basis, part)
+        compiler_params=limit,
+        cost_estimate=pl.CostEstimate(
+            flops=2 * tile * width * width, bytes_accessed=2**21, transcendentals=0
+        ),
+        name="near_edge",
+    )(near, edge, arm, basis, part)
+    far_rows, send = pl.pallas_call(
+        functools.partial(far_edge_kernel, orders),
+        out_shape=(rows_shape, jax.ShapeDtypeStruct((width, wide), bf16)),
+        in_specs=[whole()] * 5,
+        out_specs=(whole(), whole()),
+        compiler_params=limit,
+        name="far_edge",
+    )(far, edge, arm, basis, part)
     image, *keep = pl.pallas_call(
         functools.partial(keep_kernel, orders),
         out_shape=(
             jax.ShapeDtypeStruct((nrows, width), bf16),
             *([jax.ShapeDtypeStruct((width, wide), f32)] if halved else []),
         ),
-        in_specs=[whole(), whole(), whole(), whole(pl.ANY)],
+        in_specs=[whole(), whole(), whole(), whole(), whole(pl.ANY)],
         out_specs=(whole(pl.ANY), *([whole()] if halved else [])),
         scratch_shapes=[pltpu.SemaphoreType.DMA((2 * parts,))],
-        input_output_aliases={3: 0},
+        input_output_aliases={4: 0},
         compiler_params=pltpu.CompilerParams(vmem_limit_bytes=32 * 2**20),
         cost_estimate=pl.CostEstimate(
             flops=4 * tile * width * width, bytes_accessed=2**21, transcendentals=0
         ),
         name="kept_half",
-    )(basis, rows, part, image)
+    )(basis, near_rows, far_rows, part, image)
     if halved:
         got = lax.ppermute(send, "col", [(0, 1), (1, 0)])
         total = (keep[0] + got.astype(f32)).astype(bf16)

time: 27.8 us -> 29.9 us (1.076)
  local copies, waits for them, and re-layouts: 0.55 us -> 2.91 us
  starting transfers between devices: 4.9 us -> 3.93 us
  blocking collectives: 13.8 us -> 14.5 us
  Pallas kernels: 6.07 us -> 6.43 us
  waiting for transfers between devices: 0.74 us -> 0.41 us
    ppermute x1, starting transfers between devices: 4 us -> 0.52 us  [local(): near = lax.ppermute(near_send, AXES, swaps + [(j, i) for i, j in swaps])]
    ppermute x1, starting transfers between devices: 0.1 us -> 2.61 us  [local(): got = lax.ppermute(send, 'col', [(0, 1), (1, 0)])]
    unnamed x10 -> x12, local copies, waits for them, and re-layouts: 0.55 us -> 2.91 us
    all_to_all x1, blocking collectives: 13.8 us -> 14.5 us  [local(): lax.all_to_all(total, AXES, 0, 0, axis_index_groups=groups, tiled=True)]
    pallas_call x1 -> x2, Pallas kernels: 0.63 us -> 1.02 us  [the longest x1 0.53 us: local(): pl.pallas_call(functools.partial(far_edge_kernel, orders), out_shape=(row...]
    ppermute x1, waiting for transfers between devices: 0.73 us -> 0.41 us  [local(): got = lax.ppermute(send, 'col', [(0, 1), (1, 0)])]
  transfers between devices with their start and end apart: 3 -> 3, of which waited for: 1 -> 1; matrix products, arithmetic and copies ran while one was open for 0% -> 0% of each run, Pallas kernels for 17% -> 20%
where the time goes in v22:
time: 29.9 us; the launch traced here: 29.6 us
  blocking collectives  14.5 us (48%)
  Pallas kernels  6.43 us (22%)
  starting transfers between devices  3.93 us (13%)
  local copies, waits for them, and re-layouts  2.91 us (10%)
  between operations  0.76 us (3%)
  other arithmetic  0.72 us (2%)
  waiting for transfers between devices  0.41 us (1%)
    all_to_all x1, blocking collectives, local(): lax.all_to_all(total, AXES, 0, 0, axis_index_groups=groups, tiled=True)  14.5 us
    pallas_call x1, Pallas kernels, local(): pl.pallas_call(inner_kernel, out_shape=(jax.ShapeDtypeStruct((nrows, widt...  3.81 us
    unnamed x12, local copies, waits for them, and re-layouts  2.91 us
    ppermute x1, starting transfers between devices, local(): got = lax.ppermute(send, 'col', [(0, 1), (1, 0)])  2.61 us
    pallas_call x1, Pallas kernels, local(): pl.pallas_call(far_kernel, out_shape=edge_shape, in_specs=[whole(pltpu.HB...  0.84 us
    ppermute x1, starting transfers between devices, local(): far = lax.ppermute(far_send, AXES, swaps + [(j, i) for i, j in swaps])  0.8 us
    pallas_call x1, Pallas kernels, local(): pl.pallas_call(functools.partial(keep_kernel, orders), out_shape=(jax.Sha...  0.75 us
    mul x1, other arithmetic, local(): projected = jnp.sum(got.astype(f32), axis=0) * (1.0 / (nrows * count))  0.62 us
  transfers between devices with their start and end apart: 3, of which 1 were waited for; matrix products, arithmetic and copies ran while one was open for 0% of the time, Pallas kernels for 20%

profile of v22, /device:TPU:0, one launch (start us, length us, event | category | flops | bytes accessed | tf_op | source)
XLA Modules:
  0.0 29.6 jit_solution(13905319168247938930)
XLA Ops:
  0.6 0.0 copy-start
  0.6 1.4 %copy-done = bf16[1536,512]{1,0:T(8,128)(2,1)S(1)} copy-done((bf16[1536,512]{1,0:T(8,128)(2,1)S(1)}, bf16[1536,512]{1,0:T(8,128)(2,1)}, u32[]{:S(2)}) %copy-start) | copy-done | bytes 1572888
  2.1 0.5 %collective-permute-start = (bf16[128,512]{1,0:T(8,128)(2,1)S(1)}, bf16[128,512]{1,0:T(8,128)(2,1)S(1)}, u32[]{:S(2)}, u32[]{:S(2)}) collective-permute-start(bf16[128,512]{1,0:T(8,128)(2,1)S(1)} %near_rows.1), channel_id=1, source_target_pairs={{0,1},{2,3},{4,5},{6,7},{8,9},{10,11},{12,13},{14,15},{16,17},{18,... | collective-permute-start | bytes 393224 | tf_op jit(solution)/shard_map/ppermute | solution.py:274
  2.6 0.8 %far_rows.1.rows_ref = bf16[128,512]{1,0:T(8,128)(2,1)S(1)} custom-call(bf16[1536,512]{1,0:T(8,128)(2,1)} %basis_ref.9), custom_call_target="tpu_custom_call" | custom-call | tf_op jit(solution)/shard_map/far_rows/pallas_call | solution.py:242
  3.4 0.0 copy-start.1
  3.4 0.0 copy-start.2
  3.4 0.0 copy-start.3
  3.5 0.0 copy-start.4
  3.5 0.0 copy-start.5
  3.5 0.8 %collective-permute-start.1 = (bf16[128,512]{1,0:T(8,128)(2,1)S(1)}, bf16[128,512]{1,0:T(8,128)(2,1)S(1)}, u32[]{:S(2)}, u32[]{:S(2)}) collective-permute-start(bf16[128,512]{1,0:T(8,128)(2,1)S(1)} %hand_on.1), channel_id=1, source_target_pairs={{1,2},{3,4},{5,6},{7,8},{9,10},{11,12},{13,14},{15,16},{17,18},{19... | collective-permute-start | bytes 393224 | tf_op jit(solution)/shard_map/ppermute | solution.py:272
  4.3 0.5 %copy-done.1 = bf16[1536,512]{1,0:T(8,128)(2,1)S(1)} copy-done((bf16[1536,512]{1,0:T(8,128)(2,1)S(1)}, bf16[1536,512]{1,0:T(8,128)(2,1)}, u32[]{:S(2)}) %copy-start.1) | copy-done | bytes 1572888
  4.8 1.0 %copy-done.2 = bf16[24,8,64,64]{3,2,1,0:T(8,128)(2,1)S(1)} copy-done((bf16[24,8,64,64]{3,2,1,0:T(8,128)(2,1)S(1)}, bf16[24,8,64,64]{3,2,1,0:T(8,128)(2,1)}, u32[]{:S(2)}) %copy-start.2) | copy-done | bytes 1572888
  5.8 0.0 copy-done.5
  5.8 3.8 %inner.1 = (bf16[1536,512]{1,0:T(8,128)(2,1)}, f32[2,128,512]{2,1,0:T(8,128)S(1)}, bf16[2,256,128]{2,1,0:T(8,128)(2,1)S(1)}, f32[2,512,256]{2,1,0:T(8,128)S(1)}) custom-call(s32[8,24]{1,0:T(8,128)S(1)} %bitcast.4, s32[24]{0:T(128)S(1)} %copy-done.5, bf16[24,8,64,64]{3,2,1,0:T(8,128)(2,1)S(1)} %copy-done.2, bf16[1536,512]{1,0:T(8,128)(2,1)S(1)} %copy-done.1, ...), custom_call_target="tpu_custom_call" | custom-call | flops 2013265920 | bytes 8388608 | tf_op jit(solution)/shard_map/inner/pallas_call | solution.py:285
  9.6 0.0 collective-permute-done.near_ref
  9.6 0.5 %near_edge.1 = (bf16[2,128,256]{2,1,0:T(8,128)(2,1)S(1)}, f32[2,512,256]{2,1,0:T(8,128)S(1)}) custom-call(bf16[128,512]{1,0:T(8,128)(2,1)S(1)} %collective-permute-done.near_ref, f32[2,128,512]{2,1,0:T(8,128)S(1)} %get-tuple-element.12.edge_ref, bf16[2,256,128]{2,1,0:T(8,128)(2,1)S(1)} %get-tuple-element.13.arm_ref, bf16[1536,512]{1,0:T(8,128)(2,1)S(1)} %copy-done.1, ...), custom_call_target="tpu_custom_call" | custom-call | flops 67108864 | bytes 2097152 | tf_op jit(solution)/shard_map/near_edge/pallas_call | solution.py:316
  10.1 0.0 collective-permute-done.1.far_ref
  10.1 0.5 %far_edge.1 = (bf16[2,128,256]{2,1,0:T(8,128)(2,1)S(1)}, bf16[512,256]{1,0:T(8,128)(2,1)S(1)}) custom-call(bf16[128,512]{1,0:T(8,128)(2,1)S(1)} %collective-permute-done.1.far_ref, f32[2,128,512]{2,1,0:T(8,128)S(1)} %get-tuple-element.12.edge_ref, bf16[2,256,128]{2,1,0:T(8,128)(2,1)S(1)} %get-tuple-element.13.arm_ref, bf16[1536,512]{1,0:T(8,128)(2,1)S(1)} %copy-done.1, ...), custom_call_target="tpu_custom_call" | custom-call | tf_op jit(solution)/shard_map/far_edge/pallas_call | solution.py:327
  10.7 2.6 %collective-permute-start.2 = (bf16[512,256]{1,0:T(8,128)(2,1)S(1)}, bf16[512,256]{1,0:T(8,128)(2,1)S(1)}, u32[]{:S(2)}, u32[]{:S(2)}) collective-permute-start(bf16[512,256]{1,0:T(8,128)(2,1)S(1)} %get-tuple-element.21), channel_id=1, source_target_pairs={{0,1},{1,0},{2,3},{3,2},{4,5},{5,4},{6,7},{7,6},{8,9},{9,8},{10,11... | collective-permute-start | bytes 786440 | tf_op jit(solution)/shard_map/ppermute | solution.py:352
  13.3 0.7 %kept_half.1 = (bf16[1536,512]{1,0:T(8,128)(2,1)}, f32[512,256]{1,0:T(8,128)S(1)}) custom-call(bf16[1536,512]{1,0:T(8,128)(2,1)S(1)} %copy-done.1, bf16[2,128,256]{2,1,0:T(8,128)(2,1)S(1)} %get-tuple-element.15.near_ref, bf16[2,128,256]{2,1,0:T(8,128)(2,1)S(1)} %get-tuple-element.17.far_ref, ...), custom_call_target="tpu_custom_call", output_to_operand_aliasing={{0}: (4, {})} | custom-call | flops 134217728 | bytes 2097152 | tf_op jit(solution)/shard_map/kept_half/pallas_call | solution.py:335
  14.0 0.4 %collective-permute-done.2 = bf16[512,256]{1,0:T(8,128)(2,1)S(1)} collective-permute-done((bf16[512,256]{1,0:T(8,128)(2,1)S(1)}, bf16[512,256]{1,0:T(8,128)(2,1)S(1)}, u32[]{:S(2)}, u32[]{:S(2)}) %collective-permute-start.2) | collective-permute-done | bytes 262176 | tf_op jit(solution)/shard_map/ppermute | solution.py:352
  14.4 0.1 add_convert_fusion
  14.5 14.5 %all_to_all.5 = bf16[16,32,256]{2,1,0:T(8,128)(2,1)S(1)} all-to-all(bf16[16,32,256]{2,1,0:T(8,128)(2,1)S(1)} %bitcast.5), channel_id=1, replica_groups={{24,16,8,0,26,18,10,2,28,20,12,4,30,22,14,6},{25,17,9,1,31,23,15,7,29,2..., dimensions={0} | all-to-all | bytes 524288 | tf_op jit(solution)/shard_map/all_to_all | solution.py:356
  29.0 0.6 %broadcast_multiply_fusion = f32[32,256]{1,0:T(8,128)} fusion(f32[32,256]{1,0:T(8,128)S(1)} %convert_reduce_fusion), kind=kLoop, calls=%fused_computation.2 | loop fusion | flops 8192 | bytes 65536 | tf_op jit(solution)/shard_map/mul | solution.py:362
  (5 shorter events, 0.1 us)
Async XLA Ops:
  0.6 1.4 %copy-start = (bf16[1536,512]{1,0:T(8,128)(2,1)S(1)}, bf16[1536,512]{1,0:T(8,128)(2,1)}, u32[]{:S(2)}) copy-start(bf16[1536,512]{1,0:T(8,128)(2,1)} %basis_ref.9) | copy-start | bytes 4718596
  2.1 7.6 %collective-permute-start = (bf16[128,512]{1,0:T(8,128)(2,1)S(1)}, bf16[128,512]{1,0:T(8,128)(2,1)S(1)}, u32[]{:S(2)}, u32[]{:S(2)}) collective-permute-start(bf16[128,512]{1,0:T(8,128)(2,1)S(1)} %near_rows.1), channel_id=1, source_target_pairs={{0,1},{2,3},{4,5},{6,7},{8,9},{10,11},{12,13},{14,15},{16,17},{18,... | collective-permute-start | bytes 393224 | tf_op jit(solution)/shard_map/ppermute | solution.py:274
  3.4 1.4 %copy-start.1 = (bf16[1536,512]{1,0:T(8,128)(2,1)S(1)}, bf16[1536,512]{1,0:T(8,128)(2,1)}, u32[]{:S(2)}) copy-start(bf16[1536,512]{1,0:T(8,128)(2,1)} %basis_ref.9) | copy-start | bytes 4718596
  3.4 2.4 %copy-start.2 = (bf16[24,8,64,64]{3,2,1,0:T(8,128)(2,1)S(1)}, bf16[24,8,64,64]{3,2,1,0:T(8,128)(2,1)}, u32[]{:S(2)}) copy-start(bf16[24,8,64,64]{3,2,1,0:T(8,128)(2,1)} %jac_ref.1) | copy-start | bytes 4718596
  3.4 2.3 %copy-start.3 = (f32[1536]{0:T(1024)S(1)}, f32[1536]{0:T(1024)}, u32[]{:S(2)}) copy-start(f32[1536]{0:T(1024)} %param.9) | copy-start | bytes 18436
  3.5 2.3 %copy-start.4 = (s32[24,8]{0,1:T(8,128)S(1)}, s32[24,8]{0,1:T(8,128)}, u32[]{:S(2)}) copy-start(s32[24,8]{0,1:T(8,128)} %param.7) | copy-start | bytes 2308
  3.5 2.3 %copy-start.5 = (s32[24]{0:T(128)S(1)}, s32[24]{0:T(128)}, u32[]{:S(2)}) copy-start(s32[24]{0:T(128)} %live_ref.1) | copy-start | bytes 292
  3.5 6.6 %collective-permute-start.1 = (bf16[128,512]{1,0:T(8,128)(2,1)S(1)}, bf16[128,512]{1,0:T(8,128)(2,1)S(1)}, u32[]{:S(2)}, u32[]{:S(2)}) collective-permute-start(bf16[128,512]{1,0:T(8,128)(2,1)S(1)} %hand_on.1), channel_id=1, source_target_pairs={{1,2},{3,4},{5,6},{7,8},{9,10},{11,12},{13,14},{15,16},{17,18},{19... | collective-permute-start | bytes 393224 | tf_op jit(solution)/shard_map/ppermute | solution.py:272
  10.7 3.8 %collective-permute-start.2 = (bf16[512,256]{1,0:T(8,128)(2,1)S(1)}, bf16[512,256]{1,0:T(8,128)(2,1)S(1)}, u32[]{:S(2)}, u32[]{:S(2)}) collective-permute-start(bf16[512,256]{1,0:T(8,128)(2,1)S(1)} %get-tuple-element.21), channel_id=1, source_target_pairs={{0,1},{1,0},{2,3},{3,2},{4,5},{5,4},{6,7},{7,6},{8,9},{9,8},{10,11... | collective-permute-start | bytes 786440 | tf_op jit(solution)/shard_map/ppermute | solution.py:352

commit v23 on v21

--- a/solution.py
+++ b/solution.py
@@ -267,7 +267,7 @@
         orders = [list(range(down))] * 2
         if (width // down) % 16 == 0:
             lines = [[o * inner + i for o in reversed(range(outer))] for i in range(inner)]
-            orders = [sum(lines, []), sum(lines[:1] + lines[:0:-1], [])]
+            orders = [sum(lines[1:] + lines[:1], []), sum(lines[1::-1] + lines[:1:-1], [])]
     image, edge, arm, part = pl.pallas_call(
         inner_kernel,
         out_shape=(

time: 27.8 us -> 28.8 us (1.036)
  blocking collectives: 13.8 us -> 14.8 us
    all_to_all x1, blocking collectives: 13.8 us -> 14.8 us  [local(): lax.all_to_all(total, AXES, 0, 0, axis_index_groups=groups, tiled=True)]
  transfers between devices with their start and end apart: 3 -> 3, of which waited for: 1 -> 1; matrix products, arithmetic and copies ran while one was open for 0% -> 0% of each run, Pallas kernels for 17% -> 16%
where the time goes in v23:
time: 28.8 us; the launch traced here: 28.5 us
  blocking collectives  14.8 us (51%)
  Pallas kernels  6.05 us (21%)
  starting transfers between devices  4.9 us (17%)
  waiting for transfers between devices  0.75 us (3%)
  between operations  0.75 us (3%)
  other arithmetic  0.72 us (2%)
  local copies, waits for them, and re-layouts  0.55 us (2%)
    all_to_all x1, blocking collectives, local(): lax.all_to_all(total, AXES, 0, 0, axis_index_groups=groups, tiled=True)  14.8 us
    ppermute x1, starting transfers between devices, local(): near = lax.ppermute(near_send, AXES, swaps + [(j, i) for i, j in swaps])  4 us
    pallas_call x1, Pallas kernels, local(): pl.pallas_call(inner_kernel, out_shape=(jax.ShapeDtypeStruct((nrows, widt...  3.8 us
    pallas_call x1, Pallas kernels, local(): pl.pallas_call(far_kernel, out_shape=edge_shape, in_specs=[whole(pltpu.HB...  0.86 us
    ppermute x1, starting transfers between devices, local(): far = lax.ppermute(far_send, AXES, swaps + [(j, i) for i, j in swaps])  0.8 us
    ppermute x1, waiting for transfers between devices, local(): got = lax.ppermute(send, 'col', [(0, 1), (1, 0)])  0.75 us
    pallas_call x1, Pallas kernels, local(): pl.pallas_call(functools.partial(keep_kernel, orders), out_shape=(jax.Sha...  0.74 us
    pallas_call x1, Pallas kernels, local(): pl.pallas_call(functools.partial(edge_kernel, orders), out_shape=(jax.Sha...  0.63 us
  transfers between devices with their start and end apart: 3, of which 1 were waited for; matrix products, arithmetic and copies ran while one was open for 0% of the time, Pallas kernels for 16%

profile of v23, /device:TPU:0, one launch (start us, length us, event | category | flops | bytes accessed | tf_op | source)
XLA Modules:
  0.0 28.5 jit_solution(12141640107597477660)
XLA Ops:
  0.6 0.9 %far_rows.1.rows_ref = bf16[128,512]{1,0:T(8,128)(2,1)S(1)} custom-call(bf16[1536,512]{1,0:T(8,128)(2,1)} %basis_ref.7), custom_call_target="tpu_custom_call" | custom-call | tf_op jit(solution)/shard_map/far_rows/pallas_call | solution.py:228
  1.5 0.0 copy-start
  1.5 0.0 copy-start.1
  1.5 0.0 copy-start.2
  1.6 0.0 copy-start.3
  1.6 0.0 copy-start.4
  1.6 0.8 %collective-permute-start = (bf16[128,512]{1,0:T(8,128)(2,1)S(1)}, bf16[128,512]{1,0:T(8,128)(2,1)S(1)}, u32[]{:S(2)}, u32[]{:S(2)}) collective-permute-start(bf16[128,512]{1,0:T(8,128)(2,1)S(1)} %hand_on.1), channel_id=1, source_target_pairs={{1,2},{3,4},{5,6},{7,8},{9,10},{11,12},{13,14},{15,16},{17,18},{19... | collective-permute-start | bytes 393224 | tf_op jit(solution)/shard_map/ppermute | solution.py:258
  2.4 0.5 %copy-done = bf16[1536,512]{1,0:T(8,128)(2,1)S(1)} copy-done((bf16[1536,512]{1,0:T(8,128)(2,1)S(1)}, bf16[1536,512]{1,0:T(8,128)(2,1)}, u32[]{:S(2)}) %copy-start) | copy-done | bytes 1572888
  2.9 4.0 %collective-permute-start.1 = (bf16[128,512]{1,0:T(8,128)(2,1)S(1)}, bf16[128,512]{1,0:T(8,128)(2,1)S(1)}, u32[]{:S(2)}, u32[]{:S(2)}) collective-permute-start(bf16[128,512]{1,0:T(8,128)(2,1)S(1)} %near_rows.1), channel_id=1, source_target_pairs={{0,1},{2,3},{4,5},{6,7},{8,9},{10,11},{12,13},{14,15},{16,17},{18,... | collective-permute-start | bytes 393224 | tf_op jit(solution)/shard_map/ppermute | solution.py:260
  6.9 0.0 copy-done.1
  6.9 0.0 copy-done.2
  6.9 0.0 copy-done.3
  6.9 0.0 copy-done.4
  6.9 3.8 %inner.1 = (bf16[1536,512]{1,0:T(8,128)(2,1)}, f32[2,128,512]{2,1,0:T(8,128)S(1)}, bf16[2,256,128]{2,1,0:T(8,128)(2,1)S(1)}, f32[2,512,256]{2,1,0:T(8,128)S(1)}) custom-call(s32[8,24]{1,0:T(8,128)S(1)} %bitcast.4, s32[24]{0:T(128)S(1)} %copy-done.4, bf16[24,8,64,64]{3,2,1,0:T(8,128)(2,1)S(1)} %copy-done.1, bf16[1536,512]{1,0:T(8,128)(2,1)S(1)} %copy-done, ...), custom_call_target="tpu_custom_call" | custom-call | flops 2013265920 | bytes 8388608 | tf_op jit(solution)/shard_map/inner/pallas_call | solution.py:271
  10.7 0.0 collective-permute-done.far_ref
  10.8 0.0 collective-permute-done.1.near_ref
  10.8 0.6 %edges.1 = (bf16[2,256,256]{2,1,0:T(8,128)(2,1)S(1)}, bf16[512,256]{1,0:T(8,128)(2,1)S(1)}) custom-call(bf16[128,512]{1,0:T(8,128)(2,1)S(1)} %collective-permute-done.far_ref, bf16[128,512]{1,0:T(8,128)(2,1)S(1)} %collective-permute-done.1.near_ref, f32[2,128,512]{2,1,0:T(8,128)S(1)} %get-tuple-element.10.edge_ref, ...), custom_call_target="tpu_custom_call" | custom-call | tf_op jit(solution)/shard_map/edges/pallas_call | solution.py:300
  11.4 0.1 collective-permute-start.2
  11.5 0.7 %kept_half.1 = (bf16[1536,512]{1,0:T(8,128)(2,1)}, f32[512,256]{1,0:T(8,128)S(1)}) custom-call(bf16[1536,512]{1,0:T(8,128)(2,1)S(1)} %copy-done, bf16[2,256,256]{2,1,0:T(8,128)(2,1)S(1)} %get-tuple-element.13.rows_ref, f32[2,512,256]{2,1,0:T(8,128)S(1)} %get-tuple-element.12.part_ref, ...), custom_call_target="tpu_custom_call", output_to_operand_aliasing={{0}: (3, {})} | custom-call | flops 134217728 | bytes 2097152 | tf_op jit(solution)/shard_map/kept_half/pallas_call | solution.py:311
  12.3 0.7 %collective-permute-done.2 = bf16[512,256]{1,0:T(8,128)(2,1)S(1)} collective-permute-done((bf16[512,256]{1,0:T(8,128)(2,1)S(1)}, bf16[512,256]{1,0:T(8,128)(2,1)S(1)}, u32[]{:S(2)}, u32[]{:S(2)}) %collective-permute-start.2) | collective-permute-done | bytes 262176 | tf_op jit(solution)/shard_map/ppermute | solution.py:328
  13.0 0.1 add_convert_fusion
  13.1 14.8 %all_to_all.5 = bf16[16,32,256]{2,1,0:T(8,128)(2,1)S(1)} all-to-all(bf16[16,32,256]{2,1,0:T(8,128)(2,1)S(1)} %bitcast.5), channel_id=1, replica_groups={{26,18,10,2,28,20,12,4,30,22,14,6,24,16,8,0},{27,19,11,3,25,17,9,1,31,2..., dimensions={0} | all-to-all | bytes 524288 | tf_op jit(solution)/shard_map/all_to_all | solution.py:332
  27.9 0.6 %broadcast_multiply_fusion = f32[32,256]{1,0:T(8,128)} fusion(f32[32,256]{1,0:T(8,128)S(1)} %convert_reduce_fusion), kind=kLoop, calls=%fused_computation.2 | loop fusion | flops 8192 | bytes 65536 | tf_op jit(solution)/shard_map/mul | solution.py:338
  (3 shorter events, 0.1 us)
Async XLA Ops:
  1.5 1.4 %copy-start = (bf16[1536,512]{1,0:T(8,128)(2,1)S(1)}, bf16[1536,512]{1,0:T(8,128)(2,1)}, u32[]{:S(2)}) copy-start(bf16[1536,512]{1,0:T(8,128)(2,1)} %basis_ref.7) | copy-start | bytes 4718596
  1.5 5.4 %copy-start.1 = (bf16[24,8,64,64]{3,2,1,0:T(8,128)(2,1)S(1)}, bf16[24,8,64,64]{3,2,1,0:T(8,128)(2,1)}, u32[]{:S(2)}) copy-start(bf16[24,8,64,64]{3,2,1,0:T(8,128)(2,1)} %jac_ref.1) | copy-start | bytes 4718596
  1.5 5.4 %copy-start.2 = (f32[1536]{0:T(1024)S(1)}, f32[1536]{0:T(1024)}, u32[]{:S(2)}) copy-start(f32[1536]{0:T(1024)} %param.9) | copy-start | bytes 18436
  1.6 5.4 %copy-start.3 = (s32[24,8]{0,1:T(8,128)S(1)}, s32[24,8]{0,1:T(8,128)}, u32[]{:S(2)}) copy-start(s32[24,8]{0,1:T(8,128)} %param.7) | copy-start | bytes 2308
  1.6 5.4 %copy-start.4 = (s32[24]{0:T(128)S(1)}, s32[24]{0:T(128)}, u32[]{:S(2)}) copy-start(s32[24]{0:T(128)} %live_ref.1) | copy-start | bytes 292
  1.6 9.2 %collective-permute-start = (bf16[128,512]{1,0:T(8,128)(2,1)S(1)}, bf16[128,512]{1,0:T(8,128)(2,1)S(1)}, u32[]{:S(2)}, u32[]{:S(2)}) collective-permute-start(bf16[128,512]{1,0:T(8,128)(2,1)S(1)} %hand_on.1), channel_id=1, source_target_pairs={{1,2},{3,4},{5,6},{7,8},{9,10},{11,12},{13,14},{15,16},{17,18},{19... | collective-permute-start | bytes 393224 | tf_op jit(solution)/shard_map/ppermute | solution.py:258
  2.9 7.8 %collective-permute-start.1 = (bf16[128,512]{1,0:T(8,128)(2,1)S(1)}, bf16[128,512]{1,0:T(8,128)(2,1)S(1)}, u32[]{:S(2)}, u32[]{:S(2)}) collective-permute-start(bf16[128,512]{1,0:T(8,128)(2,1)S(1)} %near_rows.1), channel_id=1, source_target_pairs={{0,1},{2,3},{4,5},{6,7},{8,9},{10,11},{12,13},{14,15},{16,17},{18,... | collective-permute-start | bytes 393224 | tf_op jit(solution)/shard_map/ppermute | solution.py:260
  11.4 1.6 %collective-permute-start.2 = (bf16[512,256]{1,0:T(8,128)(2,1)S(1)}, bf16[512,256]{1,0:T(8,128)(2,1)S(1)}, u32[]{:S(2)}, u32[]{:S(2)}) collective-permute-start(bf16[512,256]{1,0:T(8,128)(2,1)S(1)} %get-tuple-element.17), channel_id=1, source_target_pairs={{0,1},{1,0},{2,3},{3,2},{4,5},{5,4},{6,7},{7,6},{8,9},{9,8},{10,11... | collective-permute-start | bytes 786440 | tf_op jit(solution)/shard_map/ppermute | solution.py:328

commit v24 on v23

--- a/solution.py
+++ b/solution.py
@@ -267,7 +267,7 @@
         orders = [list(range(down))] * 2
         if (width // down) % 16 == 0:
             lines = [[o * inner + i for o in reversed(range(outer))] for i in range(inner)]
-            orders = [sum(lines[1:] + lines[:1], []), sum(lines[1::-1] + lines[:1:-1], [])]
+            orders = [sum(lines[:1] + lines[:0:-1], []), sum(lines, [])]
     image, edge, arm, part = pl.pallas_call(
         inner_kernel,
         out_shape=(

time: 28.8 us -> 28.5 us (0.990)
  blocking collectives: 14.8 us -> 14.5 us
where the time goes in v24:
time: 28.5 us; the launch traced here: 28.2 us
  blocking collectives  14.5 us (51%)
  Pallas kernels  6.07 us (21%)
  starting transfers between devices  4.9 us (17%)
  between operations  0.75 us (3%)
  waiting for transfers between devices  0.74 us (3%)
  other arithmetic  0.72 us (3%)
  local copies, waits for them, and re-layouts  0.55 us (2%)
    all_to_all x1, blocking collectives, local(): lax.all_to_all(total, AXES, 0, 0, axis_index_groups=groups, tiled=True)  14.5 us
    ppermute x1, starting transfers between devices, local(): near = lax.ppermute(near_send, AXES, swaps + [(j, i) for i, j in swaps])  4 us
    pallas_call x1, Pallas kernels, local(): pl.pallas_call(inner_kernel, out_shape=(jax.ShapeDtypeStruct((nrows, widt...  3.8 us
    pallas_call x1, Pallas kernels, local(): pl.pallas_call(far_kernel, out_shape=edge_shape, in_specs=[whole(pltpu.HB...  0.86 us
    ppermute x1, starting transfers between devices, local(): far = lax.ppermute(far_send, AXES, swaps + [(j, i) for i, j in swaps])  0.8 us
    pallas_call x1, Pallas kernels, local(): pl.pallas_call(functools.partial(keep_kernel, orders), out_shape=(jax.Sha...  0.76 us
    ppermute x1, waiting for transfers between devices, local(): got = lax.ppermute(send, 'col', [(0, 1), (1, 0)])  0.73 us
    pallas_call x1, Pallas kernels, local(): pl.pallas_call(functools.partial(edge_kernel, orders), out_shape=(jax.Sha...  0.63 us
  transfers between devices with their start and end apart: 3, of which 1 were waited for; matrix products, arithmetic and copies ran while one was open for 0% of the time, Pallas kernels for 16%

profile of v24, /device:TPU:0, one launch (start us, length us, event | category | flops | bytes accessed | tf_op | source)
XLA Modules:
  0.0 28.2 jit_solution(6710643792316465777)
XLA Ops:
  0.6 0.9 %far_rows.1.rows_ref = bf16[128,512]{1,0:T(8,128)(2,1)S(1)} custom-call(bf16[1536,512]{1,0:T(8,128)(2,1)} %basis_ref.7), custom_call_target="tpu_custom_call" | custom-call | tf_op jit(solution)/shard_map/far_rows/pallas_call | solution.py:228
  1.5 0.0 copy-start
  1.5 0.0 copy-start.1
  1.5 0.0 copy-start.2
  1.6 0.0 copy-start.3
  1.6 0.0 copy-start.4
  1.6 0.8 %collective-permute-start = (bf16[128,512]{1,0:T(8,128)(2,1)S(1)}, bf16[128,512]{1,0:T(8,128)(2,1)S(1)}, u32[]{:S(2)}, u32[]{:S(2)}) collective-permute-start(bf16[128,512]{1,0:T(8,128)(2,1)S(1)} %hand_on.1), channel_id=1, source_target_pairs={{1,2},{3,4},{5,6},{7,8},{9,10},{11,12},{13,14},{15,16},{17,18},{19... | collective-permute-start | bytes 393224 | tf_op jit(solution)/shard_map/ppermute | solution.py:258
  2.4 0.5 %copy-done = bf16[1536,512]{1,0:T(8,128)(2,1)S(1)} copy-done((bf16[1536,512]{1,0:T(8,128)(2,1)S(1)}, bf16[1536,512]{1,0:T(8,128)(2,1)}, u32[]{:S(2)}) %copy-start) | copy-done | bytes 1572888
  2.9 4.0 %collective-permute-start.1 = (bf16[128,512]{1,0:T(8,128)(2,1)S(1)}, bf16[128,512]{1,0:T(8,128)(2,1)S(1)}, u32[]{:S(2)}, u32[]{:S(2)}) collective-permute-start(bf16[128,512]{1,0:T(8,128)(2,1)S(1)} %near_rows.1), channel_id=1, source_target_pairs={{0,1},{2,3},{4,5},{6,7},{8,9},{10,11},{12,13},{14,15},{16,17},{18,... | collective-permute-start | bytes 393224 | tf_op jit(solution)/shard_map/ppermute | solution.py:260
  6.9 0.0 copy-done.1
  6.9 0.0 copy-done.2
  6.9 0.0 copy-done.3
  6.9 0.0 copy-done.4
  6.9 3.8 %inner.1 = (bf16[1536,512]{1,0:T(8,128)(2,1)}, f32[2,128,512]{2,1,0:T(8,128)S(1)}, bf16[2,256,128]{2,1,0:T(8,128)(2,1)S(1)}, f32[2,512,256]{2,1,0:T(8,128)S(1)}) custom-call(s32[8,24]{1,0:T(8,128)S(1)} %bitcast.4, s32[24]{0:T(128)S(1)} %copy-done.4, bf16[24,8,64,64]{3,2,1,0:T(8,128)(2,1)S(1)} %copy-done.1, bf16[1536,512]{1,0:T(8,128)(2,1)S(1)} %copy-done, ...), custom_call_target="tpu_custom_call" | custom-call | flops 2013265920 | bytes 8388608 | tf_op jit(solution)/shard_map/inner/pallas_call | solution.py:271
  10.7 0.0 collective-permute-done.far_ref
  10.8 0.0 collective-permute-done.1.near_ref
  10.8 0.6 %edges.1 = (bf16[2,256,256]{2,1,0:T(8,128)(2,1)S(1)}, bf16[512,256]{1,0:T(8,128)(2,1)S(1)}) custom-call(bf16[128,512]{1,0:T(8,128)(2,1)S(1)} %collective-permute-done.far_ref, bf16[128,512]{1,0:T(8,128)(2,1)S(1)} %collective-permute-done.1.near_ref, f32[2,128,512]{2,1,0:T(8,128)S(1)} %get-tuple-element.10.edge_ref, ...), custom_call_target="tpu_custom_call" | custom-call | tf_op jit(solution)/shard_map/edges/pallas_call | solution.py:300
  11.4 0.1 collective-permute-start.2
  11.5 0.8 %kept_half.1 = (bf16[1536,512]{1,0:T(8,128)(2,1)}, f32[512,256]{1,0:T(8,128)S(1)}) custom-call(bf16[1536,512]{1,0:T(8,128)(2,1)S(1)} %copy-done, bf16[2,256,256]{2,1,0:T(8,128)(2,1)S(1)} %get-tuple-element.13.rows_ref, f32[2,512,256]{2,1,0:T(8,128)S(1)} %get-tuple-element.12.part_ref, ...), custom_call_target="tpu_custom_call", output_to_operand_aliasing={{0}: (3, {})} | custom-call | flops 134217728 | bytes 2097152 | tf_op jit(solution)/shard_map/kept_half/pallas_call | solution.py:311
  12.3 0.7 %collective-permute-done.2 = bf16[512,256]{1,0:T(8,128)(2,1)S(1)} collective-permute-done((bf16[512,256]{1,0:T(8,128)(2,1)S(1)}, bf16[512,256]{1,0:T(8,128)(2,1)S(1)}, u32[]{:S(2)}, u32[]{:S(2)}) %collective-permute-start.2) | collective-permute-done | bytes 262176 | tf_op jit(solution)/shard_map/ppermute | solution.py:328
  13.0 0.1 add_convert_fusion
  13.1 14.5 %all_to_all.5 = bf16[16,32,256]{2,1,0:T(8,128)(2,1)S(1)} all-to-all(bf16[16,32,256]{2,1,0:T(8,128)(2,1)S(1)} %bitcast.5), channel_id=1, replica_groups={{24,16,8,0,30,22,14,6,28,20,12,4,26,18,10,2},{25,17,9,1,27,19,11,3,29,2..., dimensions={0} | all-to-all | bytes 524288 | tf_op jit(solution)/shard_map/all_to_all | solution.py:332
  27.6 0.6 %broadcast_multiply_fusion = f32[32,256]{1,0:T(8,128)} fusion(f32[32,256]{1,0:T(8,128)S(1)} %convert_reduce_fusion), kind=kLoop, calls=%fused_computation.2 | loop fusion | flops 8192 | bytes 65536 | tf_op jit(solution)/shard_map/mul | solution.py:338
  (3 shorter events, 0.1 us)
Async XLA Ops:
  1.5 1.4 %copy-start = (bf16[1536,512]{1,0:T(8,128)(2,1)S(1)}, bf16[1536,512]{1,0:T(8,128)(2,1)}, u32[]{:S(2)}) copy-start(bf16[1536,512]{1,0:T(8,128)(2,1)} %basis_ref.7) | copy-start | bytes 4718596
  1.5 5.4 %copy-start.1 = (bf16[24,8,64,64]{3,2,1,0:T(8,128)(2,1)S(1)}, bf16[24,8,64,64]{3,2,1,0:T(8,128)(2,1)}, u32[]{:S(2)}) copy-start(bf16[24,8,64,64]{3,2,1,0:T(8,128)(2,1)} %jac_ref.1) | copy-start | bytes 4718596
  1.5 5.4 %copy-start.2 = (f32[1536]{0:T(1024)S(1)}, f32[1536]{0:T(1024)}, u32[]{:S(2)}) copy-start(f32[1536]{0:T(1024)} %param.9) | copy-start | bytes 18436
  1.6 5.4 %copy-start.3 = (s32[24,8]{0,1:T(8,128)S(1)}, s32[24,8]{0,1:T(8,128)}, u32[]{:S(2)}) copy-start(s32[24,8]{0,1:T(8,128)} %param.7) | copy-start | bytes 2308
  1.6 5.4 %copy-start.4 = (s32[24]{0:T(128)S(1)}, s32[24]{0:T(128)}, u32[]{:S(2)}) copy-start(s32[24]{0:T(128)} %live_ref.1) | copy-start | bytes 292
  1.6 9.2 %collective-permute-start = (bf16[128,512]{1,0:T(8,128)(2,1)S(1)}, bf16[128,512]{1,0:T(8,128)(2,1)S(1)}, u32[]{:S(2)}, u32[]{:S(2)}) collective-permute-start(bf16[128,512]{1,0:T(8,128)(2,1)S(1)} %hand_on.1), channel_id=1, source_target_pairs={{1,2},{3,4},{5,6},{7,8},{9,10},{11,12},{13,14},{15,16},{17,18},{19... | collective-permute-start | bytes 393224 | tf_op jit(solution)/shard_map/ppermute | solution.py:258
  2.9 7.8 %collective-permute-start.1 = (bf16[128,512]{1,0:T(8,128)(2,1)S(1)}, bf16[128,512]{1,0:T(8,128)(2,1)S(1)}, u32[]{:S(2)}, u32[]{:S(2)}) collective-permute-start(bf16[128,512]{1,0:T(8,128)(2,1)S(1)} %near_rows.1), channel_id=1, source_target_pairs={{0,1},{2,3},{4,5},{6,7},{8,9},{10,11},{12,13},{14,15},{16,17},{18,... | collective-permute-start | bytes 393224 | tf_op jit(solution)/shard_map/ppermute | solution.py:260
  11.4 1.6 %collective-permute-start.2 = (bf16[512,256]{1,0:T(8,128)(2,1)S(1)}, bf16[512,256]{1,0:T(8,128)(2,1)S(1)}, u32[]{:S(2)}, u32[]{:S(2)}) collective-permute-start(bf16[512,256]{1,0:T(8,128)(2,1)S(1)} %get-tuple-element.17), channel_id=1, source_target_pairs={{0,1},{1,0},{2,3},{3,2},{4,5},{5,4},{6,7},{7,6},{8,9},{9,8},{10,11... | collective-permute-start | bytes 786440 | tf_op jit(solution)/shard_map/ppermute | solution.py:328

commit v25 on v21

--- a/solution.py
+++ b/solution.py
@@ -324,18 +324,19 @@
         ),
         name="kept_half",
     )(basis, rows, part, image)
+    scale = 1.0 / (nrows * count)
     if halved:
         got = lax.ppermute(send, "col", [(0, 1), (1, 0)])
-        total = (keep[0] + got.astype(f32)).astype(bf16)
+        total = ((keep[0] + got.astype(f32)) * scale).astype(bf16)
         total = total.reshape(down, width // down, wide)
         groups = [[m * across + c for m in orders[c]] for c in range(across)]
         got = lax.all_to_all(total, AXES, 0, 0, axis_index_groups=groups, tiled=True)
     else:
-        total = send.reshape(down, width // down, across, width // across)
+        total = (send.astype(f32) * scale).astype(bf16).reshape(down, width // down, across, width // across)
         total = total.transpose(0, 2, 1, 3)
         total = total.reshape(count, width // down, width // across)
         got = lax.all_to_all(total, AXES, 0, 0, tiled=True)
-    projected = jnp.sum(got.astype(f32), axis=0) * (1.0 / (nrows * count))
+    projected = jnp.sum(got.astype(f32), axis=0)
     return (image, projected)
 
 

time: 27.8 us -> 27.8 us (level)
    mul x1 -> x0, other arithmetic: 0.62 us -> none  [local(): projected = jnp.sum(got.astype(f32), axis=0) * (1.0 / (nrows * count))]
    reduce_sum x1, other arithmetic: 0.04 us -> 0.66 us  [local(): projected = jnp.sum(got.astype(f32), axis=0)]
where the time goes in v25:
time: 27.8 us; the launch traced here: 27.6 us
  blocking collectives  13.8 us (50%)
  Pallas kernels  6.07 us (22%)
  starting transfers between devices  4.9 us (18%)
  between operations  0.75 us (3%)
  waiting for transfers between devices  0.74 us (3%)
  other arithmetic  0.72 us (3%)
  local copies, waits for them, and re-layouts  0.55 us (2%)
    all_to_all x1, blocking collectives, local(): lax.all_to_all(total, AXES, 0, 0, axis_index_groups=groups, tiled=True)  13.8 us
    ppermute x1, starting transfers between devices, local(): near = lax.ppermute(near_send, AXES, swaps + [(j, i) for i, j in swaps])  4 us
    pallas_call x1, Pallas kernels, local(): pl.pallas_call(inner_kernel, out_shape=(jax.ShapeDtypeStruct((nrows, widt...  3.8 us
    pallas_call x1, Pallas kernels, local(): pl.pallas_call(far_kernel, out_shape=edge_shape, in_specs=[whole(pltpu.HB...  0.86 us
    ppermute x1, starting transfers between devices, local(): far = lax.ppermute(far_send, AXES, swaps + [(j, i) for i, j in swaps])  0.8 us
    pallas_call x1, Pallas kernels, local(): pl.pallas_call(functools.partial(keep_kernel, orders), out_shape=(jax.Sha...  0.76 us
    ppermute x1, waiting for transfers between devices, local(): got = lax.ppermute(send, 'col', [(0, 1), (1, 0)])  0.73 us
    reduce_sum x1, other arithmetic, local(): projected = jnp.sum(got.astype(f32), axis=0)  0.66 us
  transfers between devices with their start and end apart: 3, of which 1 were waited for; matrix products, arithmetic and copies ran while one was open for 0% of the time, Pallas kernels for 17%

profile of v25, /device:TPU:0, one launch (start us, length us, event | category | flops | bytes accessed | tf_op | source)
XLA Modules:
  0.0 27.6 jit_solution(18295578775745043705)
XLA Ops:
  0.6 0.9 %far_rows.1.rows_ref = bf16[128,512]{1,0:T(8,128)(2,1)S(1)} custom-call(bf16[1536,512]{1,0:T(8,128)(2,1)} %basis_ref.7), custom_call_target="tpu_custom_call" | custom-call | tf_op jit(solution)/shard_map/far_rows/pallas_call | solution.py:228
  1.5 0.0 copy-start
  1.5 0.0 copy-start.1
  1.5 0.0 copy-start.2
  1.6 0.0 copy-start.3
  1.6 0.0 copy-start.4
  1.6 0.8 %collective-permute-start = (bf16[128,512]{1,0:T(8,128)(2,1)S(1)}, bf16[128,512]{1,0:T(8,128)(2,1)S(1)}, u32[]{:S(2)}, u32[]{:S(2)}) collective-permute-start(bf16[128,512]{1,0:T(8,128)(2,1)S(1)} %hand_on.1), channel_id=1, source_target_pairs={{1,2},{3,4},{5,6},{7,8},{9,10},{11,12},{13,14},{15,16},{17,18},{19... | collective-permute-start | bytes 393224 | tf_op jit(solution)/shard_map/ppermute | solution.py:258
  2.4 0.5 %copy-done = bf16[1536,512]{1,0:T(8,128)(2,1)S(1)} copy-done((bf16[1536,512]{1,0:T(8,128)(2,1)S(1)}, bf16[1536,512]{1,0:T(8,128)(2,1)}, u32[]{:S(2)}) %copy-start) | copy-done | bytes 1572888
  2.9 4.0 %collective-permute-start.1 = (bf16[128,512]{1,0:T(8,128)(2,1)S(1)}, bf16[128,512]{1,0:T(8,128)(2,1)S(1)}, u32[]{:S(2)}, u32[]{:S(2)}) collective-permute-start(bf16[128,512]{1,0:T(8,128)(2,1)S(1)} %near_rows.1), channel_id=1, source_target_pairs={{0,1},{2,3},{4,5},{6,7},{8,9},{10,11},{12,13},{14,15},{16,17},{18,... | collective-permute-start | bytes 393224 | tf_op jit(solution)/shard_map/ppermute | solution.py:260
  6.9 0.0 copy-done.1
  6.9 0.0 copy-done.2
  6.9 0.0 copy-done.3
  6.9 0.0 copy-done.4
  6.9 3.8 %inner.1 = (bf16[1536,512]{1,0:T(8,128)(2,1)}, f32[2,128,512]{2,1,0:T(8,128)S(1)}, bf16[2,256,128]{2,1,0:T(8,128)(2,1)S(1)}, f32[2,512,256]{2,1,0:T(8,128)S(1)}) custom-call(s32[8,24]{1,0:T(8,128)S(1)} %bitcast.4, s32[24]{0:T(128)S(1)} %copy-done.4, bf16[24,8,64,64]{3,2,1,0:T(8,128)(2,1)S(1)} %copy-done.1, bf16[1536,512]{1,0:T(8,128)(2,1)S(1)} %copy-done, ...), custom_call_target="tpu_custom_call" | custom-call | flops 2013265920 | bytes 8388608 | tf_op jit(solution)/shard_map/inner/pallas_call | solution.py:271
  10.7 0.0 collective-permute-done.far_ref
  10.8 0.0 collective-permute-done.1.near_ref
  10.8 0.6 %edges.1 = (bf16[2,256,256]{2,1,0:T(8,128)(2,1)S(1)}, bf16[512,256]{1,0:T(8,128)(2,1)S(1)}) custom-call(bf16[128,512]{1,0:T(8,128)(2,1)S(1)} %collective-permute-done.far_ref, bf16[128,512]{1,0:T(8,128)(2,1)S(1)} %collective-permute-done.1.near_ref, f32[2,128,512]{2,1,0:T(8,128)S(1)} %get-tuple-element.10.edge_ref, ...), custom_call_target="tpu_custom_call" | custom-call | tf_op jit(solution)/shard_map/edges/pallas_call | solution.py:300
  11.4 0.1 collective-permute-start.2
  11.5 0.8 %kept_half.1 = (bf16[1536,512]{1,0:T(8,128)(2,1)}, f32[512,256]{1,0:T(8,128)S(1)}) custom-call(bf16[1536,512]{1,0:T(8,128)(2,1)S(1)} %copy-done, bf16[2,256,256]{2,1,0:T(8,128)(2,1)S(1)} %get-tuple-element.13.rows_ref, f32[2,512,256]{2,1,0:T(8,128)S(1)} %get-tuple-element.12.part_ref, ...), custom_call_target="tpu_custom_call", output_to_operand_aliasing={{0}: (3, {})} | custom-call | flops 134217728 | bytes 2097152 | tf_op jit(solution)/shard_map/kept_half/pallas_call | solution.py:311
  12.3 0.7 %collective-permute-done.2 = bf16[512,256]{1,0:T(8,128)(2,1)S(1)} collective-permute-done((bf16[512,256]{1,0:T(8,128)(2,1)S(1)}, bf16[512,256]{1,0:T(8,128)(2,1)S(1)}, u32[]{:S(2)}, u32[]{:S(2)}) %collective-permute-start.2) | collective-permute-done | bytes 262176 | tf_op jit(solution)/shard_map/ppermute | solution.py:329
  13.0 0.1 multiply_convert_fusion
  13.1 13.8 %all_to_all.5 = bf16[16,32,256]{2,1,0:T(8,128)(2,1)S(1)} all-to-all(bf16[16,32,256]{2,1,0:T(8,128)(2,1)S(1)} %bitcast.5), channel_id=1, replica_groups={{24,16,8,0,26,18,10,2,28,20,12,4,30,22,14,6},{25,17,9,1,31,23,15,7,29,2..., dimensions={0} | all-to-all | bytes 524288 | tf_op jit(solution)/shard_map/all_to_all | solution.py:333
  26.9 0.7 %convert_reduce_fusion = f32[32,256]{1,0:T(8,128)} fusion(bf16[16,32,256]{2,1,0:T(8,128)(2,1)S(1)} %all_to_all.5), kind=kLoop, calls=%fused_computation | loop fusion | flops 253952 | bytes 294912 | tf_op jit(solution)/shard_map/reduce_sum | solution.py:339
  (2 shorter events, 0.0 us)
Async XLA Ops:
  1.5 1.4 %copy-start = (bf16[1536,512]{1,0:T(8,128)(2,1)S(1)}, bf16[1536,512]{1,0:T(8,128)(2,1)}, u32[]{:S(2)}) copy-start(bf16[1536,512]{1,0:T(8,128)(2,1)} %basis_ref.7) | copy-start | bytes 4718596
  1.5 5.4 %copy-start.1 = (bf16[24,8,64,64]{3,2,1,0:T(8,128)(2,1)S(1)}, bf16[24,8,64,64]{3,2,1,0:T(8,128)(2,1)}, u32[]{:S(2)}) copy-start(bf16[24,8,64,64]{3,2,1,0:T(8,128)(2,1)} %jac_ref.1) | copy-start | bytes 4718596
  1.5 5.4 %copy-start.2 = (f32[1536]{0:T(1024)S(1)}, f32[1536]{0:T(1024)}, u32[]{:S(2)}) copy-start(f32[1536]{0:T(1024)} %param.9) | copy-start | bytes 18436
  1.6 5.4 %copy-start.3 = (s32[24,8]{0,1:T(8,128)S(1)}, s32[24,8]{0,1:T(8,128)}, u32[]{:S(2)}) copy-start(s32[24,8]{0,1:T(8,128)} %param.7) | copy-start | bytes 2308
  1.6 5.4 %copy-start.4 = (s32[24]{0:T(128)S(1)}, s32[24]{0:T(128)}, u32[]{:S(2)}) copy-start(s32[24]{0:T(128)} %live_ref.1) | copy-start | bytes 292
  1.6 9.2 %collective-permute-start = (bf16[128,512]{1,0:T(8,128)(2,1)S(1)}, bf16[128,512]{1,0:T(8,128)(2,1)S(1)}, u32[]{:S(2)}, u32[]{:S(2)}) collective-permute-start(bf16[128,512]{1,0:T(8,128)(2,1)S(1)} %hand_on.1), channel_id=1, source_target_pairs={{1,2},{3,4},{5,6},{7,8},{9,10},{11,12},{13,14},{15,16},{17,18},{19... | collective-permute-start | bytes 393224 | tf_op jit(solution)/shard_map/ppermute | solution.py:258
  2.9 7.8 %collective-permute-start.1 = (bf16[128,512]{1,0:T(8,128)(2,1)S(1)}, bf16[128,512]{1,0:T(8,128)(2,1)S(1)}, u32[]{:S(2)}, u32[]{:S(2)}) collective-permute-start(bf16[128,512]{1,0:T(8,128)(2,1)S(1)} %near_rows.1), channel_id=1, source_target_pairs={{0,1},{2,3},{4,5},{6,7},{8,9},{10,11},{12,13},{14,15},{16,17},{18,... | collective-permute-start | bytes 393224 | tf_op jit(solution)/shard_map/ppermute | solution.py:260
  11.4 1.6 %collective-permute-start.2 = (bf16[512,256]{1,0:T(8,128)(2,1)S(1)}, bf16[512,256]{1,0:T(8,128)(2,1)S(1)}, u32[]{:S(2)}, u32[]{:S(2)}) collective-permute-start(bf16[512,256]{1,0:T(8,128)(2,1)S(1)} %get-tuple-element.17), channel_id=1, source_target_pairs={{0,1},{1,0},{2,3},{3,2},{4,5},{5,4},{6,7},{7,6},{8,9},{9,8},{10,11... | collective-permute-start | bytes 786440 | tf_op jit(solution)/shard_map/ppermute | solution.py:329

commit v26 on v25

--- a/solution.py
+++ b/solution.py
@@ -267,7 +267,7 @@
         orders = [list(range(down))] * 2
         if (width // down) % 16 == 0:
             lines = [[o * inner + i for o in reversed(range(outer))] for i in range(inner)]
-            orders = [sum(lines, []), sum(lines[:1] + lines[:0:-1], [])]
+            orders = [sum(lines, [])] * 2
     image, edge, arm, part = pl.pallas_call(
         inner_kernel,
         out_shape=(

time: 27.8 us -> 27.8 us (level)
  no operation moved by 1% of the time
where the time goes in v26:
time: 27.8 us; the launch traced here: 27.6 us
  blocking collectives  13.8 us (50%)
  Pallas kernels  6.07 us (22%)
  starting transfers between devices  4.9 us (18%)
  waiting for transfers between devices  0.74 us (3%)
  between operations  0.74 us (3%)
  other arithmetic  0.72 us (3%)
  local copies, waits for them, and re-layouts  0.55 us (2%)
    all_to_all x1, blocking collectives, local(): lax.all_to_all(total, AXES, 0, 0, axis_index_groups=groups, tiled=True)  13.8 us
    ppermute x1, starting transfers between devices, local(): near = lax.ppermute(near_send, AXES, swaps + [(j, i) for i, j in swaps])  4 us
    pallas_call x1, Pallas kernels, local(): pl.pallas_call(inner_kernel, out_shape=(jax.ShapeDtypeStruct((nrows, widt...  3.8 us
    pallas_call x1, Pallas kernels, local(): pl.pallas_call(far_kernel, out_shape=edge_shape, in_specs=[whole(pltpu.HB...  0.86 us
    ppermute x1, starting transfers between devices, local(): far = lax.ppermute(far_send, AXES, swaps + [(j, i) for i, j in swaps])  0.8 us
    pallas_call x1, Pallas kernels, local(): pl.pallas_call(functools.partial(keep_kernel, orders), out_shape=(jax.Sha...  0.76 us
    ppermute x1, waiting for transfers between devices, local(): got = lax.ppermute(send, 'col', [(0, 1), (1, 0)])  0.73 us
    reduce_sum x1, other arithmetic, local(): projected = jnp.sum(got.astype(f32), axis=0)  0.66 us
  transfers between devices with their start and end apart: 3, of which 1 were waited for; matrix products, arithmetic and copies ran while one was open for 0% of the time, Pallas kernels for 17%

profile of v26, /device:TPU:0, one launch (start us, length us, event | category | flops | bytes accessed | tf_op | source)
XLA Modules:
  0.0 27.6 jit_solution(17122768702471176059)
XLA Ops:
  0.6 0.9 %far_rows.1.rows_ref = bf16[128,512]{1,0:T(8,128)(2,1)S(1)} custom-call(bf16[1536,512]{1,0:T(8,128)(2,1)} %basis_ref.7), custom_call_target="tpu_custom_call" | custom-call | tf_op jit(solution)/shard_map/far_rows/pallas_call | solution.py:228
  1.5 0.0 copy-start
  1.5 0.0 copy-start.1
  1.5 0.0 copy-start.2
  1.6 0.0 copy-start.3
  1.6 0.0 copy-start.4
  1.6 0.8 %collective-permute-start = (bf16[128,512]{1,0:T(8,128)(2,1)S(1)}, bf16[128,512]{1,0:T(8,128)(2,1)S(1)}, u32[]{:S(2)}, u32[]{:S(2)}) collective-permute-start(bf16[128,512]{1,0:T(8,128)(2,1)S(1)} %hand_on.1), channel_id=1, source_target_pairs={{1,2},{3,4},{5,6},{7,8},{9,10},{11,12},{13,14},{15,16},{17,18},{19... | collective-permute-start | bytes 393224 | tf_op jit(solution)/shard_map/ppermute | solution.py:258
  2.4 0.5 %copy-done = bf16[1536,512]{1,0:T(8,128)(2,1)S(1)} copy-done((bf16[1536,512]{1,0:T(8,128)(2,1)S(1)}, bf16[1536,512]{1,0:T(8,128)(2,1)}, u32[]{:S(2)}) %copy-start) | copy-done | bytes 1572888
  2.9 4.0 %collective-permute-start.1 = (bf16[128,512]{1,0:T(8,128)(2,1)S(1)}, bf16[128,512]{1,0:T(8,128)(2,1)S(1)}, u32[]{:S(2)}, u32[]{:S(2)}) collective-permute-start(bf16[128,512]{1,0:T(8,128)(2,1)S(1)} %near_rows.1), channel_id=1, source_target_pairs={{0,1},{2,3},{4,5},{6,7},{8,9},{10,11},{12,13},{14,15},{16,17},{18,... | collective-permute-start | bytes 393224 | tf_op jit(solution)/shard_map/ppermute | solution.py:260
  6.9 0.0 copy-done.1
  6.9 0.0 copy-done.2
  6.9 0.0 copy-done.3
  6.9 0.0 copy-done.4
  6.9 3.8 %inner.1 = (bf16[1536,512]{1,0:T(8,128)(2,1)}, f32[2,128,512]{2,1,0:T(8,128)S(1)}, bf16[2,256,128]{2,1,0:T(8,128)(2,1)S(1)}, f32[2,512,256]{2,1,0:T(8,128)S(1)}) custom-call(s32[8,24]{1,0:T(8,128)S(1)} %bitcast.4, s32[24]{0:T(128)S(1)} %copy-done.4, bf16[24,8,64,64]{3,2,1,0:T(8,128)(2,1)S(1)} %copy-done.1, bf16[1536,512]{1,0:T(8,128)(2,1)S(1)} %copy-done, ...), custom_call_target="tpu_custom_call" | custom-call | flops 2013265920 | bytes 8388608 | tf_op jit(solution)/shard_map/inner/pallas_call | solution.py:271
  10.7 0.0 collective-permute-done.far_ref
  10.8 0.0 collective-permute-done.1.near_ref
  10.8 0.6 %edges.1 = (bf16[2,256,256]{2,1,0:T(8,128)(2,1)S(1)}, bf16[512,256]{1,0:T(8,128)(2,1)S(1)}) custom-call(bf16[128,512]{1,0:T(8,128)(2,1)S(1)} %collective-permute-done.far_ref, bf16[128,512]{1,0:T(8,128)(2,1)S(1)} %collective-permute-done.1.near_ref, f32[2,128,512]{2,1,0:T(8,128)S(1)} %get-tuple-element.10.edge_ref, ...), custom_call_target="tpu_custom_call" | custom-call | tf_op jit(solution)/shard_map/edges/pallas_call | solution.py:300
  11.4 0.1 collective-permute-start.2
  11.5 0.8 %kept_half.1 = (bf16[1536,512]{1,0:T(8,128)(2,1)}, f32[512,256]{1,0:T(8,128)S(1)}) custom-call(bf16[1536,512]{1,0:T(8,128)(2,1)S(1)} %copy-done, bf16[2,256,256]{2,1,0:T(8,128)(2,1)S(1)} %get-tuple-element.13.rows_ref, f32[2,512,256]{2,1,0:T(8,128)S(1)} %get-tuple-element.12.part_ref, ...), custom_call_target="tpu_custom_call", output_to_operand_aliasing={{0}: (3, {})} | custom-call | flops 134217728 | bytes 2097152 | tf_op jit(solution)/shard_map/kept_half/pallas_call | solution.py:311
  12.3 0.7 %collective-permute-done.2 = bf16[512,256]{1,0:T(8,128)(2,1)S(1)} collective-permute-done((bf16[512,256]{1,0:T(8,128)(2,1)S(1)}, bf16[512,256]{1,0:T(8,128)(2,1)S(1)}, u32[]{:S(2)}, u32[]{:S(2)}) %collective-permute-start.2) | collective-permute-done | bytes 262176 | tf_op jit(solution)/shard_map/ppermute | solution.py:329
  13.0 0.1 multiply_convert_fusion
  13.1 13.8 %all_to_all.5 = bf16[16,32,256]{2,1,0:T(8,128)(2,1)S(1)} all-to-all(bf16[16,32,256]{2,1,0:T(8,128)(2,1)S(1)} %bitcast.5), channel_id=1, replica_groups={{24,16,8,0,26,18,10,2,28,20,12,4,30,22,14,6},{25,17,9,1,27,19,11,3,29,2..., dimensions={0} | all-to-all | bytes 524288 | tf_op jit(solution)/shard_map/all_to_all | solution.py:333
  26.9 0.7 %convert_reduce_fusion = f32[32,256]{1,0:T(8,128)} fusion(bf16[16,32,256]{2,1,0:T(8,128)(2,1)S(1)} %all_to_all.5), kind=kLoop, calls=%fused_computation | loop fusion | flops 253952 | bytes 294912 | tf_op jit(solution)/shard_map/reduce_sum | solution.py:339
  (2 shorter events, 0.0 us)
Async XLA Ops:
  1.5 1.4 %copy-start = (bf16[1536,512]{1,0:T(8,128)(2,1)S(1)}, bf16[1536,512]{1,0:T(8,128)(2,1)}, u32[]{:S(2)}) copy-start(bf16[1536,512]{1,0:T(8,128)(2,1)} %basis_ref.7) | copy-start | bytes 4718596
  1.5 5.4 %copy-start.1 = (bf16[24,8,64,64]{3,2,1,0:T(8,128)(2,1)S(1)}, bf16[24,8,64,64]{3,2,1,0:T(8,128)(2,1)}, u32[]{:S(2)}) copy-start(bf16[24,8,64,64]{3,2,1,0:T(8,128)(2,1)} %jac_ref.1) | copy-start | bytes 4718596
  1.5 5.4 %copy-start.2 = (f32[1536]{0:T(1024)S(1)}, f32[1536]{0:T(1024)}, u32[]{:S(2)}) copy-start(f32[1536]{0:T(1024)} %param.9) | copy-start | bytes 18436
  1.6 5.4 %copy-start.3 = (s32[24,8]{0,1:T(8,128)S(1)}, s32[24,8]{0,1:T(8,128)}, u32[]{:S(2)}) copy-start(s32[24,8]{0,1:T(8,128)} %param.7) | copy-start | bytes 2308
  1.6 5.4 %copy-start.4 = (s32[24]{0:T(128)S(1)}, s32[24]{0:T(128)}, u32[]{:S(2)}) copy-start(s32[24]{0:T(128)} %live_ref.1) | copy-start | bytes 292
  1.6 9.2 %collective-permute-start = (bf16[128,512]{1,0:T(8,128)(2,1)S(1)}, bf16[128,512]{1,0:T(8,128)(2,1)S(1)}, u32[]{:S(2)}, u32[]{:S(2)}) collective-permute-start(bf16[128,512]{1,0:T(8,128)(2,1)S(1)} %hand_on.1), channel_id=1, source_target_pairs={{1,2},{3,4},{5,6},{7,8},{9,10},{11,12},{13,14},{15,16},{17,18},{19... | collective-permute-start | bytes 393224 | tf_op jit(solution)/shard_map/ppermute | solution.py:258
  2.9 7.8 %collective-permute-start.1 = (bf16[128,512]{1,0:T(8,128)(2,1)S(1)}, bf16[128,512]{1,0:T(8,128)(2,1)S(1)}, u32[]{:S(2)}, u32[]{:S(2)}) collective-permute-start(bf16[128,512]{1,0:T(8,128)(2,1)S(1)} %near_rows.1), channel_id=1, source_target_pairs={{0,1},{2,3},{4,5},{6,7},{8,9},{10,11},{12,13},{14,15},{16,17},{18,... | collective-permute-start | bytes 393224 | tf_op jit(solution)/shard_map/ppermute | solution.py:260
  11.4 1.6 %collective-permute-start.2 = (bf16[512,256]{1,0:T(8,128)(2,1)S(1)}, bf16[512,256]{1,0:T(8,128)(2,1)S(1)}, u32[]{:S(2)}, u32[]{:S(2)}) collective-permute-start(bf16[512,256]{1,0:T(8,128)(2,1)S(1)} %get-tuple-element.17), channel_id=1, source_target_pairs={{0,1},{1,0},{2,3},{3,2},{4,5},{5,4},{6,7},{7,6},{8,9},{9,8},{10,11... | collective-permute-start | bytes 786440 | tf_op jit(solution)/shard_map/ppermute | solution.py:329
